TPU v7x, 32 devices: a whole 2x2x4 slice. The times are simulated.
32 devices in a mesh: group: 2 (over x), wide: 8 (over z, y), narrow: 2 (over core).
Axes of the slice: x: 2, y: 2, z: 4, core: 2. Of those that a mesh axis runs over, the one named last changes fastest.
Arguments:
- voxels: bfloat16 [65536, 512], P(('group', 'wide', 'narrow')), parts along dimension 0, may hold values from -6 to 6
- w_qkv: bfloat16 [512, 1536], replicated, may hold values from -0.25 to 0.25
- w_out: bfloat16 [512, 512], replicated, may hold values from -0.25 to 0.25
- w_feature: bfloat16 [512, 256], replicated, may hold values from -0.25 to 0.25
- conv_first: bfloat16 [3, 3, 256, 256], replicated, may hold values from -0.125 to 0.125
- conv_second: bfloat16 [3, 3, 256, 256], replicated, may hold values from -0.125 to 0.125
- row_brick: int32 [512, 1], P(('group', 'wide', 'narrow')), parts along dimension 0, may hold values from 0 to 7; in each aligned block of 16 rows (0 to 15, 16 to 31, ...) at most 4 rows name the same one
- cell_place: int32 [65536], P(('group', 'wide', 'narrow')), parts along dimension 0, may hold values from 0 to 255
Outputs:
- flow_field: float32 [128, 64, 256], P(('group', 'wide'), 'narrow'), parts along dimension 0
There are 2 independent parts, one for each index of `group`. A program takes and returns all parts, laid end to end along the dimension named above; an argument that names none is the same for every part. Nothing has to cross between parts.
Inputs may be any that keep to these rules, and one draw needn't show every extreme that they name: `row_brick`: within the rows of one device (16 rows in a row), no brick row is named more than 4 times, and some brick row exactly 4 times.
All inputs are finite; a program needn't handle non-finite values.
Results may differ from a plain program's by a relative error of at most 0.014.
Values may be sent and summed in bfloat16 or wider, within the bound.
No kernel may reach another device: no remote copies, remote signals or barrier semaphores. Data moves between devices by JAX's collectives and lax.ppermute only.
A program may use at most 128 MiB of HBM per device.

v0:
```python
import jax
import jax.numpy as jnp
from jax import lax
from jax.sharding import PartitionSpec as P

D = 512
HEADS = 4
HEAD = 128
PF = 256
ROW = 128
BLK = 256
BX = 8
BY = 32


epsilon = 1e-06
layout_names = ("NHWC", "HWIO", "NHWC")


def prefix_2(array, axis, combine, identity):
    count, place = (lax.axis_size(axis), lax.axis_index(axis))
    everything = lax.all_gather(array.astype(jnp.bfloat16), axis)
    start = jnp.broadcast_to(jnp.asarray(identity, array.dtype), array.shape)

    def hop(k, before):
        reached = k < place
        new = combine(before, everything[k].astype(array.dtype))
        return jnp.where(reached, new, before)

    return lax.fori_loop(0, count, hop, start)


def with_halo(array, sides, width):
    for axis, dim in sides:
        count, length = (lax.axis_size(axis), array.shape[dim])
        up = [(i, (i + 1) % count) for i in range(count - 1)]
        down = [(j, i) for i, j in up]
        last = lax.slice_in_dim(array, length - width, length, axis=dim)
        leading = lax.slice_in_dim(array, 0, width, axis=dim)
        before = lax.ppermute(last, axis, up)
        after = lax.ppermute(leading, axis, down)
        array = jnp.concatenate([before, array, after], axis=dim)
    return array


def convolve_valid(padded, weight):
    return lax.conv_general_dilated(
        padded[None],
        weight,
        (1, 1),
        "VALID",
        dimension_numbers=layout_names,
        preferred_element_type=jnp.float32,
    )[0]


def add_states(earlier, later):
    return earlier + later


def per_device(voxels, w_qkv, w_out, w_feature, conv_first, conv_second, row_brick, cell_place):
    token_count = voxels.shape[0]
    block_count = token_count // BLK
    projected = jnp.dot(voxels, w_qkv, preferred_element_type=jnp.float32).astype(jnp.bfloat16)
    split_rows = projected.reshape(block_count, BLK, 3, HEADS, HEAD)
    query_rows = split_rows[:, :, 0]
    key_rows = split_rows[:, :, 1]
    value_rows = split_rows[:, :, 2]
    block_states = jnp.einsum(
        "bshd,bshe->bhde", key_rows, value_rows, preferred_element_type=jnp.float32
    )
    own_total = jnp.sum(block_states, axis=0)
    zero_state = jnp.zeros_like(own_total)
    prefix = prefix_2(own_total, ("wide", "narrow"), add_states, zero_state)
    within = jnp.concatenate(
        [jnp.zeros_like(block_states[:1]), jnp.cumsum(block_states, axis=0)[:-1]], axis=0
    )
    start_states = prefix[None] + within
    carried = jnp.einsum(
        "bthd,bhde->bthe",
        query_rows.astype(jnp.float32),
        start_states,
        precision=lax.Precision.HIGHEST,
    )
    causal_mask = jnp.arange(BLK)[:, None] >= jnp.arange(BLK)[None, :]
    scores = jnp.einsum("bthd,bshd->bhts", query_rows, key_rows, preferred_element_type=jnp.float32)
    scores = jnp.where(causal_mask[None, None], scores, 0.0).astype(jnp.bfloat16)
    local_part = jnp.einsum(
        "bhts,bshe->bthe", scores, value_rows, preferred_element_type=jnp.float32
    )
    attended = (carried + local_part).reshape(token_count, HEADS, HEAD)
    mean_square = jnp.mean(attended * attended, axis=-1, keepdims=True)
    normed = (
        (attended * lax.rsqrt(mean_square + epsilon)).astype(jnp.bfloat16).reshape(token_count, D)
    )
    hidden = (
        voxels.astype(jnp.float32) + jnp.dot(normed, w_out, preferred_element_type=jnp.float32)
    ).astype(jnp.bfloat16)
    rows_local = token_count // ROW
    brick_rows = row_brick[:, 0]
    wide_count = lax.axis_size("wide")
    slot_most = max(2, 2 * rows_local // wide_count)
    onehot = (brick_rows[:, None] == jnp.arange(wide_count, dtype=jnp.int32)[None, :]).astype(
        jnp.int32
    )
    slot_rank = jnp.sum((jnp.cumsum(onehot, axis=0) - onehot) * onehot, axis=1)
    cell_count = BX * BY
    place_rows = cell_place.reshape(rows_local, ROW)
    send_place = (
        jnp.full((wide_count, slot_most, ROW), cell_count, jnp.int32)
        .at[brick_rows, slot_rank]
        .set(place_rows)
    )
    features = jnp.dot(hidden, w_feature, preferred_element_type=jnp.float32).astype(jnp.bfloat16)
    payload = features.reshape(rows_local, ROW, PF)
    send_rows = (
        jnp.zeros((wide_count, slot_most, ROW, PF), jnp.bfloat16)
        .at[brick_rows, slot_rank]
        .set(payload)
    )
    received, received_place = (
        lax.all_to_all(send_rows, "wide", split_axis=0, concat_axis=0, tiled=True),
        lax.all_to_all(send_place, "wide", split_axis=0, concat_axis=0, tiled=True),
    )
    gathered_features = received.reshape(-1, PF)
    pooled = jax.ops.segment_sum(
        gathered_features.astype(jnp.float32),
        received_place.reshape(-1),
        num_segments=cell_count + 1,
    )
    pooled = pooled[:cell_count].astype(jnp.bfloat16).reshape(BX, BY, PF)
    extended = with_halo(pooled, (("wide", 0), ("narrow", 1)), 1)
    inner_field = jax.nn.gelu(convolve_valid(extended, conv_first), approximate=True).astype(
        jnp.bfloat16
    )
    inner_extended = with_halo(inner_field, (("wide", 0), ("narrow", 1)), 1)
    flow_field = convolve_valid(inner_extended, conv_second)
    return flow_field


def solution(mesh):
    placed = (
        P(("group", "wide", "narrow"), None),
        P(),
        P(),
        P(),
        P(),
        P(),
        P(("group", "wide", "narrow"), None),
        P(("group", "wide", "narrow")),
    )
    return jax.shard_map(
        per_device,
        mesh=mesh,
        in_specs=placed,
        out_specs=P(("group", "wide"), "narrow", None),
        check_vma=False,
    )
```

profile of v0, /device:TPU:0, one launch (start us, length us, event | category | flops | bytes accessed | tf_op | source)
XLA Modules:
  0.0 239.5 jit_solution(4230859452679784016)
XLA Ops:
  6.5 1.4 copy-done
  7.9 7.1 %convolution_convert_fusion = bf16[2048,1536]{1,0:T(8,128)(2,1)} fusion(bf16[2048,512]{1,0:T(8,128)(2,1)} %param.10, bf16[512,1536]{1,0:T(8,128)(2,1)S(1)} %copy-done), kind=kOutput, calls=%fused_computation.5 | convolution fusion | flops 3224371200 | bytes 9961472 | tf_op jit(solution)/shard_map/dot_general | solution.py:64
  15.0 11.3 %reshape.77 = bf16[8,256,3,4,128]{4,3,2,1,0:T(4,128)(2,1)} reshape(bf16[2048,1536]{1,0:T(8,128)(2,1)} %convolution_convert_fusion) | data formatting | bytes 12582912 | tf_op jit(solution)/shard_map/reshape | solution.py:65
  26.4 5.4 %fusion.51 = (bf16[8,256,1,4,128]{4,3,2,1,0:T(4,128)(2,1)}, bf16[8,256,1,4,128]{4,3,2,1,0:T(4,128)(2,1)}, bf16[8,256,1,4,128]{4,3,2,1,0:T(4,128)(2,1)}) fusion(bf16[8,256,3,4,128]{4,3,2,1,0:T(4,128)(2,1)} %reshape.77), kind=kLoop, calls=%fused_computation.85 | loop fusion | bytes 12582912 | tf_op jit(solution)/shard_map/slice | solution.py:66
  31.7 4.2 %copy.49 = bf16[8,256,1,4,128]{1,4,3,0,2:T(8,128)(2,1)} copy(bf16[8,256,1,4,128]{4,3,2,1,0:T(4,128)(2,1)} %get-tuple-element.109) | data formatting | bytes 4194304
  35.9 5.0 %fusion.53 = (bf16[4,128,128]{2,1,0:T(8,128)(2,1)}, f32[8,4,128,128]{3,2,1,0:T(8,128)}) fusion(bf16[8,256,1,4,128]{4,3,2,1,0:T(4,128)(2,1)} %get-tuple-element.110, bf16[8,256,1,4,128]{1,4,3,0,2:T(8,128)(2,1)} %copy.49), kind=kOutput, calls=%fused_computation.87 | convolution fusion | flops 268894208 | bytes 6422528 | tf_op jit(solution)/shard_map/bshd,bshe->bhde/dot_general | solution.py:69
  41.9 2.3 scatter_fusion
  44.1 7.3 %all-to-all-start = ((s32[8,4,128]{2,1,0:T(4,128)}), s32[8,4,128]{2,1,0:T(4,128)S(1)}, u32[]{:S(2)}, u32[]{:S(2)}) async-start(s32[8,4,128]{2,1,0:T(4,128)} %scatter_fusion), calls=%async_computation | async-start | bytes 32768 | tf_op jit(solution)/shard_map/all_to_all | solution.py:123
  51.4 1.8 fusion.54
  53.2 1.4 slice.73
  54.6 7.4 %fusion = f32[8,4,128,256]{3,2,1,0:T(8,128)} fusion(pred[256,256]{1,0:T(8,128)(4,1)S(1)} %iota_compare_fusion.1, bf16[8,256,1,4,128]{1,4,3,0,2:T(8,128)(2,1)} %copy.49, bf16[8,256,1,4,128]{4,3,2,1,0:T(4,128)(2,1)} %get-tuple-element.110, bf16[8,256,1,4,128]{4,3,2,1,0:T(4,128)(2,1)} %get-tuple-element.108), kind=kOutput, calls=%fused_computation.6 | convolution fusion | flops 1077936128 | bytes 10551296 | tf_op jit(solution)/shard_map/bhts,bshe->bthe/dot_general | solution.py:88
  62.0 23.3 %all-gather.3.cloned.1.call-done = bf16[64,128,128]{2,1,0:T(8,128)(2,1)} async-done(((bf16[4,128,128]{2,1,0:T(8,128)(2,1)}), bf16[64,128,128]{2,1,0:T(8,128)(2,1)}) %all-gather.3.cloned.1.call-update) | async-done | bytes 2097168 | tf_op jit(solution)/shard_map/all_gather | solution.py:22
  85.3 17.1 %while.14 = (s32[]{:T(128)}, f32[4,128,128]{2,1,0:T(8,128)S(1)}, s32[]{:T(128)}, bf16[16,4,128,128]{3,2,1,0:T(8,128)(2,1)}, s32[]{:T(128)}, /*index=5*/s32[]{:T(128)}) while((s32[]{:T(128)}, f32[4,128,128]{2,1,0:T(8,128)S(1)}, s32[]{:T(128)}, bf16[16,4,128,128]{3,2,1,0:T(8,128)(2,1)}, s32[]{:T(128)}, /*index=5*/s32[]{:T(128)}) %tuple.45), condition=%wide.region_5.6_spmd.clone, body=%wide.region_4.5_spmd.clone.sunk | while | flops 262148 | bytes 655453 | solution.py:30
  86.3 1.0 add_select_fusion.2
  87.4 1.0 add_select_fusion.2
  88.4 1.0 add_select_fusion.2
  89.5 1.0 add_select_fusion.2
  90.6 1.0 add_select_fusion.2
  91.6 1.0 add_select_fusion.2
  92.7 1.0 add_select_fusion.2
  93.8 1.0 add_select_fusion.2
  94.8 1.0 add_select_fusion.2
  95.9 1.0 add_select_fusion.2
  96.9 1.0 add_select_fusion.2
  98.0 1.0 add_select_fusion.2
  100.1 1.0 add_select_fusion.2
  101.2 1.0 add_select_fusion.2
  102.4 5.8 %multiply_reduce_fusion = (f32[8,256,4]{1,2,0:T(4,128)S(1)}, f32[8,256,4,128]{1,3,2,0:T(8,128)S(1)}) fusion(f32[8,4,128,256]{3,2,1,0:T(8,128)} %fusion, bf16[8,256,1,4,128]{4,3,2,1,0:T(4,128)(2,1)} %get-tuple-element.108, f32[7,4,128,128]{3,2,1,0:T(8,128)} %slice.73, f32[4,128,128]{2,1,0:T(8,128)S(1)} %get-tuple-element.84), kind=kOutput, calls=%fused_computation.12 | convolution fusion | flops 1614274560 | bytes 12615680 | tf_op jit(solution)/shard_map/bthd,bhde->bthe/dot_general | solution.py:79
  108.2 2.4 %copy.34 = f32[8,256,4,128]{1,0,3,2:T(8,128)S(1)} copy(f32[8,256,4,128]{1,3,2,0:T(8,128)S(1)} %get-tuple-element.122) | data formatting | bytes 8388608 | tf_op jit(solution)/shard_map/add | solution.py:91
  110.7 2.0 copy.52
  112.7 1.9 fusion.3
  114.5 4.2 %convolution_convert_fusion.1 = bf16[2048,256]{1,0:T(8,128)(2,1)S(1)} fusion(bf16[512,256]{1,0:T(8,128)(2,1)S(1)} %copy-done.6, bf16[2048,512]{1,0:T(8,128)(2,1)} %param.10, bf16[2048,512]{0,1:T(8,128)(2,1)} %fusion.3, bf16[512,512]{1,0:T(8,128)(2,1)S(1)} %copy-done.5), kind=kOutput, calls=%fused_computation.17 | convolution fusion | flops 1614282752 | bytes 6029312 | tf_op jit(solution)/shard_map/dot_general | solution.py:114
  118.7 1.6 broadcast_in_dim.43
  120.3 3.2 %scatter_fusion.1 = bf16[8,4,128,256]{3,2,1,0:T(8,128)(2,1)} fusion(bf16[8,4,128,256]{3,2,1,0:T(8,128)(2,1)} %broadcast_in_dim.43, s32[16]{0:T(128)S(1)} %fusion.42, bf16[16,128,256]{2,1,0:T(8,128)(2,1)S(1)} %bitcast.95), kind=kCustom, calls=%fused_computation.1 | custom fusion | bytes 3145856 | tf_op jit(solution)/shard_map/scatter | solution.py:119
  123.5 53.2 %all_to_all.10 = bf16[8,4,128,256]{3,2,1,0:T(8,128)(2,1)} all-to-all(bf16[8,4,128,256]{3,2,1,0:T(8,128)(2,1)} %scatter_fusion.1), channel_id=1, replica_groups=mesh['group'=2,'wide'=8,'narrow'=2] {'wide'}, dimensions={0} | all-to-all | bytes 4194304 | tf_op jit(solution)/shard_map/all_to_all | solution.py:122
  176.7 27.3 %scatter_custom_fusion.2 = f32[257,256]{1,0:T(8,128)S(1)} fusion(s32[4096]{0:T(1024)S(1)} %bitcast.98, bf16[4096,256]{1,0:T(8,128)(2,1)} %bitcast.89, f32[]{:T(128)} %constant.53.clone.1), kind=kCustom, calls=%fused_computation.7 | custom fusion | flops 2097152 | bytes 2360324 | tf_op jit(solution)/shard_map/scatter-add | solution.py:126
  204.1 1.4 collective-permute-start
  205.5 1.3 collective-permute-start.1
  206.9 4.2 %collective-permute-done.1 = bf16[1,32,256]{2,1,0:T(8,128)(2,1)S(1)} collective-permute-done((bf16[1,32,256]{2,1,0:T(8,128)(2,1)S(1)}, bf16[1,32,256]{2,1,0:T(8,128)(2,1)S(1)}, u32[]{:S(2)}, u32[]{:S(2)}) %collective-permute-start.1) | collective-permute-done | bytes 16416 | tf_op jit(solution)/shard_map/ppermute | solution.py:41
  211.2 1.3 collective-permute-start.2
  212.5 1.3 collective-permute-start.3
  213.8 1.8 collective-permute-done.3
  216.7 4.0 %collective-permute-start.4 = (bf16[1,32,256]{2,0,1:T(2,128)(2,1)S(1)}, bf16[1,32,256]{2,0,1:T(2,128)(2,1)S(1)}, u32[]{:S(2)}, u32[]{:S(2)}) collective-permute-start(bf16[1,32,256]{2,0,1:T(2,128)(2,1)S(1)} %get-tuple-element.117), channel_id=1, source_target_pairs={{0,2},{2,4},{4,6},{6,8},{8,10},{10,12},{12,14},{1,3},{3,5},{5,7},{... | collective-permute-start | bytes 49160 | tf_op jit(solution)/shard_map/ppermute | solution.py:40
  220.7 1.3 collective-permute-start.5
  222.3 4.2 %collective-permute-done.5 = bf16[1,32,256]{2,0,1:T(2,128)(2,1)S(1)} collective-permute-done((bf16[1,32,256]{2,0,1:T(2,128)(2,1)S(1)}, bf16[1,32,256]{2,0,1:T(2,128)(2,1)S(1)}, u32[]{:S(2)}, u32[]{:S(2)}) %collective-permute-start.5) | collective-permute-done | bytes 16416 | tf_op jit(solution)/shard_map/ppermute | solution.py:41
  226.5 1.3 collective-permute-start.6
  227.8 1.3 collective-permute-start.7
  229.1 1.8 collective-permute-done.7
  (54 shorter events, 6.3 us)
Async XLA Ops:
  6.5 1.4 copy-start
  6.5 78.7 %all-gather.3.cloned.1.call-start = ((), (), s32[]{:S(2)}) async-start(), calls=%async_computation.2 | async-start | bytes 2228224 | tf_op jit(solution)/shard_map/all_gather | solution.py:22
  35.9 5.0 %copy-start.2 = (s32[16,1]{0,1:T(1,128)S(1)}, s32[16,1]{0,1:T(1,128)}, u32[]{:S(2)}) copy-start(s32[16,1]{0,1:T(1,128)} %param.16) | copy-start | bytes 196
  35.9 5.9 %copy-start.1 = (s32[2048]{0:T(1024)S(1)}, s32[2048]{0:T(1024)}, u32[]{:S(2)}) copy-start(s32[2048]{0:T(1024)} %param.17) | copy-start | bytes 24580
  44.1 79.4 %all-to-all-start = ((s32[8,4,128]{2,1,0:T(4,128)}), s32[8,4,128]{2,1,0:T(4,128)S(1)}, u32[]{:S(2)}, u32[]{:S(2)}) async-start(s32[8,4,128]{2,1,0:T(4,128)} %scatter_fusion), calls=%async_computation | async-start | bytes 32768 | tf_op jit(solution)/shard_map/all_to_all | solution.py:123
  112.7 1.9 copy-start.5
  112.7 1.9 copy-start.6
  176.7 39.1 %copy-start.7 = (pred[8,5]{0,1:T(8,128)(4,1)S(1)}, pred[8,5]{0,1:T(8,128)(4,1)}, u32[]{:S(2)}) copy-start(pred[8,5]{0,1:T(8,128)(4,1)} %constant.79) | copy-start | bytes 124
  204.0 11.8 %copy-start.3 = (bf16[3,3,256,256]{3,2,1,0:T(8,128)(2,1)S(1)}, bf16[3,3,256,256]{3,2,1,0:T(8,128)(2,1)}, u32[]{:S(2)}) copy-start(bf16[3,3,256,256]{3,2,1,0:T(8,128)(2,1)} %param.14) | copy-start | bytes 3538948
  204.1 2.9 %collective-permute-start = (bf16[1,32,256]{2,1,0:T(8,128)(2,1)S(1)}, bf16[1,32,256]{2,1,0:T(8,128)(2,1)S(1)}, u32[]{:S(2)}, u32[]{:S(2)}) collective-permute-start(bf16[1,32,256]{2,1,0:T(8,128)(2,1)S(1)} %get-tuple-element.115), channel_id=1, source_target_pairs={{0,2},{2,4},{4,6},{6,8},{8,10},{10,12},{12,14},{1,3},{3,5},{5,7},{... | collective-permute-start | bytes 49160 | tf_op jit(solution)/shard_map/ppermute | solution.py:40
  205.5 5.6 %collective-permute-start.1 = (bf16[1,32,256]{2,1,0:T(8,128)(2,1)S(1)}, bf16[1,32,256]{2,1,0:T(8,128)(2,1)S(1)}, u32[]{:S(2)}, u32[]{:S(2)}) collective-permute-start(bf16[1,32,256]{2,1,0:T(8,128)(2,1)S(1)} %get-tuple-element.116), channel_id=1, source_target_pairs={{2,0},{4,2},{6,4},{8,6},{10,8},{12,10},{14,12},{3,1},{5,3},{7,5},{... | collective-permute-start | bytes 49160 | tf_op jit(solution)/shard_map/ppermute | solution.py:41
  211.2 2.6 %collective-permute-start.2 = (bf16[10,1,256]{2,1,0:T(2,128)(2,1)S(1)}, bf16[10,1,256]{2,1,0:T(2,128)(2,1)S(1)}, u32[]{:S(2)}, u32[]{:S(2)}) collective-permute-start(bf16[10,1,256]{2,1,0:T(2,128)(2,1)S(1)} %get-tuple-element.113), channel_id=1, source_target_pairs={{0,1},{2,3},{4,5},{6,7},{8,9},{10,11},{12,13},{14,15},{16,17},{18,... | collective-permute-start | bytes 15368 | tf_op jit(solution)/shard_map/ppermute | solution.py:40
  212.5 3.1 %collective-permute-start.3 = (bf16[10,1,256]{2,1,0:T(2,128)(2,1)S(1)}, bf16[10,1,256]{2,1,0:T(2,128)(2,1)S(1)}, u32[]{:S(2)}, u32[]{:S(2)}) collective-permute-start(bf16[10,1,256]{2,1,0:T(2,128)(2,1)S(1)} %get-tuple-element.114), channel_id=1, source_target_pairs={{1,0},{3,2},{5,4},{7,6},{9,8},{11,10},{13,12},{15,14},{17,16},{19,... | collective-permute-start | bytes 15368 | tf_op jit(solution)/shard_map/ppermute | solution.py:41
  216.4 14.7 %copy-start.4 = (bf16[3,3,256,256]{3,2,1,0:T(8,128)(2,1)S(1)}, bf16[3,3,256,256]{3,2,1,0:T(8,128)(2,1)}, u32[]{:S(2)}) copy-start(bf16[3,3,256,256]{3,2,1,0:T(8,128)(2,1)} %param.15) | copy-start | bytes 3538948
  216.7 5.6 %collective-permute-start.4 = (bf16[1,32,256]{2,0,1:T(2,128)(2,1)S(1)}, bf16[1,32,256]{2,0,1:T(2,128)(2,1)S(1)}, u32[]{:S(2)}, u32[]{:S(2)}) collective-permute-start(bf16[1,32,256]{2,0,1:T(2,128)(2,1)S(1)} %get-tuple-element.117), channel_id=1, source_target_pairs={{0,2},{2,4},{4,6},{6,8},{8,10},{10,12},{12,14},{1,3},{3,5},{5,7},{... | collective-permute-start | bytes 49160 | tf_op jit(solution)/shard_map/ppermute | solution.py:40
  220.7 5.8 %collective-permute-start.5 = (bf16[1,32,256]{2,0,1:T(2,128)(2,1)S(1)}, bf16[1,32,256]{2,0,1:T(2,128)(2,1)S(1)}, u32[]{:S(2)}, u32[]{:S(2)}) collective-permute-start(bf16[1,32,256]{2,0,1:T(2,128)(2,1)S(1)} %get-tuple-element.118), channel_id=1, source_target_pairs={{2,0},{4,2},{6,4},{8,6},{10,8},{12,10},{14,12},{3,1},{5,3},{7,5},{... | collective-permute-start | bytes 49160 | tf_op jit(solution)/shard_map/ppermute | solution.py:41
  226.5 2.6 %collective-permute-start.6 = (bf16[10,1,256]{2,0,1:T(8,128)(2,1)S(1)}, bf16[10,1,256]{2,0,1:T(8,128)(2,1)S(1)}, u32[]{:S(2)}, u32[]{:S(2)}) collective-permute-start(bf16[10,1,256]{2,0,1:T(8,128)(2,1)S(1)} %get-tuple-element.111), channel_id=1, source_target_pairs={{0,1},{2,3},{4,5},{6,7},{8,9},{10,11},{12,13},{14,15},{16,17},{18,... | collective-permute-start | bytes 15368 | tf_op jit(solution)/shard_map/ppermute | solution.py:40
  227.8 3.1 %collective-permute-start.7 = (bf16[10,1,256]{2,0,1:T(8,128)(2,1)S(1)}, bf16[10,1,256]{2,0,1:T(8,128)(2,1)S(1)}, u32[]{:S(2)}, u32[]{:S(2)}) collective-permute-start(bf16[10,1,256]{2,0,1:T(8,128)(2,1)S(1)} %get-tuple-element.112), channel_id=1, source_target_pairs={{1,0},{3,2},{5,4},{7,6},{9,8},{11,10},{13,12},{15,14},{17,16},{19,... | collective-permute-start | bytes 15368 | tf_op jit(solution)/shard_map/ppermute | solution.py:41
Sparse Core Ops, SparseCore 0:
  41.1 44.1 all-gather.2
where the time goes:
time: 241 us; the launch traced here: 239 us
  blocking collectives  53.2 us (22%)
  other arithmetic  48.3 us (20%)
  local copies, waits for them, and re-layouts  37.1 us (15%)
  waiting for transfers between devices  35.6 us (15%)
  matrix products  30.6 us (13%)
  starting transfers between devices  20.4 us (8%)
  between operations  13.8 us (6%)
    all_to_all x1, blocking collectives, per_device(): lax.all_to_all(send_rows, 'wide', split_axis=0, concat_axis=0, tiled=True)  53.2 us
    scatter-add x1, other arithmetic, per_device(): jax.ops.segment_sum(gathered_features.astype(jnp.float32), received_place...  27.3 us
    all_gather x1, waiting for transfers between devices, prefix_2(): everything = lax.all_gather(array.astype(jnp.bfloat16), axis)  23.3 us
    select_n x16, other arithmetic, hop(): return jnp.where(reached, new, before)  16.6 us
    ppermute x4, waiting for transfers between devices, with_halo(): after = lax.ppermute(leading, axis, down)  12 us
    reshape x1, local copies, waits for them, and re-layouts, per_device(): split_rows = projected.reshape(block_count, BLK, 3, HEADS, HEAD)  11.3 us
    ppermute x4, starting transfers between devices, with_halo(): before = lax.ppermute(last, axis, up)  7.97 us
    unnamed x18, local copies, waits for them, and re-layouts  7.6 us
  transfers between devices with their start and end apart: 10, of which 7 were waited for; matrix products, arithmetic and copies ran while one was open for 21% of the time, Pallas kernels for 0%

commit v1 on v0

v1 whole, which is shorter than its diff:
```python
import functools

import jax
import jax.numpy as jnp
from jax import lax
from jax.experimental import pallas as pl
from jax.experimental.pallas import tpu as pltpu
from jax.sharding import PartitionSpec as P

HEADS = 4
HEAD = 128
ROW = 128
BLK = 256
BX = 8
BY = 32
EPS = 1e-06
LINE = BY + 16

F32 = jnp.float32
BF16 = jnp.bfloat16


def dot(a, b):
    return jnp.dot(a, b, preferred_element_type=F32)


def dot_t(a, b):
    return lax.dot_general(a, b, (((0,), (0,)), ((), ())), preferred_element_type=F32)


def dot_nt(a, b):
    return lax.dot_general(a, b, (((1,), (1,)), ((), ())), preferred_element_type=F32)


def params(mib=48):
    return pltpu.CompilerParams(vmem_limit_bytes=mib << 20)


def head_cols(h):
    return slice(h * HEAD, (h + 1) * HEAD)


def key_value_kernel(x_ref, wk_ref, wv_ref, k_ref, v_ref, total_ref, acc):
    step = pl.program_id(0)

    @pl.when(step == 0)
    def _():
        acc[...] = jnp.zeros_like(acc)

    x = x_ref[...]
    k = dot(x, wk_ref[...]).astype(BF16)
    v = dot(x, wv_ref[...]).astype(BF16)
    k_ref[...] = k
    v_ref[...] = v
    for pair in range(HEADS // 2):
        cols = slice(pair * 2 * HEAD, (pair + 1) * 2 * HEAD)
        outer = dot_t(k[:, cols], v[:, cols])
        acc[2 * pair] += outer[:HEAD, :HEAD]
        acc[2 * pair + 1] += outer[HEAD:, HEAD:]

    @pl.when(step == pl.num_programs(0) - 1)
    def _():
        total_ref[...] = acc[...].astype(BF16)


def key_value(voxels, w_qkv, block):
    tokens, width = voxels.shape
    inner = HEADS * HEAD
    tile = pl.BlockSpec((block, inner), lambda i: (i, 0))
    return pl.pallas_call(
        key_value_kernel,
        grid=(tokens // block,),
        in_specs=[
            pl.BlockSpec((block, width), lambda i: (i, 0)),
            pl.BlockSpec((width, inner), lambda i: (0, 1)),
            pl.BlockSpec((width, inner), lambda i: (0, 2)),
        ],
        out_specs=[tile, tile, pl.BlockSpec((HEADS, HEAD, HEAD), lambda i: (0, 0, 0))],
        out_shape=[
            jax.ShapeDtypeStruct((tokens, inner), BF16),
            jax.ShapeDtypeStruct((tokens, inner), BF16),
            jax.ShapeDtypeStruct((HEADS, HEAD, HEAD), BF16),
        ],
        scratch_shapes=[pltpu.VMEM((HEADS, HEAD, HEAD), F32)],
        compiler_params=params(),
        name="key_value",
    )(voxels, w_qkv, w_qkv)


def local_kernel(x_ref, wq_ref, k_ref, v_ref, q_ref, part_ref, state):
    step = pl.program_id(0)

    @pl.when(step == 0)
    def _():
        state[...] = jnp.zeros_like(state)

    q = dot(x_ref[...], wq_ref[...]).astype(BF16)
    q_ref[...] = q
    causal = lax.broadcasted_iota(jnp.int32, (BLK, BLK), 0) >= lax.broadcasted_iota(
        jnp.int32, (BLK, BLK), 1
    )
    for h in range(HEADS):
        cols = head_cols(h)
        qh, kh, vh = q[:, cols], k_ref[:, cols], v_ref[:, cols]
        scores = jnp.where(causal, dot_nt(qh, kh), 0.0).astype(BF16)
        part_ref[:, cols] = dot(scores, vh) + dot(qh, state[h].astype(BF16))
        state[h] += dot_t(kh, vh)


def local_attention(voxels, w_qkv, k, v):
    tokens, width = voxels.shape
    inner = HEADS * HEAD
    tile = pl.BlockSpec((BLK, inner), lambda i: (i, 0))
    return pl.pallas_call(
        local_kernel,
        grid=(tokens // BLK,),
        in_specs=[
            pl.BlockSpec((BLK, width), lambda i: (i, 0)),
            pl.BlockSpec((width, inner), lambda i: (0, 0)),
            tile,
            tile,
        ],
        out_specs=[tile, tile],
        out_shape=[
            jax.ShapeDtypeStruct((tokens, inner), BF16),
            jax.ShapeDtypeStruct((tokens, inner), F32),
        ],
        scratch_shapes=[pltpu.VMEM((HEADS, HEAD, HEAD), F32)],
        compiler_params=params(),
        cost_estimate=pl.CostEstimate(
            flops=2 * tokens * inner * (width + 2 * BLK + 2 * HEAD),
            bytes_accessed=tokens * inner * 12,
            transcendentals=0,
        ),
        name="local_attention",
    )(voxels, w_qkv, k, v)


def finish_kernel(
    orders, brick_ref, q_ref, part_ref, x_ref, state_ref, wo_ref, wf_ref, place_ref, *refs
):
    outs, acc, normed = refs[:-2], refs[-2], refs[-1]
    step = pl.program_id(0)

    @pl.when(step == 0)
    def _():
        acc[...] = jnp.zeros_like(acc)

    for h in range(HEADS):
        cols = head_cols(h)
        attended = part_ref[:, cols] + dot(q_ref[:, cols], state_ref[h])
        mean_square = jnp.mean(attended * attended, axis=-1, keepdims=True)
        normed[:, cols] = (attended * lax.rsqrt(mean_square + EPS)).astype(BF16)
    hidden = (x_ref[...].astype(F32) + dot(normed[...], wo_ref[...])).astype(BF16)
    features = dot(hidden, wf_ref[...]).astype(BF16)
    cells = BX * BY
    rows = place_ref.shape[0]
    for r in range(rows):
        here = lax.broadcasted_iota(jnp.int32, (cells, ROW), 0) == place_ref[r]
        onehot = jnp.where(here, 1.0, 0.0).astype(BF16)
        acc[brick_ref[step * rows + r]] += dot(onehot, features[r * ROW : (r + 1) * ROW])

    @pl.when(step == pl.num_programs(0) - 1)
    def _():
        bricks = acc.shape[0]
        half_cells = cells // 2
        for part, order in enumerate(orders):
            for i in range(bricks):
                place = 0
                for bit in order:
                    place = 2 * place + ((i >> bit) & 1)
                which, slot = divmod(place, bricks // 2)
                outs[2 * part + which][slot] = acc[
                    i, part * half_cells : (part + 1) * half_cells
                ].astype(BF16)


def finish(q, part, voxels, state, w_out, w_feature, places, bricks, count, orders, block):
    tokens, width = voxels.shape
    inner = HEADS * HEAD
    channels = w_feature.shape[1]
    cells = BX * BY
    rows = block // ROW
    tile = lambda cols: pl.BlockSpec((block, cols), lambda i, *_: (i, 0))
    whole = lambda array: pl.BlockSpec(array.shape, lambda i, *_: (0,) * array.ndim)
    out = jax.ShapeDtypeStruct((count // 2, cells // 2, channels), BF16)
    return pl.pallas_call(
        functools.partial(finish_kernel, orders),
        grid_spec=pltpu.PrefetchScalarGridSpec(
            num_scalar_prefetch=1,
            grid=(tokens // block,),
            in_specs=[
                tile(inner),
                tile(inner),
                tile(width),
                whole(state),
                whole(w_out),
                whole(w_feature),
                pl.BlockSpec((rows, 1, ROW), lambda i, *_: (i, 0, 0)),
            ],
            out_specs=[whole(out)] * 4,
            scratch_shapes=[
                pltpu.VMEM((count, cells, channels), F32),
                pltpu.VMEM((block, inner), BF16),
            ],
        ),
        out_shape=[out] * 4,
        compiler_params=params(),
        name="finish",
    )(bricks, q, part, voxels, state, w_out, w_feature, places)


def field_kernel(
    edge_ref, own_ref, above_ref, below_ref, left_ref, right_ref, w1_ref, w2_ref, out_ref, field, wide
):
    lines = BX + 4
    shown = wide.shape[0]
    field[...] = jnp.zeros_like(field)
    for r in range(lines):
        at = 16 + r * LINE
        if r < 2:
            line = above_ref[r]
        elif r < BX + 2:
            line = own_ref[r - 2]
        else:
            line = below_ref[r - BX - 2]
        field[at : at + BY] = line.astype(F32)
        field[at - 2 : at] = left_ref[r].astype(F32)
        field[at + BY : at + BY + 2] = right_ref[r].astype(F32)

    channels = field.shape[1]

    def widen():
        for shift in range(3):
            wide[:, shift * channels : (shift + 1) * channels] = field[
                7 + shift : 7 + shift + shown
            ].astype(BF16)

    def convolve(w_ref, first, count):
        return sum(
            dot(wide[(first + dy - 1) * LINE : (first + dy - 1 + count) * LINE], w_ref[dy])
            for dy in range(3)
        )

    widen()
    inner = jax.nn.gelu(convolve(w1_ref, 1, BX + 2), approximate=True)
    column = lax.broadcasted_iota(jnp.int32, (LINE, 1), 0) - 8
    inside = (column >= edge_ref[2]) & (column < edge_ref[3])
    for r in range(1, BX + 3):
        keep = inside
        if r == 1:
            keep = keep & (edge_ref[0] == 0)
        if r == BX + 2:
            keep = keep & (edge_ref[1] == 0)
        field[8 + r * LINE : 8 + (r + 1) * LINE] = jnp.where(
            keep, inner[(r - 1) * LINE : r * LINE], 0.0
        )
    widen()
    flow = convolve(w2_ref, 2, BX)
    for r in range(BX):
        out_ref[r] = flow[r * LINE + 8 : r * LINE + 8 + BY]


def field_flow(edges, own, above, below, left, right, conv_first, conv_second):
    channels = own.shape[-1]
    vmem = pl.BlockSpec(memory_space=pltpu.VMEM)
    lines = BX + 4
    return pl.pallas_call(
        field_kernel,
        in_specs=[pl.BlockSpec(memory_space=pltpu.SMEM)] + [vmem] * 7,
        out_specs=vmem,
        out_shape=jax.ShapeDtypeStruct((BX, BY, channels), F32),
        scratch_shapes=[
            pltpu.VMEM((16 + lines * LINE, channels), F32),
            pltpu.VMEM((lines * LINE, 3 * channels), BF16),
        ],
        compiler_params=params(),
        name="field_flow",
    )(
        edges,
        own,
        above,
        below,
        left,
        right,
        conv_first.reshape(3, 3 * channels, channels),
        conv_second.reshape(3, 3 * channels, channels),
    )


def swap(array, axis, bit):
    count = lax.axis_size(axis)
    return lax.ppermute(array, axis, [(i, i ^ (1 << bit)) for i in range(count)])


def shift(array, axis, by):
    count = lax.axis_size(axis)
    return lax.ppermute(
        array, axis, [(i, i + by) for i in range(count) if 0 <= i + by < count]
    )


def exclusive_state(total):
    count, place = lax.axis_size("narrow"), lax.axis_index("narrow")
    shares = total.reshape(count, -1, HEAD, HEAD)
    pieces = []
    for k in range(count):
        if k == 0:
            pieces.append(lax.dynamic_index_in_dim(shares, place, 0, keepdims=False))
            continue
        target = lax.rem(place + k, count)
        out = lax.dynamic_index_in_dim(shares, target, 0, keepdims=False)
        pieces.append(lax.ppermute(out, "narrow", [(i, (i + k) % count) for i in range(count)]))
    pieces = [piece.astype(F32) for piece in pieces]
    running = sum(pieces)
    before = jnp.zeros_like(running)
    devices, position = lax.axis_size("wide"), lax.axis_index("wide")
    for bit in range(devices.bit_length() - 1):
        other = swap(running.astype(BF16), "wide", bit).astype(F32)
        before = before + jnp.where((position >> bit) & 1 == 1, other, 0.0)
        running = running + other
    result = []
    for k in range(count):
        receiver = lax.rem(place + k, count)
        value = before
        for j in range(count):
            source = lax.rem(place - j + count, count)
            value = value + jnp.where(source < receiver, pieces[j], 0.0)
        value = value.astype(BF16)
        if k > 0:
            value = lax.ppermute(value, "narrow", [(i, (i + k) % count) for i in range(count)])
        result.append(value)
    stacked = jnp.stack(result)
    order = jnp.array([(p - h) % count for p in range(count) for h in range(count)]).reshape(
        count, count
    )
    whole = stacked[order[place]] if count > 2 else jnp.where(
        place == 0, stacked, stacked[::-1]
    )
    return whole.reshape(HEADS, HEAD, HEAD)


def reduce_bricks(parts, orders):
    parts = [list(pair) for pair in parts]
    for level in range(len(orders[0])):
        arrived = [
            swap(gone, "wide", order[level]) for (_, gone), order in zip(parts, orders)
        ]
        for pair, more in zip(parts, arrived):
            total = (pair[0].astype(F32) + more.astype(F32)).astype(BF16)
            half = total.shape[0] // 2
            pair[0], pair[1] = total[:half] if half else total, total[half:]
    return [pair[0] if pair[0].shape[0] else pair[1] for pair in parts]


def per_device(voxels, w_qkv, w_out, w_feature, conv_first, conv_second, row_brick, cell_place):
    tokens = voxels.shape[0]
    channels = w_feature.shape[1]
    wide_count, wide_place = lax.axis_size("wide"), lax.axis_index("wide")
    narrow_count, narrow_place = lax.axis_size("narrow"), lax.axis_index("narrow")
    block = min(512, tokens)

    k, v, total = key_value(voxels, w_qkv, block)
    state = exclusive_state(total)
    q, part = local_attention(voxels, w_qkv, k, v)

    bits = list(range(wide_count.bit_length() - 1))
    orders = [bits, bits[1::-1] + bits[2:]]
    bricks = row_brick[:, 0] ^ wide_place
    places = cell_place.reshape(-1, 1, ROW)
    kept_a, sent_a, kept_b, sent_b = finish(
        q, part, voxels, state, w_out, w_feature, places, bricks, wide_count, orders, block
    )
    top, bottom = reduce_bricks([(kept_a, sent_a), (kept_b, sent_b)], orders)
    own = jnp.concatenate([top[0], bottom[0]], axis=0).reshape(BX, BY, channels)

    if narrow_count == 2:
        edge = jnp.where(narrow_place == 0, own[:, BY - 2 :], own[:, :2])
        other = swap(edge, "narrow", 0)
        left = jnp.where(narrow_place == 1, other, jnp.zeros_like(other))
        right = jnp.where(narrow_place == 0, other, jnp.zeros_like(other))
    else:
        left = shift(own[:, BY - 2 :], "narrow", 1)
        right = shift(own[:, :2], "narrow", -1)
    strip = jnp.concatenate([own, left, right], axis=1)
    above = shift(strip[BX - 2 :], "wide", 1)
    below = shift(strip[:2], "wide", -1)
    left = jnp.concatenate([above[:, BY : BY + 2], left, below[:, BY : BY + 2]], axis=0)
    right = jnp.concatenate([above[:, BY + 2 :], right, below[:, BY + 2 :]], axis=0)
    edges = jnp.stack(
        [
            (wide_place == 0).astype(jnp.int32),
            (wide_place == wide_count - 1).astype(jnp.int32),
            jnp.where(narrow_place == 0, 0, -1),
            jnp.where(narrow_place == narrow_count - 1, BY, BY + 1),
        ]
    ).astype(jnp.int32)
    return field_flow(
        edges, own, above[:, :BY], below[:, :BY], left, right, conv_first, conv_second
    )


def solution(mesh):
    placed = (
        P(("group", "wide", "narrow"), None),
        P(),
        P(),
        P(),
        P(),
        P(),
        P(("group", "wide", "narrow"), None),
        P(("group", "wide", "narrow")),
    )
    return jax.shard_map(
        per_device,
        mesh=mesh,
        in_specs=placed,
        out_specs=P(("group", "wide"), "narrow", None),
        check_vma=False,
    )
```

time: 241 us -> 82.7 us (0.34)
  blocking collectives: 53.2 us -> 0 us
  other arithmetic: 48.3 us -> 0.65 us
  matrix products: 30.6 us -> 0 us
  local copies, waits for them, and re-layouts: 37.1 us -> 8.61 us
  Pallas kernels: 0 us -> 26.2 us
  between operations: 13.8 us -> 0.3 us
  waiting for transfers between devices: 35.6 us -> 23.1 us
    all_to_all x1 -> x0, blocking collectives: 53.2 us -> none  [per_device(): lax.all_to_all(send_rows, 'wide', split_axis=0, concat_axis=0, tiled=True)]
    dot_general x5 -> x0, matrix products: 29.4 us -> none  [the longest x1 7.36 us: per_device(): jnp.einsum('bhts,bshe->bthe', scores, value_rows, preferred_element_type=...]
    scatter-add x1 -> x0, other arithmetic: 27.3 us -> none  [per_device(): jax.ops.segment_sum(gathered_features.astype(jnp.float32), received_place...]
    pallas_call x0 -> x4, Pallas kernels: none -> 26.2 us  [the longest x1 10.1 us: local_attention(): pl.pallas_call(local_kernel, grid=(tokens // BLK,), in_specs=[pl.BlockSpe...]
    all_gather x1 -> x0, waiting for transfers between devices: 23.3 us -> none  [prefix_2(): everything = lax.all_gather(array.astype(jnp.bfloat16), axis)]
    select_n x16 -> x3, other arithmetic: 16.6 us -> 0.07 us  [the longest x1 0.03 us: exclusive_state(): jnp.where(place == 0, stacked, stacked[::-1])]
    reshape x1 -> x0, local copies, waits for them, and re-layouts: 11.3 us -> none  [per_device(): split_rows = projected.reshape(block_count, BLK, 3, HEADS, HEAD)]
    ppermute x8 -> x14, waiting for transfers between devices: 12.3 us -> 23.1 us  [the longest x10 19.3 us: swap(): return lax.ppermute(array, axis, [(i, i ^ 1 << bit) for i in range(count)])]
  transfers between devices with their start and end apart: 10 -> 14, of which waited for: 7 -> 11; matrix products, arithmetic and copies ran while one was open for 21% -> 0% of each run, Pallas kernels for 0% -> 12%
where the time goes in v1:
time: 82.7 us; the launch traced here: 81.1 us
  Pallas kernels  26.2 us (32%)
  waiting for transfers between devices  23.1 us (28%)
  starting transfers between devices  22.3 us (27%)
  local copies, waits for them, and re-layouts  8.61 us (10%)
    ppermute x10, waiting for transfers between devices, swap(): return lax.ppermute(array, axis, [(i, i ^ 1 << bit) for i in range(count)])  19.3 us
    ppermute x10, starting transfers between devices, swap(): return lax.ppermute(array, axis, [(i, i ^ 1 << bit) for i in range(count)])  15.9 us
    pallas_call x1, Pallas kernels, local_attention(): pl.pallas_call(local_kernel, grid=(tokens // BLK,), in_specs=[pl.BlockSpe...  10.1 us
    unnamed x26, local copies, waits for them, and re-layouts  8.55 us
    pallas_call x1, Pallas kernels, finish(): pl.pallas_call(functools.partial(finish_kernel, orders), grid_spec=pltpu....  7.29 us
    ppermute x2, starting transfers between devices, shift(): lax.ppermute(array, axis, [(i, i + by) for i in range(count) if 0 <= i +...  5.83 us
    pallas_call x1, Pallas kernels, key_value(): pl.pallas_call(key_value_kernel, grid=(tokens // block,), in_specs=[pl.Bl...  5.23 us
    pallas_call x1, Pallas kernels, field_flow(): pl.pallas_call(field_kernel, in_specs=[pl.BlockSpec(memory_space=pltpu.SM...  3.53 us
  transfers between devices with their start and end apart: 14, of which 11 were waited for; matrix products, arithmetic and copies ran while one was open for 0% of the time, Pallas kernels for 12%

profile of v1, /device:TPU:0, one launch (start us, length us, event | category | flops | bytes accessed | tf_op | source)
XLA Modules:
  0.0 81.1 jit_solution(13832425223604763350)
XLA Ops:
  0.0 1.4 %copy-done.1 = bf16[512,1536]{1,0:T(8,128)(2,1)S(1)} copy-done((bf16[512,1536]{1,0:T(8,128)(2,1)S(1)}, bf16[512,1536]{1,0:T(8,128)(2,1)}, u32[]{:S(2)}) %copy-start.1) | copy-done | bytes 1572888
  1.4 5.2 %key_value.1 = (bf16[2048,512]{1,0:T(8,128)(2,1)S(1)}, bf16[2048,512]{1,0:T(8,128)(2,1)S(1)}, bf16[4,128,128]{2,1,0:T(8,128)(2,1)S(1)}) custom-call(bf16[2048,512]{1,0:T(8,128)(2,1)} %x_ref.5, bf16[512,1536]{1,0:T(8,128)(2,1)S(1)} %copy-done.1, bf16[512,1536]{1,0:T(8,128)(2,1)S(1)} %copy-done.1), custom_call_target="tpu_custom_call" | custom-call | tf_op jit(solution)/shard_map/key_value/pallas_call | solution.py:70
  6.6 0.0 copy-start.10
  6.7 1.4 %copy-done.10 = bf16[2048,512]{1,0:T(8,128)(2,1)} copy-done((bf16[2048,512]{1,0:T(8,128)(2,1)}, bf16[2048,512]{1,0:T(8,128)(2,1)S(1)}, u32[]{:S(2)}) %copy-start.10) | copy-done | bytes 2097176
  8.0 1.4 %copy-done.11 = bf16[2048,512]{1,0:T(8,128)(2,1)} copy-done((bf16[2048,512]{1,0:T(8,128)(2,1)}, bf16[2048,512]{1,0:T(8,128)(2,1)S(1)}, u32[]{:S(2)}) %copy-start.11) | copy-done | bytes 2097176
  9.4 0.5 collective-permute-start
  9.9 0.9 %collective-permute-done = bf16[2,128,128]{2,1,0:T(8,128)(2,1)S(1)} collective-permute-done((bf16[2,128,128]{2,1,0:T(8,128)(2,1)S(1)}, bf16[2,128,128]{2,1,0:T(8,128)(2,1)S(1)}, u32[]{:S(2)}, u32[]{:S(2)}) %collective-permute-start) | collective-permute-done | bytes 65568 | tf_op jit(solution)/shard_map/ppermute | solution.py:313
  10.8 2.9 %collective-permute-start.1 = (bf16[2,128,128]{2,1,0:T(8,128)(2,1)S(1)}, bf16[2,128,128]{2,1,0:T(8,128)(2,1)S(1)}, u32[]{:S(2)}, u32[]{:S(2)}) collective-permute-start(bf16[2,128,128]{2,1,0:T(8,128)(2,1)S(1)} %fusion.8), channel_id=1, source_target_pairs={{0,2},{2,0},{4,6},{6,4},{8,10},{10,8},{12,14},{14,12},{1,3},{3,1},... | collective-permute-start | bytes 196616 | tf_op jit(solution)/shard_map/ppermute | solution.py:293
  13.7 2.4 %collective-permute-done.1 = bf16[2,128,128]{2,1,0:T(8,128)(2,1)S(1)} collective-permute-done((bf16[2,128,128]{2,1,0:T(8,128)(2,1)S(1)}, bf16[2,128,128]{2,1,0:T(8,128)(2,1)S(1)}, u32[]{:S(2)}, u32[]{:S(2)}) %collective-permute-start.1) | collective-permute-done | bytes 65568 | tf_op jit(solution)/shard_map/ppermute | solution.py:293
  16.2 2.0 %collective-permute-start.2 = (bf16[2,128,128]{2,1,0:T(8,128)(2,1)S(1)}, bf16[2,128,128]{2,1,0:T(8,128)(2,1)S(1)}, u32[]{:S(2)}, u32[]{:S(2)}) collective-permute-start(bf16[2,128,128]{2,1,0:T(8,128)(2,1)S(1)} %fusion.9), channel_id=1, source_target_pairs={{0,4},{2,6},{4,0},{6,2},{8,12},{10,14},{12,8},{14,10},{1,5},{3,7},... | collective-permute-start | bytes 196616 | tf_op jit(solution)/shard_map/ppermute | solution.py:293
  18.2 2.4 %collective-permute-done.2 = bf16[2,128,128]{2,1,0:T(8,128)(2,1)S(1)} collective-permute-done((bf16[2,128,128]{2,1,0:T(8,128)(2,1)S(1)}, bf16[2,128,128]{2,1,0:T(8,128)(2,1)S(1)}, u32[]{:S(2)}, u32[]{:S(2)}) %collective-permute-start.2) | collective-permute-done | bytes 65568 | tf_op jit(solution)/shard_map/ppermute | solution.py:293
  20.6 3.0 %collective-permute-start.3 = (bf16[2,128,128]{2,1,0:T(8,128)(2,1)S(1)}, bf16[2,128,128]{2,1,0:T(8,128)(2,1)S(1)}, u32[]{:S(2)}, u32[]{:S(2)}) collective-permute-start(bf16[2,128,128]{2,1,0:T(8,128)(2,1)S(1)} %fusion.4), channel_id=1, source_target_pairs={{0,8},{2,10},{4,12},{6,14},{8,0},{10,2},{12,4},{14,6},{1,9},{3,11}... | collective-permute-start | bytes 196616 | tf_op jit(solution)/shard_map/ppermute | solution.py:293
  23.5 0.0 copy-done
  23.5 1.4 %copy-done.2 = bf16[512,1536]{1,0:T(8,128)(2,1)S(1)} copy-done((bf16[512,1536]{1,0:T(8,128)(2,1)S(1)}, bf16[512,1536]{1,0:T(8,128)(2,1)}, u32[]{:S(2)}) %copy-start.2) | copy-done | bytes 1572888
  25.0 10.1 %local_attention.1 = (bf16[2048,512]{1,0:T(8,128)(2,1)S(1)}, f32[2048,512]{1,0:T(8,128)}) custom-call(bf16[2048,512]{1,0:T(8,128)(2,1)S(1)} %copy-done, bf16[512,1536]{1,0:T(8,128)(2,1)S(1)} %copy-done.2, bf16[2048,512]{1,0:T(8,128)(2,1)} %copy-done.10, bf16[2048,512]{1,0:T(8,128)(2,1)} %copy-done.11), custom_call_target="tpu_custom_call" | custom-call | flops 2684354560 | bytes 12582912 | tf_op jit(solution)/shard_map/local_attention/pallas_call | solution.py:114
  35.1 1.4 %copy-done.3 = bf16[2048,512]{1,0:T(8,128)(2,1)} copy-done((bf16[2048,512]{1,0:T(8,128)(2,1)}, bf16[2048,512]{1,0:T(8,128)(2,1)S(1)}, u32[]{:S(2)}) %copy-start.3) | copy-done | bytes 2097176
  36.4 0.0 collective-permute-done.3
  36.5 0.1 fusion.12
  36.5 0.1 collective-permute-start.4
  36.6 0.0 copy-done.12
  36.6 1.2 %collective-permute-done.4 = bf16[2,128,128]{2,1,0:T(8,128)(2,1)S(1)} collective-permute-done((bf16[2,128,128]{2,1,0:T(8,128)(2,1)S(1)}, bf16[2,128,128]{2,1,0:T(8,128)(2,1)S(1)}, u32[]{:S(2)}, u32[]{:S(2)}) %collective-permute-start.4) | collective-permute-done | bytes 65568 | tf_op jit(solution)/shard_map/ppermute | solution.py:331
  37.9 0.0 copy-done.7
  38.0 1.6 %copy-done.4 = bf16[2048,512]{1,0:T(8,128)(2,1)S(1)} copy-done((bf16[2048,512]{1,0:T(8,128)(2,1)S(1)}, bf16[2048,512]{1,0:T(8,128)(2,1)}, u32[]{:S(2)}) %copy-start.4) | copy-done | bytes 2097176
  39.5 7.3 %finish.1 = (bf16[4,128,256]{2,1,0:T(8,128)(2,1)S(1)}, bf16[4,128,256]{2,1,0:T(8,128)(2,1)S(1)}, bf16[4,128,256]{2,1,0:T(8,128)(2,1)S(1)}, bf16[4,128,256]{2,1,0:T(8,128)(2,1)S(1)}) custom-call(s32[16]{0:T(128)S(1)} %xor_bitcast_fusion.brick_ref, bf16[2048,512]{1,0:T(8,128)(2,1)S(1)} %copy-done.4, f32[2048,512]{1,0:T(8,128)} %get-tuple-element.17.part_ref, ...), custom_call_target="tpu_custom_call" | custom-call | tf_op jit(solution)/shard_map/finish/pallas_call | solution.py:187
  46.8 1.6 %collective-permute-start.5 = (bf16[4,128,256]{2,1,0:T(8,128)(2,1)S(1)}, bf16[4,128,256]{2,1,0:T(8,128)(2,1)S(1)}, u32[]{:S(2)}, u32[]{:S(2)}) collective-permute-start(bf16[4,128,256]{2,1,0:T(8,128)(2,1)S(1)} %get-tuple-element.20), channel_id=1, source_target_pairs={{0,2},{2,0},{4,6},{6,4},{8,10},{10,8},{12,14},{14,12},{1,3},{3,1},... | collective-permute-start | bytes 786440 | tf_op jit(solution)/shard_map/ppermute | solution.py:293
  48.4 1.6 %collective-permute-start.8 = (bf16[4,128,256]{2,1,0:T(8,128)(2,1)S(1)}, bf16[4,128,256]{2,1,0:T(8,128)(2,1)S(1)}, u32[]{:S(2)}, u32[]{:S(2)}) collective-permute-start(bf16[4,128,256]{2,1,0:T(8,128)(2,1)S(1)} %get-tuple-element.22), channel_id=1, source_target_pairs={{0,4},{2,6},{4,0},{6,2},{8,12},{10,14},{12,8},{14,10},{1,5},{3,7},... | collective-permute-start | bytes 786440 | tf_op jit(solution)/shard_map/ppermute | solution.py:293
  50.0 5.3 %collective-permute-done.5 = bf16[4,128,256]{2,1,0:T(8,128)(2,1)S(1)} collective-permute-done((bf16[4,128,256]{2,1,0:T(8,128)(2,1)S(1)}, bf16[4,128,256]{2,1,0:T(8,128)(2,1)S(1)}, u32[]{:S(2)}, u32[]{:S(2)}) %collective-permute-start.5) | collective-permute-done | bytes 262176 | tf_op jit(solution)/shard_map/ppermute | solution.py:293
  55.3 0.1 add_convert_fusion.1
  55.4 1.6 %collective-permute-start.6 = (bf16[2,128,256]{2,1,0:T(8,128)(2,1)S(1)}, bf16[2,128,256]{2,1,0:T(8,128)(2,1)S(1)}, u32[]{:S(2)}, u32[]{:S(2)}) collective-permute-start(bf16[2,128,256]{2,1,0:T(8,128)(2,1)S(1)} %slice.73), channel_id=1, source_target_pairs={{0,4},{2,6},{4,0},{6,2},{8,12},{10,14},{12,8},{14,10},{1,5},{3,7},... | collective-permute-start | bytes 393224 | tf_op jit(solution)/shard_map/ppermute | solution.py:293
  57.0 0.0 collective-permute-done.8
  57.0 0.1 add_convert_fusion
  57.1 1.6 %collective-permute-start.9 = (bf16[2,128,256]{2,1,0:T(8,128)(2,1)S(1)}, bf16[2,128,256]{2,1,0:T(8,128)(2,1)S(1)}, u32[]{:S(2)}, u32[]{:S(2)}) collective-permute-start(bf16[2,128,256]{2,1,0:T(8,128)(2,1)S(1)} %slice.77), channel_id=1, source_target_pairs={{0,2},{2,0},{4,6},{6,4},{8,10},{10,8},{12,14},{14,12},{1,3},{3,1},... | collective-permute-start | bytes 393224 | tf_op jit(solution)/shard_map/ppermute | solution.py:293
  58.7 1.7 %collective-permute-done.6 = bf16[2,128,256]{2,1,0:T(8,128)(2,1)S(1)} collective-permute-done((bf16[2,128,256]{2,1,0:T(8,128)(2,1)S(1)}, bf16[2,128,256]{2,1,0:T(8,128)(2,1)S(1)}, u32[]{:S(2)}, u32[]{:S(2)}) %collective-permute-start.6) | collective-permute-done | bytes 131104 | tf_op jit(solution)/shard_map/ppermute | solution.py:293
  60.4 0.2 collective-permute-start.7
  60.6 1.5 %collective-permute-done.9 = bf16[2,128,256]{2,1,0:T(8,128)(2,1)S(1)} collective-permute-done((bf16[2,128,256]{2,1,0:T(8,128)(2,1)S(1)}, bf16[2,128,256]{2,1,0:T(8,128)(2,1)S(1)}, u32[]{:S(2)}, u32[]{:S(2)}) %collective-permute-start.9) | collective-permute-done | bytes 131104 | tf_op jit(solution)/shard_map/ppermute | solution.py:293
  62.2 1.4 %collective-permute-start.10 = (bf16[1,128,256]{2,1,0:T(8,128)(2,1)S(1)}, bf16[1,128,256]{2,1,0:T(8,128)(2,1)S(1)}, u32[]{:S(2)}, u32[]{:S(2)}) collective-permute-start(bf16[1,128,256]{2,1,0:T(8,128)(2,1)S(1)} %slice.79), channel_id=1, source_target_pairs={{0,8},{2,10},{4,12},{6,14},{8,0},{10,2},{12,4},{14,6},{1,9},{3,11}... | collective-permute-start | bytes 196616 | tf_op jit(solution)/shard_map/ppermute | solution.py:293
  63.6 2.5 %collective-permute-done.7 = bf16[1,128,256]{2,1,0:T(8,128)(2,1)S(1)} collective-permute-done((bf16[1,128,256]{2,1,0:T(8,128)(2,1)S(1)}, bf16[1,128,256]{2,1,0:T(8,128)(2,1)S(1)}, u32[]{:S(2)}, u32[]{:S(2)}) %collective-permute-start.7) | collective-permute-done | bytes 65568 | tf_op jit(solution)/shard_map/ppermute | solution.py:293
  66.1 2.4 %collective-permute-done.10 = bf16[1,128,256]{2,1,0:T(8,128)(2,1)S(1)} collective-permute-done((bf16[1,128,256]{2,1,0:T(8,128)(2,1)S(1)}, bf16[1,128,256]{2,1,0:T(8,128)(2,1)S(1)}, u32[]{:S(2)}, u32[]{:S(2)}) %collective-permute-start.10) | collective-permute-done | bytes 65568 | tf_op jit(solution)/shard_map/ppermute | solution.py:293
  68.6 0.1 collective-permute-start.11
  68.7 1.1 %collective-permute-done.11 = bf16[8,2,256]{2,1,0:T(2,128)(2,1)S(1)} collective-permute-done((bf16[8,2,256]{2,1,0:T(2,128)(2,1)S(1)}, bf16[8,2,256]{2,1,0:T(2,128)(2,1)S(1)}, u32[]{:S(2)}, u32[]{:S(2)}) %collective-permute-start.11) | collective-permute-done | bytes 8224 | tf_op jit(solution)/shard_map/ppermute | solution.py:293
  69.9 1.3 %collective-permute-start.13 = (bf16[2,36,256]{2,1,0:T(8,128)(2,1)S(1)}, bf16[2,36,256]{2,1,0:T(8,128)(2,1)S(1)}, u32[]{:S(2)}, u32[]{:S(2)}) collective-permute-start(bf16[2,36,256]{2,1,0:T(8,128)(2,1)S(1)} %get-tuple-element.25), channel_id=1, source_target_pairs={{2,0},{4,2},{6,4},{8,6},{10,8},{12,10},{14,12},{3,1},{5,3},{7,5},{... | collective-permute-start | bytes 110600 | tf_op jit(solution)/shard_map/ppermute | solution.py:298
  71.2 0.1 pad_add_fusion.edge_ref
  71.2 4.5 %collective-permute-start.12 = (bf16[2,36,256]{2,1,0:T(8,128)(2,1)S(1)}, bf16[2,36,256]{2,1,0:T(8,128)(2,1)S(1)}, u32[]{:S(2)}, u32[]{:S(2)}) collective-permute-start(bf16[2,36,256]{2,1,0:T(8,128)(2,1)S(1)} %get-tuple-element.26), channel_id=1, source_target_pairs={{0,2},{2,4},{4,6},{6,8},{8,10},{10,12},{12,14},{1,3},{3,5},{5,7},{... | collective-permute-start | bytes 110600 | tf_op jit(solution)/shard_map/ppermute | solution.py:298
  75.8 0.0 collective-permute-done.13
  75.8 1.6 %collective-permute-done.12 = bf16[2,36,256]{2,1,0:T(8,128)(2,1)S(1)} collective-permute-done((bf16[2,36,256]{2,1,0:T(8,128)(2,1)S(1)}, bf16[2,36,256]{2,1,0:T(8,128)(2,1)S(1)}, u32[]{:S(2)}, u32[]{:S(2)}) %collective-permute-start.12) | collective-permute-done | bytes 36896 | tf_op jit(solution)/shard_map/ppermute | solution.py:298
  77.5 0.0 copy-done.5
  77.5 0.0 copy-done.6
  77.5 3.5 %field_flow.1 = f32[8,32,256]{2,1,0:T(8,128)} custom-call(s32[4]{0:T(128)S(1)} %pad_add_fusion.edge_ref, bf16[8,32,256]{2,1,0:T(8,128)(2,1)S(1)} %bitcast.30, bf16[2,32,256]{2,1,0:T(8,128)(2,1)S(1)} %slice.82.above_ref, bf16[2,32,256]{2,1,0:T(8,128)(2,1)S(1)} %slice.83.below_ref, bf16[12,2,256]{2,1,0:T(2,128)(2,1)S(1)} %get-tuple-element.33.left_ref, ...), custom_call_target="tpu_custom_call" | custom-call | tf_op jit(solution)/shard_map/field_flow/pallas_call | solution.py:268
  (38 shorter events, 0.4 us)
Async XLA Ops:
  0.0 1.4 %copy-start.1 = (bf16[512,1536]{1,0:T(8,128)(2,1)S(1)}, bf16[512,1536]{1,0:T(8,128)(2,1)}, u32[]{:S(2)}) copy-start(bf16[512,1536]{1,0:T(8,128)(2,1)} %wq_ref.1) | copy-start | bytes 4718596
  1.4 22.1 %copy-start = (bf16[2048,512]{1,0:T(8,128)(2,1)S(1)}, bf16[2048,512]{1,0:T(8,128)(2,1)}, u32[]{:S(2)}) copy-start(bf16[2048,512]{1,0:T(8,128)(2,1)} %x_ref.5) | copy-start | bytes 6291460
  6.6 1.4 %copy-start.10 = (bf16[2048,512]{1,0:T(8,128)(2,1)}, bf16[2048,512]{1,0:T(8,128)(2,1)S(1)}, u32[]{:S(2)}) copy-start(bf16[2048,512]{1,0:T(8,128)(2,1)S(1)} %get-tuple-element.14.k_ref) | copy-start | bytes 6291460
  8.0 1.4 %copy-start.11 = (bf16[2048,512]{1,0:T(8,128)(2,1)}, bf16[2048,512]{1,0:T(8,128)(2,1)S(1)}, u32[]{:S(2)}) copy-start(bf16[2048,512]{1,0:T(8,128)(2,1)S(1)} %get-tuple-element.15.v_ref) | copy-start | bytes 6291460
  9.4 1.4 %collective-permute-start = (bf16[2,128,128]{2,1,0:T(8,128)(2,1)S(1)}, bf16[2,128,128]{2,1,0:T(8,128)(2,1)S(1)}, u32[]{:S(2)}, u32[]{:S(2)}) collective-permute-start(bf16[2,128,128]{2,1,0:T(8,128)(2,1)S(1)} %dynamic-slice_bitcast_fusion), channel_id=1, source_target_pairs={{0,1},{1,0},{2,3},{3,2},{4,5},{5,4},{6,7},{7,6},{8,9},{9,8},{10,11... | collective-permute-start | bytes 196616 | tf_op jit(solution)/shard_map/ppermute | solution.py:313
  10.8 5.3 %collective-permute-start.1 = (bf16[2,128,128]{2,1,0:T(8,128)(2,1)S(1)}, bf16[2,128,128]{2,1,0:T(8,128)(2,1)S(1)}, u32[]{:S(2)}, u32[]{:S(2)}) collective-permute-start(bf16[2,128,128]{2,1,0:T(8,128)(2,1)S(1)} %fusion.8), channel_id=1, source_target_pairs={{0,2},{2,0},{4,6},{6,4},{8,10},{10,8},{12,14},{14,12},{1,3},{3,1},... | collective-permute-start | bytes 196616 | tf_op jit(solution)/shard_map/ppermute | solution.py:293
  16.2 4.3 %collective-permute-start.2 = (bf16[2,128,128]{2,1,0:T(8,128)(2,1)S(1)}, bf16[2,128,128]{2,1,0:T(8,128)(2,1)S(1)}, u32[]{:S(2)}, u32[]{:S(2)}) collective-permute-start(bf16[2,128,128]{2,1,0:T(8,128)(2,1)S(1)} %fusion.9), channel_id=1, source_target_pairs={{0,4},{2,6},{4,0},{6,2},{8,12},{10,14},{12,8},{14,10},{1,5},{3,7},... | collective-permute-start | bytes 196616 | tf_op jit(solution)/shard_map/ppermute | solution.py:293
  20.6 15.9 %collective-permute-start.3 = (bf16[2,128,128]{2,1,0:T(8,128)(2,1)S(1)}, bf16[2,128,128]{2,1,0:T(8,128)(2,1)S(1)}, u32[]{:S(2)}, u32[]{:S(2)}) collective-permute-start(bf16[2,128,128]{2,1,0:T(8,128)(2,1)S(1)} %fusion.4), channel_id=1, source_target_pairs={{0,8},{2,10},{4,12},{6,14},{8,0},{10,2},{12,4},{14,6},{1,9},{3,11}... | collective-permute-start | bytes 196616 | tf_op jit(solution)/shard_map/ppermute | solution.py:293
  23.5 1.4 %copy-start.2 = (bf16[512,1536]{1,0:T(8,128)(2,1)S(1)}, bf16[512,1536]{1,0:T(8,128)(2,1)}, u32[]{:S(2)}) copy-start(bf16[512,1536]{1,0:T(8,128)(2,1)} %wq_ref.1) | copy-start | bytes 4718596
  24.9 11.7 %copy-start.12 = (s32[16,1]{0,1:T(1,128)S(1)}, s32[16,1]{0,1:T(1,128)}, u32[]{:S(2)}) copy-start(s32[16,1]{0,1:T(1,128)} %param.14) | copy-start | bytes 196
  25.0 13.0 %copy-start.7 = (bf16[512,512]{1,0:T(8,128)(2,1)S(1)}, bf16[512,512]{1,0:T(8,128)(2,1)}, u32[]{:S(2)}) copy-start(bf16[512,512]{1,0:T(8,128)(2,1)} %wo_ref.1) | copy-start | bytes 1572868
  25.0 13.0 %copy-start.8 = (bf16[512,256]{1,0:T(8,128)(2,1)S(1)}, bf16[512,256]{1,0:T(8,128)(2,1)}, u32[]{:S(2)}) copy-start(bf16[512,256]{1,0:T(8,128)(2,1)} %wf_ref.1) | copy-start | bytes 786436
  25.0 13.0 %copy-start.9 = (s32[2048]{0:T(1024)S(1)}, s32[2048]{0:T(1024)}, u32[]{:S(2)}) copy-start(s32[2048]{0:T(1024)} %param.15) | copy-start | bytes 24580
  35.1 1.4 %copy-start.3 = (bf16[2048,512]{1,0:T(8,128)(2,1)}, bf16[2048,512]{1,0:T(8,128)(2,1)S(1)}, u32[]{:S(2)}) copy-start(bf16[2048,512]{1,0:T(8,128)(2,1)S(1)} %get-tuple-element.16.q_ref) | copy-start | bytes 6291460
  36.5 1.3 %collective-permute-start.4 = (bf16[2,128,128]{2,1,0:T(8,128)(2,1)S(1)}, bf16[2,128,128]{2,1,0:T(8,128)(2,1)S(1)}, u32[]{:S(2)}, u32[]{:S(2)}) collective-permute-start(bf16[2,128,128]{2,1,0:T(8,128)(2,1)S(1)} %get-tuple-element.24), channel_id=1, source_target_pairs={{0,1},{1,0},{2,3},{3,2},{4,5},{5,4},{6,7},{7,6},{8,9},{9,8},{10,11... | collective-permute-start | bytes 196616 | tf_op jit(solution)/shard_map/ppermute | solution.py:331
  37.9 1.6 %copy-start.4 = (bf16[2048,512]{1,0:T(8,128)(2,1)S(1)}, bf16[2048,512]{1,0:T(8,128)(2,1)}, u32[]{:S(2)}) copy-start(bf16[2048,512]{1,0:T(8,128)(2,1)} %copy-done.3) | copy-start | bytes 6291460
  46.8 8.4 %collective-permute-start.5 = (bf16[4,128,256]{2,1,0:T(8,128)(2,1)S(1)}, bf16[4,128,256]{2,1,0:T(8,128)(2,1)S(1)}, u32[]{:S(2)}, u32[]{:S(2)}) collective-permute-start(bf16[4,128,256]{2,1,0:T(8,128)(2,1)S(1)} %get-tuple-element.20), channel_id=1, source_target_pairs={{0,2},{2,0},{4,6},{6,4},{8,10},{10,8},{12,14},{14,12},{1,3},{3,1},... | collective-permute-start | bytes 786440 | tf_op jit(solution)/shard_map/ppermute | solution.py:293
  48.4 8.6 %collective-permute-start.8 = (bf16[4,128,256]{2,1,0:T(8,128)(2,1)S(1)}, bf16[4,128,256]{2,1,0:T(8,128)(2,1)S(1)}, u32[]{:S(2)}, u32[]{:S(2)}) collective-permute-start(bf16[4,128,256]{2,1,0:T(8,128)(2,1)S(1)} %get-tuple-element.22), channel_id=1, source_target_pairs={{0,4},{2,6},{4,0},{6,2},{8,12},{10,14},{12,8},{14,10},{1,5},{3,7},... | collective-permute-start | bytes 786440 | tf_op jit(solution)/shard_map/ppermute | solution.py:293
  55.3 22.2 %copy-start.5 = (bf16[3,3,256,256]{3,2,1,0:T(8,128)(2,1)S(1)}, bf16[3,3,256,256]{3,2,1,0:T(8,128)(2,1)}, u32[]{:S(2)}) copy-start(bf16[3,3,256,256]{3,2,1,0:T(8,128)(2,1)} %param.12) | copy-start | bytes 3538948
  55.3 22.3 %copy-start.6 = (bf16[3,3,256,256]{3,2,1,0:T(8,128)(2,1)S(1)}, bf16[3,3,256,256]{3,2,1,0:T(8,128)(2,1)}, u32[]{:S(2)}) copy-start(bf16[3,3,256,256]{3,2,1,0:T(8,128)(2,1)} %param.13) | copy-start | bytes 3538948
  55.4 5.0 %collective-permute-start.6 = (bf16[2,128,256]{2,1,0:T(8,128)(2,1)S(1)}, bf16[2,128,256]{2,1,0:T(8,128)(2,1)S(1)}, u32[]{:S(2)}, u32[]{:S(2)}) collective-permute-start(bf16[2,128,256]{2,1,0:T(8,128)(2,1)S(1)} %slice.73), channel_id=1, source_target_pairs={{0,4},{2,6},{4,0},{6,2},{8,12},{10,14},{12,8},{14,10},{1,5},{3,7},... | collective-permute-start | bytes 393224 | tf_op jit(solution)/shard_map/ppermute | solution.py:293
  57.1 5.0 %collective-permute-start.9 = (bf16[2,128,256]{2,1,0:T(8,128)(2,1)S(1)}, bf16[2,128,256]{2,1,0:T(8,128)(2,1)S(1)}, u32[]{:S(2)}, u32[]{:S(2)}) collective-permute-start(bf16[2,128,256]{2,1,0:T(8,128)(2,1)S(1)} %slice.77), channel_id=1, source_target_pairs={{0,2},{2,0},{4,6},{6,4},{8,10},{10,8},{12,14},{14,12},{1,3},{3,1},... | collective-permute-start | bytes 393224 | tf_op jit(solution)/shard_map/ppermute | solution.py:293
  60.4 5.6 %collective-permute-start.7 = (bf16[1,128,256]{2,1,0:T(8,128)(2,1)S(1)}, bf16[1,128,256]{2,1,0:T(8,128)(2,1)S(1)}, u32[]{:S(2)}, u32[]{:S(2)}) collective-permute-start(bf16[1,128,256]{2,1,0:T(8,128)(2,1)S(1)} %slice.75), channel_id=1, source_target_pairs={{0,8},{2,10},{4,12},{6,14},{8,0},{10,2},{12,4},{14,6},{1,9},{3,11}... | collective-permute-start | bytes 196616 | tf_op jit(solution)/shard_map/ppermute | solution.py:293
  62.2 6.3 %collective-permute-start.10 = (bf16[1,128,256]{2,1,0:T(8,128)(2,1)S(1)}, bf16[1,128,256]{2,1,0:T(8,128)(2,1)S(1)}, u32[]{:S(2)}, u32[]{:S(2)}) collective-permute-start(bf16[1,128,256]{2,1,0:T(8,128)(2,1)S(1)} %slice.79), channel_id=1, source_target_pairs={{0,8},{2,10},{4,12},{6,14},{8,0},{10,2},{12,4},{14,6},{1,9},{3,11}... | collective-permute-start | bytes 196616 | tf_op jit(solution)/shard_map/ppermute | solution.py:293
  68.6 1.2 %collective-permute-start.11 = (bf16[8,2,256]{2,1,0:T(2,128)(2,1)S(1)}, bf16[8,2,256]{2,1,0:T(2,128)(2,1)S(1)}, u32[]{:S(2)}, u32[]{:S(2)}) collective-permute-start(bf16[8,2,256]{2,1,0:T(2,128)(2,1)S(1)} %broadcast_select_fusion.1), channel_id=1, source_target_pairs={{0,1},{1,0},{2,3},{3,2},{4,5},{5,4},{6,7},{7,6},{8,9},{9,8},{10,11... | collective-permute-start | bytes 24584 | tf_op jit(solution)/shard_map/ppermute | solution.py:293
  69.9 5.9 %collective-permute-start.13 = (bf16[2,36,256]{2,1,0:T(8,128)(2,1)S(1)}, bf16[2,36,256]{2,1,0:T(8,128)(2,1)S(1)}, u32[]{:S(2)}, u32[]{:S(2)}) collective-permute-start(bf16[2,36,256]{2,1,0:T(8,128)(2,1)S(1)} %get-tuple-element.25), channel_id=1, source_target_pairs={{2,0},{4,2},{6,4},{8,6},{10,8},{12,10},{14,12},{3,1},{5,3},{7,5},{... | collective-permute-start | bytes 110600 | tf_op jit(solution)/shard_map/ppermute | solution.py:298
  71.2 6.2 %collective-permute-start.12 = (bf16[2,36,256]{2,1,0:T(8,128)(2,1)S(1)}, bf16[2,36,256]{2,1,0:T(8,128)(2,1)S(1)}, u32[]{:S(2)}, u32[]{:S(2)}) collective-permute-start(bf16[2,36,256]{2,1,0:T(8,128)(2,1)S(1)} %get-tuple-element.26), channel_id=1, source_target_pairs={{0,2},{2,4},{4,6},{6,8},{8,10},{10,12},{12,14},{1,3},{3,5},{5,7},{... | collective-permute-start | bytes 110600 | tf_op jit(solution)/shard_map/ppermute | solution.py:298

commit v2 on v1

v2 whole, which is shorter than its diff:
```python
import functools

import jax
import jax.numpy as jnp
from jax import lax
from jax.experimental import pallas as pl
from jax.experimental.pallas import tpu as pltpu
from jax.sharding import PartitionSpec as P

HEADS = 4
HEAD = 128
ROW = 128
BLK = 256
BX = 8
BY = 32
EPS = 1e-06
LINE = BY + 16

F32 = jnp.float32
BF16 = jnp.bfloat16


def dot(a, b):
    return jnp.dot(a, b, preferred_element_type=F32)


def dot_t(a, b):
    return lax.dot_general(a, b, (((0,), (0,)), ((), ())), preferred_element_type=F32)


def dot_nt(a, b):
    return lax.dot_general(a, b, (((1,), (1,)), ((), ())), preferred_element_type=F32)


KEY_VALUE_KIB = 44 * 1024


def params(kib=24 * 1024):
    return pltpu.CompilerParams(vmem_limit_bytes=kib << 10)


def head_cols(h):
    return slice(h * HEAD, (h + 1) * HEAD)


def key_value_kernel(
    chunks, x_ref, w_ref, x, k_ref, v_ref, before_ref, *refs
):
    totals, sems = refs[:-1], refs[-1]
    tokens = x.shape[0]
    inner = HEADS * HEAD
    rows = tokens // chunks
    blocks = rows // BLK
    loads = [
        pltpu.make_async_copy(
            x_ref.at[pl.ds(c * rows, rows)], x.at[pl.ds(c * rows, rows)], sems.at[c]
        )
        for c in range(chunks)
    ]
    for load in loads:
        load.start()
    running = [jnp.zeros((HEAD, HEAD), F32) for _ in range(HEADS)]
    for c in range(chunks):
        loads[c].wait()
        here = slice(c * rows, (c + 1) * rows)
        k = dot(x[here], w_ref[:, inner : 2 * inner]).astype(BF16)
        k_ref[here] = k
        v = dot(x[here], w_ref[:, 2 * inner :]).astype(BF16)
        v_ref[here] = v
        for b in range(blocks):
            block = slice(b * BLK, (b + 1) * BLK)
            for h in range(HEADS):
                before_ref[c * blocks + b, h] = running[h].astype(BF16)
            for pair in range(HEADS // 2):
                cols = slice(pair * 2 * HEAD, (pair + 1) * 2 * HEAD)
                outer = dot_t(k[block, cols], v[block, cols])
                running[2 * pair] += outer[:HEAD, :HEAD]
                running[2 * pair + 1] += outer[HEAD:, HEAD:]
    share = HEADS // len(totals)
    for h in range(HEADS):
        for k, total_ref in enumerate(totals):

            @pl.when((lax.axis_index("narrow") + k) % len(totals) == h // share)
            def _(total_ref=total_ref, h=h):
                total_ref[h % share] = running[h].astype(BF16)


def key_value(voxels, w_qkv, chunks, cores):
    tokens, width = voxels.shape
    inner = HEADS * HEAD
    hbm = pl.BlockSpec(memory_space=pl.ANY)
    vmem = pl.BlockSpec(memory_space=pltpu.VMEM)
    flat = jax.ShapeDtypeStruct((tokens, inner), BF16)
    states = jax.ShapeDtypeStruct((tokens // BLK, HEADS, HEAD, HEAD), BF16)
    share = jax.ShapeDtypeStruct((HEADS // cores, HEAD, HEAD), BF16)
    return pl.pallas_call(
        functools.partial(key_value_kernel, chunks),
        in_specs=[hbm, vmem],
        out_specs=[vmem] * (4 + cores),
        out_shape=[jax.ShapeDtypeStruct(voxels.shape, BF16), flat, flat, states] + [share] * cores,
        scratch_shapes=[pltpu.SemaphoreType.DMA((chunks,))],
        compiler_params=params(KEY_VALUE_KIB),
        name="key_value",
    )(voxels, w_qkv)


def local_kernel(first, count, x_ref, w_ref, k_ref, v_ref, before_ref, q_ref, part_ref):
    causal = lax.broadcasted_iota(jnp.int32, (BLK, BLK), 0) >= lax.broadcasted_iota(
        jnp.int32, (BLK, BLK), 1
    )
    here = slice(first * BLK, (first + count) * BLK)
    q = dot(x_ref[here], w_ref[:, : HEADS * HEAD]).astype(BF16)
    q_ref[...] = q
    for b in range(count):
        rows = slice((first + b) * BLK, (first + b + 1) * BLK)
        own = slice(b * BLK, (b + 1) * BLK)
        for h in range(HEADS):
            cols = head_cols(h)
            scores = dot_nt(q[own, cols], k_ref[rows, cols])
            scores = jnp.where(causal, scores, 0.0).astype(BF16)
            part_ref[own, cols] = dot(scores, v_ref[rows, cols]) + dot(
                q[own, cols], before_ref[first + b, h]
            )


def local_attention(x, w_qkv, k, v, before, first, count):
    width = x.shape[1]
    inner = HEADS * HEAD
    vmem = pl.BlockSpec(memory_space=pltpu.VMEM)
    rows = count * BLK
    return pl.pallas_call(
        functools.partial(local_kernel, first, count),
        in_specs=[vmem] * 5,
        out_specs=[vmem, vmem],
        out_shape=[
            jax.ShapeDtypeStruct((rows, inner), BF16),
            jax.ShapeDtypeStruct((rows, inner), F32),
        ],
        compiler_params=params(),
        cost_estimate=pl.CostEstimate(
            flops=2 * rows * inner * (width + 2 * BLK + HEAD),
            bytes_accessed=rows * inner * 12,
            transcendentals=0,
        ),
        name="local_attention",
    )(x, w_qkv, k, v, before)


def gather_kernel(*refs):
    ins, (running_ref, packed_ref) = refs[:-2], refs[-2:]
    running = sum(ref[...].astype(F32) for ref in ins)
    running_ref[...] = running
    packed_ref[...] = running.astype(BF16)


def scan_kernel(bit, running_ref, before_ref, other_ref, new_running, new_before, packed):
    other = other_ref[...].astype(F32)
    running = running_ref[...] + other
    new_running[...] = running
    packed[...] = running.astype(BF16)
    later = ((lax.axis_index("wide") >> bit) & 1).astype(F32)
    new_before[...] = before_ref[...] + later * other


def spread_kernel(cores, bit, before_ref, other_ref, *refs):
    pieces, outs = refs[:cores], refs[cores:]
    place = lax.axis_index("narrow")
    later = ((lax.axis_index("wide") >> bit) & 1).astype(F32)
    before = before_ref[...] + later * other_ref[...].astype(F32)
    for k, out in enumerate(outs):
        receiver = (place + k) % cores
        value = before
        for j, piece in enumerate(pieces):
            source = (place - j + cores) % cores
            value = value + jnp.where(source < receiver, 1.0, 0.0) * piece[...].astype(F32)
        out[...] = value.astype(BF16)


def small_call(kernel, name, inputs, dtypes, shape):
    vmem = pl.BlockSpec(memory_space=pltpu.VMEM)
    smem = pl.BlockSpec(memory_space=pltpu.SMEM)
    return pl.pallas_call(
        kernel,
        in_specs=[smem if array.dtype == jnp.int32 else vmem for array in inputs],
        out_specs=[vmem] * len(dtypes),
        out_shape=[jax.ShapeDtypeStruct(shape, dtype) for dtype in dtypes],
        compiler_params=params(4 * 1024),
        name=name,
    )(*inputs)


def finish_kernel(orders, spans, cores, brick_ref, *refs):
    pieces = len(spans)
    refs = list(refs)
    take = lambda n: [refs.pop(0) for _ in range(n)]
    q_refs, part_refs, state_refs = take(pieces), take(pieces), take(cores)
    x_ref, wo_ref, wf_ref, cell_ref = take(4)
    outs = take(4)
    acc, normed, state = refs
    share = HEADS // cores
    for k, ref in enumerate(state_refs):
        owner = (lax.axis_index("narrow") - k + cores) % cores
        for j in range(share):
            state[owner * share + j] = ref[j]
    acc[...] = jnp.zeros_like(acc)
    cells = BX * BY
    for (first, count), q_ref, part_ref in zip(spans, q_refs, part_refs):
        here = slice(first * BLK, (first + count) * BLK)
        for h in range(HEADS):
            cols = head_cols(h)
            attended = part_ref[:, cols] + dot(q_ref[:, cols], state[h])
            mean_square = jnp.mean(attended * attended, axis=-1, keepdims=True)
            normed[here, cols] = (attended * lax.rsqrt(mean_square + EPS)).astype(BF16)
        hidden = (x_ref[here].astype(F32) + dot(normed[here], wo_ref[...])).astype(BF16)
        features = dot(hidden, wf_ref[...]).astype(BF16)
        for r in range(count * BLK // ROW):
            row = first * BLK // ROW + r
            match = lax.broadcasted_iota(jnp.int32, (cells, ROW), 0) == cell_ref[row : row + 1]
            onehot = jnp.where(match, 1.0, 0.0).astype(BF16)
            brick = brick_ref[row] ^ lax.axis_index("wide")
            acc[brick] += dot(onehot, features[r * ROW : (r + 1) * ROW])
    bricks = acc.shape[0]
    half_cells = cells // 2
    for part, order in enumerate(orders):
        for i in range(bricks):
            place = 0
            for bit in order:
                place = 2 * place + ((i >> bit) & 1)
            which, slot = divmod(place, bricks // 2)
            outs[2 * part + which][slot] = acc[
                i, part * half_cells : (part + 1) * half_cells
            ].astype(BF16)


def finish(spans, bricks, qs, parts, states, x, w_out, w_feature, cell_rows, count, orders):
    tokens = x.shape[0]
    channels = w_feature.shape[1]
    cells = BX * BY
    vmem = pl.BlockSpec(memory_space=pltpu.VMEM)
    smem = pl.BlockSpec(memory_space=pltpu.SMEM)
    out = jax.ShapeDtypeStruct((count // 2, cells // 2, channels), BF16)
    return pl.pallas_call(
        functools.partial(finish_kernel, orders, spans, len(states)),
        in_specs=[smem] + [vmem] * (2 * len(spans) + len(states) + 4),
        out_specs=[vmem] * 4,
        out_shape=[out] * 4,
        scratch_shapes=[
            pltpu.VMEM((count, cells, channels), F32),
            pltpu.VMEM((tokens, HEADS * HEAD), BF16),
            pltpu.VMEM((HEADS, HEAD, HEAD), BF16),
        ],
        compiler_params=params(),
        name="finish",
    )(bricks, *qs, *parts, *states, x, w_out, w_feature, cell_rows)


def field_kernel(
    edge_ref, own_ref, above_ref, below_ref, left_ref, right_ref, w1_ref, w2_ref, out_ref, field, wide
):
    lines = BX + 4
    shown = wide.shape[0]
    field[...] = jnp.zeros_like(field)
    for r in range(lines):
        at = 16 + r * LINE
        if r < 2:
            line = above_ref[r]
        elif r < BX + 2:
            line = own_ref[r - 2]
        else:
            line = below_ref[r - BX - 2]
        field[at : at + BY] = line.astype(F32)
        field[at - 2 : at] = left_ref[r].astype(F32)
        field[at + BY : at + BY + 2] = right_ref[r].astype(F32)

    channels = field.shape[1]

    def widen():
        for shift in range(3):
            wide[:, shift * channels : (shift + 1) * channels] = field[
                7 + shift : 7 + shift + shown
            ].astype(BF16)

    def convolve(w_ref, first, count):
        return sum(
            dot(wide[(first + dy - 1) * LINE : (first + dy - 1 + count) * LINE], w_ref[dy])
            for dy in range(3)
        )

    widen()
    inner = jax.nn.gelu(convolve(w1_ref, 1, BX + 2), approximate=True)
    column = lax.broadcasted_iota(jnp.int32, (LINE, 1), 0) - 8
    inside = (column >= edge_ref[2]) & (column < edge_ref[3])
    for r in range(1, BX + 3):
        keep = inside
        if r == 1:
            keep = keep & (edge_ref[0] == 0)
        if r == BX + 2:
            keep = keep & (edge_ref[1] == 0)
        field[8 + r * LINE : 8 + (r + 1) * LINE] = jnp.where(
            keep, inner[(r - 1) * LINE : r * LINE], 0.0
        )
    widen()
    flow = convolve(w2_ref, 2, BX)
    for r in range(BX):
        out_ref[r] = flow[r * LINE + 8 : r * LINE + 8 + BY]


def field_flow(edges, own, above, below, left, right, conv_first, conv_second):
    channels = own.shape[-1]
    vmem = pl.BlockSpec(memory_space=pltpu.VMEM)
    lines = BX + 4
    return pl.pallas_call(
        field_kernel,
        in_specs=[pl.BlockSpec(memory_space=pltpu.SMEM)] + [vmem] * 7,
        out_specs=vmem,
        out_shape=jax.ShapeDtypeStruct((BX, BY, channels), F32),
        scratch_shapes=[
            pltpu.VMEM((16 + lines * LINE, channels), F32),
            pltpu.VMEM((lines * LINE, 3 * channels), BF16),
        ],
        compiler_params=params(16 * 1024),
        name="field_flow",
    )(
        edges,
        own,
        above,
        below,
        left,
        right,
        conv_first.reshape(3, 3 * channels, channels),
        conv_second.reshape(3, 3 * channels, channels),
    )


def swap(array, axis, bit):
    count = lax.axis_size(axis)
    return lax.ppermute(array, axis, [(i, i ^ (1 << bit)) for i in range(count)])


def shift(array, axis, by):
    count = lax.axis_size(axis)
    return lax.ppermute(
        array, axis, [(i, i + by) for i in range(count) if 0 <= i + by < count]
    )


def rotate(array, axis, by):
    count = lax.axis_size(axis)
    return lax.ppermute(array, axis, [(i, (i + by) % count) for i in range(count)])


def exchange_lines(strip):
    groups, count, cores = (lax.axis_size(axis) for axis in ("group", "wide", "narrow"))
    place = lax.axis_index("wide")
    got = []
    for start in range(2):
        pairs = []
        for g in range(groups):
            for w in range(count):
                other = w + 1 if w % 2 == start else w - 1
                far = g
                if not 0 <= other < count:
                    other, far = w, g ^ 1 if groups % 2 == 0 else g
                for c in range(cores):
                    pairs.append(((g * count + w) * cores + c, (far * count + other) * cores + c))
        upper = place % 2 == start
        out = jnp.where(upper, strip[BX - 2 :], strip[:2])
        got.append(lax.ppermute(out, ("group", "wide", "narrow"), pairs))
    above = jnp.where(place % 2 == 1, got[0], got[1])
    below = jnp.where(place % 2 == 1, got[1], got[0])
    above = jnp.where(place > 0, above, jnp.zeros_like(above))
    below = jnp.where(place < count - 1, below, jnp.zeros_like(below))
    return above, below


def earlier_state(totals, works):
    cores, shape = len(totals), totals[0].shape
    works, done = list(works), []
    pieces = [totals[0]] + [rotate(totals[k], "narrow", k) for k in range(1, cores)]
    running, packed = small_call(gather_kernel, "gather", pieces, [F32, BF16], shape)
    before = jnp.zeros(shape, F32)
    bits = lax.axis_size("wide").bit_length() - 1
    for bit in range(bits):
        held = None
        if works:
            held, packed = works.pop(0)(packed)
        other = swap(packed, "wide", bit)
        if held is not None:
            held, other = lax.optimization_barrier((held, other))
            done.append(held)
        if bit == bits - 1:
            break
        running, before, packed = small_call(
            functools.partial(scan_kernel, bit),
            "scan",
            [running, before, other],
            [F32, F32, BF16],
            shape,
        )
    outs = small_call(
        functools.partial(spread_kernel, cores, bits - 1),
        "spread",
        [before, other] + pieces,
        [BF16] * cores,
        shape,
    )
    states = [outs[0]] + [rotate(outs[k], "narrow", k) for k in range(1, cores)]
    while works:
        done.append(works.pop(0)(packed)[0])
    return states, done


def reduce_bricks(parts, orders):
    parts = [list(pair) for pair in parts]
    for level in range(len(orders[0])):
        arrived = [
            swap(gone, "wide", order[level]) for (_, gone), order in zip(parts, orders)
        ]
        for pair, more in zip(parts, arrived):
            total = (pair[0].astype(F32) + more.astype(F32)).astype(BF16)
            half = total.shape[0] // 2
            pair[0], pair[1] = total[:half] if half else total, total[half:]
    return [pair[0] if pair[0].shape[0] else pair[1] for pair in parts]


def per_device(voxels, w_qkv, w_out, w_feature, conv_first, conv_second, row_brick, cell_place):
    tokens = voxels.shape[0]
    channels = w_feature.shape[1]
    wide_count, wide_place = lax.axis_size("wide"), lax.axis_index("wide")
    narrow_count, narrow_place = lax.axis_size("narrow"), lax.axis_index("narrow")

    blocks = tokens // BLK
    x, k, v, before, *totals = key_value(voxels, w_qkv, max(1, blocks // 2), narrow_count)
    cuts = sorted({blocks * i // 3 for i in range(4)})
    spans = [(first, last - first) for first, last in zip(cuts, cuts[1:])]

    def work(span):
        def run(array):
            array, k_now = lax.optimization_barrier((array, k))
            return local_attention(x, w_qkv, k_now, v, before, *span), array

        return run

    states, pieces = earlier_state(totals, [work(span) for span in spans])

    bits = list(range(wide_count.bit_length() - 1))
    orders = [bits, bits[1::-1] + bits[2:]]
    kept_a, sent_a, kept_b, sent_b = finish(
        spans,
        row_brick[:, 0],
        [q for q, _ in pieces],
        [part for _, part in pieces],
        states,
        x,
        w_out,
        w_feature,
        cell_place.reshape(-1, ROW),
        wide_count,
        orders,
    )
    top, bottom = reduce_bricks([(kept_a, sent_a), (kept_b, sent_b)], orders)
    own = jnp.concatenate([top[0], bottom[0]], axis=0).reshape(BX, BY, channels)

    if narrow_count == 2:
        edge = jnp.where(narrow_place == 0, own[:, BY - 2 :], own[:, :2])
        other = swap(edge, "narrow", 0)
        left = jnp.where(narrow_place == 1, other, jnp.zeros_like(other))
        right = jnp.where(narrow_place == 0, other, jnp.zeros_like(other))
    else:
        left = shift(own[:, BY - 2 :], "narrow", 1)
        right = shift(own[:, :2], "narrow", -1)
    strip = jnp.concatenate([own, left, right], axis=1)
    above, below = exchange_lines(strip)
    left = jnp.concatenate([above[:, BY : BY + 2], left, below[:, BY : BY + 2]], axis=0)
    right = jnp.concatenate([above[:, BY + 2 :], right, below[:, BY + 2 :]], axis=0)
    edges = jnp.stack(
        [
            (wide_place == 0).astype(jnp.int32),
            (wide_place == wide_count - 1).astype(jnp.int32),
            jnp.where(narrow_place == 0, 0, -1),
            jnp.where(narrow_place == narrow_count - 1, BY, BY + 1),
        ]
    ).astype(jnp.int32)
    return field_flow(
        edges, own, above[:, :BY], below[:, :BY], left, right, conv_first, conv_second
    )


def solution(mesh):
    placed = (
        P(("group", "wide", "narrow"), None),
        P(),
        P(),
        P(),
        P(),
        P(),
        P(("group", "wide", "narrow"), None),
        P(("group", "wide", "narrow")),
    )
    return jax.shard_map(
        per_device,
        mesh=mesh,
        in_specs=placed,
        out_specs=P(("group", "wide"), "narrow", None),
        check_vma=False,
    )
```

time: 82.7 us -> 62.9 us (0.76); the launches traced: 81.1 us -> 62.8 us
  local copies, waits for them, and re-layouts: 8.61 us -> 1.5 us
  Pallas kernels: 26.2 us -> 19.7 us
  waiting for transfers between devices: 23.1 us -> 17.1 us
  starting transfers between devices: 22.3 us -> 23.7 us
    unnamed x26 -> x14, local copies, waits for them, and re-layouts: 8.55 us -> 1.43 us
    ppermute x10, waiting for transfers between devices: 19.3 us -> 12.5 us  [swap(): return lax.ppermute(array, axis, [(i, i ^ 1 << bit) for i in range(count)])]
    pallas_call x3 -> x9, Pallas kernels: 22.6 us -> 16.2 us  [the longest x3 5.21 us: local_attention(): pl.pallas_call(functools.partial(local_kernel, first, count), in_specs=[v...]
    ppermute x10, starting transfers between devices: 15.9 us -> 20.1 us  [swap(): return lax.ppermute(array, axis, [(i, i ^ 1 << bit) for i in range(count)])]
    ppermute x4, starting transfers between devices: 6.35 us -> 3.68 us  [the longest x2 3.08 us: exchange_lines(): got.append(lax.ppermute(out, ('group', 'wide', 'narrow'), pairs))]
  transfers between devices with their start and end apart: 14 -> 14, of which waited for: 11 -> 12; matrix products, arithmetic and copies ran while one was open for 0% -> 1% of each run, Pallas kernels for 12% -> 8%
where the time goes in v2:
time: 62.9 us; the launch traced here: 62.8 us
  starting transfers between devices  23.7 us (38%)
  Pallas kernels  19.7 us (31%)
  waiting for transfers between devices  17.1 us (27%)
  local copies, waits for them, and re-layouts  1.5 us (2%)
    ppermute x10, starting transfers between devices, swap(): return lax.ppermute(array, axis, [(i, i ^ 1 << bit) for i in range(count)])  20.1 us
    ppermute x10, waiting for transfers between devices, swap(): return lax.ppermute(array, axis, [(i, i ^ 1 << bit) for i in range(count)])  12.5 us
    pallas_call x3, Pallas kernels, local_attention(): pl.pallas_call(functools.partial(local_kernel, first, count), in_specs=[v...  5.21 us
    pallas_call x1, Pallas kernels, finish(): pl.pallas_call(functools.partial(finish_kernel, orders, spans, len(states...  5.2 us
    pallas_call x1, Pallas kernels, key_value(): pl.pallas_call(functools.partial(key_value_kernel, chunks), in_specs=[hbm...  4.98 us
    pallas_call x1, Pallas kernels, field_flow(): pl.pallas_call(field_kernel, in_specs=[pl.BlockSpec(memory_space=pltpu.SM...  3.53 us
    ppermute x2, starting transfers between devices, exchange_lines(): got.append(lax.ppermute(out, ('group', 'wide', 'narrow'), pairs))  3.08 us
    ppermute x2, waiting for transfers between devices, exchange_lines(): got.append(lax.ppermute(out, ('group', 'wide', 'narrow'), pairs))  2.43 us
  transfers between devices with their start and end apart: 14, of which 12 were waited for; matrix products, arithmetic and copies ran while one was open for 1% of the time, Pallas kernels for 8%

profile of v2, /device:TPU:0, one launch (start us, length us, event | category | flops | bytes accessed | tf_op | source)
XLA Modules:
  0.0 62.8 jit_solution(11272026433096047563)
XLA Ops:
  0.0 1.4 %copy-done = bf16[512,1536]{1,0:T(8,128)(2,1)S(1)} copy-done((bf16[512,1536]{1,0:T(8,128)(2,1)S(1)}, bf16[512,1536]{1,0:T(8,128)(2,1)}, u32[]{:S(2)}) %copy-start) | copy-done | bytes 1572888
  1.4 5.0 %key_value.1 = (bf16[2048,512]{1,0:T(8,128)(2,1)S(1)}, bf16[2048,512]{1,0:T(8,128)(2,1)S(1)}, bf16[2048,512]{1,0:T(8,128)(2,1)S(1)}, bf16[8,4,128,128]{3,2,1,0:T...) custom-call(bf16[2048,512]{1,0:T(8,128)(2,1)} %x_ref.1, bf16[512,1536]{1,0:T(8,128)(2,1)S(1)} %copy-done), custom_call_target="tpu_custom_call" | custom-call | tf_op jit(solution)/shard_map/key_value/pallas_call | solution.py:96
  6.4 0.5 collective-permute-start
  6.9 0.9 %collective-permute-done.refs_1_ = bf16[2,128,128]{2,1,0:T(8,128)(2,1)S(1)} collective-permute-done((bf16[2,128,128]{2,1,0:T(8,128)(2,1)S(1)}, bf16[2,128,128]{2,1,0:T(8,128)(2,1)S(1)}, u32[]{:S(2)}, u32[]{:S(2)}) %collective-permute-start) | collective-permute-done | bytes 65568 | tf_op jit(solution)/shard_map/ppermute | solution.py:349
  7.8 2.9 %collective-permute-start.1 = (bf16[2,128,128]{2,1,0:T(8,128)(2,1)S(1)}, bf16[2,128,128]{2,1,0:T(8,128)(2,1)S(1)}, u32[]{:S(2)}, u32[]{:S(2)}) collective-permute-start(bf16[2,128,128]{2,1,0:T(8,128)(2,1)S(1)} %get-tuple-element.55), channel_id=1, source_target_pairs={{0,2},{2,0},{4,6},{6,4},{8,10},{10,8},{12,14},{14,12},{1,3},{3,1},... | collective-permute-start | bytes 196616 | tf_op jit(solution)/shard_map/ppermute | solution.py:337
  10.8 1.3 %local_attention.3 = (bf16[512,512]{1,0:T(8,128)(2,1)S(1)}, f32[512,512]{1,0:T(8,128)S(1)}) custom-call(bf16[2048,512]{1,0:T(8,128)(2,1)S(1)} %get-tuple-element.45.x_ref.refs_8_, bf16[512,1536]{1,0:T(8,128)(2,1)S(1)} %copy-done, bf16[2048,512]{1,0:T(8,128)(2,1)S(1)} %get-tuple-element.69.k_ref, bf16[2048,512]{1,0:T(8,128)(2,1)S(1)} %get-tuple-element.51.v_ref, ...), custom_call_target="tpu_custom_call" | custom-call | flops 603979776 | bytes 3145728 | tf_op jit(solution)/shard_map/local_attention/pallas_call | solution.py:131
  12.1 1.1 %collective-permute-done.1.other_ref = bf16[2,128,128]{2,1,0:T(8,128)(2,1)S(1)} collective-permute-done((bf16[2,128,128]{2,1,0:T(8,128)(2,1)S(1)}, bf16[2,128,128]{2,1,0:T(8,128)(2,1)S(1)}, u32[]{:S(2)}, u32[]{:S(2)}) %collective-permute-start.1) | collective-permute-done | bytes 65568 | tf_op jit(solution)/shard_map/ppermute | solution.py:337
  13.2 2.0 %collective-permute-start.2 = (bf16[2,128,128]{2,1,0:T(8,128)(2,1)S(1)}, bf16[2,128,128]{2,1,0:T(8,128)(2,1)S(1)}, u32[]{:S(2)}, u32[]{:S(2)}) collective-permute-start(bf16[2,128,128]{2,1,0:T(8,128)(2,1)S(1)} %get-tuple-element.63), channel_id=1, source_target_pairs={{0,4},{2,6},{4,0},{6,2},{8,12},{10,14},{12,8},{14,10},{1,5},{3,7},... | collective-permute-start | bytes 196616 | tf_op jit(solution)/shard_map/ppermute | solution.py:337
  15.2 1.9 %local_attention.4 = (bf16[768,512]{1,0:T(8,128)(2,1)S(1)}, f32[768,512]{1,0:T(8,128)S(1)}) custom-call(bf16[2048,512]{1,0:T(8,128)(2,1)S(1)} %get-tuple-element.45.x_ref.refs_8_, bf16[512,1536]{1,0:T(8,128)(2,1)S(1)} %copy-done, bf16[2048,512]{1,0:T(8,128)(2,1)S(1)} %get-tuple-element.69.k_ref, bf16[2048,512]{1,0:T(8,128)(2,1)S(1)} %get-tuple-element.51.v_ref, ...), custom_call_target="tpu_custom_call" | custom-call | flops 905969664 | bytes 4718592 | tf_op jit(solution)/shard_map/local_attention/pallas_call | solution.py:131
  17.2 0.4 collective-permute-done.2.other_ref
  17.6 0.7 %scan.3 = (f32[2,128,128]{2,1,0:T(8,128)}, f32[2,128,128]{2,1,0:T(8,128)S(1)}, bf16[2,128,128]{2,1,0:T(8,128)(2,1)S(1)}) custom-call(f32[2,128,128]{2,1,0:T(8,128)S(1)} %get-tuple-element.65.running_ref, f32[2,128,128]{2,1,0:T(8,128)S(1)} %get-tuple-element.66.before_ref, bf16[2,128,128]{2,1,0:T(8,128)(2,1)S(1)} %collective-permute-done.2.other_ref), custom_call_target="tpu_custom_call" | custom-call | tf_op jit(solution)/shard_map/scan/pallas_call | solution.py:182
  18.3 3.0 %collective-permute-start.3 = (bf16[2,128,128]{2,1,0:T(8,128)(2,1)S(1)}, bf16[2,128,128]{2,1,0:T(8,128)(2,1)S(1)}, u32[]{:S(2)}, u32[]{:S(2)}) collective-permute-start(bf16[2,128,128]{2,1,0:T(8,128)(2,1)S(1)} %get-tuple-element.72), channel_id=1, source_target_pairs={{0,8},{2,10},{4,12},{6,14},{8,0},{10,2},{12,4},{14,6},{1,9},{3,11}... | collective-permute-start | bytes 196616 | tf_op jit(solution)/shard_map/ppermute | solution.py:337
  21.2 1.9 %local_attention.5 = (bf16[768,512]{1,0:T(8,128)(2,1)S(1)}, f32[768,512]{1,0:T(8,128)S(1)}) custom-call(bf16[2048,512]{1,0:T(8,128)(2,1)S(1)} %get-tuple-element.45.x_ref.refs_8_, bf16[512,1536]{1,0:T(8,128)(2,1)S(1)} %copy-done, bf16[2048,512]{1,0:T(8,128)(2,1)S(1)} %get-tuple-element.69.k_ref, bf16[2048,512]{1,0:T(8,128)(2,1)S(1)} %get-tuple-element.51.v_ref, ...), custom_call_target="tpu_custom_call" | custom-call | flops 905969664 | bytes 4718592 | tf_op jit(solution)/shard_map/local_attention/pallas_call | solution.py:131
  23.2 0.3 collective-permute-done.3.other_ref
  23.5 0.1 spread.1
  23.6 0.1 collective-permute-start.4
  23.6 1.2 %collective-permute-done.4.refs_7_ = bf16[2,128,128]{2,1,0:T(8,128)(2,1)S(1)} collective-permute-done((bf16[2,128,128]{2,1,0:T(8,128)(2,1)S(1)}, bf16[2,128,128]{2,1,0:T(8,128)(2,1)S(1)}, u32[]{:S(2)}, u32[]{:S(2)}) %collective-permute-start.4) | collective-permute-done | bytes 65568 | tf_op jit(solution)/shard_map/ppermute | solution.py:349
  24.9 0.0 copy-done.3
  24.9 0.0 copy-done.4
  24.9 0.0 copy-done.5
  24.9 0.0 copy-done.6
  24.9 5.2 %finish.1 = (bf16[4,128,256]{2,1,0:T(8,128)(2,1)S(1)}, bf16[4,128,256]{2,1,0:T(8,128)(2,1)S(1)}, bf16[4,128,256]{2,1,0:T(8,128)(2,1)S(1)}, bf16[4,128,256]{2,1,0:T(8,128)(2,1)S(1)}) custom-call(s32[16]{0:T(128)S(1)} %bitcast.19, bf16[512,512]{1,0:T(8,128)(2,1)S(1)} %get-tuple-element.56.refs_0_, bf16[768,512]{1,0:T(8,128)(2,1)S(1)} %get-tuple-element.64.refs_1_, ...), custom_call_target="tpu_custom_call" | custom-call | tf_op jit(solution)/shard_map/finish/pallas_call | solution.py:242
  30.1 1.9 %collective-permute-start.5 = (bf16[4,128,256]{2,1,0:T(8,128)(2,1)S(1)}, bf16[4,128,256]{2,1,0:T(8,128)(2,1)S(1)}, u32[]{:S(2)}, u32[]{:S(2)}) collective-permute-start(bf16[4,128,256]{2,1,0:T(8,128)(2,1)S(1)} %get-tuple-element.82), channel_id=1, source_target_pairs={{0,2},{2,0},{4,6},{6,4},{8,10},{10,8},{12,14},{14,12},{1,3},{3,1},... | collective-permute-start | bytes 786440 | tf_op jit(solution)/shard_map/ppermute | solution.py:337
  32.0 1.6 %collective-permute-start.8 = (bf16[4,128,256]{2,1,0:T(8,128)(2,1)S(1)}, bf16[4,128,256]{2,1,0:T(8,128)(2,1)S(1)}, u32[]{:S(2)}, u32[]{:S(2)}) collective-permute-start(bf16[4,128,256]{2,1,0:T(8,128)(2,1)S(1)} %get-tuple-element.84), channel_id=1, source_target_pairs={{0,4},{2,6},{4,0},{6,2},{8,12},{10,14},{12,8},{14,10},{1,5},{3,7},... | collective-permute-start | bytes 786440 | tf_op jit(solution)/shard_map/ppermute | solution.py:337
  33.6 5.0 %collective-permute-done.5 = bf16[4,128,256]{2,1,0:T(8,128)(2,1)S(1)} collective-permute-done((bf16[4,128,256]{2,1,0:T(8,128)(2,1)S(1)}, bf16[4,128,256]{2,1,0:T(8,128)(2,1)S(1)}, u32[]{:S(2)}, u32[]{:S(2)}) %collective-permute-start.5) | collective-permute-done | bytes 262176 | tf_op jit(solution)/shard_map/ppermute | solution.py:337
  38.6 0.1 add_convert_fusion.1
  38.7 1.9 %collective-permute-start.6 = (bf16[2,128,256]{2,1,0:T(8,128)(2,1)S(1)}, bf16[2,128,256]{2,1,0:T(8,128)(2,1)S(1)}, u32[]{:S(2)}, u32[]{:S(2)}) collective-permute-start(bf16[2,128,256]{2,1,0:T(8,128)(2,1)S(1)} %slice.75), channel_id=1, source_target_pairs={{0,4},{2,6},{4,0},{6,2},{8,12},{10,14},{12,8},{14,10},{1,5},{3,7},... | collective-permute-start | bytes 393224 | tf_op jit(solution)/shard_map/ppermute | solution.py:337
  40.6 0.0 collective-permute-done.8
  40.6 0.1 add_convert_fusion
  40.7 0.0 copy-start.1
  40.7 0.0 copy-start.2
  40.7 1.6 %collective-permute-start.9 = (bf16[2,128,256]{2,1,0:T(8,128)(2,1)S(1)}, bf16[2,128,256]{2,1,0:T(8,128)(2,1)S(1)}, u32[]{:S(2)}, u32[]{:S(2)}) collective-permute-start(bf16[2,128,256]{2,1,0:T(8,128)(2,1)S(1)} %slice.79), channel_id=1, source_target_pairs={{0,2},{2,0},{4,6},{6,4},{8,10},{10,8},{12,14},{14,12},{1,3},{3,1},... | collective-permute-start | bytes 393224 | tf_op jit(solution)/shard_map/ppermute | solution.py:337
  42.3 1.5 %collective-permute-done.6 = bf16[2,128,256]{2,1,0:T(8,128)(2,1)S(1)} collective-permute-done((bf16[2,128,256]{2,1,0:T(8,128)(2,1)S(1)}, bf16[2,128,256]{2,1,0:T(8,128)(2,1)S(1)}, u32[]{:S(2)}, u32[]{:S(2)}) %collective-permute-start.6) | collective-permute-done | bytes 131104 | tf_op jit(solution)/shard_map/ppermute | solution.py:337
  43.8 3.1 %collective-permute-start.7 = (bf16[1,128,256]{2,1,0:T(8,128)(2,1)S(1)}, bf16[1,128,256]{2,1,0:T(8,128)(2,1)S(1)}, u32[]{:S(2)}, u32[]{:S(2)}) collective-permute-start(bf16[1,128,256]{2,1,0:T(8,128)(2,1)S(1)} %slice.77), channel_id=1, source_target_pairs={{0,8},{2,10},{4,12},{6,14},{8,0},{10,2},{12,4},{14,6},{1,9},{3,11}... | collective-permute-start | bytes 196616 | tf_op jit(solution)/shard_map/ppermute | solution.py:337
  46.9 0.0 collective-permute-done.9
  46.9 2.1 %collective-permute-start.10 = (bf16[1,128,256]{2,1,0:T(8,128)(2,1)S(1)}, bf16[1,128,256]{2,1,0:T(8,128)(2,1)S(1)}, u32[]{:S(2)}, u32[]{:S(2)}) collective-permute-start(bf16[1,128,256]{2,1,0:T(8,128)(2,1)S(1)} %slice.81), channel_id=1, source_target_pairs={{0,8},{2,10},{4,12},{6,14},{8,0},{10,2},{12,4},{14,6},{1,9},{3,11}... | collective-permute-start | bytes 196616 | tf_op jit(solution)/shard_map/ppermute | solution.py:337
  49.0 0.6 collective-permute-done.7
  49.6 2.5 %collective-permute-done.10 = bf16[1,128,256]{2,1,0:T(8,128)(2,1)S(1)} collective-permute-done((bf16[1,128,256]{2,1,0:T(8,128)(2,1)S(1)}, bf16[1,128,256]{2,1,0:T(8,128)(2,1)S(1)}, u32[]{:S(2)}, u32[]{:S(2)}) %collective-permute-start.10) | collective-permute-done | bytes 65568 | tf_op jit(solution)/shard_map/ppermute | solution.py:337
  52.2 0.1 collective-permute-start.11
  52.3 1.1 %collective-permute-done.11 = bf16[8,2,256]{2,1,0:T(2,128)(2,1)S(1)} collective-permute-done((bf16[8,2,256]{2,1,0:T(2,128)(2,1)S(1)}, bf16[8,2,256]{2,1,0:T(2,128)(2,1)S(1)}, u32[]{:S(2)}, u32[]{:S(2)}) %collective-permute-start.11) | collective-permute-done | bytes 8224 | tf_op jit(solution)/shard_map/ppermute | solution.py:337
  53.5 1.6 %collective-permute-start.12 = (bf16[2,36,256]{2,1,0:T(8,128)(2,1)S(1)}, bf16[2,36,256]{2,1,0:T(8,128)(2,1)S(1)}, u32[]{:S(2)}, u32[]{:S(2)}) collective-permute-start(bf16[2,36,256]{2,1,0:T(8,128)(2,1)S(1)} %broadcast_select_fusion), channel_id=1, source_target_pairs={{0,2},{1,3},{2,0},{3,1},{4,6},{5,7},{6,4},{7,5},{8,10},{9,11},{10,... | collective-permute-start | bytes 110600 | tf_op jit(solution)/shard_map/ppermute | solution.py:368
  55.1 1.5 %collective-permute-start.13 = (bf16[2,36,256]{2,1,0:T(8,128)(2,1)S(1)}, bf16[2,36,256]{2,1,0:T(8,128)(2,1)S(1)}, u32[]{:S(2)}, u32[]{:S(2)}) collective-permute-start(bf16[2,36,256]{2,1,0:T(8,128)(2,1)S(1)} %get-tuple-element.85), channel_id=1, source_target_pairs={{0,16},{1,17},{2,4},{3,5},{4,2},{5,3},{6,8},{7,9},{8,6},{9,7},{10,... | collective-permute-start | bytes 110600 | tf_op jit(solution)/shard_map/ppermute | solution.py:368
  56.6 0.1 pad_add_fusion.edge_ref
  56.7 0.9 %collective-permute-done.12 = bf16[2,36,256]{2,1,0:T(8,128)(2,1)S(1)} collective-permute-done((bf16[2,36,256]{2,1,0:T(8,128)(2,1)S(1)}, bf16[2,36,256]{2,1,0:T(8,128)(2,1)S(1)}, u32[]{:S(2)}, u32[]{:S(2)}) %collective-permute-start.12) | collective-permute-done | bytes 36896 | tf_op jit(solution)/shard_map/ppermute | solution.py:368
  57.6 1.5 %collective-permute-done.13 = bf16[2,36,256]{2,1,0:T(8,128)(2,1)S(1)} collective-permute-done((bf16[2,36,256]{2,1,0:T(8,128)(2,1)S(1)}, bf16[2,36,256]{2,1,0:T(8,128)(2,1)S(1)}, u32[]{:S(2)}, u32[]{:S(2)}) %collective-permute-start.13) | collective-permute-done | bytes 36896 | tf_op jit(solution)/shard_map/ppermute | solution.py:368
  59.2 0.0 copy-done.1
  59.3 0.0 copy-done.2
  59.3 3.5 %field_flow.1 = f32[8,32,256]{2,1,0:T(8,128)} custom-call(s32[4]{0:T(128)S(1)} %pad_add_fusion.edge_ref, bf16[8,32,256]{2,1,0:T(8,128)(2,1)S(1)} %bitcast.15, bf16[2,32,256]{2,1,0:T(8,128)(2,1)S(1)} %slice.84.above_ref, bf16[2,32,256]{2,1,0:T(8,128)(2,1)S(1)} %slice.85.below_ref, bf16[12,2,256]{2,1,0:T(2,128)(2,1)S(1)} %get-tuple-element.96.left_ref, ...), custom_call_target="tpu_custom_call" | custom-call | tf_op jit(solution)/shard_map/field_flow/pallas_call | solution.py:312
  (27 shorter events, 0.4 us)
Async XLA Ops:
  0.0 1.4 %copy-start = (bf16[512,1536]{1,0:T(8,128)(2,1)S(1)}, bf16[512,1536]{1,0:T(8,128)(2,1)}, u32[]{:S(2)}) copy-start(bf16[512,1536]{1,0:T(8,128)(2,1)} %w_ref.7) | copy-start | bytes 4718596
  6.4 1.4 %collective-permute-start = (bf16[2,128,128]{2,1,0:T(8,128)(2,1)S(1)}, bf16[2,128,128]{2,1,0:T(8,128)(2,1)S(1)}, u32[]{:S(2)}, u32[]{:S(2)}) collective-permute-start(bf16[2,128,128]{2,1,0:T(8,128)(2,1)S(1)} %get-tuple-element.47), channel_id=1, source_target_pairs={{0,1},{1,0},{2,3},{3,2},{4,5},{5,4},{6,7},{7,6},{8,9},{9,8},{10,11... | collective-permute-start | bytes 196616 | tf_op jit(solution)/shard_map/ppermute | solution.py:349
  7.8 5.3 %collective-permute-start.1 = (bf16[2,128,128]{2,1,0:T(8,128)(2,1)S(1)}, bf16[2,128,128]{2,1,0:T(8,128)(2,1)S(1)}, u32[]{:S(2)}, u32[]{:S(2)}) collective-permute-start(bf16[2,128,128]{2,1,0:T(8,128)(2,1)S(1)} %get-tuple-element.55), channel_id=1, source_target_pairs={{0,2},{2,0},{4,6},{6,4},{8,10},{10,8},{12,14},{14,12},{1,3},{3,1},... | collective-permute-start | bytes 196616 | tf_op jit(solution)/shard_map/ppermute | solution.py:337
  13.2 4.3 %collective-permute-start.2 = (bf16[2,128,128]{2,1,0:T(8,128)(2,1)S(1)}, bf16[2,128,128]{2,1,0:T(8,128)(2,1)S(1)}, u32[]{:S(2)}, u32[]{:S(2)}) collective-permute-start(bf16[2,128,128]{2,1,0:T(8,128)(2,1)S(1)} %get-tuple-element.63), channel_id=1, source_target_pairs={{0,4},{2,6},{4,0},{6,2},{8,12},{10,14},{12,8},{14,10},{1,5},{3,7},... | collective-permute-start | bytes 196616 | tf_op jit(solution)/shard_map/ppermute | solution.py:337
  18.2 6.7 %copy-start.3 = (bf16[512,512]{1,0:T(8,128)(2,1)S(1)}, bf16[512,512]{1,0:T(8,128)(2,1)}, u32[]{:S(2)}) copy-start(bf16[512,512]{1,0:T(8,128)(2,1)} %refs_9_.1) | copy-start | bytes 1572868
  18.2 6.7 %copy-start.4 = (bf16[512,256]{1,0:T(8,128)(2,1)S(1)}, bf16[512,256]{1,0:T(8,128)(2,1)}, u32[]{:S(2)}) copy-start(bf16[512,256]{1,0:T(8,128)(2,1)} %refs_10_.1) | copy-start | bytes 786436
  18.2 6.7 %copy-start.5 = (s32[2048]{0:T(1024)S(1)}, s32[2048]{0:T(1024)}, u32[]{:S(2)}) copy-start(s32[2048]{0:T(1024)} %param.15) | copy-start | bytes 24580
  18.2 6.7 %copy-start.6 = (s32[16,1]{0,1:T(1,128)S(1)}, s32[16,1]{0,1:T(1,128)}, u32[]{:S(2)}) copy-start(s32[16,1]{0,1:T(1,128)} %param.14) | copy-start | bytes 196
  18.3 5.2 %collective-permute-start.3 = (bf16[2,128,128]{2,1,0:T(8,128)(2,1)S(1)}, bf16[2,128,128]{2,1,0:T(8,128)(2,1)S(1)}, u32[]{:S(2)}, u32[]{:S(2)}) collective-permute-start(bf16[2,128,128]{2,1,0:T(8,128)(2,1)S(1)} %get-tuple-element.72), channel_id=1, source_target_pairs={{0,8},{2,10},{4,12},{6,14},{8,0},{10,2},{12,4},{14,6},{1,9},{3,11}... | collective-permute-start | bytes 196616 | tf_op jit(solution)/shard_map/ppermute | solution.py:337
  23.6 1.3 %collective-permute-start.4 = (bf16[2,128,128]{2,1,0:T(8,128)(2,1)S(1)}, bf16[2,128,128]{2,1,0:T(8,128)(2,1)S(1)}, u32[]{:S(2)}, u32[]{:S(2)}) collective-permute-start(bf16[2,128,128]{2,1,0:T(8,128)(2,1)S(1)} %get-tuple-element.80), channel_id=1, source_target_pairs={{0,1},{1,0},{2,3},{3,2},{4,5},{5,4},{6,7},{7,6},{8,9},{9,8},{10,11... | collective-permute-start | bytes 196616 | tf_op jit(solution)/shard_map/ppermute | solution.py:349
  30.1 8.5 %collective-permute-start.5 = (bf16[4,128,256]{2,1,0:T(8,128)(2,1)S(1)}, bf16[4,128,256]{2,1,0:T(8,128)(2,1)S(1)}, u32[]{:S(2)}, u32[]{:S(2)}) collective-permute-start(bf16[4,128,256]{2,1,0:T(8,128)(2,1)S(1)} %get-tuple-element.82), channel_id=1, source_target_pairs={{0,2},{2,0},{4,6},{6,4},{8,10},{10,8},{12,14},{14,12},{1,3},{3,1},... | collective-permute-start | bytes 786440 | tf_op jit(solution)/shard_map/ppermute | solution.py:337
  32.0 8.6 %collective-permute-start.8 = (bf16[4,128,256]{2,1,0:T(8,128)(2,1)S(1)}, bf16[4,128,256]{2,1,0:T(8,128)(2,1)S(1)}, u32[]{:S(2)}, u32[]{:S(2)}) collective-permute-start(bf16[4,128,256]{2,1,0:T(8,128)(2,1)S(1)} %get-tuple-element.84), channel_id=1, source_target_pairs={{0,4},{2,6},{4,0},{6,2},{8,12},{10,14},{12,8},{14,10},{1,5},{3,7},... | collective-permute-start | bytes 786440 | tf_op jit(solution)/shard_map/ppermute | solution.py:337
  38.7 5.0 %collective-permute-start.6 = (bf16[2,128,256]{2,1,0:T(8,128)(2,1)S(1)}, bf16[2,128,256]{2,1,0:T(8,128)(2,1)S(1)}, u32[]{:S(2)}, u32[]{:S(2)}) collective-permute-start(bf16[2,128,256]{2,1,0:T(8,128)(2,1)S(1)} %slice.75), channel_id=1, source_target_pairs={{0,4},{2,6},{4,0},{6,2},{8,12},{10,14},{12,8},{14,10},{1,5},{3,7},... | collective-permute-start | bytes 393224 | tf_op jit(solution)/shard_map/ppermute | solution.py:337
  40.7 18.6 %copy-start.1 = (bf16[3,3,256,256]{3,2,1,0:T(8,128)(2,1)S(1)}, bf16[3,3,256,256]{3,2,1,0:T(8,128)(2,1)}, u32[]{:S(2)}) copy-start(bf16[3,3,256,256]{3,2,1,0:T(8,128)(2,1)} %param.12) | copy-start | bytes 3538948
  40.7 18.6 %copy-start.2 = (bf16[3,3,256,256]{3,2,1,0:T(8,128)(2,1)S(1)}, bf16[3,3,256,256]{3,2,1,0:T(8,128)(2,1)}, u32[]{:S(2)}) copy-start(bf16[3,3,256,256]{3,2,1,0:T(8,128)(2,1)} %param.13) | copy-start | bytes 3538948
  40.7 6.2 %collective-permute-start.9 = (bf16[2,128,256]{2,1,0:T(8,128)(2,1)S(1)}, bf16[2,128,256]{2,1,0:T(8,128)(2,1)S(1)}, u32[]{:S(2)}, u32[]{:S(2)}) collective-permute-start(bf16[2,128,256]{2,1,0:T(8,128)(2,1)S(1)} %slice.79), channel_id=1, source_target_pairs={{0,2},{2,0},{4,6},{6,4},{8,10},{10,8},{12,14},{14,12},{1,3},{3,1},... | collective-permute-start | bytes 393224 | tf_op jit(solution)/shard_map/ppermute | solution.py:337
  43.8 5.8 %collective-permute-start.7 = (bf16[1,128,256]{2,1,0:T(8,128)(2,1)S(1)}, bf16[1,128,256]{2,1,0:T(8,128)(2,1)S(1)}, u32[]{:S(2)}, u32[]{:S(2)}) collective-permute-start(bf16[1,128,256]{2,1,0:T(8,128)(2,1)S(1)} %slice.77), channel_id=1, source_target_pairs={{0,8},{2,10},{4,12},{6,14},{8,0},{10,2},{12,4},{14,6},{1,9},{3,11}... | collective-permute-start | bytes 196616 | tf_op jit(solution)/shard_map/ppermute | solution.py:337
  46.9 5.2 %collective-permute-start.10 = (bf16[1,128,256]{2,1,0:T(8,128)(2,1)S(1)}, bf16[1,128,256]{2,1,0:T(8,128)(2,1)S(1)}, u32[]{:S(2)}, u32[]{:S(2)}) collective-permute-start(bf16[1,128,256]{2,1,0:T(8,128)(2,1)S(1)} %slice.81), channel_id=1, source_target_pairs={{0,8},{2,10},{4,12},{6,14},{8,0},{10,2},{12,4},{14,6},{1,9},{3,11}... | collective-permute-start | bytes 196616 | tf_op jit(solution)/shard_map/ppermute | solution.py:337
  52.2 1.2 %collective-permute-start.11 = (bf16[8,2,256]{2,1,0:T(2,128)(2,1)S(1)}, bf16[8,2,256]{2,1,0:T(2,128)(2,1)S(1)}, u32[]{:S(2)}, u32[]{:S(2)}) collective-permute-start(bf16[8,2,256]{2,1,0:T(2,128)(2,1)S(1)} %broadcast_select_fusion.3), channel_id=1, source_target_pairs={{0,1},{1,0},{2,3},{3,2},{4,5},{5,4},{6,7},{7,6},{8,9},{9,8},{10,11... | collective-permute-start | bytes 24584 | tf_op jit(solution)/shard_map/ppermute | solution.py:337
  53.5 4.1 %collective-permute-start.12 = (bf16[2,36,256]{2,1,0:T(8,128)(2,1)S(1)}, bf16[2,36,256]{2,1,0:T(8,128)(2,1)S(1)}, u32[]{:S(2)}, u32[]{:S(2)}) collective-permute-start(bf16[2,36,256]{2,1,0:T(8,128)(2,1)S(1)} %broadcast_select_fusion), channel_id=1, source_target_pairs={{0,2},{1,3},{2,0},{3,1},{4,6},{5,7},{6,4},{7,5},{8,10},{9,11},{10,... | collective-permute-start | bytes 110600 | tf_op jit(solution)/shard_map/ppermute | solution.py:368
  55.1 4.0 %collective-permute-start.13 = (bf16[2,36,256]{2,1,0:T(8,128)(2,1)S(1)}, bf16[2,36,256]{2,1,0:T(8,128)(2,1)S(1)}, u32[]{:S(2)}, u32[]{:S(2)}) collective-permute-start(bf16[2,36,256]{2,1,0:T(8,128)(2,1)S(1)} %get-tuple-element.85), channel_id=1, source_target_pairs={{0,16},{1,17},{2,4},{3,5},{4,2},{5,3},{6,8},{7,9},{8,6},{9,7},{10,... | collective-permute-start | bytes 110600 | tf_op jit(solution)/shard_map/ppermute | solution.py:368

commit v3 on v2

v3 whole, which is shorter than its diff:
```python
import functools

import jax
import jax.numpy as jnp
from jax import lax
from jax.experimental import pallas as pl
from jax.experimental.pallas import tpu as pltpu
from jax.sharding import PartitionSpec as P

HEADS = 4
HEAD = 128
ROW = 128
BLK = 256
BX = 8
BY = 32
EPS = 1e-06
GAP = 16
LINE = GAP + BY

F32 = jnp.float32
BF16 = jnp.bfloat16


def dot(a, b):
    return jnp.dot(a, b, preferred_element_type=F32)


def dot_t(a, b):
    return lax.dot_general(a, b, (((0,), (0,)), ((), ())), preferred_element_type=F32)


def dot_nt(a, b):
    return lax.dot_general(a, b, (((1,), (1,)), ((), ())), preferred_element_type=F32)


KEY_VALUE_KIB = 46592


def params(kib=24 * 1024):
    return pltpu.CompilerParams(vmem_limit_bytes=kib << 10)


def head_cols(h):
    return slice(h * HEAD, (h + 1) * HEAD)


def key_value_kernel(spans, x_ref, w_ref, *refs):
    refs = list(refs)
    take = lambda n: [refs.pop(0) for _ in range(n)]
    xs, ks, vs = take(len(spans)), take(len(spans)), take(len(spans))
    wq, before_ref = take(2)
    totals, (w, sems) = refs[:-2], refs[-2:]
    inner = HEADS * HEAD

    def columns(part, target):
        return pltpu.make_async_copy(
            w_ref.at[:, pl.ds(part * inner, inner)], target, sems.at[len(spans) + part]
        )

    loads = [
        pltpu.make_async_copy(x_ref.at[pl.ds(first * BLK, count * BLK)], x, sems.at[n])
        for n, ((first, count), x) in enumerate(zip(spans, xs))
    ]
    w_loads = [columns(0, wq), columns(1, w.at[0]), columns(2, w.at[1])]
    w_loads[1].start()
    loads[0].start()
    w_loads[2].start()
    for load in loads[1:]:
        load.start()
    w_loads[0].start()
    running = [jnp.zeros((HEAD, HEAD), F32) for _ in range(HEADS)]
    for n, ((first, count), x, k_ref, v_ref) in enumerate(zip(spans, xs, ks, vs)):
        if n == 0:
            w_loads[1].wait()
        loads[n].wait()
        k = dot(x[...], w[0]).astype(BF16)
        k_ref[...] = k
        if n == 0:
            w_loads[2].wait()
        v = dot(x[...], w[1]).astype(BF16)
        v_ref[...] = v
        for b in range(count):
            block = slice(b * BLK, (b + 1) * BLK)
            for h in range(HEADS):
                before_ref[first + b, h] = running[h].astype(BF16)
            for pair in range(HEADS // 2):
                cols = slice(pair * 2 * HEAD, (pair + 1) * 2 * HEAD)
                outer = dot_t(k[block, cols], v[block, cols])
                running[2 * pair] += outer[:HEAD, :HEAD]
                running[2 * pair + 1] += outer[HEAD:, HEAD:]
    share = HEADS // len(totals)
    for h in range(HEADS):
        for k, total_ref in enumerate(totals):

            @pl.when((lax.axis_index("narrow") + k) % len(totals) == h // share)
            def _(total_ref=total_ref, h=h):
                total_ref[h % share] = running[h].astype(BF16)

    w_loads[0].wait()


def key_value(spans, voxels, w_qkv, cores):
    tokens, width = voxels.shape
    inner = HEADS * HEAD
    hbm = pl.BlockSpec(memory_space=pl.ANY)
    vmem = pl.BlockSpec(memory_space=pltpu.VMEM)
    rows = [count * BLK for _, count in spans]
    out_shape = [jax.ShapeDtypeStruct((n, cols), BF16) for cols in (width, inner, inner) for n in rows]
    out_shape.append(jax.ShapeDtypeStruct((width, inner), BF16))
    out_shape.append(jax.ShapeDtypeStruct((tokens // BLK, HEADS, HEAD, HEAD), BF16))
    out_shape += [jax.ShapeDtypeStruct((HEADS // cores, HEAD, HEAD), BF16)] * cores
    outs = list(
        pl.pallas_call(
            functools.partial(key_value_kernel, spans),
            in_specs=[hbm, hbm],
            out_specs=[vmem] * len(out_shape),
            out_shape=out_shape,
            scratch_shapes=[
                pltpu.VMEM((2, width, inner), BF16),
                pltpu.SemaphoreType.DMA((len(spans) + 3,)),
            ],
            compiler_params=params(KEY_VALUE_KIB),
            name="key_value",
        )(voxels, w_qkv)
    )
    n = len(spans)
    return outs[:n], outs[n : 2 * n], outs[2 * n : 3 * n], outs[3 * n], outs[3 * n + 1], outs[3 * n + 2 :]


def local_kernel(first, count, weights, x_ref, wq_ref, k_ref, v_ref, before_ref, *refs):
    wf_ref, q_ref, part_ref, own_ref = refs[weights : weights + 4]
    causal = lax.broadcasted_iota(jnp.int32, (BLK, BLK), 0) >= lax.broadcasted_iota(
        jnp.int32, (BLK, BLK), 1
    )
    q = dot(x_ref[...], wq_ref[...]).astype(BF16)
    q_ref[...] = q
    own_ref[...] = dot(x_ref[...], wf_ref[...])
    for b in range(count):
        rows = slice(b * BLK, (b + 1) * BLK)
        for h in range(HEADS):
            cols = head_cols(h)
            scores = dot_nt(q[rows, cols], k_ref[rows, cols])
            scores = jnp.where(causal, scores, 0.0).astype(BF16)
            part_ref[rows, cols] = dot(scores, v_ref[rows, cols]) + dot(
                q[rows, cols], before_ref[first + b, h]
            )
    if weights:
        refs[-1][...] = dot(refs[0][...], wf_ref[...]).astype(BF16)


def local_attention(x, w_q, k, v, before, w_out, w_feature, first, count):
    rows, width = x.shape
    inner = HEADS * HEAD
    channels = w_feature.shape[1]
    vmem = pl.BlockSpec(memory_space=pltpu.VMEM)
    inputs = [x, w_q, k, v, before] + [w_out] * (w_out is not None) + [w_feature]
    out_shape = [
        jax.ShapeDtypeStruct((rows, inner), BF16),
        jax.ShapeDtypeStruct((rows, inner), F32),
        jax.ShapeDtypeStruct((rows, channels), F32),
    ]
    if w_out is not None:
        out_shape.append(jax.ShapeDtypeStruct(w_feature.shape, BF16))
    return pl.pallas_call(
        functools.partial(local_kernel, first, count, int(w_out is not None)),
        in_specs=[vmem] * len(inputs),
        out_specs=[vmem] * len(out_shape),
        out_shape=out_shape,
        compiler_params=params(),
        cost_estimate=pl.CostEstimate(
            flops=2 * rows * inner * (width + 2 * BLK + HEAD),
            bytes_accessed=rows * inner * 12,
            transcendentals=0,
        ),
        name="local_attention",
    )(*inputs)


def gather_kernel(*refs):
    ins, (running_ref, packed_ref) = refs[:-2], refs[-2:]
    running = sum(ref[...].astype(F32) for ref in ins)
    running_ref[...] = running
    packed_ref[...] = running.astype(BF16)


def scan_kernel(bit, running_ref, before_ref, other_ref, new_before, packed, *new_running):
    other = other_ref[...].astype(F32)
    running = running_ref[...] + other
    packed[...] = running.astype(BF16)
    for ref in new_running:
        ref[...] = running
    later = ((lax.axis_index("wide") >> bit) & 1).astype(F32)
    new_before[...] = before_ref[...] + later * other


def spread_kernel(cores, bit, before_ref, other_ref, *refs):
    pieces, outs = refs[:cores], refs[cores:]
    place = lax.axis_index("narrow")
    later = ((lax.axis_index("wide") >> bit) & 1).astype(F32)
    before = before_ref[...] + later * other_ref[...].astype(F32)
    for k, out in enumerate(outs):
        receiver = (place + k) % cores
        value = before
        for j, piece in enumerate(pieces):
            source = (place - j + cores) % cores
            value = value + jnp.where(source < receiver, 1.0, 0.0) * piece[...].astype(F32)
        out[...] = value.astype(BF16)


def small_call(kernel, name, inputs, dtypes, shape):
    vmem = pl.BlockSpec(memory_space=pltpu.VMEM)
    smem = pl.BlockSpec(memory_space=pltpu.SMEM)
    return pl.pallas_call(
        kernel,
        in_specs=[smem if array.dtype == jnp.int32 else vmem for array in inputs],
        out_specs=[vmem] * len(dtypes),
        out_shape=[jax.ShapeDtypeStruct(shape, dtype) for dtype in dtypes],
        compiler_params=params(4 * 1024),
        name=name,
    )(*inputs)


def ones_blocks(width):
    rows, cols = (lax.broadcasted_iota(jnp.int32, (width, width), axis) for axis in range(2))
    return jnp.where(rows // HEAD == cols // HEAD, 1.0, 0.0).astype(BF16)


def block_state(state_ref, scratch):
    scratch[...] = jnp.zeros_like(scratch)
    for j in range(state_ref.shape[0]):
        scratch[head_cols(j), head_cols(j)] = state_ref[j]
    return scratch[...]


def norm_share(q, part, state, ones):
    attended = part + dot(q, state)
    squares = dot((attended * attended).astype(BF16), ones)
    return (attended * lax.rsqrt(squares * (1 / HEAD) + EPS)).astype(BF16)


def share_columns(cores, before):
    width = HEADS // cores * HEAD
    owner = (lax.axis_index("narrow") - before + cores) % cores
    return pl.ds(pl.multiple_of(owner * width, width), width)


def own_share_kernel(cores, state_ref, *refs):
    pieces = len(refs) // 3
    qs, parts, outs, scratch = refs[:pieces], refs[pieces : 2 * pieces], refs[2 * pieces : -1], refs[-1]
    cols = share_columns(cores, 0)
    state, ones = block_state(state_ref, scratch), ones_blocks(scratch.shape[0])
    for q, part, out in zip(qs, parts, outs):
        out[...] = norm_share(q[:, cols], part[:, cols], state, ones)


def own_share(cores, state, qs, parts):
    width = HEADS // cores * HEAD
    vmem = pl.BlockSpec(memory_space=pltpu.VMEM)
    rows = sum(q.shape[0] for q in qs)
    return pl.pallas_call(
        functools.partial(own_share_kernel, cores),
        in_specs=[vmem] * (1 + 2 * len(qs)),
        out_specs=[vmem] * len(qs),
        out_shape=[jax.ShapeDtypeStruct((q.shape[0], width), BF16) for q in qs],
        scratch_shapes=[pltpu.VMEM((width, width), BF16)],
        compiler_params=params(),
        cost_estimate=pl.CostEstimate(
            flops=4 * rows * width * width, bytes_accessed=rows * width * 8, transcendentals=0
        ),
        name="own_share",
    )(state, *qs, *parts)


def finish_kernel(orders, spans, cores, brick_ref, *refs):
    pieces = len(spans)
    refs = list(refs)
    take = lambda n: [refs.pop(0) for _ in range(n)]
    q_refs, part_refs, normed_refs, own_refs = (take(pieces) for _ in range(4))
    state_refs = take(cores - 1)
    w_ref, cell_ref = take(2)
    outs = take(4)
    acc, scratch = refs
    shares = [share_columns(cores, k) for k in range(cores)]
    ones = ones_blocks(scratch.shape[1])
    states = [block_state(ref, scratch.at[k]) for k, ref in enumerate(state_refs)]
    acc[...] = jnp.zeros_like(acc)
    cells = BX * BY
    for n, (first, count) in enumerate(spans):
        features = own_refs[n][...] + dot(normed_refs[n][...], w_ref[shares[0], :])
        for state, cols in zip(states, shares[1:]):
            normed = norm_share(q_refs[n][:, cols], part_refs[n][:, cols], state, ones)
            features += dot(normed, w_ref[cols, :])
        features = features.astype(BF16)
        for r in range(count * BLK // ROW):
            row = first * BLK // ROW + r
            match = lax.broadcasted_iota(jnp.int32, (cells, ROW), 0) == cell_ref[row : row + 1]
            onehot = jnp.where(match, 1.0, 0.0).astype(BF16)
            brick = brick_ref[row] ^ lax.axis_index("wide")
            acc[brick] += dot(onehot, features[r * ROW : (r + 1) * ROW])
    ranges = [[(0, 2 * BY), (cells - 2 * BY, cells)], [(2 * BY, cells - 2 * BY)]]
    bricks = acc.shape[0]
    for part, order in enumerate(orders):
        for i in range(bricks):
            place = 0
            for bit in order:
                place = 2 * place + ((i >> bit) & 1)
            which, slot = divmod(place, bricks // 2)
            to = 0
            for first, last in ranges[part]:
                outs[2 * part + which][slot, to : to + last - first] = acc[i, first:last].astype(BF16)
                to += last - first


def finish(spans, bricks, qs, parts, normed, own, states, weights, cell_rows, count, orders):
    channels = weights.shape[1]
    cores = len(states) + 1
    width = HEADS // cores * HEAD
    cells = BX * BY
    vmem = pl.BlockSpec(memory_space=pltpu.VMEM)
    smem = pl.BlockSpec(memory_space=pltpu.SMEM)
    out = jax.ShapeDtypeStruct((count // 2, cells // 2, channels), BF16)
    return pl.pallas_call(
        functools.partial(finish_kernel, orders, spans, cores),
        in_specs=[smem] + [vmem] * (4 * len(spans) + cores + 1),
        out_specs=[vmem] * 4,
        out_shape=[out] * 4,
        scratch_shapes=[
            pltpu.VMEM((count, cells, channels), F32),
            pltpu.VMEM((max(1, cores - 1), width, width), BF16),
        ],
        compiler_params=params(),
        name="finish",
    )(bricks, *qs, *parts, *normed, *own, *states, weights, cell_rows)


def field_kernel(lines_ref, sides_ref, w1_ref, w2_ref, out_ref, field):
    lines = BX + 4
    wide, narrow = lax.axis_index("wide"), lax.axis_index("narrow")
    first_line, last_line = wide == 0, wide == lax.axis_size("wide") - 1
    first_column, last_column = narrow == 0, narrow == lax.axis_size("narrow") - 1
    for r in range(lines):
        field[r * LINE : r * LINE + GAP] = sides_ref[r]
        field[r * LINE + GAP : (r + 1) * LINE] = lines_ref[r]
    field[lines * LINE :] = sides_ref[lines]

    def convolve(w_ref, start, count):
        lhs = jnp.concatenate(
            [field[start + dy * LINE : start + dy * LINE + count] for dy in (-1, 0, 1)], axis=1
        )
        left, middle, right = [
            dot(lhs, jnp.concatenate([w_ref[dy, dx] for dy in range(3)], axis=0))
            for dx in range(3)
        ]
        return pltpu.roll(left, 1, 0) + middle + pltpu.roll(right, count - 1, 0)

    count = (BX + 2) * LINE + GAP
    inner = jax.nn.gelu(convolve(w1_ref, LINE, count), approximate=True)
    at = lax.broadcasted_iota(jnp.int32, (count, 1), 0)
    outside = first_line & (at <= LINE) | last_line & (at > (BX + 1) * LINE)
    for r in range(BX + 2):
        outside |= first_column & (at == r * LINE + GAP - 1)
        outside |= last_column & (at == (r + 1) * LINE)
    field[LINE : LINE + count] = jnp.where(outside, 0.0, inner).astype(BF16)
    flow = convolve(w2_ref, 2 * LINE, BX * LINE + GAP)
    for r in range(BX):
        out_ref[r] = flow[r * LINE + GAP : (r + 1) * LINE]


def field_flow(lines, left, right, conv_first, conv_second):
    count, _, channels = lines.shape
    vmem = pl.BlockSpec(memory_space=pltpu.VMEM)
    sides = jnp.pad(right, ((1, 0), (0, GAP - 2), (0, 0))) + jnp.pad(
        left, ((0, 1), (GAP - 2, 0), (0, 0))
    )
    return pl.pallas_call(
        field_kernel,
        in_specs=[vmem] * 4,
        out_specs=vmem,
        out_shape=jax.ShapeDtypeStruct((BX, BY, channels), F32),
        scratch_shapes=[pltpu.VMEM((count * LINE + GAP, channels), BF16)],
        compiler_params=params(16 * 1024),
        name="field_flow",
    )(lines, sides, conv_first, conv_second)


def swap(array, axis, bit):
    count = lax.axis_size(axis)
    return lax.ppermute(array, axis, [(i, i ^ (1 << bit)) for i in range(count)])


def shift(array, axis, by):
    count = lax.axis_size(axis)
    return lax.ppermute(
        array, axis, [(i, i + by) for i in range(count) if 0 <= i + by < count]
    )


def rotate(array, axis, by):
    count = lax.axis_size(axis)
    return lax.ppermute(array, axis, [(i, (i + by) % count) for i in range(count)])


def side_columns(lines):
    if lax.axis_size("narrow") != 2:
        return shift(lines[:, BY - 2 :], "narrow", 1), shift(lines[:, :2], "narrow", -1)
    first = lax.axis_index("narrow") == 0
    other = swap(jnp.where(first, lines[:, BY - 2 :], lines[:, :2]), "narrow", 0)
    nothing = jnp.zeros_like(other)
    return jnp.where(first, nothing, other), jnp.where(first, other, nothing)


def exchange_lines(strip):
    groups, count, cores = (lax.axis_size(axis) for axis in ("group", "wide", "narrow"))
    place = lax.axis_index("wide")
    got = []
    for start in range(2):
        pairs = []
        for g in range(groups):
            for w in range(count):
                other = w + 1 if w % 2 == start else w - 1
                far = g
                if not 0 <= other < count:
                    other, far = w, g ^ 1 if groups % 2 == 0 else g
                for c in range(cores):
                    pairs.append(((g * count + w) * cores + c, (far * count + other) * cores + c))
        upper = place % 2 == start
        out = jnp.where(upper, strip[2:], strip[:2])
        got.append(lax.ppermute(out, ("group", "wide", "narrow"), pairs))
    above = jnp.where(place % 2 == 1, got[0], got[1])
    below = jnp.where(place % 2 == 1, got[1], got[0])
    above = jnp.where(place > 0, above, jnp.zeros_like(above))
    below = jnp.where(place < count - 1, below, jnp.zeros_like(below))
    return above, below


def earlier_state(totals, works):
    cores, shape = len(totals), totals[0].shape
    works, done = list(works), []
    pieces = [totals[0]] + [rotate(totals[k], "narrow", k) for k in range(1, cores)]
    running, packed = small_call(gather_kernel, "gather", pieces, [F32, BF16], shape)
    before = jnp.zeros(shape, F32)
    bits = lax.axis_size("wide").bit_length() - 1
    for bit in range(bits):
        held = None
        if works:
            held, packed = works.pop(0)(packed)
        other = swap(packed, "wide", bit)
        if held is not None:
            held, other = lax.optimization_barrier((held, other))
            done.append(held)
        if bit == bits - 1:
            break
        before, packed, *more = small_call(
            functools.partial(scan_kernel, bit),
            "scan",
            [running, before, other],
            [F32, BF16] + [F32] * (bit < bits - 2),
            shape,
        )
        running = more[0] if more else None
    outs = small_call(
        functools.partial(spread_kernel, cores, bits - 1),
        "spread",
        [before, other] + pieces,
        [BF16] * cores,
        shape,
    )
    states = [outs[0]] + [rotate(outs[k], "narrow", k) for k in range(1, cores)]
    while works:
        done.append(works.pop(0)(packed)[0])
    return states, done


def reduce_bricks(parts, orders):
    parts = [list(pair) for pair in parts]
    for level in range(len(orders[0])):
        arrived = [
            swap(gone, "wide", order[level]) for (_, gone), order in zip(parts, orders)
        ]
        for pair, more in zip(parts, arrived):
            total = (pair[0].astype(F32) + more.astype(F32)).astype(BF16)
            half = total.shape[0] // 2
            pair[0], pair[1] = total[:half] if half else total, total[half:]
    return [pair[0] if pair[0].shape[0] else pair[1] for pair in parts]


def per_device(voxels, w_qkv, w_out, w_feature, conv_first, conv_second, row_brick, cell_place):
    tokens = voxels.shape[0]
    channels = w_feature.shape[1]
    wide_count, wide_place = lax.axis_size("wide"), lax.axis_index("wide")
    narrow_count, narrow_place = lax.axis_size("narrow"), lax.axis_index("narrow")

    blocks = tokens // BLK
    cuts = sorted({blocks * i // 3 for i in range(4)})
    spans = [(first, last - first) for first, last in zip(cuts, cuts[1:])]
    xs, ks, vs, w_q, before, totals = key_value(spans, voxels, w_qkv, narrow_count)

    def work(n):
        def run(array):
            array, k = lax.optimization_barrier((array, ks[n]))
            weight = w_out if n == 0 else None
            return local_attention(
                xs[n], w_q, k, vs[n], before, weight, w_feature, *spans[n]
            ), array

        return run

    states, pieces = earlier_state(totals, [work(n) for n in range(len(spans))])
    weights = pieces[0][3]
    qs, parts, own = ([piece[i] for piece in pieces] for i in range(3))
    normed = own_share(narrow_count, states[0], qs, parts)

    bits = list(range(wide_count.bit_length() - 1))
    orders = [bits, bits[1::-1] + bits[2:]]
    kept_a, sent_a, kept_b, sent_b = finish(
        spans,
        row_brick[:, 0],
        qs,
        parts,
        normed,
        own,
        states[1:],
        weights,
        cell_place.reshape(-1, ROW),
        wide_count,
        orders,
    )
    outer, middle = reduce_bricks([(kept_a, sent_a), (kept_b, sent_b)], orders)
    outer, middle = (part.reshape(-1, BY, channels) for part in (outer, middle))
    above, below = exchange_lines(outer)
    lines = jnp.concatenate([above, outer[:2], middle, outer[2:], below], axis=0)
    left, right = side_columns(lines)
    return field_flow(lines, left, right, conv_first, conv_second)


def solution(mesh):
    placed = (
        P(("group", "wide", "narrow"), None),
        P(),
        P(),
        P(),
        P(),
        P(),
        P(("group", "wide", "narrow"), None),
        P(("group", "wide", "narrow")),
    )
    return jax.shard_map(
        per_device,
        mesh=mesh,
        in_specs=placed,
        out_specs=P(("group", "wide"), "narrow", None),
        check_vma=False,
    )
```

time: 62.9 us -> 55.8 us (0.89)
  waiting for transfers between devices: 17.1 us -> 12.8 us
  Pallas kernels: 19.7 us -> 18 us
  local copies, waits for them, and re-layouts: 1.5 us -> 0.09 us
    ppermute x10, waiting for transfers between devices: 12.5 us -> 9.18 us  [swap(): return lax.ppermute(array, axis, [(i, i ^ 1 << bit) for i in range(count)])]
    unnamed x14 -> x15, local copies, waits for them, and re-layouts: 1.43 us -> 0.04 us
    pallas_call x6 -> x7, Pallas kernels: 18.9 us -> 17.8 us  [the longest x3 6.13 us: local_attention(): pl.pallas_call(functools.partial(local_kernel, first, count, int(w_out is...]
    ppermute x2, waiting for transfers between devices: 2.14 us -> 1.23 us  [rotate(): lax.ppermute(array, axis, [(i, (i + by) % count) for i in range(count)])]
    pallas_call x4, Pallas kernels: 0.8 us -> 0.15 us  [small_call(): pl.pallas_call(kernel, in_specs=[smem if array.dtype == jnp.int32 else vm...]
  transfers between devices with their start and end apart: 14 -> 14, of which waited for: 12 -> 10; matrix products, arithmetic and copies ran while one was open for 1% -> 1% of each run, Pallas kernels for 8% -> 13%
where the time goes in v3:
time: 55.8 us; the launch traced here: 55.5 us
  starting transfers between devices  24 us (43%)
  Pallas kernels  18 us (32%)
  waiting for transfers between devices  12.8 us (23%)
    ppermute x10, starting transfers between devices, swap(): return lax.ppermute(array, axis, [(i, i ^ 1 << bit) for i in range(count)])  20 us
    ppermute x10, waiting for transfers between devices, swap(): return lax.ppermute(array, axis, [(i, i ^ 1 << bit) for i in range(count)])  9.18 us
    pallas_call x3, Pallas kernels, local_attention(): pl.pallas_call(functools.partial(local_kernel, first, count, int(w_out is...  6.13 us
    pallas_call x1, Pallas kernels, key_value(): pl.pallas_call(functools.partial(key_value_kernel, spans), in_specs=[hbm,...  5.02 us
    pallas_call x1, Pallas kernels, finish(): pl.pallas_call(functools.partial(finish_kernel, orders, spans, cores), in...  3.41 us
    ppermute x2, starting transfers between devices, exchange_lines(): got.append(lax.ppermute(out, ('group', 'wide', 'narrow'), pairs))  3.37 us
    ppermute x2, waiting for transfers between devices, exchange_lines(): got.append(lax.ppermute(out, ('group', 'wide', 'narrow'), pairs))  2.4 us
    pallas_call x1, Pallas kernels, field_flow(): pl.pallas_call(field_kernel, in_specs=[vmem] * 4, out_specs=vmem, out_sha...  2.38 us
  transfers between devices with their start and end apart: 14, of which 10 were waited for; matrix products, arithmetic and copies ran while one was open for 1% of the time, Pallas kernels for 13%

profile of v3, /device:TPU:0, one launch (start us, length us, event | category | flops | bytes accessed | tf_op | source)
XLA Modules:
  0.0 55.5 jit_solution(440884795336713783)
XLA Ops:
  0.0 0.0 copy-start.3
  0.0 0.0 copy-start
  0.0 5.0 %key_value.1 = (bf16[512,512]{1,0:T(8,128)(2,1)S(1)}, bf16[768,512]{1,0:T(8,128)(2,1)S(1)}, bf16[768,512]{1,0:T(8,128)(2,1)S(1)}, bf16[512,512]{1,0:T(8,128)(2,1...) custom-call(bf16[2048,512]{1,0:T(8,128)(2,1)} %x_ref.1, ...), custom_call_target="tpu_custom_call" | custom-call | tf_op jit(solution)/shard_map/key_value/pallas_call | solution.py:113
  5.0 0.5 collective-permute-start
  5.5 0.9 %collective-permute-done.refs_1_ = bf16[2,128,128]{2,1,0:T(8,128)(2,1)S(1)} collective-permute-done((bf16[2,128,128]{2,1,0:T(8,128)(2,1)S(1)}, bf16[2,128,128]{2,1,0:T(8,128)(2,1)S(1)}, u32[]{:S(2)}, u32[]{:S(2)}) %collective-permute-start) | collective-permute-done | bytes 65568 | tf_op jit(solution)/shard_map/ppermute | solution.py:400
  6.5 2.9 %collective-permute-start.1 = (bf16[2,128,128]{2,1,0:T(8,128)(2,1)S(1)}, bf16[2,128,128]{2,1,0:T(8,128)(2,1)S(1)}, u32[]{:S(2)}, u32[]{:S(2)}) collective-permute-start(bf16[2,128,128]{2,1,0:T(8,128)(2,1)S(1)} %get-tuple-element.76), channel_id=1, source_target_pairs={{0,2},{2,0},{4,6},{6,4},{8,10},{10,8},{12,14},{14,12},{1,3},{3,1},... | collective-permute-start | bytes 196616 | tf_op jit(solution)/shard_map/ppermute | solution.py:388
  9.4 0.0 copy-done.3
  9.4 0.0 copy-done
  9.4 1.7 %local_attention.3 = (bf16[512,512]{1,0:T(8,128)(2,1)S(1)}, f32[512,512]{1,0:T(8,128)S(1)}, f32[512,256]{1,0:T(8,128)S(1)}, bf16[512,256]{1,0:T(8,128)(2,1)S(1)}) custom-call(bf16[512,512]{1,0:T(8,128)(2,1)S(1)} %get-tuple-element.63.x_ref, bf16[512,512]{1,0:T(8,128)(2,1)S(1)} %get-tuple-element.64.wq_ref, bf16[512,512]{1,0:T(8,128)(2,1)S(1)} %get-tuple-element.69.k_ref, ...), custom_call_target="tpu_custom_call" | custom-call | flops 603979776 | bytes 3145728 | tf_op jit(solution)/shard_map/local_attention/pallas_call | solution.py:164
  11.1 0.7 %collective-permute-done.1.other_ref = bf16[2,128,128]{2,1,0:T(8,128)(2,1)S(1)} collective-permute-done((bf16[2,128,128]{2,1,0:T(8,128)(2,1)S(1)}, bf16[2,128,128]{2,1,0:T(8,128)(2,1)S(1)}, u32[]{:S(2)}, u32[]{:S(2)}) %collective-permute-start.1) | collective-permute-done | bytes 65568 | tf_op jit(solution)/shard_map/ppermute | solution.py:388
  11.9 2.0 %collective-permute-start.2 = (bf16[2,128,128]{2,1,0:T(8,128)(2,1)S(1)}, bf16[2,128,128]{2,1,0:T(8,128)(2,1)S(1)}, u32[]{:S(2)}, u32[]{:S(2)}) collective-permute-start(bf16[2,128,128]{2,1,0:T(8,128)(2,1)S(1)} %get-tuple-element.88), channel_id=1, source_target_pairs={{0,4},{2,6},{4,0},{6,2},{8,12},{10,14},{12,8},{14,10},{1,5},{3,7},... | collective-permute-start | bytes 196616 | tf_op jit(solution)/shard_map/ppermute | solution.py:388
  13.8 2.2 %local_attention.4 = (bf16[768,512]{1,0:T(8,128)(2,1)S(1)}, f32[768,512]{1,0:T(8,128)S(1)}, f32[768,256]{1,0:T(8,128)S(1)}) custom-call(bf16[768,512]{1,0:T(8,128)(2,1)S(1)} %get-tuple-element.78.x_ref, bf16[512,512]{1,0:T(8,128)(2,1)S(1)} %get-tuple-element.64.wq_ref, bf16[768,512]{1,0:T(8,128)(2,1)S(1)} %get-tuple-element.83.k_ref, ...), custom_call_target="tpu_custom_call" | custom-call | flops 905969664 | bytes 4718592 | tf_op jit(solution)/shard_map/local_attention/pallas_call | solution.py:164
  16.1 0.1 collective-permute-done.2.other_ref
  16.2 3.0 %collective-permute-start.3 = (bf16[2,128,128]{2,1,0:T(8,128)(2,1)S(1)}, bf16[2,128,128]{2,1,0:T(8,128)(2,1)S(1)}, u32[]{:S(2)}, u32[]{:S(2)}) collective-permute-start(bf16[2,128,128]{2,1,0:T(8,128)(2,1)S(1)} %get-tuple-element.101), channel_id=1, source_target_pairs={{0,8},{2,10},{4,12},{6,14},{8,0},{10,2},{12,4},{14,6},{1,9},{3,11}... | collective-permute-start | bytes 196616 | tf_op jit(solution)/shard_map/ppermute | solution.py:388
  19.2 2.2 %local_attention.5 = (bf16[768,512]{1,0:T(8,128)(2,1)S(1)}, f32[768,512]{1,0:T(8,128)S(1)}, f32[768,256]{1,0:T(8,128)S(1)}) custom-call(bf16[768,512]{1,0:T(8,128)(2,1)S(1)} %get-tuple-element.90.x_ref, bf16[512,512]{1,0:T(8,128)(2,1)S(1)} %get-tuple-element.64.wq_ref, bf16[768,512]{1,0:T(8,128)(2,1)S(1)} %get-tuple-element.96.k_ref, ...), custom_call_target="tpu_custom_call" | custom-call | flops 905969664 | bytes 4718592 | tf_op jit(solution)/shard_map/local_attention/pallas_call | solution.py:164
  21.4 0.0 collective-permute-done.3.other_ref
  21.5 0.1 spread.1
  21.5 0.1 collective-permute-start.4
  21.6 0.0 copy-start.4
  21.6 0.0 copy-start.5
  21.7 0.9 %own_share.1 = (bf16[512,256]{1,0:T(8,128)(2,1)S(1)}, bf16[768,256]{1,0:T(8,128)(2,1)S(1)}, bf16[768,256]{1,0:T(8,128)(2,1)S(1)}) custom-call(bf16[2,128,128]{2,1,0:T(8,128)(2,1)S(1)} %get-tuple-element.108.state_ref, bf16[512,512]{1,0:T(8,128)(2,1)S(1)} %get-tuple-element.77.refs_0_, bf16[768,512]{1,0:T(8,128)(2,1)S(1)} %get-tuple-element.89.refs_1_, ...), custom_call_target="tpu_custom_call" | custom-call | flops 536870912 | bytes 4194304 | tf_op jit(solution)/shard_map/own_share/pallas_call | solution.py:260
  22.5 0.3 collective-permute-done.4.refs_12_
  22.9 0.0 copy-done.4
  22.9 0.0 copy-done.5
  22.9 3.4 %finish.1 = (bf16[4,128,256]{2,1,0:T(8,128)(2,1)S(1)}, bf16[4,128,256]{2,1,0:T(8,128)(2,1)S(1)}, bf16[4,128,256]{2,1,0:T(8,128)(2,1)S(1)}, bf16[4,128,256]{2,1,0:T(8,128)(2,1)S(1)}) custom-call(s32[16]{0:T(128)S(1)} %bitcast.6, bf16[512,512]{1,0:T(8,128)(2,1)S(1)} %get-tuple-element.77.refs_0_, bf16[768,512]{1,0:T(8,128)(2,1)S(1)} %get-tuple-element.89.refs_1_, ...), custom_call_target="tpu_custom_call" | custom-call | tf_op jit(solution)/shard_map/finish/pallas_call | solution.py:322
  26.3 1.9 %collective-permute-start.5 = (bf16[4,128,256]{2,1,0:T(8,128)(2,1)S(1)}, bf16[4,128,256]{2,1,0:T(8,128)(2,1)S(1)}, u32[]{:S(2)}, u32[]{:S(2)}) collective-permute-start(bf16[4,128,256]{2,1,0:T(8,128)(2,1)S(1)} %get-tuple-element.118), channel_id=1, source_target_pairs={{0,2},{2,0},{4,6},{6,4},{8,10},{10,8},{12,14},{14,12},{1,3},{3,1},... | collective-permute-start | bytes 786440 | tf_op jit(solution)/shard_map/ppermute | solution.py:388
  28.2 1.6 %collective-permute-start.10 = (bf16[4,128,256]{2,1,0:T(8,128)(2,1)S(1)}, bf16[4,128,256]{2,1,0:T(8,128)(2,1)S(1)}, u32[]{:S(2)}, u32[]{:S(2)}) collective-permute-start(bf16[4,128,256]{2,1,0:T(8,128)(2,1)S(1)} %get-tuple-element.120), channel_id=1, source_target_pairs={{0,4},{2,6},{4,0},{6,2},{8,12},{10,14},{12,8},{14,10},{1,5},{3,7},... | collective-permute-start | bytes 786440 | tf_op jit(solution)/shard_map/ppermute | solution.py:388
  29.8 5.1 %collective-permute-done.5 = bf16[4,128,256]{2,1,0:T(8,128)(2,1)S(1)} collective-permute-done((bf16[4,128,256]{2,1,0:T(8,128)(2,1)S(1)}, bf16[4,128,256]{2,1,0:T(8,128)(2,1)S(1)}, u32[]{:S(2)}, u32[]{:S(2)}) %collective-permute-start.5) | collective-permute-done | bytes 262176 | tf_op jit(solution)/shard_map/ppermute | solution.py:388
  34.8 0.1 add_convert_fusion.1
  34.9 1.9 %collective-permute-start.6 = (bf16[2,128,256]{2,1,0:T(8,128)(2,1)S(1)}, bf16[2,128,256]{2,1,0:T(8,128)(2,1)S(1)}, u32[]{:S(2)}, u32[]{:S(2)}) collective-permute-start(bf16[2,128,256]{2,1,0:T(8,128)(2,1)S(1)} %slice.61), channel_id=1, source_target_pairs={{0,4},{2,6},{4,0},{6,2},{8,12},{10,14},{12,8},{14,10},{1,5},{3,7},... | collective-permute-start | bytes 393224 | tf_op jit(solution)/shard_map/ppermute | solution.py:388
  36.8 0.0 collective-permute-done.10
  36.8 0.1 add_convert_fusion
  36.9 1.6 %collective-permute-start.11 = (bf16[2,128,256]{2,1,0:T(8,128)(2,1)S(1)}, bf16[2,128,256]{2,1,0:T(8,128)(2,1)S(1)}, u32[]{:S(2)}, u32[]{:S(2)}) collective-permute-start(bf16[2,128,256]{2,1,0:T(8,128)(2,1)S(1)} %slice.67), channel_id=1, source_target_pairs={{0,2},{2,0},{4,6},{6,4},{8,10},{10,8},{12,14},{14,12},{1,3},{3,1},... | collective-permute-start | bytes 393224 | tf_op jit(solution)/shard_map/ppermute | solution.py:388
  38.5 1.5 %collective-permute-done.6 = bf16[2,128,256]{2,1,0:T(8,128)(2,1)S(1)} collective-permute-done((bf16[2,128,256]{2,1,0:T(8,128)(2,1)S(1)}, bf16[2,128,256]{2,1,0:T(8,128)(2,1)S(1)}, u32[]{:S(2)}, u32[]{:S(2)}) %collective-permute-start.6) | collective-permute-done | bytes 131104 | tf_op jit(solution)/shard_map/ppermute | solution.py:388
  40.0 3.1 %collective-permute-start.7 = (bf16[1,128,256]{2,1,0:T(8,128)(2,1)S(1)}, bf16[1,128,256]{2,1,0:T(8,128)(2,1)S(1)}, u32[]{:S(2)}, u32[]{:S(2)}) collective-permute-start(bf16[1,128,256]{2,1,0:T(8,128)(2,1)S(1)} %slice.63), channel_id=1, source_target_pairs={{0,8},{2,10},{4,12},{6,14},{8,0},{10,2},{12,4},{14,6},{1,9},{3,11}... | collective-permute-start | bytes 196616 | tf_op jit(solution)/shard_map/ppermute | solution.py:388
  43.1 0.0 collective-permute-done.11
  43.1 2.1 %collective-permute-start.12 = (bf16[1,128,256]{2,1,0:T(8,128)(2,1)S(1)}, bf16[1,128,256]{2,1,0:T(8,128)(2,1)S(1)}, u32[]{:S(2)}, u32[]{:S(2)}) collective-permute-start(bf16[1,128,256]{2,1,0:T(8,128)(2,1)S(1)} %slice.69), channel_id=1, source_target_pairs={{0,8},{2,10},{4,12},{6,14},{8,0},{10,2},{12,4},{14,6},{1,9},{3,11}... | collective-permute-start | bytes 196616 | tf_op jit(solution)/shard_map/ppermute | solution.py:388
  45.2 0.6 %collective-permute-done.7 = bf16[1,128,256]{2,1,0:T(8,128)(2,1)S(1)} collective-permute-done((bf16[1,128,256]{2,1,0:T(8,128)(2,1)S(1)}, bf16[1,128,256]{2,1,0:T(8,128)(2,1)S(1)}, u32[]{:S(2)}, u32[]{:S(2)}) %collective-permute-start.7) | collective-permute-done | bytes 65568 | tf_op jit(solution)/shard_map/ppermute | solution.py:388
  45.9 1.9 %collective-permute-start.8 = (bf16[2,32,256]{2,1,0:T(8,128)(2,1)S(1)}, bf16[2,32,256]{2,1,0:T(8,128)(2,1)S(1)}, u32[]{:S(2)}, u32[]{:S(2)}) collective-permute-start(bf16[2,32,256]{2,1,0:T(8,128)(2,1)S(1)} %get-tuple-element.122), channel_id=1, source_target_pairs={{0,2},{1,3},{2,0},{3,1},{4,6},{5,7},{6,4},{7,5},{8,10},{9,11},{10,... | collective-permute-start | bytes 98312 | tf_op jit(solution)/shard_map/ppermute | solution.py:428
  47.8 1.5 %collective-permute-start.9 = (bf16[2,32,256]{2,1,0:T(8,128)(2,1)S(1)}, bf16[2,32,256]{2,1,0:T(8,128)(2,1)S(1)}, u32[]{:S(2)}, u32[]{:S(2)}) collective-permute-start(bf16[2,32,256]{2,1,0:T(8,128)(2,1)S(1)} %get-tuple-element.121), channel_id=1, source_target_pairs={{0,16},{1,17},{2,4},{3,5},{4,2},{5,3},{6,8},{7,9},{8,6},{9,7},{10,... | collective-permute-start | bytes 98312 | tf_op jit(solution)/shard_map/ppermute | solution.py:428
  49.2 0.0 collective-permute-done.12
  49.3 0.6 %collective-permute-done.8 = bf16[2,32,256]{2,1,0:T(8,128)(2,1)S(1)} collective-permute-done((bf16[2,32,256]{2,1,0:T(8,128)(2,1)S(1)}, bf16[2,32,256]{2,1,0:T(8,128)(2,1)S(1)}, u32[]{:S(2)}, u32[]{:S(2)}) %collective-permute-start.8) | collective-permute-done | bytes 32800 | tf_op jit(solution)/shard_map/ppermute | solution.py:428
  49.8 1.8 %collective-permute-done.9 = bf16[2,32,256]{2,1,0:T(8,128)(2,1)S(1)} collective-permute-done((bf16[2,32,256]{2,1,0:T(8,128)(2,1)S(1)}, bf16[2,32,256]{2,1,0:T(8,128)(2,1)S(1)}, u32[]{:S(2)}, u32[]{:S(2)}) %collective-permute-start.9) | collective-permute-done | bytes 32800 | tf_op jit(solution)/shard_map/ppermute | solution.py:428
  51.8 0.1 collective-permute-start.13
  51.9 1.2 %collective-permute-done.13 = bf16[12,2,256]{2,1,0:T(2,128)(2,1)S(1)} collective-permute-done((bf16[12,2,256]{2,1,0:T(2,128)(2,1)S(1)}, bf16[12,2,256]{2,1,0:T(2,128)(2,1)S(1)}, u32[]{:S(2)}, u32[]{:S(2)}) %collective-permute-start.13) | collective-permute-done | bytes 12320 | tf_op jit(solution)/shard_map/ppermute | solution.py:388
  53.1 0.0 copy-done.1
  53.1 0.0 copy-done.2
  53.1 2.4 %field_flow.1 = f32[8,32,256]{2,1,0:T(8,128)} custom-call(bf16[12,32,256]{2,1,0:T(8,128)(2,1)S(1)} %select_dynamic-update-slice_fusion.lines_ref, bf16[13,16,256]{2,1,0:T(8,128)(2,1)S(1)} %pad_add_fusion.sides_ref, bf16[3,3,256,256]{3,2,1,0:T(8,128)(2,1)S(1)} %copy-done.1, bf16[3,3,256,256]{3,2,1,0:T(8,128)(2,1)S(1)} %copy-done.2), custom_call_target="tpu_custom_call" | custom-call | tf_op jit(solution)/shard_map/field_flow/pallas_call | solution.py:375
  (24 shorter events, 0.4 us)
Async XLA Ops:
  0.0 9.4 %copy-start.3 = (bf16[512,512]{1,0:T(8,128)(2,1)S(1)}, bf16[512,512]{1,0:T(8,128)(2,1)}, u32[]{:S(2)}) copy-start(bf16[512,512]{1,0:T(8,128)(2,1)} %refs_0_.3) | copy-start | bytes 1572868
  0.0 9.4 %copy-start = (bf16[512,256]{1,0:T(8,128)(2,1)S(1)}, bf16[512,256]{1,0:T(8,128)(2,1)}, u32[]{:S(2)}) copy-start(bf16[512,256]{1,0:T(8,128)(2,1)} %refs_0_.5) | copy-start | bytes 786436
  5.0 1.4 %collective-permute-start = (bf16[2,128,128]{2,1,0:T(8,128)(2,1)S(1)}, bf16[2,128,128]{2,1,0:T(8,128)(2,1)S(1)}, u32[]{:S(2)}, u32[]{:S(2)}) collective-permute-start(bf16[2,128,128]{2,1,0:T(8,128)(2,1)S(1)} %get-tuple-element.66), channel_id=1, source_target_pairs={{0,1},{1,0},{2,3},{3,2},{4,5},{5,4},{6,7},{7,6},{8,9},{9,8},{10,11... | collective-permute-start | bytes 196616 | tf_op jit(solution)/shard_map/ppermute | solution.py:400
  6.5 5.3 %collective-permute-start.1 = (bf16[2,128,128]{2,1,0:T(8,128)(2,1)S(1)}, bf16[2,128,128]{2,1,0:T(8,128)(2,1)S(1)}, u32[]{:S(2)}, u32[]{:S(2)}) collective-permute-start(bf16[2,128,128]{2,1,0:T(8,128)(2,1)S(1)} %get-tuple-element.76), channel_id=1, source_target_pairs={{0,2},{2,0},{4,6},{6,4},{8,10},{10,8},{12,14},{14,12},{1,3},{3,1},... | collective-permute-start | bytes 196616 | tf_op jit(solution)/shard_map/ppermute | solution.py:388
  11.9 4.3 %collective-permute-start.2 = (bf16[2,128,128]{2,1,0:T(8,128)(2,1)S(1)}, bf16[2,128,128]{2,1,0:T(8,128)(2,1)S(1)}, u32[]{:S(2)}, u32[]{:S(2)}) collective-permute-start(bf16[2,128,128]{2,1,0:T(8,128)(2,1)S(1)} %get-tuple-element.88), channel_id=1, source_target_pairs={{0,4},{2,6},{4,0},{6,2},{8,12},{10,14},{12,8},{14,10},{1,5},{3,7},... | collective-permute-start | bytes 196616 | tf_op jit(solution)/shard_map/ppermute | solution.py:388
  16.2 5.2 %collective-permute-start.3 = (bf16[2,128,128]{2,1,0:T(8,128)(2,1)S(1)}, bf16[2,128,128]{2,1,0:T(8,128)(2,1)S(1)}, u32[]{:S(2)}, u32[]{:S(2)}) collective-permute-start(bf16[2,128,128]{2,1,0:T(8,128)(2,1)S(1)} %get-tuple-element.101), channel_id=1, source_target_pairs={{0,8},{2,10},{4,12},{6,14},{8,0},{10,2},{12,4},{14,6},{1,9},{3,11}... | collective-permute-start | bytes 196616 | tf_op jit(solution)/shard_map/ppermute | solution.py:388
  21.5 1.3 %collective-permute-start.4 = (bf16[2,128,128]{2,1,0:T(8,128)(2,1)S(1)}, bf16[2,128,128]{2,1,0:T(8,128)(2,1)S(1)}, u32[]{:S(2)}, u32[]{:S(2)}) collective-permute-start(bf16[2,128,128]{2,1,0:T(8,128)(2,1)S(1)} %get-tuple-element.115), channel_id=1, source_target_pairs={{0,1},{1,0},{2,3},{3,2},{4,5},{5,4},{6,7},{7,6},{8,9},{9,8},{10,11... | collective-permute-start | bytes 196616 | tf_op jit(solution)/shard_map/ppermute | solution.py:400
  21.6 1.2 %copy-start.4 = (s32[2048]{0:T(1024)S(1)}, s32[2048]{0:T(1024)}, u32[]{:S(2)}) copy-start(s32[2048]{0:T(1024)} %param.15) | copy-start | bytes 24580
  21.6 1.2 %copy-start.5 = (s32[16,1]{0,1:T(1,128)S(1)}, s32[16,1]{0,1:T(1,128)}, u32[]{:S(2)}) copy-start(s32[16,1]{0,1:T(1,128)} %param.14) | copy-start | bytes 196
  26.3 8.5 %collective-permute-start.5 = (bf16[4,128,256]{2,1,0:T(8,128)(2,1)S(1)}, bf16[4,128,256]{2,1,0:T(8,128)(2,1)S(1)}, u32[]{:S(2)}, u32[]{:S(2)}) collective-permute-start(bf16[4,128,256]{2,1,0:T(8,128)(2,1)S(1)} %get-tuple-element.118), channel_id=1, source_target_pairs={{0,2},{2,0},{4,6},{6,4},{8,10},{10,8},{12,14},{14,12},{1,3},{3,1},... | collective-permute-start | bytes 786440 | tf_op jit(solution)/shard_map/ppermute | solution.py:388
  28.2 8.6 %collective-permute-start.10 = (bf16[4,128,256]{2,1,0:T(8,128)(2,1)S(1)}, bf16[4,128,256]{2,1,0:T(8,128)(2,1)S(1)}, u32[]{:S(2)}, u32[]{:S(2)}) collective-permute-start(bf16[4,128,256]{2,1,0:T(8,128)(2,1)S(1)} %get-tuple-element.120), channel_id=1, source_target_pairs={{0,4},{2,6},{4,0},{6,2},{8,12},{10,14},{12,8},{14,10},{1,5},{3,7},... | collective-permute-start | bytes 786440 | tf_op jit(solution)/shard_map/ppermute | solution.py:388
  34.9 5.0 %collective-permute-start.6 = (bf16[2,128,256]{2,1,0:T(8,128)(2,1)S(1)}, bf16[2,128,256]{2,1,0:T(8,128)(2,1)S(1)}, u32[]{:S(2)}, u32[]{:S(2)}) collective-permute-start(bf16[2,128,256]{2,1,0:T(8,128)(2,1)S(1)} %slice.61), channel_id=1, source_target_pairs={{0,4},{2,6},{4,0},{6,2},{8,12},{10,14},{12,8},{14,10},{1,5},{3,7},... | collective-permute-start | bytes 393224 | tf_op jit(solution)/shard_map/ppermute | solution.py:388
  36.8 16.3 %copy-start.1 = (bf16[3,3,256,256]{3,2,1,0:T(8,128)(2,1)S(1)}, bf16[3,3,256,256]{3,2,1,0:T(8,128)(2,1)}, u32[]{:S(2)}) copy-start(bf16[3,3,256,256]{3,2,1,0:T(8,128)(2,1)} %w1_ref.1) | copy-start | bytes 3538948
  36.8 16.3 %copy-start.2 = (bf16[3,3,256,256]{3,2,1,0:T(8,128)(2,1)S(1)}, bf16[3,3,256,256]{3,2,1,0:T(8,128)(2,1)}, u32[]{:S(2)}) copy-start(bf16[3,3,256,256]{3,2,1,0:T(8,128)(2,1)} %w2_ref.1) | copy-start | bytes 3538948
  36.9 6.2 %collective-permute-start.11 = (bf16[2,128,256]{2,1,0:T(8,128)(2,1)S(1)}, bf16[2,128,256]{2,1,0:T(8,128)(2,1)S(1)}, u32[]{:S(2)}, u32[]{:S(2)}) collective-permute-start(bf16[2,128,256]{2,1,0:T(8,128)(2,1)S(1)} %slice.67), channel_id=1, source_target_pairs={{0,2},{2,0},{4,6},{6,4},{8,10},{10,8},{12,14},{14,12},{1,3},{3,1},... | collective-permute-start | bytes 393224 | tf_op jit(solution)/shard_map/ppermute | solution.py:388
  40.0 5.8 %collective-permute-start.7 = (bf16[1,128,256]{2,1,0:T(8,128)(2,1)S(1)}, bf16[1,128,256]{2,1,0:T(8,128)(2,1)S(1)}, u32[]{:S(2)}, u32[]{:S(2)}) collective-permute-start(bf16[1,128,256]{2,1,0:T(8,128)(2,1)S(1)} %slice.63), channel_id=1, source_target_pairs={{0,8},{2,10},{4,12},{6,14},{8,0},{10,2},{12,4},{14,6},{1,9},{3,11}... | collective-permute-start | bytes 196616 | tf_op jit(solution)/shard_map/ppermute | solution.py:388
  43.1 6.1 %collective-permute-start.12 = (bf16[1,128,256]{2,1,0:T(8,128)(2,1)S(1)}, bf16[1,128,256]{2,1,0:T(8,128)(2,1)S(1)}, u32[]{:S(2)}, u32[]{:S(2)}) collective-permute-start(bf16[1,128,256]{2,1,0:T(8,128)(2,1)S(1)} %slice.69), channel_id=1, source_target_pairs={{0,8},{2,10},{4,12},{6,14},{8,0},{10,2},{12,4},{14,6},{1,9},{3,11}... | collective-permute-start | bytes 196616 | tf_op jit(solution)/shard_map/ppermute | solution.py:388
  45.9 4.0 %collective-permute-start.8 = (bf16[2,32,256]{2,1,0:T(8,128)(2,1)S(1)}, bf16[2,32,256]{2,1,0:T(8,128)(2,1)S(1)}, u32[]{:S(2)}, u32[]{:S(2)}) collective-permute-start(bf16[2,32,256]{2,1,0:T(8,128)(2,1)S(1)} %get-tuple-element.122), channel_id=1, source_target_pairs={{0,2},{1,3},{2,0},{3,1},{4,6},{5,7},{6,4},{7,5},{8,10},{9,11},{10,... | collective-permute-start | bytes 98312 | tf_op jit(solution)/shard_map/ppermute | solution.py:428
  47.8 3.9 %collective-permute-start.9 = (bf16[2,32,256]{2,1,0:T(8,128)(2,1)S(1)}, bf16[2,32,256]{2,1,0:T(8,128)(2,1)S(1)}, u32[]{:S(2)}, u32[]{:S(2)}) collective-permute-start(bf16[2,32,256]{2,1,0:T(8,128)(2,1)S(1)} %get-tuple-element.121), channel_id=1, source_target_pairs={{0,16},{1,17},{2,4},{3,5},{4,2},{5,3},{6,8},{7,9},{8,6},{9,7},{10,... | collective-permute-start | bytes 98312 | tf_op jit(solution)/shard_map/ppermute | solution.py:428
  51.8 1.2 %collective-permute-start.13 = (bf16[12,2,256]{2,1,0:T(2,128)(2,1)S(1)}, bf16[12,2,256]{2,1,0:T(2,128)(2,1)S(1)}, u32[]{:S(2)}, u32[]{:S(2)}) collective-permute-start(bf16[12,2,256]{2,1,0:T(2,128)(2,1)S(1)} %broadcast_select_fusion.4), channel_id=1, source_target_pairs={{0,1},{1,0},{2,3},{3,2},{4,5},{5,4},{6,7},{7,6},{8,9},{9,8},{10,11... | collective-permute-start | bytes 36872 | tf_op jit(solution)/shard_map/ppermute | solution.py:388

commit v4 on v3

--- a/solution.py
+++ b/solution.py
@@ -127,14 +127,12 @@
     return outs[:n], outs[n : 2 * n], outs[2 * n : 3 * n], outs[3 * n], outs[3 * n + 1], outs[3 * n + 2 :]
 
 
-def local_kernel(first, count, weights, x_ref, wq_ref, k_ref, v_ref, before_ref, *refs):
-    wf_ref, q_ref, part_ref, own_ref = refs[weights : weights + 4]
+def local_kernel(first, count, x_ref, wq_ref, k_ref, v_ref, before_ref, q_ref, part_ref):
     causal = lax.broadcasted_iota(jnp.int32, (BLK, BLK), 0) >= lax.broadcasted_iota(
         jnp.int32, (BLK, BLK), 1
     )
     q = dot(x_ref[...], wq_ref[...]).astype(BF16)
     q_ref[...] = q
-    own_ref[...] = dot(x_ref[...], wf_ref[...])
     for b in range(count):
         rows = slice(b * BLK, (b + 1) * BLK)
         for h in range(HEADS):
@@ -144,28 +142,20 @@
             part_ref[rows, cols] = dot(scores, v_ref[rows, cols]) + dot(
                 q[rows, cols], before_ref[first + b, h]
             )
-    if weights:
-        refs[-1][...] = dot(refs[0][...], wf_ref[...]).astype(BF16)
-
-
-def local_attention(x, w_q, k, v, before, w_out, w_feature, first, count):
+
+
+def local_attention(x, w_q, k, v, before, first, count):
     rows, width = x.shape
     inner = HEADS * HEAD
-    channels = w_feature.shape[1]
-    vmem = pl.BlockSpec(memory_space=pltpu.VMEM)
-    inputs = [x, w_q, k, v, before] + [w_out] * (w_out is not None) + [w_feature]
-    out_shape = [
-        jax.ShapeDtypeStruct((rows, inner), BF16),
-        jax.ShapeDtypeStruct((rows, inner), F32),
-        jax.ShapeDtypeStruct((rows, channels), F32),
-    ]
-    if w_out is not None:
-        out_shape.append(jax.ShapeDtypeStruct(w_feature.shape, BF16))
+    vmem = pl.BlockSpec(memory_space=pltpu.VMEM)
     return pl.pallas_call(
-        functools.partial(local_kernel, first, count, int(w_out is not None)),
-        in_specs=[vmem] * len(inputs),
-        out_specs=[vmem] * len(out_shape),
-        out_shape=out_shape,
+        functools.partial(local_kernel, first, count),
+        in_specs=[vmem] * 5,
+        out_specs=[vmem] * 2,
+        out_shape=[
+            jax.ShapeDtypeStruct((rows, inner), BF16),
+            jax.ShapeDtypeStruct((rows, inner), F32),
+        ],
         compiler_params=params(),
         cost_estimate=pl.CostEstimate(
             flops=2 * rows * inner * (width + 2 * BLK + HEAD),
@@ -173,7 +163,35 @@
             transcendentals=0,
         ),
         name="local_attention",
-    )(*inputs)
+    )(x, w_q, k, v, before)
+
+
+def direct_kernel(*refs):
+    count = len(refs) // 2 - 1
+    xs, (wo_ref, wf_ref), outs = refs[:count], refs[count : count + 2], refs[count + 2 :]
+    for x, out in zip(xs, outs):
+        out[...] = dot(x[...], wf_ref[...])
+    outs[-1][...] = dot(wo_ref[...], wf_ref[...]).astype(BF16)
+
+
+def direct_features(xs, w_out, w_feature):
+    channels = w_feature.shape[1]
+    vmem = pl.BlockSpec(memory_space=pltpu.VMEM)
+    rows = sum(x.shape[0] for x in xs)
+    return pl.pallas_call(
+        direct_kernel,
+        in_specs=[vmem] * (len(xs) + 2),
+        out_specs=[vmem] * (len(xs) + 1),
+        out_shape=[jax.ShapeDtypeStruct((x.shape[0], channels), F32) for x in xs]
+        + [jax.ShapeDtypeStruct(w_feature.shape, BF16)],
+        compiler_params=params(),
+        cost_estimate=pl.CostEstimate(
+            flops=2 * (rows + w_out.shape[0]) * w_out.shape[1] * channels,
+            bytes_accessed=rows * channels * 8,
+            transcendentals=0,
+        ),
+        name="direct_features",
+    )(*xs, w_out, w_feature)
 
 
 def gather_kernel(*refs):
@@ -183,21 +201,28 @@
     packed_ref[...] = running.astype(BF16)
 
 
-def scan_kernel(bit, running_ref, before_ref, other_ref, new_before, packed, *new_running):
-    other = other_ref[...].astype(F32)
-    running = running_ref[...] + other
+def earlier_sum(bits, others):
+    digit = (lax.axis_index("wide") >> bits[0]) & ((1 << len(bits)) - 1)
+    return sum(
+        ((digit ^ (k + 1)) < digit).astype(F32) * other for k, other in enumerate(others)
+    )
+
+
+def scan_kernel(bits, count, running_ref, before_ref, *refs):
+    others = [ref[...].astype(F32) for ref in refs[:count]]
+    new_before, packed, *new_running = refs[count:]
+    running = running_ref[...] + sum(others)
     packed[...] = running.astype(BF16)
     for ref in new_running:
         ref[...] = running
-    later = ((lax.axis_index("wide") >> bit) & 1).astype(F32)
-    new_before[...] = before_ref[...] + later * other
-
-
-def spread_kernel(cores, bit, before_ref, other_ref, *refs):
-    pieces, outs = refs[:cores], refs[cores:]
+    new_before[...] = before_ref[...] + earlier_sum(bits, others)
+
+
+def spread_kernel(cores, bits, count, before_ref, *refs):
+    others = [ref[...].astype(F32) for ref in refs[:count]]
+    pieces, outs = refs[count : count + cores], refs[count + cores :]
     place = lax.axis_index("narrow")
-    later = ((lax.axis_index("wide") >> bit) & 1).astype(F32)
-    before = before_ref[...] + later * other_ref[...].astype(F32)
+    before = before_ref[...] + earlier_sum(bits, others)
     for k, out in enumerate(outs):
         receiver = (place + k) % cores
         value = before
@@ -271,66 +296,126 @@
     )(state, *qs, *parts)
 
 
-def finish_kernel(orders, spans, cores, brick_ref, *refs):
+def list_rows(brick_ref, most, slots, fill):
+    for i in range(slots.shape[0]):
+        slots[i] = -1
+    for b in range(fill.shape[0]):
+        fill[b] = 0
+    for r in range(brick_ref.shape[0]):
+        brick = brick_ref[r] ^ lax.axis_index("wide")
+        used = fill[brick]
+        slots[brick * most + used] = r
+        fill[brick] = used + 1
+
+
+def cell_numbers(middle):
+    number = lax.broadcasted_iota(jnp.int32, (BX * BY // 2, 1), 0)
+    if middle:
+        return number + 2 * BY
+    return number + jnp.where(number < 2 * BY, 0, BX * BY // 2)
+
+
+def cell_sums(brick, numbers, most, slots, cell_ref, features_ref):
+    onehots, rows = [], []
+    for j in range(most):
+        row = slots[brick * most + j]
+        at = jnp.maximum(row, 0)
+        match = (numbers == cell_ref[at]) & (row >= 0)
+        onehots.append(jnp.where(match, 1.0, 0.0).astype(BF16))
+        rows.append(features_ref[pl.ds(pl.multiple_of(at * ROW, ROW), ROW), :])
+    return dot(jnp.concatenate(onehots, axis=1), jnp.concatenate(rows, axis=0)).astype(BF16)
+
+
+def pool_into(outs, brick_ref, cell_ref, features_ref, slots, fill):
+    most = slots.shape[0] // fill.shape[0]
+    list_rows(brick_ref, most, slots, fill)
+    for bricks, middle, out in outs:
+        numbers = cell_numbers(middle)
+        for n, brick in enumerate(bricks):
+            out[n] = cell_sums(brick, numbers, most, slots, cell_ref, features_ref)
+
+
+def features_kernel(bricks, spans, cores, brick_ref, *refs):
     pieces = len(spans)
     refs = list(refs)
     take = lambda n: [refs.pop(0) for _ in range(n)]
     q_refs, part_refs, normed_refs, own_refs = (take(pieces) for _ in range(4))
     state_refs = take(cores - 1)
-    w_ref, cell_ref = take(2)
-    outs = take(4)
-    acc, scratch = refs
+    w_ref, cell_ref, features_ref, out = take(4)
+    scratch, slots, fill = refs
     shares = [share_columns(cores, k) for k in range(cores)]
     ones = ones_blocks(scratch.shape[1])
     states = [block_state(ref, scratch.at[k]) for k, ref in enumerate(state_refs)]
-    acc[...] = jnp.zeros_like(acc)
-    cells = BX * BY
     for n, (first, count) in enumerate(spans):
         features = own_refs[n][...] + dot(normed_refs[n][...], w_ref[shares[0], :])
         for state, cols in zip(states, shares[1:]):
             normed = norm_share(q_refs[n][:, cols], part_refs[n][:, cols], state, ones)
             features += dot(normed, w_ref[cols, :])
-        features = features.astype(BF16)
-        for r in range(count * BLK // ROW):
-            row = first * BLK // ROW + r
-            match = lax.broadcasted_iota(jnp.int32, (cells, ROW), 0) == cell_ref[row : row + 1]
-            onehot = jnp.where(match, 1.0, 0.0).astype(BF16)
-            brick = brick_ref[row] ^ lax.axis_index("wide")
-            acc[brick] += dot(onehot, features[r * ROW : (r + 1) * ROW])
-    ranges = [[(0, 2 * BY), (cells - 2 * BY, cells)], [(2 * BY, cells - 2 * BY)]]
-    bricks = acc.shape[0]
-    for part, order in enumerate(orders):
-        for i in range(bricks):
-            place = 0
-            for bit in order:
-                place = 2 * place + ((i >> bit) & 1)
-            which, slot = divmod(place, bricks // 2)
-            to = 0
-            for first, last in ranges[part]:
-                outs[2 * part + which][slot, to : to + last - first] = acc[i, first:last].astype(BF16)
-                to += last - first
-
-
-def finish(spans, bricks, qs, parts, normed, own, states, weights, cell_rows, count, orders):
-    channels = weights.shape[1]
+        features_ref[first * BLK : (first + count) * BLK] = features.astype(BF16)
+    pool_into([(bricks, False, out)], brick_ref, cell_ref, features_ref, slots, fill)
+
+
+def list_scratch(count, most):
+    return [pltpu.SMEM((count * most,), jnp.int32), pltpu.SMEM((count,), jnp.int32)]
+
+
+def sums_shape(count, channels):
+    return jax.ShapeDtypeStruct((count, BX * BY // 2, channels), BF16)
+
+
+def voxel_features(
+    spans, bricks, qs, parts, normed, own, states, weights, cell_rows, chosen, count, most
+):
+    tokens, channels = sum(q.shape[0] for q in qs), weights.shape[1]
     cores = len(states) + 1
     width = HEADS // cores * HEAD
-    cells = BX * BY
     vmem = pl.BlockSpec(memory_space=pltpu.VMEM)
     smem = pl.BlockSpec(memory_space=pltpu.SMEM)
-    out = jax.ShapeDtypeStruct((count // 2, cells // 2, channels), BF16)
     return pl.pallas_call(
-        functools.partial(finish_kernel, orders, spans, cores),
+        functools.partial(features_kernel, chosen, spans, cores),
         in_specs=[smem] + [vmem] * (4 * len(spans) + cores + 1),
-        out_specs=[vmem] * 4,
-        out_shape=[out] * 4,
-        scratch_shapes=[
-            pltpu.VMEM((count, cells, channels), F32),
-            pltpu.VMEM((max(1, cores - 1), width, width), BF16),
+        out_specs=[vmem] * 2,
+        out_shape=[
+            jax.ShapeDtypeStruct((tokens, channels), BF16),
+            sums_shape(len(chosen), channels),
         ],
+        scratch_shapes=[pltpu.VMEM((max(1, cores - 1), width, width), BF16)]
+        + list_scratch(count, most),
         compiler_params=params(),
-        name="finish",
+        name="voxel_features",
     )(bricks, *qs, *parts, *normed, *own, *states, weights, cell_rows)
+
+
+def pool_kernel(chosen, brick_ref, cell_ref, features_ref, *refs):
+    outs, (slots, fill) = refs[:-2], refs[-2:]
+    pool_into(
+        [(bricks, middle, out) for (bricks, middle), out in zip(chosen, outs)],
+        brick_ref,
+        cell_ref,
+        features_ref,
+        slots,
+        fill,
+    )
+
+
+def pool(bricks, cell_rows, features, chosen, count, most):
+    tokens, channels = features.shape
+    vmem = pl.BlockSpec(memory_space=pltpu.VMEM)
+    smem = pl.BlockSpec(memory_space=pltpu.SMEM)
+    return pl.pallas_call(
+        functools.partial(pool_kernel, chosen),
+        in_specs=[smem, vmem, vmem],
+        out_specs=[vmem] * len(chosen),
+        out_shape=[sums_shape(len(which), channels) for which, _ in chosen],
+        scratch_shapes=list_scratch(count, most),
+        compiler_params=params(),
+        cost_estimate=pl.CostEstimate(
+            flops=sum(len(which) for which, _ in chosen) * most * ROW * BX * BY * channels,
+            bytes_accessed=tokens * channels * 2,
+            transcendentals=0,
+        ),
+        name="pool",
+    )(bricks, cell_rows, features)
 
 
 def field_kernel(lines_ref, sides_ref, w1_ref, w2_ref, out_ref, field):
@@ -386,6 +471,11 @@
 def swap(array, axis, bit):
     count = lax.axis_size(axis)
     return lax.ppermute(array, axis, [(i, i ^ (1 << bit)) for i in range(count)])
+
+
+def swap_digit(array, axis, bit, by):
+    count = lax.axis_size(axis)
+    return lax.ppermute(array, axis, [(i, i ^ (by << bit)) for i in range(count)])
 
 
 def shift(array, axis, by):
@@ -433,42 +523,61 @@
     return above, below
 
 
-def earlier_state(totals, works):
+def earlier_state(totals, first_work, works):
     cores, shape = len(totals), totals[0].shape
     works, done = list(works), []
-    pieces = [totals[0]] + [rotate(totals[k], "narrow", k) for k in range(1, cores)]
+
+    def beside(work, arrays, exchange):
+        held, arrays = work(arrays)
+        done.append(held)
+        held, arrived = lax.optimization_barrier((held, exchange(arrays)))
+        done[-1] = held
+        return arrived
+
+    others = beside(
+        first_work,
+        totals[1:],
+        lambda arrays: [rotate(array, "narrow", k + 1) for k, array in enumerate(arrays)],
+    )
+    pieces = [totals[0]] + others
     running, packed = small_call(gather_kernel, "gather", pieces, [F32, BF16], shape)
     before = jnp.zeros(shape, F32)
-    bits = lax.axis_size("wide").bit_length() - 1
-    for bit in range(bits):
-        held = None
-        if works:
-            held, packed = works.pop(0)(packed)
-        other = swap(packed, "wide", bit)
-        if held is not None:
-            held, other = lax.optimization_barrier((held, other))
-            done.append(held)
-        if bit == bits - 1:
+    count = lax.axis_size("wide").bit_length() - 1
+    levels = [list(range(bit, min(bit + 2, count))) for bit in range(0, count, 2)]
+    for level, bits in enumerate(levels):
+        exchange = lambda packed: [
+            swap_digit(packed, "wide", bits[0], k) for k in range(1, 1 << len(bits))
+        ]
+        others = beside(works.pop(0), packed, exchange) if works else exchange(packed)
+        if level == len(levels) - 1:
             break
         before, packed, *more = small_call(
-            functools.partial(scan_kernel, bit),
+            functools.partial(scan_kernel, bits, len(others)),
             "scan",
-            [running, before, other],
-            [F32, BF16] + [F32] * (bit < bits - 2),
+            [running, before] + others,
+            [F32, BF16] + [F32] * (level < len(levels) - 2),
             shape,
         )
         running = more[0] if more else None
     outs = small_call(
-        functools.partial(spread_kernel, cores, bits - 1),
+        functools.partial(spread_kernel, cores, bits, len(others)),
         "spread",
-        [before, other] + pieces,
+        [before] + others + pieces,
         [BF16] * cores,
         shape,
     )
     states = [outs[0]] + [rotate(outs[k], "narrow", k) for k in range(1, cores)]
     while works:
-        done.append(works.pop(0)(packed)[0])
+        done.append(works.pop(0)(outs[0])[0])
     return states, done
+
+
+def split_order(order):
+    half = 1 << (len(order) - 1)
+    place = lambda slot: sum(
+        ((slot >> (len(order) - 1 - i)) & 1) << bit for i, bit in enumerate(order)
+    )
+    return [place(slot) for slot in range(half)], [place(slot) for slot in range(half, 2 * half)]
 
 
 def reduce_bricks(parts, orders):
@@ -491,41 +600,42 @@
     narrow_count, narrow_place = lax.axis_size("narrow"), lax.axis_index("narrow")
 
     blocks = tokens // BLK
-    cuts = sorted({blocks * i // 3 for i in range(4)})
+    cuts = sorted({blocks * i // 2 for i in range(3)})
     spans = [(first, last - first) for first, last in zip(cuts, cuts[1:])]
     xs, ks, vs, w_q, before, totals = key_value(spans, voxels, w_qkv, narrow_count)
+
+    def direct(arrays):
+        arrays, x = lax.optimization_barrier((arrays, xs[0]))
+        return direct_features([x] + xs[1:], w_out, w_feature), arrays
 
     def work(n):
         def run(array):
             array, k = lax.optimization_barrier((array, ks[n]))
-            weight = w_out if n == 0 else None
-            return local_attention(
-                xs[n], w_q, k, vs[n], before, weight, w_feature, *spans[n]
-            ), array
+            return local_attention(xs[n], w_q, k, vs[n], before, *spans[n]), array
 
         return run
 
-    states, pieces = earlier_state(totals, [work(n) for n in range(len(spans))])
-    weights = pieces[0][3]
-    qs, parts, own = ([piece[i] for piece in pieces] for i in range(3))
+    states, done = earlier_state(totals, direct, [work(n) for n in range(len(spans))])
+    own, weights = done[0][:-1], done[0][-1]
+    qs, parts = ([piece[i] for piece in done[1:]] for i in range(2))
     normed = own_share(narrow_count, states[0], qs, parts)
 
     bits = list(range(wide_count.bit_length() - 1))
     orders = [bits, bits[1::-1] + bits[2:]]
-    kept_a, sent_a, kept_b, sent_b = finish(
-        spans,
-        row_brick[:, 0],
-        qs,
-        parts,
-        normed,
-        own,
-        states[1:],
-        weights,
-        cell_place.reshape(-1, ROW),
-        wide_count,
-        orders,
-    )
-    outer, middle = reduce_bricks([(kept_a, sent_a), (kept_b, sent_b)], orders)
+    sides = [split_order(order) for order in orders]
+    cell_rows = cell_place.reshape(-1, 1, ROW)
+    most = max(2, 2 * (tokens // ROW) // wide_count)
+    bricks = row_brick[:, 0]
+    features, outer_goes = voxel_features(
+        spans, bricks, qs, parts, normed, own, states[1:], weights, cell_rows, sides[0][1], wide_count, most
+    )
+    (middle_goes,) = pool(bricks, cell_rows, features, [(sides[1][1], True)], wide_count, most)
+    outer_stays, middle_stays = pool(
+        bricks, cell_rows, features, [(sides[0][0], False), (sides[1][0], True)], wide_count, most
+    )
+    outer, middle = reduce_bricks(
+        [(outer_stays, outer_goes), (middle_stays, middle_goes)], orders
+    )
     outer, middle = (part.reshape(-1, BY, channels) for part in (outer, middle))
     above, below = exchange_lines(outer)
     lines = jnp.concatenate([above, outer[:2], middle, outer[2:], below], axis=0)

time: 55.8 us -> 55.6 us (level)
  starting transfers between devices: 24 us -> 15.5 us
  waiting for transfers between devices: 12.8 us -> 20.6 us
  Pallas kernels: 18 us -> 18.6 us
    ppermute x10 -> x7, starting transfers between devices: 20 us -> 6.17 us  [swap(): return lax.ppermute(array, axis, [(i, i ^ 1 << bit) for i in range(count)])]
    ppermute x0 -> x4, starting transfers between devices: none -> 7.17 us  [swap_digit(): return lax.ppermute(array, axis, [(i, i ^ by << bit) for i in range(count)])]
    ppermute x10 -> x7, waiting for transfers between devices: 9.18 us -> 13.1 us  [swap(): return lax.ppermute(array, axis, [(i, i ^ 1 << bit) for i in range(count)])]
    ppermute x0 -> x4, waiting for transfers between devices: none -> 3.28 us  [swap_digit(): return lax.ppermute(array, axis, [(i, i ^ by << bit) for i in range(count)])]
    ppermute x2, starting transfers between devices: 3.37 us -> 1.56 us  [exchange_lines(): got.append(lax.ppermute(out, ('group', 'wide', 'narrow'), pairs))]
    ppermute x2, waiting for transfers between devices: 2.4 us -> 3.88 us  [exchange_lines(): got.append(lax.ppermute(out, ('group', 'wide', 'narrow'), pairs))]
    ppermute x2, waiting for transfers between devices: 1.23 us -> 0.39 us  [rotate(): lax.ppermute(array, axis, [(i, (i + by) % count) for i in range(count)])]
    pallas_call x4 -> x6, Pallas kernels: 9.54 us -> 10.2 us  [the longest x2 5.03 us: local_attention(): pl.pallas_call(functools.partial(local_kernel, first, count), in_specs=[v...]
  transfers between devices with their start and end apart: 14 -> 15, of which waited for: 10 -> 11; matrix products, arithmetic and copies ran while one was open for 1% -> 1% of each run, Pallas kernels for 13% -> 16%
where the time goes in v4:
time: 55.6 us; the launch traced here: 55.5 us
  waiting for transfers between devices  20.6 us (37%)
  Pallas kernels  18.6 us (33%)
  starting transfers between devices  15.5 us (28%)
    ppermute x7, waiting for transfers between devices, swap(): return lax.ppermute(array, axis, [(i, i ^ 1 << bit) for i in range(count)])  13.1 us
    ppermute x4, starting transfers between devices, swap_digit(): return lax.ppermute(array, axis, [(i, i ^ by << bit) for i in range(count)])  7.17 us
    ppermute x7, starting transfers between devices, swap(): return lax.ppermute(array, axis, [(i, i ^ 1 << bit) for i in range(count)])  6.17 us
    pallas_call x2, Pallas kernels, local_attention(): pl.pallas_call(functools.partial(local_kernel, first, count), in_specs=[v...  5.03 us
    pallas_call x1, Pallas kernels, key_value(): pl.pallas_call(functools.partial(key_value_kernel, spans), in_specs=[hbm,...  4.96 us
    ppermute x2, waiting for transfers between devices, exchange_lines(): got.append(lax.ppermute(out, ('group', 'wide', 'narrow'), pairs))  3.88 us
    ppermute x4, waiting for transfers between devices, swap_digit(): return lax.ppermute(array, axis, [(i, i ^ by << bit) for i in range(count)])  3.28 us
    pallas_call x1, Pallas kernels, field_flow(): pl.pallas_call(field_kernel, in_specs=[vmem] * 4, out_specs=vmem, out_sha...  2.38 us
  transfers between devices with their start and end apart: 15, of which 11 were waited for; matrix products, arithmetic and copies ran while one was open for 1% of the time, Pallas kernels for 16%

profile of v4, /device:TPU:0, one launch (start us, length us, event | category | flops | bytes accessed | tf_op | source)
XLA Modules:
  0.0 55.5 jit_solution(8791253229040480996)
XLA Ops:
  0.0 5.0 %key_value.1 = (bf16[1024,512]{1,0:T(8,128)(2,1)S(1)}, bf16[1024,512]{1,0:T(8,128)(2,1)S(1)}, bf16[1024,512]{1,0:T(8,128)(2,1)S(1)}, bf16[1024,512]{1,0:T(8,128)...) custom-call(bf16[2048,512]{1,0:T(8,128)(2,1)} %x_ref.1, ...), custom_call_target="tpu_custom_call" | custom-call | tf_op jit(solution)/shard_map/key_value/pallas_call | solution.py:113
  5.0 0.5 collective-permute-start
  5.5 0.0 copy-done.2
  5.5 0.0 copy-done.3
  5.5 0.8 %direct_features.1 = (f32[1024,256]{1,0:T(8,128)S(1)}, f32[1024,256]{1,0:T(8,128)S(1)}, bf16[512,256]{1,0:T(8,128)(2,1)S(1)}) custom-call(bf16[1024,512]{1,0:T(8,128)(2,1)S(1)} %get-tuple-element.56.refs_0_.x_ref, bf16[1024,512]{1,0:T(8,128)(2,1)S(1)} %get-tuple-element.57.refs_1_.x_ref, bf16[512,512]{1,0:T(8,128)(2,1)S(1)} %copy-done.2, ...), custom_call_target="tpu_custom_call" | custom-call | flops 671088640 | bytes 4194304 | tf_op jit(solution)/shard_map/direct_features/pallas_call | solution.py:181
  6.3 0.0 collective-permute-done.refs_1_.refs_2_
  6.4 2.9 %collective-permute-start.1 = (bf16[2,128,128]{2,1,0:T(8,128)(2,1)S(1)}, bf16[2,128,128]{2,1,0:T(8,128)(2,1)S(1)}, u32[]{:S(2)}, u32[]{:S(2)}) collective-permute-start(bf16[2,128,128]{2,1,0:T(8,128)(2,1)S(1)} %get-tuple-element.70), channel_id=1, source_target_pairs={{0,2},{2,0},{4,6},{6,4},{8,10},{10,8},{12,14},{14,12},{1,3},{3,1},... | collective-permute-start | bytes 196616 | tf_op jit(solution)/shard_map/ppermute | solution.py:478
  9.4 1.6 %collective-permute-start.2 = (bf16[2,128,128]{2,1,0:T(8,128)(2,1)S(1)}, bf16[2,128,128]{2,1,0:T(8,128)(2,1)S(1)}, u32[]{:S(2)}, u32[]{:S(2)}) collective-permute-start(bf16[2,128,128]{2,1,0:T(8,128)(2,1)S(1)} %get-tuple-element.70), channel_id=1, source_target_pairs={{0,4},{2,6},{4,0},{6,2},{8,12},{10,14},{12,8},{14,10},{1,5},{3,7},... | collective-permute-start | bytes 196616 | tf_op jit(solution)/shard_map/ppermute | solution.py:478
  10.9 0.0 collective-permute-start.3
  10.9 2.5 %local_attention.2 = (bf16[1024,512]{1,0:T(8,128)(2,1)S(1)}, f32[1024,512]{1,0:T(8,128)S(1)}) custom-call(bf16[1024,512]{1,0:T(8,128)(2,1)S(1)} %get-tuple-element.56.refs_0_.x_ref, bf16[512,512]{1,0:T(8,128)(2,1)S(1)} %get-tuple-element.53.wq_ref, bf16[1024,512]{1,0:T(8,128)(2,1)S(1)} %get-tuple-element.65.k_ref, ...), custom_call_target="tpu_custom_call" | custom-call | flops 1207959552 | bytes 6291456 | tf_op jit(solution)/shard_map/local_attention/pallas_call | solution.py:151
  13.5 0.0 collective-permute-done.1.refs_0_
  13.5 0.7 %collective-permute-done.2.refs_1_ = bf16[2,128,128]{2,1,0:T(8,128)(2,1)S(1)} collective-permute-done((bf16[2,128,128]{2,1,0:T(8,128)(2,1)S(1)}, bf16[2,128,128]{2,1,0:T(8,128)(2,1)S(1)}, u32[]{:S(2)}, u32[]{:S(2)}) %collective-permute-start.2) | collective-permute-done | bytes 65568 | tf_op jit(solution)/shard_map/ppermute | solution.py:478
  14.2 1.9 %collective-permute-done.3.refs_2_ = bf16[2,128,128]{2,1,0:T(8,128)(2,1)S(1)} collective-permute-done((bf16[2,128,128]{2,1,0:T(8,128)(2,1)S(1)}, bf16[2,128,128]{2,1,0:T(8,128)(2,1)S(1)}, u32[]{:S(2)}, u32[]{:S(2)}) %collective-permute-start.3) | collective-permute-done | bytes 65568 | tf_op jit(solution)/shard_map/ppermute | solution.py:478
  16.1 0.1 scan.1
  16.2 2.6 %collective-permute-start.4 = (bf16[2,128,128]{2,1,0:T(8,128)(2,1)S(1)}, bf16[2,128,128]{2,1,0:T(8,128)(2,1)S(1)}, u32[]{:S(2)}, u32[]{:S(2)}) collective-permute-start(bf16[2,128,128]{2,1,0:T(8,128)(2,1)S(1)} %get-tuple-element.82), channel_id=1, source_target_pairs={{0,8},{2,10},{4,12},{6,14},{8,0},{10,2},{12,4},{14,6},{1,9},{3,11}... | collective-permute-start | bytes 196616 | tf_op jit(solution)/shard_map/ppermute | solution.py:478
  18.8 2.5 %local_attention.3 = (bf16[1024,512]{1,0:T(8,128)(2,1)S(1)}, f32[1024,512]{1,0:T(8,128)S(1)}) custom-call(bf16[1024,512]{1,0:T(8,128)(2,1)S(1)} %get-tuple-element.57.refs_1_.x_ref, bf16[512,512]{1,0:T(8,128)(2,1)S(1)} %get-tuple-element.53.wq_ref, bf16[1024,512]{1,0:T(8,128)(2,1)S(1)} %get-tuple-element.78.k_ref, ...), custom_call_target="tpu_custom_call" | custom-call | flops 1207959552 | bytes 6291456 | tf_op jit(solution)/shard_map/local_attention/pallas_call | solution.py:151
  21.4 0.7 %collective-permute-done.4.refs_0_ = bf16[2,128,128]{2,1,0:T(8,128)(2,1)S(1)} collective-permute-done((bf16[2,128,128]{2,1,0:T(8,128)(2,1)S(1)}, bf16[2,128,128]{2,1,0:T(8,128)(2,1)S(1)}, u32[]{:S(2)}, u32[]{:S(2)}) %collective-permute-start.4) | collective-permute-done | bytes 65568 | tf_op jit(solution)/shard_map/ppermute | solution.py:478
  22.0 0.1 spread.1
  22.1 0.1 collective-permute-start.5
  22.2 0.0 copy-start.4
  22.2 0.0 copy-start.5
  22.2 0.9 %own_share.1 = (bf16[1024,256]{1,0:T(8,128)(2,1)S(1)}, bf16[1024,256]{1,0:T(8,128)(2,1)S(1)}) custom-call(bf16[2,128,128]{2,1,0:T(8,128)(2,1)S(1)} %get-tuple-element.88.state_ref, bf16[1024,512]{1,0:T(8,128)(2,1)S(1)} %get-tuple-element.71.refs_0_, bf16[1024,512]{1,0:T(8,128)(2,1)S(1)} %get-tuple-element.83.refs_1_, ...), custom_call_target="tpu_custom_call" | custom-call | flops 536870912 | bytes 4194304 | tf_op jit(solution)/shard_map/own_share/pallas_call | solution.py:285
  23.1 0.3 collective-permute-done.5.refs_8_
  23.4 0.0 copy-done.4
  23.4 2.3 %voxel_features.1 = (bf16[2048,256]{1,0:T(8,128)(2,1)S(1)}, bf16[4,128,256]{2,1,0:T(8,128)(2,1)S(1)}) custom-call(s32[16]{0:T(128)S(1)} %bitcast.8, bf16[1024,512]{1,0:T(8,128)(2,1)S(1)} %get-tuple-element.71.refs_0_, bf16[1024,512]{1,0:T(8,128)(2,1)S(1)} %get-tuple-element.83.refs_1_, f32[1024,512]{1,0:T(8,128)S(1)} %get-tuple-element.84.refs_2_, ...), custom_call_target="tpu_custom_call" | custom-call | tf_op jit(solution)/shard_map/voxel_features/pallas_call | solution.py:374
  25.7 0.7 %collective-permute-start.6 = (bf16[4,128,256]{2,1,0:T(8,128)(2,1)S(1)}, bf16[4,128,256]{2,1,0:T(8,128)(2,1)S(1)}, u32[]{:S(2)}, u32[]{:S(2)}) collective-permute-start(bf16[4,128,256]{2,1,0:T(8,128)(2,1)S(1)} %get-tuple-element.97), channel_id=1, source_target_pairs={{0,2},{2,0},{4,6},{6,4},{8,10},{10,8},{12,14},{14,12},{1,3},{3,1},... | collective-permute-start | bytes 786440 | tf_op jit(solution)/shard_map/ppermute | solution.py:473
  26.4 0.9 %pool.3 = bf16[4,128,256]{2,1,0:T(8,128)(2,1)S(1)} custom-call(s32[16]{0:T(128)S(1)} %bitcast.9, s32[16,1,128]{2,1,0:T(1,128)S(1)} %bitcast.6, bf16[2048,256]{1,0:T(8,128)(2,1)S(1)} %get-tuple-element.95.features_ref), custom_call_target="tpu_custom_call" | custom-call | flops 134217728 | bytes 1048576 | tf_op jit(solution)/shard_map/pool/pallas_call | solution.py:405
  27.4 0.5 collective-permute-start.11
  27.9 1.1 %pool.2 = (bf16[4,128,256]{2,1,0:T(8,128)(2,1)S(1)}, bf16[4,128,256]{2,1,0:T(8,128)(2,1)S(1)}) custom-call(s32[16]{0:T(128)S(1)} %bitcast.10, s32[16,1,128]{2,1,0:T(1,128)S(1)} %bitcast.7, bf16[2048,256]{1,0:T(8,128)(2,1)S(1)} %get-tuple-element.95.features_ref), custom_call_target="tpu_custom_call" | custom-call | flops 268435456 | bytes 1048576 | tf_op jit(solution)/shard_map/pool/pallas_call | solution.py:405
  29.0 5.2 %collective-permute-done.6 = bf16[4,128,256]{2,1,0:T(8,128)(2,1)S(1)} collective-permute-done((bf16[4,128,256]{2,1,0:T(8,128)(2,1)S(1)}, bf16[4,128,256]{2,1,0:T(8,128)(2,1)S(1)}, u32[]{:S(2)}, u32[]{:S(2)}) %collective-permute-start.6) | collective-permute-done | bytes 262176 | tf_op jit(solution)/shard_map/ppermute | solution.py:473
  34.2 0.1 add_convert_fusion.1
  34.3 0.1 collective-permute-start.7
  34.4 1.2 %collective-permute-done.11 = bf16[4,128,256]{2,1,0:T(8,128)(2,1)S(1)} collective-permute-done((bf16[4,128,256]{2,1,0:T(8,128)(2,1)S(1)}, bf16[4,128,256]{2,1,0:T(8,128)(2,1)S(1)}, u32[]{:S(2)}, u32[]{:S(2)}) %collective-permute-start.11) | collective-permute-done | bytes 262176 | tf_op jit(solution)/shard_map/ppermute | solution.py:473
  35.6 0.1 add_convert_fusion
  35.6 1.5 %collective-permute-start.12 = (bf16[2,128,256]{2,1,0:T(8,128)(2,1)S(1)}, bf16[2,128,256]{2,1,0:T(8,128)(2,1)S(1)}, u32[]{:S(2)}, u32[]{:S(2)}) collective-permute-start(bf16[2,128,256]{2,1,0:T(8,128)(2,1)S(1)} %slice.67), channel_id=1, source_target_pairs={{0,2},{2,0},{4,6},{6,4},{8,10},{10,8},{12,14},{14,12},{1,3},{3,1},... | collective-permute-start | bytes 393224 | tf_op jit(solution)/shard_map/ppermute | solution.py:473
  37.1 2.2 %collective-permute-done.7 = bf16[2,128,256]{2,1,0:T(8,128)(2,1)S(1)} collective-permute-done((bf16[2,128,256]{2,1,0:T(8,128)(2,1)S(1)}, bf16[2,128,256]{2,1,0:T(8,128)(2,1)S(1)}, u32[]{:S(2)}, u32[]{:S(2)}) %collective-permute-start.7) | collective-permute-done | bytes 131104 | tf_op jit(solution)/shard_map/ppermute | solution.py:473
  39.4 2.1 %collective-permute-start.8 = (bf16[1,128,256]{2,1,0:T(8,128)(2,1)S(1)}, bf16[1,128,256]{2,1,0:T(8,128)(2,1)S(1)}, u32[]{:S(2)}, u32[]{:S(2)}) collective-permute-start(bf16[1,128,256]{2,1,0:T(8,128)(2,1)S(1)} %slice.63), channel_id=1, source_target_pairs={{0,8},{2,10},{4,12},{6,14},{8,0},{10,2},{12,4},{14,6},{1,9},{3,11}... | collective-permute-start | bytes 196616 | tf_op jit(solution)/shard_map/ppermute | solution.py:473
  41.4 0.0 collective-permute-done.12
  41.5 1.3 %collective-permute-start.13 = (bf16[1,128,256]{2,1,0:T(8,128)(2,1)S(1)}, bf16[1,128,256]{2,1,0:T(8,128)(2,1)S(1)}, u32[]{:S(2)}, u32[]{:S(2)}) collective-permute-start(bf16[1,128,256]{2,1,0:T(8,128)(2,1)S(1)} %slice.69), channel_id=1, source_target_pairs={{0,8},{2,10},{4,12},{6,14},{8,0},{10,2},{12,4},{14,6},{1,9},{3,11}... | collective-permute-start | bytes 196616 | tf_op jit(solution)/shard_map/ppermute | solution.py:473
  42.8 3.3 %collective-permute-done.8 = bf16[1,128,256]{2,1,0:T(8,128)(2,1)S(1)} collective-permute-done((bf16[1,128,256]{2,1,0:T(8,128)(2,1)S(1)}, bf16[1,128,256]{2,1,0:T(8,128)(2,1)S(1)}, u32[]{:S(2)}, u32[]{:S(2)}) %collective-permute-start.8) | collective-permute-done | bytes 65568 | tf_op jit(solution)/shard_map/ppermute | solution.py:473
  46.1 1.6 %collective-permute-start.10 = (bf16[2,32,256]{2,1,0:T(8,128)(2,1)S(1)}, bf16[2,32,256]{2,1,0:T(8,128)(2,1)S(1)}, u32[]{:S(2)}, u32[]{:S(2)}) collective-permute-start(bf16[2,32,256]{2,1,0:T(8,128)(2,1)S(1)} %get-tuple-element.99), channel_id=1, source_target_pairs={{0,16},{1,17},{2,4},{3,5},{4,2},{5,3},{6,8},{7,9},{8,6},{9,7},{10,... | collective-permute-start | bytes 98312 | tf_op jit(solution)/shard_map/ppermute | solution.py:518
  47.7 0.0 collective-permute-start.9
  47.7 0.0 collective-permute-done.13
  47.7 2.4 %collective-permute-done.10 = bf16[2,32,256]{2,1,0:T(8,128)(2,1)S(1)} collective-permute-done((bf16[2,32,256]{2,1,0:T(8,128)(2,1)S(1)}, bf16[2,32,256]{2,1,0:T(8,128)(2,1)S(1)}, u32[]{:S(2)}, u32[]{:S(2)}) %collective-permute-start.10) | collective-permute-done | bytes 32800 | tf_op jit(solution)/shard_map/ppermute | solution.py:518
  50.1 1.5 %collective-permute-done.9 = bf16[2,32,256]{2,1,0:T(8,128)(2,1)S(1)} collective-permute-done((bf16[2,32,256]{2,1,0:T(8,128)(2,1)S(1)}, bf16[2,32,256]{2,1,0:T(8,128)(2,1)S(1)}, u32[]{:S(2)}, u32[]{:S(2)}) %collective-permute-start.9) | collective-permute-done | bytes 32800 | tf_op jit(solution)/shard_map/ppermute | solution.py:518
  51.7 0.1 collective-permute-start.14
  51.8 1.2 %collective-permute-done.14 = bf16[12,2,256]{2,1,0:T(2,128)(2,1)S(1)} collective-permute-done((bf16[12,2,256]{2,1,0:T(2,128)(2,1)S(1)}, bf16[12,2,256]{2,1,0:T(2,128)(2,1)S(1)}, u32[]{:S(2)}, u32[]{:S(2)}) %collective-permute-start.14) | collective-permute-done | bytes 12320 | tf_op jit(solution)/shard_map/ppermute | solution.py:473
  53.1 2.4 %field_flow.1 = f32[8,32,256]{2,1,0:T(8,128)} custom-call(bf16[12,32,256]{2,1,0:T(8,128)(2,1)S(1)} %select_dynamic-update-slice_fusion.lines_ref, bf16[13,16,256]{2,1,0:T(8,128)(2,1)S(1)} %pad_add_fusion.sides_ref, bf16[3,3,256,256]{3,2,1,0:T(8,128)(2,1)S(1)} %copy-done, bf16[3,3,256,256]{3,2,1,0:T(8,128)(2,1)S(1)} %copy-done.1), custom_call_target="tpu_custom_call" | custom-call | tf_op jit(solution)/shard_map/field_flow/pallas_call | solution.py:460
  (27 shorter events, 0.3 us)
Async XLA Ops:
  0.0 5.5 %copy-start.2 = (bf16[512,512]{1,0:T(8,128)(2,1)S(1)}, bf16[512,512]{1,0:T(8,128)(2,1)}, u32[]{:S(2)}) copy-start(bf16[512,512]{1,0:T(8,128)(2,1)} %refs_2_.1) | copy-start | bytes 1572868
  0.0 5.5 %copy-start.3 = (bf16[512,256]{1,0:T(8,128)(2,1)S(1)}, bf16[512,256]{1,0:T(8,128)(2,1)}, u32[]{:S(2)}) copy-start(bf16[512,256]{1,0:T(8,128)(2,1)} %refs_3_.1) | copy-start | bytes 786436
  5.0 1.4 %collective-permute-start = (bf16[2,128,128]{2,1,0:T(8,128)(2,1)S(1)}, bf16[2,128,128]{2,1,0:T(8,128)(2,1)S(1)}, u32[]{:S(2)}, u32[]{:S(2)}) collective-permute-start(bf16[2,128,128]{2,1,0:T(8,128)(2,1)S(1)} %get-tuple-element.61), channel_id=1, source_target_pairs={{0,1},{1,0},{2,3},{3,2},{4,5},{5,4},{6,7},{7,6},{8,9},{9,8},{10,11... | collective-permute-start | bytes 196616 | tf_op jit(solution)/shard_map/ppermute | solution.py:490
  6.4 7.0 %collective-permute-start.1 = (bf16[2,128,128]{2,1,0:T(8,128)(2,1)S(1)}, bf16[2,128,128]{2,1,0:T(8,128)(2,1)S(1)}, u32[]{:S(2)}, u32[]{:S(2)}) collective-permute-start(bf16[2,128,128]{2,1,0:T(8,128)(2,1)S(1)} %get-tuple-element.70), channel_id=1, source_target_pairs={{0,2},{2,0},{4,6},{6,4},{8,10},{10,8},{12,14},{14,12},{1,3},{3,1},... | collective-permute-start | bytes 196616 | tf_op jit(solution)/shard_map/ppermute | solution.py:478
  9.4 4.8 %collective-permute-start.2 = (bf16[2,128,128]{2,1,0:T(8,128)(2,1)S(1)}, bf16[2,128,128]{2,1,0:T(8,128)(2,1)S(1)}, u32[]{:S(2)}, u32[]{:S(2)}) collective-permute-start(bf16[2,128,128]{2,1,0:T(8,128)(2,1)S(1)} %get-tuple-element.70), channel_id=1, source_target_pairs={{0,4},{2,6},{4,0},{6,2},{8,12},{10,14},{12,8},{14,10},{1,5},{3,7},... | collective-permute-start | bytes 196616 | tf_op jit(solution)/shard_map/ppermute | solution.py:478
  10.9 5.2 %collective-permute-start.3 = (bf16[2,128,128]{2,1,0:T(8,128)(2,1)S(1)}, bf16[2,128,128]{2,1,0:T(8,128)(2,1)S(1)}, u32[]{:S(2)}, u32[]{:S(2)}) collective-permute-start(bf16[2,128,128]{2,1,0:T(8,128)(2,1)S(1)} %get-tuple-element.70), channel_id=1, source_target_pairs={{0,6},{2,4},{4,2},{6,0},{8,14},{10,12},{12,10},{14,8},{1,7},{3,5},... | collective-permute-start | bytes 196616 | tf_op jit(solution)/shard_map/ppermute | solution.py:478
  16.2 5.8 %collective-permute-start.4 = (bf16[2,128,128]{2,1,0:T(8,128)(2,1)S(1)}, bf16[2,128,128]{2,1,0:T(8,128)(2,1)S(1)}, u32[]{:S(2)}, u32[]{:S(2)}) collective-permute-start(bf16[2,128,128]{2,1,0:T(8,128)(2,1)S(1)} %get-tuple-element.82), channel_id=1, source_target_pairs={{0,8},{2,10},{4,12},{6,14},{8,0},{10,2},{12,4},{14,6},{1,9},{3,11}... | collective-permute-start | bytes 196616 | tf_op jit(solution)/shard_map/ppermute | solution.py:478
  22.1 1.3 %collective-permute-start.5 = (bf16[2,128,128]{2,1,0:T(8,128)(2,1)S(1)}, bf16[2,128,128]{2,1,0:T(8,128)(2,1)S(1)}, u32[]{:S(2)}, u32[]{:S(2)}) collective-permute-start(bf16[2,128,128]{2,1,0:T(8,128)(2,1)S(1)} %get-tuple-element.93), channel_id=1, source_target_pairs={{0,1},{1,0},{2,3},{3,2},{4,5},{5,4},{6,7},{7,6},{8,9},{9,8},{10,11... | collective-permute-start | bytes 196616 | tf_op jit(solution)/shard_map/ppermute | solution.py:490
  22.2 1.2 %copy-start.4 = (s32[2048]{0:T(1024)S(1)}, s32[2048]{0:T(1024)}, u32[]{:S(2)}) copy-start(s32[2048]{0:T(1024)} %param.15) | copy-start | bytes 24580
  22.2 1.2 %copy-start.5 = (s32[16,1]{0,1:T(1,128)S(1)}, s32[16,1]{0,1:T(1,128)}, u32[]{:S(2)}) copy-start(s32[16,1]{0,1:T(1,128)} %param.14) | copy-start | bytes 196
  25.7 8.4 %collective-permute-start.6 = (bf16[4,128,256]{2,1,0:T(8,128)(2,1)S(1)}, bf16[4,128,256]{2,1,0:T(8,128)(2,1)S(1)}, u32[]{:S(2)}, u32[]{:S(2)}) collective-permute-start(bf16[4,128,256]{2,1,0:T(8,128)(2,1)S(1)} %get-tuple-element.97), channel_id=1, source_target_pairs={{0,2},{2,0},{4,6},{6,4},{8,10},{10,8},{12,14},{14,12},{1,3},{3,1},... | collective-permute-start | bytes 786440 | tf_op jit(solution)/shard_map/ppermute | solution.py:473
  27.4 8.2 %collective-permute-start.11 = (bf16[4,128,256]{2,1,0:T(8,128)(2,1)S(1)}, bf16[4,128,256]{2,1,0:T(8,128)(2,1)S(1)}, u32[]{:S(2)}, u32[]{:S(2)}) collective-permute-start(bf16[4,128,256]{2,1,0:T(8,128)(2,1)S(1)} %pool.3), channel_id=1, source_target_pairs={{0,4},{2,6},{4,0},{6,2},{8,12},{10,14},{12,8},{14,10},{1,5},{3,7},... | collective-permute-start | bytes 786440 | tf_op jit(solution)/shard_map/ppermute | solution.py:473
  34.2 18.9 %copy-start = (bf16[3,3,256,256]{3,2,1,0:T(8,128)(2,1)S(1)}, bf16[3,3,256,256]{3,2,1,0:T(8,128)(2,1)}, u32[]{:S(2)}) copy-start(bf16[3,3,256,256]{3,2,1,0:T(8,128)(2,1)} %w1_ref.1) | copy-start | bytes 3538948
  34.2 18.9 %copy-start.1 = (bf16[3,3,256,256]{3,2,1,0:T(8,128)(2,1)S(1)}, bf16[3,3,256,256]{3,2,1,0:T(8,128)(2,1)}, u32[]{:S(2)}) copy-start(bf16[3,3,256,256]{3,2,1,0:T(8,128)(2,1)} %w2_ref.1) | copy-start | bytes 3538948
  34.3 5.0 %collective-permute-start.7 = (bf16[2,128,256]{2,1,0:T(8,128)(2,1)S(1)}, bf16[2,128,256]{2,1,0:T(8,128)(2,1)S(1)}, u32[]{:S(2)}, u32[]{:S(2)}) collective-permute-start(bf16[2,128,256]{2,1,0:T(8,128)(2,1)S(1)} %slice.61), channel_id=1, source_target_pairs={{0,4},{2,6},{4,0},{6,2},{8,12},{10,14},{12,8},{14,10},{1,5},{3,7},... | collective-permute-start | bytes 393224 | tf_op jit(solution)/shard_map/ppermute | solution.py:473
  35.6 5.8 %collective-permute-start.12 = (bf16[2,128,256]{2,1,0:T(8,128)(2,1)S(1)}, bf16[2,128,256]{2,1,0:T(8,128)(2,1)S(1)}, u32[]{:S(2)}, u32[]{:S(2)}) collective-permute-start(bf16[2,128,256]{2,1,0:T(8,128)(2,1)S(1)} %slice.67), channel_id=1, source_target_pairs={{0,2},{2,0},{4,6},{6,4},{8,10},{10,8},{12,14},{14,12},{1,3},{3,1},... | collective-permute-start | bytes 393224 | tf_op jit(solution)/shard_map/ppermute | solution.py:473
  39.4 6.7 %collective-permute-start.8 = (bf16[1,128,256]{2,1,0:T(8,128)(2,1)S(1)}, bf16[1,128,256]{2,1,0:T(8,128)(2,1)S(1)}, u32[]{:S(2)}, u32[]{:S(2)}) collective-permute-start(bf16[1,128,256]{2,1,0:T(8,128)(2,1)S(1)} %slice.63), channel_id=1, source_target_pairs={{0,8},{2,10},{4,12},{6,14},{8,0},{10,2},{12,4},{14,6},{1,9},{3,11}... | collective-permute-start | bytes 196616 | tf_op jit(solution)/shard_map/ppermute | solution.py:473
  41.5 6.2 %collective-permute-start.13 = (bf16[1,128,256]{2,1,0:T(8,128)(2,1)S(1)}, bf16[1,128,256]{2,1,0:T(8,128)(2,1)S(1)}, u32[]{:S(2)}, u32[]{:S(2)}) collective-permute-start(bf16[1,128,256]{2,1,0:T(8,128)(2,1)S(1)} %slice.69), channel_id=1, source_target_pairs={{0,8},{2,10},{4,12},{6,14},{8,0},{10,2},{12,4},{14,6},{1,9},{3,11}... | collective-permute-start | bytes 196616 | tf_op jit(solution)/shard_map/ppermute | solution.py:473
  46.1 4.0 %collective-permute-start.10 = (bf16[2,32,256]{2,1,0:T(8,128)(2,1)S(1)}, bf16[2,32,256]{2,1,0:T(8,128)(2,1)S(1)}, u32[]{:S(2)}, u32[]{:S(2)}) collective-permute-start(bf16[2,32,256]{2,1,0:T(8,128)(2,1)S(1)} %get-tuple-element.99), channel_id=1, source_target_pairs={{0,16},{1,17},{2,4},{3,5},{4,2},{5,3},{6,8},{7,9},{8,6},{9,7},{10,... | collective-permute-start | bytes 98312 | tf_op jit(solution)/shard_map/ppermute | solution.py:518
  47.7 3.9 %collective-permute-start.9 = (bf16[2,32,256]{2,1,0:T(8,128)(2,1)S(1)}, bf16[2,32,256]{2,1,0:T(8,128)(2,1)S(1)}, u32[]{:S(2)}, u32[]{:S(2)}) collective-permute-start(bf16[2,32,256]{2,1,0:T(8,128)(2,1)S(1)} %get-tuple-element.100), channel_id=1, source_target_pairs={{0,2},{1,3},{2,0},{3,1},{4,6},{5,7},{6,4},{7,5},{8,10},{9,11},{10,... | collective-permute-start | bytes 98312 | tf_op jit(solution)/shard_map/ppermute | solution.py:518
  51.7 1.2 %collective-permute-start.14 = (bf16[12,2,256]{2,1,0:T(2,128)(2,1)S(1)}, bf16[12,2,256]{2,1,0:T(2,128)(2,1)S(1)}, u32[]{:S(2)}, u32[]{:S(2)}) collective-permute-start(bf16[12,2,256]{2,1,0:T(2,128)(2,1)S(1)} %broadcast_select_fusion.4), channel_id=1, source_target_pairs={{0,1},{1,0},{2,3},{3,2},{4,5},{5,4},{6,7},{7,6},{8,9},{9,8},{10,11... | collective-permute-start | bytes 36872 | tf_op jit(solution)/shard_map/ppermute | solution.py:473

commit v5 on v4

--- a/solution.py
+++ b/solution.py
@@ -269,31 +269,33 @@
     return pl.ds(pl.multiple_of(owner * width, width), width)
 
 
-def own_share_kernel(cores, state_ref, *refs):
-    pieces = len(refs) // 3
-    qs, parts, outs, scratch = refs[:pieces], refs[pieces : 2 * pieces], refs[2 * pieces : -1], refs[-1]
+def own_share_kernel(cores, state_ref, w_ref, *refs):
+    pieces = len(refs) // 4
+    qs, parts, direct, outs = (refs[i * pieces : (i + 1) * pieces] for i in range(4))
+    scratch = refs[-1]
     cols = share_columns(cores, 0)
     state, ones = block_state(state_ref, scratch), ones_blocks(scratch.shape[0])
-    for q, part, out in zip(qs, parts, outs):
-        out[...] = norm_share(q[:, cols], part[:, cols], state, ones)
-
-
-def own_share(cores, state, qs, parts):
+    for q, part, start, out in zip(qs, parts, direct, outs):
+        normed = norm_share(q[:, cols], part[:, cols], state, ones)
+        out[...] = start[...] + dot(normed, w_ref[cols, :])
+
+
+def own_share(cores, state, weights, qs, parts, direct):
     width = HEADS // cores * HEAD
     vmem = pl.BlockSpec(memory_space=pltpu.VMEM)
     rows = sum(q.shape[0] for q in qs)
     return pl.pallas_call(
         functools.partial(own_share_kernel, cores),
-        in_specs=[vmem] * (1 + 2 * len(qs)),
+        in_specs=[vmem] * (2 + 3 * len(qs)),
         out_specs=[vmem] * len(qs),
-        out_shape=[jax.ShapeDtypeStruct((q.shape[0], width), BF16) for q in qs],
+        out_shape=[jax.ShapeDtypeStruct(start.shape, F32) for start in direct],
         scratch_shapes=[pltpu.VMEM((width, width), BF16)],
         compiler_params=params(),
         cost_estimate=pl.CostEstimate(
-            flops=4 * rows * width * width, bytes_accessed=rows * width * 8, transcendentals=0
+            flops=6 * rows * width * width, bytes_accessed=rows * width * 8, transcendentals=0
         ),
         name="own_share",
-    )(state, *qs, *parts)
+    )(state, weights, *qs, *parts, *direct)
 
 
 def list_rows(brick_ref, most, slots, fill):
@@ -339,7 +341,7 @@
     pieces = len(spans)
     refs = list(refs)
     take = lambda n: [refs.pop(0) for _ in range(n)]
-    q_refs, part_refs, normed_refs, own_refs = (take(pieces) for _ in range(4))
+    q_refs, part_refs, own_refs = (take(pieces) for _ in range(3))
     state_refs = take(cores - 1)
     w_ref, cell_ref, features_ref, out = take(4)
     scratch, slots, fill = refs
@@ -347,7 +349,7 @@
     ones = ones_blocks(scratch.shape[1])
     states = [block_state(ref, scratch.at[k]) for k, ref in enumerate(state_refs)]
     for n, (first, count) in enumerate(spans):
-        features = own_refs[n][...] + dot(normed_refs[n][...], w_ref[shares[0], :])
+        features = own_refs[n][...]
         for state, cols in zip(states, shares[1:]):
             normed = norm_share(q_refs[n][:, cols], part_refs[n][:, cols], state, ones)
             features += dot(normed, w_ref[cols, :])
@@ -364,7 +366,7 @@
 
 
 def voxel_features(
-    spans, bricks, qs, parts, normed, own, states, weights, cell_rows, chosen, count, most
+    spans, bricks, qs, parts, own, states, weights, cell_rows, chosen, count, most
 ):
     tokens, channels = sum(q.shape[0] for q in qs), weights.shape[1]
     cores = len(states) + 1
@@ -373,7 +375,7 @@
     smem = pl.BlockSpec(memory_space=pltpu.SMEM)
     return pl.pallas_call(
         functools.partial(features_kernel, chosen, spans, cores),
-        in_specs=[smem] + [vmem] * (4 * len(spans) + cores + 1),
+        in_specs=[smem] + [vmem] * (3 * len(spans) + cores + 1),
         out_specs=[vmem] * 2,
         out_shape=[
             jax.ShapeDtypeStruct((tokens, channels), BF16),
@@ -383,7 +385,7 @@
         + list_scratch(count, most),
         compiler_params=params(),
         name="voxel_features",
-    )(bricks, *qs, *parts, *normed, *own, *states, weights, cell_rows)
+    )(bricks, *qs, *parts, *own, *states, weights, cell_rows)
 
 
 def pool_kernel(chosen, brick_ref, cell_ref, features_ref, *refs):
@@ -499,7 +501,7 @@
     return jnp.where(first, nothing, other), jnp.where(first, other, nothing)
 
 
-def exchange_lines(strip):
+def exchange_lines(strip, with_it):
     groups, count, cores = (lax.axis_size(axis) for axis in ("group", "wide", "narrow"))
     place = lax.axis_index("wide")
     got = []
@@ -516,11 +518,12 @@
         upper = place % 2 == start
         out = jnp.where(upper, strip[2:], strip[:2])
         got.append(lax.ppermute(out, ("group", "wide", "narrow"), pairs))
+    got, with_it = lax.optimization_barrier((got, with_it))
     above = jnp.where(place % 2 == 1, got[0], got[1])
     below = jnp.where(place % 2 == 1, got[1], got[0])
     above = jnp.where(place > 0, above, jnp.zeros_like(above))
     below = jnp.where(place < count - 1, below, jnp.zeros_like(below))
-    return above, below
+    return above, below, with_it
 
 
 def earlier_state(totals, first_work, works):
@@ -580,17 +583,35 @@
     return [place(slot) for slot in range(half)], [place(slot) for slot in range(half, 2 * half)]
 
 
-def reduce_bricks(parts, orders):
-    parts = [list(pair) for pair in parts]
-    for level in range(len(orders[0])):
-        arrived = [
-            swap(gone, "wide", order[level]) for (_, gone), order in zip(parts, orders)
-        ]
-        for pair, more in zip(parts, arrived):
-            total = (pair[0].astype(F32) + more.astype(F32)).astype(BF16)
-            half = total.shape[0] // 2
-            pair[0], pair[1] = total[:half] if half else total, total[half:]
-    return [pair[0] if pair[0].shape[0] else pair[1] for pair in parts]
+def reduce_level(stays, goes, bit, with_it=None):
+    arrived = [swap(array, "wide", bit) for array in reversed(goes)][::-1]
+    if with_it is not None:
+        arrived, with_it = lax.optimization_barrier((arrived, with_it))
+    sums = [
+        (here.astype(F32) + more.astype(F32)).astype(BF16) for here, more in zip(stays, arrived)
+    ]
+    return sums, with_it
+
+
+def next_level(sums):
+    if len(sums) == 1:
+        half = sums[0].shape[0] // 2
+        return [sums[0][:half]], [sums[0][half:]]
+    return sums[:1], sums[1:]
+
+
+def reduce_both(outer, middle, orders):
+    levels = len(orders[0])
+    for level in range(levels):
+        if level > 0:
+            middle_sums, _ = reduce_level(*middle, orders[1][level - 1])
+            middle = next_level(middle_sums)
+        if level > 1:
+            outer_sums, middle = reduce_level(*outer, orders[0][level], middle)
+        else:
+            outer_sums, _ = reduce_level(*outer, orders[0][level])
+        outer = next_level(outer_sums)
+    return outer_sums[0][0], reduce_level(*middle, orders[1][-1])[0][0][0]
 
 
 def per_device(voxels, w_qkv, w_out, w_feature, conv_first, conv_second, row_brick, cell_place):
@@ -618,26 +639,27 @@
     states, done = earlier_state(totals, direct, [work(n) for n in range(len(spans))])
     own, weights = done[0][:-1], done[0][-1]
     qs, parts = ([piece[i] for piece in done[1:]] for i in range(2))
-    normed = own_share(narrow_count, states[0], qs, parts)
+    own = own_share(narrow_count, states[0], weights, qs, parts, own)
 
     bits = list(range(wide_count.bit_length() - 1))
     orders = [bits, bits[1::-1] + bits[2:]]
-    sides = [split_order(order) for order in orders]
+    halves = lambda places: (places[: len(places) // 2], places[len(places) // 2 :])
+    stay, go = zip(*(map(halves, split_order(order)) for order in orders))
     cell_rows = cell_place.reshape(-1, 1, ROW)
     most = max(2, 2 * (tokens // ROW) // wide_count)
     bricks = row_brick[:, 0]
-    features, outer_goes = voxel_features(
-        spans, bricks, qs, parts, normed, own, states[1:], weights, cell_rows, sides[0][1], wide_count, most
-    )
-    (middle_goes,) = pool(bricks, cell_rows, features, [(sides[1][1], True)], wide_count, most)
-    outer_stays, middle_stays = pool(
-        bricks, cell_rows, features, [(sides[0][0], False), (sides[1][0], True)], wide_count, most
-    )
-    outer, middle = reduce_bricks(
-        [(outer_stays, outer_goes), (middle_stays, middle_goes)], orders
+    features, outer_first = voxel_features(
+        spans, bricks, qs, parts, own, states[1:], weights, cell_rows, go[0][1], wide_count, most
+    )
+    pooled = lambda *chosen: pool(bricks, cell_rows, features, chosen, wide_count, most)
+    (middle_first,) = pooled((go[1][1], True))
+    outer_later, middle_later = pooled((go[0][0], False), (go[1][0], True))
+    sums = pooled(*((stay[middle][n], middle == 1) for middle in range(2) for n in range(2)))
+    outer, middle = reduce_both(
+        (sums[:2], [outer_later, outer_first]), (sums[2:], [middle_later, middle_first]), orders
     )
     outer, middle = (part.reshape(-1, BY, channels) for part in (outer, middle))
-    above, below = exchange_lines(outer)
+    above, below, middle = exchange_lines(outer, middle)
     lines = jnp.concatenate([above, outer[:2], middle, outer[2:], below], axis=0)
     left, right = side_columns(lines)
     return field_flow(lines, left, right, conv_first, conv_second)

time: 55.6 us -> 54.9 us (0.987)
  waiting for transfers between devices: 20.6 us -> 14.7 us
  starting transfers between devices: 15.5 us -> 20 us
  Pallas kernels: 18.6 us -> 19.4 us
    ppermute x2, waiting for transfers between devices: 3.88 us -> 0.53 us  [exchange_lines(): got.append(lax.ppermute(out, ('group', 'wide', 'narrow'), pairs))]
    ppermute x7 -> x9, starting transfers between devices: 6.17 us -> 9.32 us  [swap(): return lax.ppermute(array, axis, [(i, i ^ 1 << bit) for i in range(count)])]
    ppermute x7 -> x9, waiting for transfers between devices: 13.1 us -> 10.7 us  [swap(): return lax.ppermute(array, axis, [(i, i ^ 1 << bit) for i in range(count)])]
    ppermute x2, starting transfers between devices: 1.56 us -> 2.93 us  [exchange_lines(): got.append(lax.ppermute(out, ('group', 'wide', 'narrow'), pairs))]
    pallas_call x2 -> x3, Pallas kernels: 2.04 us -> 2.91 us  [pool(): pl.pallas_call(functools.partial(pool_kernel, chosen), in_specs=[smem, vm...]
  transfers between devices with their start and end apart: 15 -> 17, of which waited for: 11 -> 11; matrix products, arithmetic and copies ran while one was open for 1% -> 0% of each run, Pallas kernels for 16% -> 18%
where the time goes in v5:
time: 54.9 us; the launch traced here: 54.7 us
  starting transfers between devices  20 us (36%)
  Pallas kernels  19.4 us (35%)
  waiting for transfers between devices  14.7 us (27%)
    ppermute x9, waiting for transfers between devices, swap(): return lax.ppermute(array, axis, [(i, i ^ 1 << bit) for i in range(count)])  10.7 us
    ppermute x9, starting transfers between devices, swap(): return lax.ppermute(array, axis, [(i, i ^ 1 << bit) for i in range(count)])  9.32 us
    ppermute x4, starting transfers between devices, swap_digit(): return lax.ppermute(array, axis, [(i, i ^ by << bit) for i in range(count)])  7.17 us
    pallas_call x2, Pallas kernels, local_attention(): pl.pallas_call(functools.partial(local_kernel, first, count), in_specs=[v...  5.03 us
    pallas_call x1, Pallas kernels, key_value(): pl.pallas_call(functools.partial(key_value_kernel, spans), in_specs=[hbm,...  4.96 us
    ppermute x4, waiting for transfers between devices, swap_digit(): return lax.ppermute(array, axis, [(i, i ^ by << bit) for i in range(count)])  3.28 us
    ppermute x2, starting transfers between devices, exchange_lines(): got.append(lax.ppermute(out, ('group', 'wide', 'narrow'), pairs))  2.93 us
    pallas_call x3, Pallas kernels, pool(): pl.pallas_call(functools.partial(pool_kernel, chosen), in_specs=[smem, vm...  2.91 us
  transfers between devices with their start and end apart: 17, of which 11 were waited for; matrix products, arithmetic and copies ran while one was open for 0% of the time, Pallas kernels for 18%

profile of v5, /device:TPU:0, one launch (start us, length us, event | category | flops | bytes accessed | tf_op | source)
XLA Modules:
  0.0 54.7 jit_solution(17239905051506441673)
XLA Ops:
  0.0 5.0 %key_value.1 = (bf16[1024,512]{1,0:T(8,128)(2,1)S(1)}, bf16[1024,512]{1,0:T(8,128)(2,1)S(1)}, bf16[1024,512]{1,0:T(8,128)(2,1)S(1)}, bf16[1024,512]{1,0:T(8,128)...) custom-call(bf16[2048,512]{1,0:T(8,128)(2,1)} %x_ref.1, ...), custom_call_target="tpu_custom_call" | custom-call | tf_op jit(solution)/shard_map/key_value/pallas_call | solution.py:113
  5.0 0.5 collective-permute-start
  5.5 0.8 %direct_features.1 = (f32[1024,256]{1,0:T(8,128)S(1)}, f32[1024,256]{1,0:T(8,128)S(1)}, bf16[512,256]{1,0:T(8,128)(2,1)S(1)}) custom-call(bf16[1024,512]{1,0:T(8,128)(2,1)S(1)} %get-tuple-element.66.refs_0_.x_ref, bf16[1024,512]{1,0:T(8,128)(2,1)S(1)} %get-tuple-element.67.refs_1_.x_ref, bf16[512,512]{1,0:T(8,128)(2,1)S(1)} %copy-done.2, ...), custom_call_target="tpu_custom_call" | custom-call | flops 671088640 | bytes 4194304 | tf_op jit(solution)/shard_map/direct_features/pallas_call | solution.py:181
  6.3 0.0 collective-permute-done.refs_1_.refs_2_
  6.4 2.9 %collective-permute-start.1 = (bf16[2,128,128]{2,1,0:T(8,128)(2,1)S(1)}, bf16[2,128,128]{2,1,0:T(8,128)(2,1)S(1)}, u32[]{:S(2)}, u32[]{:S(2)}) collective-permute-start(bf16[2,128,128]{2,1,0:T(8,128)(2,1)S(1)} %get-tuple-element.80), channel_id=1, source_target_pairs={{0,2},{2,0},{4,6},{6,4},{8,10},{10,8},{12,14},{14,12},{1,3},{3,1},... | collective-permute-start | bytes 196616 | tf_op jit(solution)/shard_map/ppermute | solution.py:480
  9.4 1.6 %collective-permute-start.2 = (bf16[2,128,128]{2,1,0:T(8,128)(2,1)S(1)}, bf16[2,128,128]{2,1,0:T(8,128)(2,1)S(1)}, u32[]{:S(2)}, u32[]{:S(2)}) collective-permute-start(bf16[2,128,128]{2,1,0:T(8,128)(2,1)S(1)} %get-tuple-element.80), channel_id=1, source_target_pairs={{0,4},{2,6},{4,0},{6,2},{8,12},{10,14},{12,8},{14,10},{1,5},{3,7},... | collective-permute-start | bytes 196616 | tf_op jit(solution)/shard_map/ppermute | solution.py:480
  10.9 2.5 %local_attention.2 = (bf16[1024,512]{1,0:T(8,128)(2,1)S(1)}, f32[1024,512]{1,0:T(8,128)S(1)}) custom-call(bf16[1024,512]{1,0:T(8,128)(2,1)S(1)} %get-tuple-element.66.refs_0_.x_ref, bf16[512,512]{1,0:T(8,128)(2,1)S(1)} %get-tuple-element.63.wq_ref, bf16[1024,512]{1,0:T(8,128)(2,1)S(1)} %get-tuple-element.75.k_ref, ...), custom_call_target="tpu_custom_call" | custom-call | flops 1207959552 | bytes 6291456 | tf_op jit(solution)/shard_map/local_attention/pallas_call | solution.py:151
  13.5 0.0 collective-permute-done.1.refs_0_
  13.5 0.7 %collective-permute-done.2.refs_1_ = bf16[2,128,128]{2,1,0:T(8,128)(2,1)S(1)} collective-permute-done((bf16[2,128,128]{2,1,0:T(8,128)(2,1)S(1)}, bf16[2,128,128]{2,1,0:T(8,128)(2,1)S(1)}, u32[]{:S(2)}, u32[]{:S(2)}) %collective-permute-start.2) | collective-permute-done | bytes 65568 | tf_op jit(solution)/shard_map/ppermute | solution.py:480
  14.2 1.9 %collective-permute-done.3.refs_2_ = bf16[2,128,128]{2,1,0:T(8,128)(2,1)S(1)} collective-permute-done((bf16[2,128,128]{2,1,0:T(8,128)(2,1)S(1)}, bf16[2,128,128]{2,1,0:T(8,128)(2,1)S(1)}, u32[]{:S(2)}, u32[]{:S(2)}) %collective-permute-start.3) | collective-permute-done | bytes 65568 | tf_op jit(solution)/shard_map/ppermute | solution.py:480
  16.1 0.1 scan.1
  16.2 2.6 %collective-permute-start.4 = (bf16[2,128,128]{2,1,0:T(8,128)(2,1)S(1)}, bf16[2,128,128]{2,1,0:T(8,128)(2,1)S(1)}, u32[]{:S(2)}, u32[]{:S(2)}) collective-permute-start(bf16[2,128,128]{2,1,0:T(8,128)(2,1)S(1)} %get-tuple-element.92), channel_id=1, source_target_pairs={{0,8},{2,10},{4,12},{6,14},{8,0},{10,2},{12,4},{14,6},{1,9},{3,11}... | collective-permute-start | bytes 196616 | tf_op jit(solution)/shard_map/ppermute | solution.py:480
  18.8 2.5 %local_attention.3 = (bf16[1024,512]{1,0:T(8,128)(2,1)S(1)}, f32[1024,512]{1,0:T(8,128)S(1)}) custom-call(bf16[1024,512]{1,0:T(8,128)(2,1)S(1)} %get-tuple-element.67.refs_1_.x_ref, bf16[512,512]{1,0:T(8,128)(2,1)S(1)} %get-tuple-element.63.wq_ref, bf16[1024,512]{1,0:T(8,128)(2,1)S(1)} %get-tuple-element.88.k_ref, ...), custom_call_target="tpu_custom_call" | custom-call | flops 1207959552 | bytes 6291456 | tf_op jit(solution)/shard_map/local_attention/pallas_call | solution.py:151
  21.4 0.7 %collective-permute-done.4.refs_0_ = bf16[2,128,128]{2,1,0:T(8,128)(2,1)S(1)} collective-permute-done((bf16[2,128,128]{2,1,0:T(8,128)(2,1)S(1)}, bf16[2,128,128]{2,1,0:T(8,128)(2,1)S(1)}, u32[]{:S(2)}, u32[]{:S(2)}) %collective-permute-start.4) | collective-permute-done | bytes 65568 | tf_op jit(solution)/shard_map/ppermute | solution.py:480
  22.0 0.1 spread.1
  22.1 0.1 collective-permute-start.5
  22.2 0.0 copy-start.4
  22.2 0.0 copy-start.5
  22.2 1.1 %own_share.1 = (f32[1024,256]{1,0:T(8,128)S(1)}, f32[1024,256]{1,0:T(8,128)S(1)}) custom-call(bf16[2,128,128]{2,1,0:T(8,128)(2,1)S(1)} %get-tuple-element.98.state_ref, bf16[512,256]{1,0:T(8,128)(2,1)S(1)} %get-tuple-element.99.w_ref.refs_7_, bf16[1024,512]{1,0:T(8,128)(2,1)S(1)} %get-tuple-element.81.refs_0_, ...), custom_call_target="tpu_custom_call" | custom-call | flops 805306368 | bytes 4194304 | tf_op jit(solution)/shard_map/own_share/pallas_call | solution.py:287
  23.3 0.1 collective-permute-done.5.refs_6_
  23.4 1.9 %voxel_features.1 = (bf16[2048,256]{1,0:T(8,128)(2,1)S(1)}, bf16[2,128,256]{2,1,0:T(8,128)(2,1)S(1)}) custom-call(s32[16]{0:T(128)S(1)} %bitcast.9, bf16[1024,512]{1,0:T(8,128)(2,1)S(1)} %get-tuple-element.81.refs_0_, bf16[1024,512]{1,0:T(8,128)(2,1)S(1)} %get-tuple-element.93.refs_1_, f32[1024,512]{1,0:T(8,128)S(1)} %get-tuple-element.94.refs_2_, ...), custom_call_target="tpu_custom_call" | custom-call | tf_op jit(solution)/shard_map/voxel_features/pallas_call | solution.py:376
  25.4 0.7 %collective-permute-start.7 = (bf16[2,128,256]{2,1,0:T(8,128)(2,1)S(1)}, bf16[2,128,256]{2,1,0:T(8,128)(2,1)S(1)}, u32[]{:S(2)}, u32[]{:S(2)}) collective-permute-start(bf16[2,128,256]{2,1,0:T(8,128)(2,1)S(1)} %get-tuple-element.109), channel_id=1, source_target_pairs={{0,2},{2,0},{4,6},{6,4},{8,10},{10,8},{12,14},{14,12},{1,3},{3,1},... | collective-permute-start | bytes 393224 | tf_op jit(solution)/shard_map/ppermute | solution.py:475
  26.0 0.9 %pool.5 = bf16[2,128,256]{2,1,0:T(8,128)(2,1)S(1)} custom-call(s32[16]{0:T(128)S(1)} %bitcast.10, s32[16,1,128]{2,1,0:T(1,128)S(1)} %bitcast.6, bf16[2048,256]{1,0:T(8,128)(2,1)S(1)} %get-tuple-element.105.features_ref), custom_call_target="tpu_custom_call" | custom-call | flops 67108864 | bytes 1048576 | tf_op jit(solution)/shard_map/pool/pallas_call | solution.py:407
  26.9 0.5 collective-permute-start.11
  27.5 0.9 %pool.4 = (bf16[2,128,256]{2,1,0:T(8,128)(2,1)S(1)}, bf16[2,128,256]{2,1,0:T(8,128)(2,1)S(1)}) custom-call(s32[16]{0:T(128)S(1)} %bitcast.11, s32[16,1,128]{2,1,0:T(1,128)S(1)} %bitcast.7, bf16[2048,256]{1,0:T(8,128)(2,1)S(1)} %get-tuple-element.105.features_ref), custom_call_target="tpu_custom_call" | custom-call | flops 134217728 | bytes 1048576 | tf_op jit(solution)/shard_map/pool/pallas_call | solution.py:407
  28.4 1.6 %collective-permute-start.10 = (bf16[2,128,256]{2,1,0:T(8,128)(2,1)S(1)}, bf16[2,128,256]{2,1,0:T(8,128)(2,1)S(1)}, u32[]{:S(2)}, u32[]{:S(2)}) collective-permute-start(bf16[2,128,256]{2,1,0:T(8,128)(2,1)S(1)} %get-tuple-element.111), channel_id=1, source_target_pairs={{0,4},{2,6},{4,0},{6,2},{8,12},{10,14},{12,8},{14,10},{1,5},{3,7},... | collective-permute-start | bytes 393224 | tf_op jit(solution)/shard_map/ppermute | solution.py:475
  30.1 1.4 %collective-permute-start.6 = (bf16[2,128,256]{2,1,0:T(8,128)(2,1)S(1)}, bf16[2,128,256]{2,1,0:T(8,128)(2,1)S(1)}, u32[]{:S(2)}, u32[]{:S(2)}) collective-permute-start(bf16[2,128,256]{2,1,0:T(8,128)(2,1)S(1)} %get-tuple-element.107), channel_id=1, source_target_pairs={{0,2},{2,0},{4,6},{6,4},{8,10},{10,8},{12,14},{14,12},{1,3},{3,1},... | collective-permute-start | bytes 393224 | tf_op jit(solution)/shard_map/ppermute | solution.py:475
  31.5 1.1 %pool.3 = (bf16[2,128,256]{2,1,0:T(8,128)(2,1)S(1)}, bf16[2,128,256]{2,1,0:T(8,128)(2,1)S(1)}, bf16[2,128,256]{2,1,0:T(8,128)(2,1)S(1)}, bf16[2,128,256]{2,1,0:T(8,128)(2,1)S(1)}) custom-call(s32[16]{0:T(128)S(1)} %bitcast.12, s32[16,1,128]{2,1,0:T(1,128)S(1)} %bitcast.8, bf16[2048,256]{1,0:T(8,128)(2,1)S(1)} %get-tuple-element.105.features_ref), custom_call_target="tpu_custom_call" | custom-call | flops 268435456 | bytes 1048576 | tf_op jit(solution)/shard_map/pool/pallas_call | solution.py:407
  32.6 0.0 collective-permute-done.7
  32.6 0.2 collective-permute-start.8
  32.8 0.6 %collective-permute-done.11 = bf16[2,128,256]{2,1,0:T(8,128)(2,1)S(1)} collective-permute-done((bf16[2,128,256]{2,1,0:T(8,128)(2,1)S(1)}, bf16[2,128,256]{2,1,0:T(8,128)(2,1)S(1)}, u32[]{:S(2)}, u32[]{:S(2)}) %collective-permute-start.11) | collective-permute-done | bytes 131104 | tf_op jit(solution)/shard_map/ppermute | solution.py:475
  33.4 1.5 %collective-permute-start.12 = (bf16[2,128,256]{2,1,0:T(8,128)(2,1)S(1)}, bf16[2,128,256]{2,1,0:T(8,128)(2,1)S(1)}, u32[]{:S(2)}, u32[]{:S(2)}) collective-permute-start(bf16[2,128,256]{2,1,0:T(8,128)(2,1)S(1)} %add_convert_fusion.1), channel_id=1, source_target_pairs={{0,2},{2,0},{4,6},{6,4},{8,10},{10,8},{12,14},{14,12},{1,3},{3,1},... | collective-permute-start | bytes 393224 | tf_op jit(solution)/shard_map/ppermute | solution.py:475
  34.8 0.4 collective-permute-done.6
  35.3 2.9 %collective-permute-done.8 = bf16[2,128,256]{2,1,0:T(8,128)(2,1)S(1)} collective-permute-done((bf16[2,128,256]{2,1,0:T(8,128)(2,1)S(1)}, bf16[2,128,256]{2,1,0:T(8,128)(2,1)S(1)}, u32[]{:S(2)}, u32[]{:S(2)}) %collective-permute-start.8) | collective-permute-done | bytes 131104 | tf_op jit(solution)/shard_map/ppermute | solution.py:475
  38.2 0.1 add_convert_fusion.3
  38.2 2.0 %collective-permute-start.9 = (bf16[1,128,256]{2,1,0:T(8,128)(2,1)S(1)}, bf16[1,128,256]{2,1,0:T(8,128)(2,1)S(1)}, u32[]{:S(2)}, u32[]{:S(2)}) collective-permute-start(bf16[1,128,256]{2,1,0:T(8,128)(2,1)S(1)} %slice.45), channel_id=1, source_target_pairs={{0,8},{2,10},{4,12},{6,14},{8,0},{10,2},{12,4},{14,6},{1,9},{3,11}... | collective-permute-start | bytes 196616 | tf_op jit(solution)/shard_map/ppermute | solution.py:475
  40.3 0.0 collective-permute-done.10
  40.3 0.0 collective-permute-done.12
  40.3 0.1 add_convert_fusion
  40.4 3.8 %collective-permute-done.9 = bf16[1,128,256]{2,1,0:T(8,128)(2,1)S(1)} collective-permute-done((bf16[1,128,256]{2,1,0:T(8,128)(2,1)S(1)}, bf16[1,128,256]{2,1,0:T(8,128)(2,1)S(1)}, u32[]{:S(2)}, u32[]{:S(2)}) %collective-permute-start.9) | collective-permute-done | bytes 65568 | tf_op jit(solution)/shard_map/ppermute | solution.py:475
  44.2 1.3 %collective-permute-start.15 = (bf16[1,128,256]{2,1,0:T(8,128)(2,1)S(1)}, bf16[1,128,256]{2,1,0:T(8,128)(2,1)S(1)}, u32[]{:S(2)}, u32[]{:S(2)}) collective-permute-start(bf16[1,128,256]{2,1,0:T(8,128)(2,1)S(1)} %get-tuple-element.115), channel_id=1, source_target_pairs={{0,8},{2,10},{4,12},{6,14},{8,0},{10,2},{12,4},{14,6},{1,9},{3,11}... | collective-permute-start | bytes 196616 | tf_op jit(solution)/shard_map/ppermute | solution.py:475
  45.6 1.4 %collective-permute-start.13 = (bf16[2,32,256]{2,1,0:T(8,128)(2,1)S(1)}, bf16[2,32,256]{2,1,0:T(8,128)(2,1)S(1)}, u32[]{:S(2)}, u32[]{:S(2)}) collective-permute-start(bf16[2,32,256]{2,1,0:T(8,128)(2,1)S(1)} %get-tuple-element.122), channel_id=1, source_target_pairs={{0,2},{1,3},{2,0},{3,1},{4,6},{5,7},{6,4},{7,5},{8,10},{9,11},{10,... | collective-permute-start | bytes 98312 | tf_op jit(solution)/shard_map/ppermute | solution.py:520
  47.0 1.5 %collective-permute-start.14 = (bf16[2,32,256]{2,1,0:T(8,128)(2,1)S(1)}, bf16[2,32,256]{2,1,0:T(8,128)(2,1)S(1)}, u32[]{:S(2)}, u32[]{:S(2)}) collective-permute-start(bf16[2,32,256]{2,1,0:T(8,128)(2,1)S(1)} %get-tuple-element.121), channel_id=1, source_target_pairs={{0,16},{1,17},{2,4},{3,5},{4,2},{5,3},{6,8},{7,9},{8,6},{9,7},{10,... | collective-permute-start | bytes 98312 | tf_op jit(solution)/shard_map/ppermute | solution.py:520
  48.5 1.9 %collective-permute-done.15 = bf16[1,128,256]{2,1,0:T(8,128)(2,1)S(1)} collective-permute-done((bf16[1,128,256]{2,1,0:T(8,128)(2,1)S(1)}, bf16[1,128,256]{2,1,0:T(8,128)(2,1)S(1)}, u32[]{:S(2)}, u32[]{:S(2)}) %collective-permute-start.15) | collective-permute-done | bytes 65568 | tf_op jit(solution)/shard_map/ppermute | solution.py:475
  50.4 0.5 collective-permute-done.14
  51.0 0.1 collective-permute-start.16
  51.1 1.2 %collective-permute-done.16 = bf16[12,2,256]{2,1,0:T(2,128)(2,1)S(1)} collective-permute-done((bf16[12,2,256]{2,1,0:T(2,128)(2,1)S(1)}, bf16[12,2,256]{2,1,0:T(2,128)(2,1)S(1)}, u32[]{:S(2)}, u32[]{:S(2)}) %collective-permute-start.16) | collective-permute-done | bytes 12320 | tf_op jit(solution)/shard_map/ppermute | solution.py:475
  52.3 2.4 %field_flow.1 = f32[8,32,256]{2,1,0:T(8,128)} custom-call(bf16[12,32,256]{2,1,0:T(8,128)(2,1)S(1)} %select_dynamic-update-slice_fusion.lines_ref, bf16[13,16,256]{2,1,0:T(8,128)(2,1)S(1)} %pad_add_fusion.sides_ref, bf16[3,3,256,256]{3,2,1,0:T(8,128)(2,1)S(1)} %copy-done, bf16[3,3,256,256]{3,2,1,0:T(8,128)(2,1)S(1)} %copy-done.1), custom_call_target="tpu_custom_call" | custom-call | tf_op jit(solution)/shard_map/field_flow/pallas_call | solution.py:462
  (30 shorter events, 0.3 us)
Async XLA Ops:
  0.0 5.5 %copy-start.2 = (bf16[512,512]{1,0:T(8,128)(2,1)S(1)}, bf16[512,512]{1,0:T(8,128)(2,1)}, u32[]{:S(2)}) copy-start(bf16[512,512]{1,0:T(8,128)(2,1)} %refs_2_.1) | copy-start | bytes 1572868
  0.0 5.5 %copy-start.3 = (bf16[512,256]{1,0:T(8,128)(2,1)S(1)}, bf16[512,256]{1,0:T(8,128)(2,1)}, u32[]{:S(2)}) copy-start(bf16[512,256]{1,0:T(8,128)(2,1)} %refs_3_.1) | copy-start | bytes 786436
  5.0 1.4 %collective-permute-start = (bf16[2,128,128]{2,1,0:T(8,128)(2,1)S(1)}, bf16[2,128,128]{2,1,0:T(8,128)(2,1)S(1)}, u32[]{:S(2)}, u32[]{:S(2)}) collective-permute-start(bf16[2,128,128]{2,1,0:T(8,128)(2,1)S(1)} %get-tuple-element.71), channel_id=1, source_target_pairs={{0,1},{1,0},{2,3},{3,2},{4,5},{5,4},{6,7},{7,6},{8,9},{9,8},{10,11... | collective-permute-start | bytes 196616 | tf_op jit(solution)/shard_map/ppermute | solution.py:492
  6.4 7.0 %collective-permute-start.1 = (bf16[2,128,128]{2,1,0:T(8,128)(2,1)S(1)}, bf16[2,128,128]{2,1,0:T(8,128)(2,1)S(1)}, u32[]{:S(2)}, u32[]{:S(2)}) collective-permute-start(bf16[2,128,128]{2,1,0:T(8,128)(2,1)S(1)} %get-tuple-element.80), channel_id=1, source_target_pairs={{0,2},{2,0},{4,6},{6,4},{8,10},{10,8},{12,14},{14,12},{1,3},{3,1},... | collective-permute-start | bytes 196616 | tf_op jit(solution)/shard_map/ppermute | solution.py:480
  9.4 4.8 %collective-permute-start.2 = (bf16[2,128,128]{2,1,0:T(8,128)(2,1)S(1)}, bf16[2,128,128]{2,1,0:T(8,128)(2,1)S(1)}, u32[]{:S(2)}, u32[]{:S(2)}) collective-permute-start(bf16[2,128,128]{2,1,0:T(8,128)(2,1)S(1)} %get-tuple-element.80), channel_id=1, source_target_pairs={{0,4},{2,6},{4,0},{6,2},{8,12},{10,14},{12,8},{14,10},{1,5},{3,7},... | collective-permute-start | bytes 196616 | tf_op jit(solution)/shard_map/ppermute | solution.py:480
  10.9 5.2 %collective-permute-start.3 = (bf16[2,128,128]{2,1,0:T(8,128)(2,1)S(1)}, bf16[2,128,128]{2,1,0:T(8,128)(2,1)S(1)}, u32[]{:S(2)}, u32[]{:S(2)}) collective-permute-start(bf16[2,128,128]{2,1,0:T(8,128)(2,1)S(1)} %get-tuple-element.80), channel_id=1, source_target_pairs={{0,6},{2,4},{4,2},{6,0},{8,14},{10,12},{12,10},{14,8},{1,7},{3,5},... | collective-permute-start | bytes 196616 | tf_op jit(solution)/shard_map/ppermute | solution.py:480
  16.2 5.8 %collective-permute-start.4 = (bf16[2,128,128]{2,1,0:T(8,128)(2,1)S(1)}, bf16[2,128,128]{2,1,0:T(8,128)(2,1)S(1)}, u32[]{:S(2)}, u32[]{:S(2)}) collective-permute-start(bf16[2,128,128]{2,1,0:T(8,128)(2,1)S(1)} %get-tuple-element.92), channel_id=1, source_target_pairs={{0,8},{2,10},{4,12},{6,14},{8,0},{10,2},{12,4},{14,6},{1,9},{3,11}... | collective-permute-start | bytes 196616 | tf_op jit(solution)/shard_map/ppermute | solution.py:480
  22.1 1.3 %collective-permute-start.5 = (bf16[2,128,128]{2,1,0:T(8,128)(2,1)S(1)}, bf16[2,128,128]{2,1,0:T(8,128)(2,1)S(1)}, u32[]{:S(2)}, u32[]{:S(2)}) collective-permute-start(bf16[2,128,128]{2,1,0:T(8,128)(2,1)S(1)} %get-tuple-element.104), channel_id=1, source_target_pairs={{0,1},{1,0},{2,3},{3,2},{4,5},{5,4},{6,7},{7,6},{8,9},{9,8},{10,11... | collective-permute-start | bytes 196616 | tf_op jit(solution)/shard_map/ppermute | solution.py:492
  22.2 1.2 %copy-start.4 = (s32[2048]{0:T(1024)S(1)}, s32[2048]{0:T(1024)}, u32[]{:S(2)}) copy-start(s32[2048]{0:T(1024)} %param.15) | copy-start | bytes 24580
  22.2 1.2 %copy-start.5 = (s32[16,1]{0,1:T(1,128)S(1)}, s32[16,1]{0,1:T(1,128)}, u32[]{:S(2)}) copy-start(s32[16,1]{0,1:T(1,128)} %param.14) | copy-start | bytes 196
  25.4 7.2 %collective-permute-start.7 = (bf16[2,128,256]{2,1,0:T(8,128)(2,1)S(1)}, bf16[2,128,256]{2,1,0:T(8,128)(2,1)S(1)}, u32[]{:S(2)}, u32[]{:S(2)}) collective-permute-start(bf16[2,128,256]{2,1,0:T(8,128)(2,1)S(1)} %get-tuple-element.109), channel_id=1, source_target_pairs={{0,2},{2,0},{4,6},{6,4},{8,10},{10,8},{12,14},{14,12},{1,3},{3,1},... | collective-permute-start | bytes 393224 | tf_op jit(solution)/shard_map/ppermute | solution.py:475
  26.9 6.4 %collective-permute-start.11 = (bf16[2,128,256]{2,1,0:T(8,128)(2,1)S(1)}, bf16[2,128,256]{2,1,0:T(8,128)(2,1)S(1)}, u32[]{:S(2)}, u32[]{:S(2)}) collective-permute-start(bf16[2,128,256]{2,1,0:T(8,128)(2,1)S(1)} %pool.5), channel_id=1, source_target_pairs={{0,4},{2,6},{4,0},{6,2},{8,12},{10,14},{12,8},{14,10},{1,5},{3,7},... | collective-permute-start | bytes 393224 | tf_op jit(solution)/shard_map/ppermute | solution.py:475
  28.4 11.9 %collective-permute-start.10 = (bf16[2,128,256]{2,1,0:T(8,128)(2,1)S(1)}, bf16[2,128,256]{2,1,0:T(8,128)(2,1)S(1)}, u32[]{:S(2)}, u32[]{:S(2)}) collective-permute-start(bf16[2,128,256]{2,1,0:T(8,128)(2,1)S(1)} %get-tuple-element.111), channel_id=1, source_target_pairs={{0,4},{2,6},{4,0},{6,2},{8,12},{10,14},{12,8},{14,10},{1,5},{3,7},... | collective-permute-start | bytes 393224 | tf_op jit(solution)/shard_map/ppermute | solution.py:475
  30.1 22.3 %copy-start = (bf16[3,3,256,256]{3,2,1,0:T(8,128)(2,1)S(1)}, bf16[3,3,256,256]{3,2,1,0:T(8,128)(2,1)}, u32[]{:S(2)}) copy-start(bf16[3,3,256,256]{3,2,1,0:T(8,128)(2,1)} %w1_ref.1) | copy-start | bytes 3538948
  30.1 22.3 %copy-start.1 = (bf16[3,3,256,256]{3,2,1,0:T(8,128)(2,1)S(1)}, bf16[3,3,256,256]{3,2,1,0:T(8,128)(2,1)}, u32[]{:S(2)}) copy-start(bf16[3,3,256,256]{3,2,1,0:T(8,128)(2,1)} %w2_ref.1) | copy-start | bytes 3538948
  30.1 5.2 %collective-permute-start.6 = (bf16[2,128,256]{2,1,0:T(8,128)(2,1)S(1)}, bf16[2,128,256]{2,1,0:T(8,128)(2,1)S(1)}, u32[]{:S(2)}, u32[]{:S(2)}) collective-permute-start(bf16[2,128,256]{2,1,0:T(8,128)(2,1)S(1)} %get-tuple-element.107), channel_id=1, source_target_pairs={{0,2},{2,0},{4,6},{6,4},{8,10},{10,8},{12,14},{14,12},{1,3},{3,1},... | collective-permute-start | bytes 393224 | tf_op jit(solution)/shard_map/ppermute | solution.py:475
  32.6 5.6 %collective-permute-start.8 = (bf16[2,128,256]{2,1,0:T(8,128)(2,1)S(1)}, bf16[2,128,256]{2,1,0:T(8,128)(2,1)S(1)}, u32[]{:S(2)}, u32[]{:S(2)}) collective-permute-start(bf16[2,128,256]{2,1,0:T(8,128)(2,1)S(1)} %add_convert_fusion.4), channel_id=1, source_target_pairs={{0,4},{2,6},{4,0},{6,2},{8,12},{10,14},{12,8},{14,10},{1,5},{3,7},... | collective-permute-start | bytes 393224 | tf_op jit(solution)/shard_map/ppermute | solution.py:475
  33.4 6.9 %collective-permute-start.12 = (bf16[2,128,256]{2,1,0:T(8,128)(2,1)S(1)}, bf16[2,128,256]{2,1,0:T(8,128)(2,1)S(1)}, u32[]{:S(2)}, u32[]{:S(2)}) collective-permute-start(bf16[2,128,256]{2,1,0:T(8,128)(2,1)S(1)} %add_convert_fusion.1), channel_id=1, source_target_pairs={{0,2},{2,0},{4,6},{6,4},{8,10},{10,8},{12,14},{14,12},{1,3},{3,1},... | collective-permute-start | bytes 393224 | tf_op jit(solution)/shard_map/ppermute | solution.py:475
  38.2 5.9 %collective-permute-start.9 = (bf16[1,128,256]{2,1,0:T(8,128)(2,1)S(1)}, bf16[1,128,256]{2,1,0:T(8,128)(2,1)S(1)}, u32[]{:S(2)}, u32[]{:S(2)}) collective-permute-start(bf16[1,128,256]{2,1,0:T(8,128)(2,1)S(1)} %slice.45), channel_id=1, source_target_pairs={{0,8},{2,10},{4,12},{6,14},{8,0},{10,2},{12,4},{14,6},{1,9},{3,11}... | collective-permute-start | bytes 196616 | tf_op jit(solution)/shard_map/ppermute | solution.py:475
  44.2 6.2 %collective-permute-start.15 = (bf16[1,128,256]{2,1,0:T(8,128)(2,1)S(1)}, bf16[1,128,256]{2,1,0:T(8,128)(2,1)S(1)}, u32[]{:S(2)}, u32[]{:S(2)}) collective-permute-start(bf16[1,128,256]{2,1,0:T(8,128)(2,1)S(1)} %get-tuple-element.115), channel_id=1, source_target_pairs={{0,8},{2,10},{4,12},{6,14},{8,0},{10,2},{12,4},{14,6},{1,9},{3,11}... | collective-permute-start | bytes 196616 | tf_op jit(solution)/shard_map/ppermute | solution.py:475
  45.6 4.8 %collective-permute-start.13 = (bf16[2,32,256]{2,1,0:T(8,128)(2,1)S(1)}, bf16[2,32,256]{2,1,0:T(8,128)(2,1)S(1)}, u32[]{:S(2)}, u32[]{:S(2)}) collective-permute-start(bf16[2,32,256]{2,1,0:T(8,128)(2,1)S(1)} %get-tuple-element.122), channel_id=1, source_target_pairs={{0,2},{1,3},{2,0},{3,1},{4,6},{5,7},{6,4},{7,5},{8,10},{9,11},{10,... | collective-permute-start | bytes 98312 | tf_op jit(solution)/shard_map/ppermute | solution.py:520
  47.0 3.9 %collective-permute-start.14 = (bf16[2,32,256]{2,1,0:T(8,128)(2,1)S(1)}, bf16[2,32,256]{2,1,0:T(8,128)(2,1)S(1)}, u32[]{:S(2)}, u32[]{:S(2)}) collective-permute-start(bf16[2,32,256]{2,1,0:T(8,128)(2,1)S(1)} %get-tuple-element.121), channel_id=1, source_target_pairs={{0,16},{1,17},{2,4},{3,5},{4,2},{5,3},{6,8},{7,9},{8,6},{9,7},{10,... | collective-permute-start | bytes 98312 | tf_op jit(solution)/shard_map/ppermute | solution.py:520
  51.0 1.2 %collective-permute-start.16 = (bf16[12,2,256]{2,1,0:T(2,128)(2,1)S(1)}, bf16[12,2,256]{2,1,0:T(2,128)(2,1)S(1)}, u32[]{:S(2)}, u32[]{:S(2)}) collective-permute-start(bf16[12,2,256]{2,1,0:T(2,128)(2,1)S(1)} %broadcast_select_fusion.4), channel_id=1, source_target_pairs={{0,1},{1,0},{2,3},{3,2},{4,5},{5,4},{6,7},{7,6},{8,9},{9,8},{10,11... | collective-permute-start | bytes 36872 | tf_op jit(solution)/shard_map/ppermute | solution.py:475

commit v6 on v5

--- a/solution.py
+++ b/solution.py
@@ -602,10 +602,14 @@
 
 def reduce_both(outer, middle, orders):
     levels = len(orders[0])
-    for level in range(levels):
-        if level > 0:
-            middle_sums, _ = reduce_level(*middle, orders[1][level - 1])
-            middle = next_level(middle_sums)
+    outer_sums, _ = reduce_level(*outer, orders[0][0])
+    stays, (later, first) = middle
+    later, outer_sums[-1] = lax.optimization_barrier((later, outer_sums[-1]))
+    middle = stays, [later, first]
+    outer = next_level(outer_sums)
+    for level in range(1, levels):
+        middle_sums, _ = reduce_level(*middle, orders[1][level - 1])
+        middle = next_level(middle_sums)
         if level > 1:
             outer_sums, middle = reduce_level(*outer, orders[0][level], middle)
         else:
@@ -652,9 +656,12 @@
         spans, bricks, qs, parts, own, states[1:], weights, cell_rows, go[0][1], wide_count, most
     )
     pooled = lambda *chosen: pool(bricks, cell_rows, features, chosen, wide_count, most)
-    (middle_first,) = pooled((go[1][1], True))
-    outer_later, middle_later = pooled((go[0][0], False), (go[1][0], True))
-    sums = pooled(*((stay[middle][n], middle == 1) for middle in range(2) for n in range(2)))
+    middle_first, outer_later, middle_later, *sums = pooled(
+        (go[1][1], True),
+        (go[0][0], False),
+        (go[1][0], True),
+        *((stay[middle][n], middle == 1) for middle in range(2) for n in range(2)),
+    )
     outer, middle = reduce_both(
         (sums[:2], [outer_later, outer_first]), (sums[2:], [middle_later, middle_first]), orders
     )

time: 54.9 us -> 53.5 us (0.974)
  starting transfers between devices: 20 us -> 16.6 us
  waiting for transfers between devices: 14.7 us -> 17.9 us
  Pallas kernels: 19.4 us -> 17.7 us
    ppermute x9, waiting for transfers between devices: 10.7 us -> 13.9 us  [swap(): return lax.ppermute(array, axis, [(i, i ^ 1 << bit) for i in range(count)])]
    ppermute x9, starting transfers between devices: 9.32 us -> 6.25 us  [swap(): return lax.ppermute(array, axis, [(i, i ^ 1 << bit) for i in range(count)])]
    pallas_call x3 -> x1, Pallas kernels: 2.91 us -> 1.29 us  [pool(): pl.pallas_call(functools.partial(pool_kernel, chosen), in_specs=[smem, vm...]
  transfers between devices with their start and end apart: 17 -> 17, of which waited for: 11 -> 12; matrix products, arithmetic and copies ran while one was open for 0% -> 0% of each run, Pallas kernels for 18% -> 16%
where the time goes in v6:
time: 53.5 us; the launch traced here: 52.9 us
  waiting for transfers between devices  17.9 us (33%)
  Pallas kernels  17.7 us (33%)
  starting transfers between devices  16.6 us (31%)
    ppermute x9, waiting for transfers between devices, swap(): return lax.ppermute(array, axis, [(i, i ^ 1 << bit) for i in range(count)])  13.9 us
    ppermute x4, starting transfers between devices, swap_digit(): return lax.ppermute(array, axis, [(i, i ^ by << bit) for i in range(count)])  7.17 us
    ppermute x9, starting transfers between devices, swap(): return lax.ppermute(array, axis, [(i, i ^ 1 << bit) for i in range(count)])  6.25 us
    pallas_call x2, Pallas kernels, local_attention(): pl.pallas_call(functools.partial(local_kernel, first, count), in_specs=[v...  5.03 us
    pallas_call x1, Pallas kernels, key_value(): pl.pallas_call(functools.partial(key_value_kernel, spans), in_specs=[hbm,...  4.96 us
    ppermute x4, waiting for transfers between devices, swap_digit(): return lax.ppermute(array, axis, [(i, i ^ by << bit) for i in range(count)])  3.28 us
    ppermute x2, starting transfers between devices, exchange_lines(): got.append(lax.ppermute(out, ('group', 'wide', 'narrow'), pairs))  2.57 us
    pallas_call x1, Pallas kernels, field_flow(): pl.pallas_call(field_kernel, in_specs=[vmem] * 4, out_specs=vmem, out_sha...  2.38 us
  transfers between devices with their start and end apart: 17, of which 12 were waited for; matrix products, arithmetic and copies ran while one was open for 0% of the time, Pallas kernels for 16%

profile of v6, /device:TPU:0, one launch (start us, length us, event | category | flops | bytes accessed | tf_op | source)
XLA Modules:
  0.0 52.9 jit_solution(5345961864299576864)
XLA Ops:
  0.0 5.0 %key_value.1 = (bf16[1024,512]{1,0:T(8,128)(2,1)S(1)}, bf16[1024,512]{1,0:T(8,128)(2,1)S(1)}, bf16[1024,512]{1,0:T(8,128)(2,1)S(1)}, bf16[1024,512]{1,0:T(8,128)...) custom-call(bf16[2048,512]{1,0:T(8,128)(2,1)} %x_ref.1, ...), custom_call_target="tpu_custom_call" | custom-call | tf_op jit(solution)/shard_map/key_value/pallas_call | solution.py:113
  5.0 0.5 collective-permute-start
  5.5 0.8 %direct_features.1 = (f32[1024,256]{1,0:T(8,128)S(1)}, f32[1024,256]{1,0:T(8,128)S(1)}, bf16[512,256]{1,0:T(8,128)(2,1)S(1)}) custom-call(bf16[1024,512]{1,0:T(8,128)(2,1)S(1)} %get-tuple-element.69.refs_0_.x_ref, bf16[1024,512]{1,0:T(8,128)(2,1)S(1)} %get-tuple-element.70.refs_1_.x_ref, bf16[512,512]{1,0:T(8,128)(2,1)S(1)} %copy-done.2, ...), custom_call_target="tpu_custom_call" | custom-call | flops 671088640 | bytes 4194304 | tf_op jit(solution)/shard_map/direct_features/pallas_call | solution.py:181
  6.3 0.0 collective-permute-done.refs_1_.refs_2_
  6.4 2.9 %collective-permute-start.1 = (bf16[2,128,128]{2,1,0:T(8,128)(2,1)S(1)}, bf16[2,128,128]{2,1,0:T(8,128)(2,1)S(1)}, u32[]{:S(2)}, u32[]{:S(2)}) collective-permute-start(bf16[2,128,128]{2,1,0:T(8,128)(2,1)S(1)} %get-tuple-element.83), channel_id=1, source_target_pairs={{0,2},{2,0},{4,6},{6,4},{8,10},{10,8},{12,14},{14,12},{1,3},{3,1},... | collective-permute-start | bytes 196616 | tf_op jit(solution)/shard_map/ppermute | solution.py:480
  9.4 1.6 %collective-permute-start.2 = (bf16[2,128,128]{2,1,0:T(8,128)(2,1)S(1)}, bf16[2,128,128]{2,1,0:T(8,128)(2,1)S(1)}, u32[]{:S(2)}, u32[]{:S(2)}) collective-permute-start(bf16[2,128,128]{2,1,0:T(8,128)(2,1)S(1)} %get-tuple-element.83), channel_id=1, source_target_pairs={{0,4},{2,6},{4,0},{6,2},{8,12},{10,14},{12,8},{14,10},{1,5},{3,7},... | collective-permute-start | bytes 196616 | tf_op jit(solution)/shard_map/ppermute | solution.py:480
  10.9 0.0 collective-permute-start.3
  10.9 2.5 %local_attention.2 = (bf16[1024,512]{1,0:T(8,128)(2,1)S(1)}, f32[1024,512]{1,0:T(8,128)S(1)}) custom-call(bf16[1024,512]{1,0:T(8,128)(2,1)S(1)} %get-tuple-element.69.refs_0_.x_ref, bf16[512,512]{1,0:T(8,128)(2,1)S(1)} %get-tuple-element.66.wq_ref, bf16[1024,512]{1,0:T(8,128)(2,1)S(1)} %get-tuple-element.78.k_ref, ...), custom_call_target="tpu_custom_call" | custom-call | flops 1207959552 | bytes 6291456 | tf_op jit(solution)/shard_map/local_attention/pallas_call | solution.py:151
  13.5 0.0 collective-permute-done.1.refs_0_
  13.5 0.7 %collective-permute-done.2.refs_1_ = bf16[2,128,128]{2,1,0:T(8,128)(2,1)S(1)} collective-permute-done((bf16[2,128,128]{2,1,0:T(8,128)(2,1)S(1)}, bf16[2,128,128]{2,1,0:T(8,128)(2,1)S(1)}, u32[]{:S(2)}, u32[]{:S(2)}) %collective-permute-start.2) | collective-permute-done | bytes 65568 | tf_op jit(solution)/shard_map/ppermute | solution.py:480
  14.2 1.9 %collective-permute-done.3.refs_2_ = bf16[2,128,128]{2,1,0:T(8,128)(2,1)S(1)} collective-permute-done((bf16[2,128,128]{2,1,0:T(8,128)(2,1)S(1)}, bf16[2,128,128]{2,1,0:T(8,128)(2,1)S(1)}, u32[]{:S(2)}, u32[]{:S(2)}) %collective-permute-start.3) | collective-permute-done | bytes 65568 | tf_op jit(solution)/shard_map/ppermute | solution.py:480
  16.1 0.1 scan.1
  16.2 2.6 %collective-permute-start.4 = (bf16[2,128,128]{2,1,0:T(8,128)(2,1)S(1)}, bf16[2,128,128]{2,1,0:T(8,128)(2,1)S(1)}, u32[]{:S(2)}, u32[]{:S(2)}) collective-permute-start(bf16[2,128,128]{2,1,0:T(8,128)(2,1)S(1)} %get-tuple-element.95), channel_id=1, source_target_pairs={{0,8},{2,10},{4,12},{6,14},{8,0},{10,2},{12,4},{14,6},{1,9},{3,11}... | collective-permute-start | bytes 196616 | tf_op jit(solution)/shard_map/ppermute | solution.py:480
  18.8 2.5 %local_attention.3 = (bf16[1024,512]{1,0:T(8,128)(2,1)S(1)}, f32[1024,512]{1,0:T(8,128)S(1)}) custom-call(bf16[1024,512]{1,0:T(8,128)(2,1)S(1)} %get-tuple-element.70.refs_1_.x_ref, bf16[512,512]{1,0:T(8,128)(2,1)S(1)} %get-tuple-element.66.wq_ref, bf16[1024,512]{1,0:T(8,128)(2,1)S(1)} %get-tuple-element.91.k_ref, ...), custom_call_target="tpu_custom_call" | custom-call | flops 1207959552 | bytes 6291456 | tf_op jit(solution)/shard_map/local_attention/pallas_call | solution.py:151
  21.4 0.7 %collective-permute-done.4.refs_0_ = bf16[2,128,128]{2,1,0:T(8,128)(2,1)S(1)} collective-permute-done((bf16[2,128,128]{2,1,0:T(8,128)(2,1)S(1)}, bf16[2,128,128]{2,1,0:T(8,128)(2,1)S(1)}, u32[]{:S(2)}, u32[]{:S(2)}) %collective-permute-start.4) | collective-permute-done | bytes 65568 | tf_op jit(solution)/shard_map/ppermute | solution.py:480
  22.0 0.1 spread.1
  22.1 0.1 collective-permute-start.5
  22.2 0.0 copy-start.4
  22.2 0.0 copy-start.5
  22.2 1.1 %own_share.1 = (f32[1024,256]{1,0:T(8,128)S(1)}, f32[1024,256]{1,0:T(8,128)S(1)}) custom-call(bf16[2,128,128]{2,1,0:T(8,128)(2,1)S(1)} %get-tuple-element.101.state_ref, bf16[512,256]{1,0:T(8,128)(2,1)S(1)} %get-tuple-element.102.w_ref.refs_7_, bf16[1024,512]{1,0:T(8,128)(2,1)S(1)} %get-tuple-element.84.refs_0_, ...), custom_call_target="tpu_custom_call" | custom-call | flops 805306368 | bytes 4194304 | tf_op jit(solution)/shard_map/own_share/pallas_call | solution.py:287
  23.3 0.1 collective-permute-done.5.refs_6_
  23.4 1.9 %voxel_features.1 = (bf16[2048,256]{1,0:T(8,128)(2,1)S(1)}, bf16[2,128,256]{2,1,0:T(8,128)(2,1)S(1)}) custom-call(s32[16]{0:T(128)S(1)} %bitcast.7, bf16[1024,512]{1,0:T(8,128)(2,1)S(1)} %get-tuple-element.84.refs_0_, bf16[1024,512]{1,0:T(8,128)(2,1)S(1)} %get-tuple-element.96.refs_1_, f32[1024,512]{1,0:T(8,128)S(1)} %get-tuple-element.97.refs_2_, ...), custom_call_target="tpu_custom_call" | custom-call | tf_op jit(solution)/shard_map/voxel_features/pallas_call | solution.py:376
  25.4 0.7 %collective-permute-start.7 = (bf16[2,128,256]{2,1,0:T(8,128)(2,1)S(1)}, bf16[2,128,256]{2,1,0:T(8,128)(2,1)S(1)}, u32[]{:S(2)}, u32[]{:S(2)}) collective-permute-start(bf16[2,128,256]{2,1,0:T(8,128)(2,1)S(1)} %get-tuple-element.113), channel_id=1, source_target_pairs={{0,2},{2,0},{4,6},{6,4},{8,10},{10,8},{12,14},{14,12},{1,3},{3,1},... | collective-permute-start | bytes 393224 | tf_op jit(solution)/shard_map/ppermute | solution.py:475
  26.0 1.3 %pool.1 = (bf16[2,128,256]{2,1,0:T(8,128)(2,1)S(1)}, bf16[2,128,256]{2,1,0:T(8,128)(2,1)S(1)}, bf16[2,128,256]{2,1,0:T(8,128)(2,1)S(1)}, bf16[2,128,256]{2,1,0:T...) custom-call(s32[16]{0:T(128)S(1)} %bitcast.8, ...), custom_call_target="tpu_custom_call" | custom-call | flops 469762048 | bytes 1048576 | tf_op jit(solution)/shard_map/pool/pallas_call | solution.py:407
  27.3 0.0 copy-start
  27.4 0.0 copy-start.1
  27.4 0.5 %collective-permute-start.11 = (bf16[2,128,256]{2,1,0:T(8,128)(2,1)S(1)}, bf16[2,128,256]{2,1,0:T(8,128)(2,1)S(1)}, u32[]{:S(2)}, u32[]{:S(2)}) collective-permute-start(bf16[2,128,256]{2,1,0:T(8,128)(2,1)S(1)} %get-tuple-element.118), channel_id=1, source_target_pairs={{0,4},{2,6},{4,0},{6,2},{8,12},{10,14},{12,8},{14,10},{1,5},{3,7},... | collective-permute-start | bytes 393224 | tf_op jit(solution)/shard_map/ppermute | solution.py:475
  27.9 1.0 %collective-permute-start.6 = (bf16[2,128,256]{2,1,0:T(8,128)(2,1)S(1)}, bf16[2,128,256]{2,1,0:T(8,128)(2,1)S(1)}, u32[]{:S(2)}, u32[]{:S(2)}) collective-permute-start(bf16[2,128,256]{2,1,0:T(8,128)(2,1)S(1)} %get-tuple-element.110), channel_id=1, source_target_pairs={{0,2},{2,0},{4,6},{6,4},{8,10},{10,8},{12,14},{14,12},{1,3},{3,1},... | collective-permute-start | bytes 393224 | tf_op jit(solution)/shard_map/ppermute | solution.py:475
  28.9 2.8 %collective-permute-done.7 = bf16[2,128,256]{2,1,0:T(8,128)(2,1)S(1)} collective-permute-done((bf16[2,128,256]{2,1,0:T(8,128)(2,1)S(1)}, bf16[2,128,256]{2,1,0:T(8,128)(2,1)S(1)}, u32[]{:S(2)}, u32[]{:S(2)}) %collective-permute-start.7) | collective-permute-done | bytes 131104 | tf_op jit(solution)/shard_map/ppermute | solution.py:475
  31.8 0.1 collective-permute-start.8
  31.8 1.1 %collective-permute-done.11 = bf16[2,128,256]{2,1,0:T(8,128)(2,1)S(1)} collective-permute-done((bf16[2,128,256]{2,1,0:T(8,128)(2,1)S(1)}, bf16[2,128,256]{2,1,0:T(8,128)(2,1)S(1)}, u32[]{:S(2)}, u32[]{:S(2)}) %collective-permute-start.11) | collective-permute-done | bytes 131104 | tf_op jit(solution)/shard_map/ppermute | solution.py:475
  33.0 1.6 %collective-permute-start.12 = (bf16[2,128,256]{2,1,0:T(8,128)(2,1)S(1)}, bf16[2,128,256]{2,1,0:T(8,128)(2,1)S(1)}, u32[]{:S(2)}, u32[]{:S(2)}) collective-permute-start(bf16[2,128,256]{2,1,0:T(8,128)(2,1)S(1)} %add_convert_fusion.1), channel_id=1, source_target_pairs={{0,2},{2,0},{4,6},{6,4},{8,10},{10,8},{12,14},{14,12},{1,3},{3,1},... | collective-permute-start | bytes 393224 | tf_op jit(solution)/shard_map/ppermute | solution.py:475
  34.6 0.2 collective-permute-start.10
  34.8 2.7 %collective-permute-done.8 = bf16[2,128,256]{2,1,0:T(8,128)(2,1)S(1)} collective-permute-done((bf16[2,128,256]{2,1,0:T(8,128)(2,1)S(1)}, bf16[2,128,256]{2,1,0:T(8,128)(2,1)S(1)}, u32[]{:S(2)}, u32[]{:S(2)}) %collective-permute-start.8) | collective-permute-done | bytes 131104 | tf_op jit(solution)/shard_map/ppermute | solution.py:475
  37.5 0.1 add_convert_fusion.3
  37.6 1.2 %collective-permute-start.9 = (bf16[1,128,256]{2,1,0:T(8,128)(2,1)S(1)}, bf16[1,128,256]{2,1,0:T(8,128)(2,1)S(1)}, u32[]{:S(2)}, u32[]{:S(2)}) collective-permute-start(bf16[1,128,256]{2,1,0:T(8,128)(2,1)S(1)} %slice.45), channel_id=1, source_target_pairs={{0,8},{2,10},{4,12},{6,14},{8,0},{10,2},{12,4},{14,6},{1,9},{3,11}... | collective-permute-start | bytes 196616 | tf_op jit(solution)/shard_map/ppermute | solution.py:475
  38.8 1.6 %collective-permute-done.10 = bf16[2,128,256]{2,1,0:T(8,128)(2,1)S(1)} collective-permute-done((bf16[2,128,256]{2,1,0:T(8,128)(2,1)S(1)}, bf16[2,128,256]{2,1,0:T(8,128)(2,1)S(1)}, u32[]{:S(2)}, u32[]{:S(2)}) %collective-permute-start.10) | collective-permute-done | bytes 131104 | tf_op jit(solution)/shard_map/ppermute | solution.py:475
  40.3 0.1 add_convert_fusion
  40.4 2.7 %collective-permute-done.9 = bf16[1,128,256]{2,1,0:T(8,128)(2,1)S(1)} collective-permute-done((bf16[1,128,256]{2,1,0:T(8,128)(2,1)S(1)}, bf16[1,128,256]{2,1,0:T(8,128)(2,1)S(1)}, u32[]{:S(2)}, u32[]{:S(2)}) %collective-permute-start.9) | collective-permute-done | bytes 65568 | tf_op jit(solution)/shard_map/ppermute | solution.py:475
  43.1 0.9 %collective-permute-start.15 = (bf16[1,128,256]{2,1,0:T(8,128)(2,1)S(1)}, bf16[1,128,256]{2,1,0:T(8,128)(2,1)S(1)}, u32[]{:S(2)}, u32[]{:S(2)}) collective-permute-start(bf16[1,128,256]{2,1,0:T(8,128)(2,1)S(1)} %get-tuple-element.121), channel_id=1, source_target_pairs={{0,8},{2,10},{4,12},{6,14},{8,0},{10,2},{12,4},{14,6},{1,9},{3,11}... | collective-permute-start | bytes 196616 | tf_op jit(solution)/shard_map/ppermute | solution.py:475
  44.1 1.1 %collective-permute-start.13 = (bf16[2,32,256]{2,1,0:T(8,128)(2,1)S(1)}, bf16[2,32,256]{2,1,0:T(8,128)(2,1)S(1)}, u32[]{:S(2)}, u32[]{:S(2)}) collective-permute-start(bf16[2,32,256]{2,1,0:T(8,128)(2,1)S(1)} %get-tuple-element.128), channel_id=1, source_target_pairs={{0,2},{1,3},{2,0},{3,1},{4,6},{5,7},{6,4},{7,5},{8,10},{9,11},{10,... | collective-permute-start | bytes 98312 | tf_op jit(solution)/shard_map/ppermute | solution.py:520
  45.1 1.5 %collective-permute-start.14 = (bf16[2,32,256]{2,1,0:T(8,128)(2,1)S(1)}, bf16[2,32,256]{2,1,0:T(8,128)(2,1)S(1)}, u32[]{:S(2)}, u32[]{:S(2)}) collective-permute-start(bf16[2,32,256]{2,1,0:T(8,128)(2,1)S(1)} %get-tuple-element.127), channel_id=1, source_target_pairs={{0,16},{1,17},{2,4},{3,5},{4,2},{5,3},{6,8},{7,9},{8,6},{9,7},{10,... | collective-permute-start | bytes 98312 | tf_op jit(solution)/shard_map/ppermute | solution.py:520
  46.6 1.8 %collective-permute-done.15 = bf16[1,128,256]{2,1,0:T(8,128)(2,1)S(1)} collective-permute-done((bf16[1,128,256]{2,1,0:T(8,128)(2,1)S(1)}, bf16[1,128,256]{2,1,0:T(8,128)(2,1)S(1)}, u32[]{:S(2)}, u32[]{:S(2)}) %collective-permute-start.15) | collective-permute-done | bytes 65568 | tf_op jit(solution)/shard_map/ppermute | solution.py:475
  48.5 0.0 collective-permute-done.13
  48.5 0.6 %collective-permute-done.14 = bf16[2,32,256]{2,1,0:T(8,128)(2,1)S(1)} collective-permute-done((bf16[2,32,256]{2,1,0:T(8,128)(2,1)S(1)}, bf16[2,32,256]{2,1,0:T(8,128)(2,1)S(1)}, u32[]{:S(2)}, u32[]{:S(2)}) %collective-permute-start.14) | collective-permute-done | bytes 32800 | tf_op jit(solution)/shard_map/ppermute | solution.py:520
  49.2 0.1 collective-permute-start.16
  49.3 1.2 %collective-permute-done.16 = bf16[12,2,256]{2,1,0:T(2,128)(2,1)S(1)} collective-permute-done((bf16[12,2,256]{2,1,0:T(2,128)(2,1)S(1)}, bf16[12,2,256]{2,1,0:T(2,128)(2,1)S(1)}, u32[]{:S(2)}, u32[]{:S(2)}) %collective-permute-start.16) | collective-permute-done | bytes 12320 | tf_op jit(solution)/shard_map/ppermute | solution.py:475
  50.5 2.4 %field_flow.1 = f32[8,32,256]{2,1,0:T(8,128)} custom-call(bf16[12,32,256]{2,1,0:T(8,128)(2,1)S(1)} %select_dynamic-update-slice_fusion.lines_ref, bf16[13,16,256]{2,1,0:T(8,128)(2,1)S(1)} %pad_add_fusion.sides_ref, bf16[3,3,256,256]{3,2,1,0:T(8,128)(2,1)S(1)} %copy-done, bf16[3,3,256,256]{3,2,1,0:T(8,128)(2,1)S(1)} %copy-done.1), custom_call_target="tpu_custom_call" | custom-call | tf_op jit(solution)/shard_map/field_flow/pallas_call | solution.py:462
  (28 shorter events, 0.3 us)
Async XLA Ops:
  0.0 5.5 %copy-start.2 = (bf16[512,512]{1,0:T(8,128)(2,1)S(1)}, bf16[512,512]{1,0:T(8,128)(2,1)}, u32[]{:S(2)}) copy-start(bf16[512,512]{1,0:T(8,128)(2,1)} %refs_2_.1) | copy-start | bytes 1572868
  0.0 5.5 %copy-start.3 = (bf16[512,256]{1,0:T(8,128)(2,1)S(1)}, bf16[512,256]{1,0:T(8,128)(2,1)}, u32[]{:S(2)}) copy-start(bf16[512,256]{1,0:T(8,128)(2,1)} %refs_3_.1) | copy-start | bytes 786436
  5.0 1.4 %collective-permute-start = (bf16[2,128,128]{2,1,0:T(8,128)(2,1)S(1)}, bf16[2,128,128]{2,1,0:T(8,128)(2,1)S(1)}, u32[]{:S(2)}, u32[]{:S(2)}) collective-permute-start(bf16[2,128,128]{2,1,0:T(8,128)(2,1)S(1)} %get-tuple-element.74), channel_id=1, source_target_pairs={{0,1},{1,0},{2,3},{3,2},{4,5},{5,4},{6,7},{7,6},{8,9},{9,8},{10,11... | collective-permute-start | bytes 196616 | tf_op jit(solution)/shard_map/ppermute | solution.py:492
  6.4 7.0 %collective-permute-start.1 = (bf16[2,128,128]{2,1,0:T(8,128)(2,1)S(1)}, bf16[2,128,128]{2,1,0:T(8,128)(2,1)S(1)}, u32[]{:S(2)}, u32[]{:S(2)}) collective-permute-start(bf16[2,128,128]{2,1,0:T(8,128)(2,1)S(1)} %get-tuple-element.83), channel_id=1, source_target_pairs={{0,2},{2,0},{4,6},{6,4},{8,10},{10,8},{12,14},{14,12},{1,3},{3,1},... | collective-permute-start | bytes 196616 | tf_op jit(solution)/shard_map/ppermute | solution.py:480
  9.4 4.8 %collective-permute-start.2 = (bf16[2,128,128]{2,1,0:T(8,128)(2,1)S(1)}, bf16[2,128,128]{2,1,0:T(8,128)(2,1)S(1)}, u32[]{:S(2)}, u32[]{:S(2)}) collective-permute-start(bf16[2,128,128]{2,1,0:T(8,128)(2,1)S(1)} %get-tuple-element.83), channel_id=1, source_target_pairs={{0,4},{2,6},{4,0},{6,2},{8,12},{10,14},{12,8},{14,10},{1,5},{3,7},... | collective-permute-start | bytes 196616 | tf_op jit(solution)/shard_map/ppermute | solution.py:480
  10.9 5.2 %collective-permute-start.3 = (bf16[2,128,128]{2,1,0:T(8,128)(2,1)S(1)}, bf16[2,128,128]{2,1,0:T(8,128)(2,1)S(1)}, u32[]{:S(2)}, u32[]{:S(2)}) collective-permute-start(bf16[2,128,128]{2,1,0:T(8,128)(2,1)S(1)} %get-tuple-element.83), channel_id=1, source_target_pairs={{0,6},{2,4},{4,2},{6,0},{8,14},{10,12},{12,10},{14,8},{1,7},{3,5},... | collective-permute-start | bytes 196616 | tf_op jit(solution)/shard_map/ppermute | solution.py:480
  16.2 5.8 %collective-permute-start.4 = (bf16[2,128,128]{2,1,0:T(8,128)(2,1)S(1)}, bf16[2,128,128]{2,1,0:T(8,128)(2,1)S(1)}, u32[]{:S(2)}, u32[]{:S(2)}) collective-permute-start(bf16[2,128,128]{2,1,0:T(8,128)(2,1)S(1)} %get-tuple-element.95), channel_id=1, source_target_pairs={{0,8},{2,10},{4,12},{6,14},{8,0},{10,2},{12,4},{14,6},{1,9},{3,11}... | collective-permute-start | bytes 196616 | tf_op jit(solution)/shard_map/ppermute | solution.py:480
  22.1 1.3 %collective-permute-start.5 = (bf16[2,128,128]{2,1,0:T(8,128)(2,1)S(1)}, bf16[2,128,128]{2,1,0:T(8,128)(2,1)S(1)}, u32[]{:S(2)}, u32[]{:S(2)}) collective-permute-start(bf16[2,128,128]{2,1,0:T(8,128)(2,1)S(1)} %get-tuple-element.107), channel_id=1, source_target_pairs={{0,1},{1,0},{2,3},{3,2},{4,5},{5,4},{6,7},{7,6},{8,9},{9,8},{10,11... | collective-permute-start | bytes 196616 | tf_op jit(solution)/shard_map/ppermute | solution.py:492
  22.2 1.2 %copy-start.4 = (s32[2048]{0:T(1024)S(1)}, s32[2048]{0:T(1024)}, u32[]{:S(2)}) copy-start(s32[2048]{0:T(1024)} %param.15) | copy-start | bytes 24580
  22.2 1.2 %copy-start.5 = (s32[16,1]{0,1:T(1,128)S(1)}, s32[16,1]{0,1:T(1,128)}, u32[]{:S(2)}) copy-start(s32[16,1]{0,1:T(1,128)} %param.14) | copy-start | bytes 196
  25.4 6.4 %collective-permute-start.7 = (bf16[2,128,256]{2,1,0:T(8,128)(2,1)S(1)}, bf16[2,128,256]{2,1,0:T(8,128)(2,1)S(1)}, u32[]{:S(2)}, u32[]{:S(2)}) collective-permute-start(bf16[2,128,256]{2,1,0:T(8,128)(2,1)S(1)} %get-tuple-element.113), channel_id=1, source_target_pairs={{0,2},{2,0},{4,6},{6,4},{8,10},{10,8},{12,14},{14,12},{1,3},{3,1},... | collective-permute-start | bytes 393224 | tf_op jit(solution)/shard_map/ppermute | solution.py:475
  27.3 23.1 %copy-start = (bf16[3,3,256,256]{3,2,1,0:T(8,128)(2,1)S(1)}, bf16[3,3,256,256]{3,2,1,0:T(8,128)(2,1)}, u32[]{:S(2)}) copy-start(bf16[3,3,256,256]{3,2,1,0:T(8,128)(2,1)} %w1_ref.1) | copy-start | bytes 3538948
  27.4 23.1 %copy-start.1 = (bf16[3,3,256,256]{3,2,1,0:T(8,128)(2,1)S(1)}, bf16[3,3,256,256]{3,2,1,0:T(8,128)(2,1)}, u32[]{:S(2)}) copy-start(bf16[3,3,256,256]{3,2,1,0:T(8,128)(2,1)} %w2_ref.1) | copy-start | bytes 3538948
  27.4 5.6 %collective-permute-start.11 = (bf16[2,128,256]{2,1,0:T(8,128)(2,1)S(1)}, bf16[2,128,256]{2,1,0:T(8,128)(2,1)S(1)}, u32[]{:S(2)}, u32[]{:S(2)}) collective-permute-start(bf16[2,128,256]{2,1,0:T(8,128)(2,1)S(1)} %get-tuple-element.118), channel_id=1, source_target_pairs={{0,4},{2,6},{4,0},{6,2},{8,12},{10,14},{12,8},{14,10},{1,5},{3,7},... | collective-permute-start | bytes 393224 | tf_op jit(solution)/shard_map/ppermute | solution.py:475
  27.9 6.9 %collective-permute-start.6 = (bf16[2,128,256]{2,1,0:T(8,128)(2,1)S(1)}, bf16[2,128,256]{2,1,0:T(8,128)(2,1)S(1)}, u32[]{:S(2)}, u32[]{:S(2)}) collective-permute-start(bf16[2,128,256]{2,1,0:T(8,128)(2,1)S(1)} %get-tuple-element.110), channel_id=1, source_target_pairs={{0,2},{2,0},{4,6},{6,4},{8,10},{10,8},{12,14},{14,12},{1,3},{3,1},... | collective-permute-start | bytes 393224 | tf_op jit(solution)/shard_map/ppermute | solution.py:475
  31.8 5.7 %collective-permute-start.8 = (bf16[2,128,256]{2,1,0:T(8,128)(2,1)S(1)}, bf16[2,128,256]{2,1,0:T(8,128)(2,1)S(1)}, u32[]{:S(2)}, u32[]{:S(2)}) collective-permute-start(bf16[2,128,256]{2,1,0:T(8,128)(2,1)S(1)} %add_convert_fusion.4), channel_id=1, source_target_pairs={{0,4},{2,6},{4,0},{6,2},{8,12},{10,14},{12,8},{14,10},{1,5},{3,7},... | collective-permute-start | bytes 393224 | tf_op jit(solution)/shard_map/ppermute | solution.py:475
  33.0 5.7 %collective-permute-start.12 = (bf16[2,128,256]{2,1,0:T(8,128)(2,1)S(1)}, bf16[2,128,256]{2,1,0:T(8,128)(2,1)S(1)}, u32[]{:S(2)}, u32[]{:S(2)}) collective-permute-start(bf16[2,128,256]{2,1,0:T(8,128)(2,1)S(1)} %add_convert_fusion.1), channel_id=1, source_target_pairs={{0,2},{2,0},{4,6},{6,4},{8,10},{10,8},{12,14},{14,12},{1,3},{3,1},... | collective-permute-start | bytes 393224 | tf_op jit(solution)/shard_map/ppermute | solution.py:475
  34.6 5.7 %collective-permute-start.10 = (bf16[2,128,256]{2,1,0:T(8,128)(2,1)S(1)}, bf16[2,128,256]{2,1,0:T(8,128)(2,1)S(1)}, u32[]{:S(2)}, u32[]{:S(2)}) collective-permute-start(bf16[2,128,256]{2,1,0:T(8,128)(2,1)S(1)} %get-tuple-element.116), channel_id=1, source_target_pairs={{0,4},{2,6},{4,0},{6,2},{8,12},{10,14},{12,8},{14,10},{1,5},{3,7},... | collective-permute-start | bytes 393224 | tf_op jit(solution)/shard_map/ppermute | solution.py:475
  37.6 5.5 %collective-permute-start.9 = (bf16[1,128,256]{2,1,0:T(8,128)(2,1)S(1)}, bf16[1,128,256]{2,1,0:T(8,128)(2,1)S(1)}, u32[]{:S(2)}, u32[]{:S(2)}) collective-permute-start(bf16[1,128,256]{2,1,0:T(8,128)(2,1)S(1)} %slice.45), channel_id=1, source_target_pairs={{0,8},{2,10},{4,12},{6,14},{8,0},{10,2},{12,4},{14,6},{1,9},{3,11}... | collective-permute-start | bytes 196616 | tf_op jit(solution)/shard_map/ppermute | solution.py:475
  43.1 5.3 %collective-permute-start.15 = (bf16[1,128,256]{2,1,0:T(8,128)(2,1)S(1)}, bf16[1,128,256]{2,1,0:T(8,128)(2,1)S(1)}, u32[]{:S(2)}, u32[]{:S(2)}) collective-permute-start(bf16[1,128,256]{2,1,0:T(8,128)(2,1)S(1)} %get-tuple-element.121), channel_id=1, source_target_pairs={{0,8},{2,10},{4,12},{6,14},{8,0},{10,2},{12,4},{14,6},{1,9},{3,11}... | collective-permute-start | bytes 196616 | tf_op jit(solution)/shard_map/ppermute | solution.py:475
  44.1 4.4 %collective-permute-start.13 = (bf16[2,32,256]{2,1,0:T(8,128)(2,1)S(1)}, bf16[2,32,256]{2,1,0:T(8,128)(2,1)S(1)}, u32[]{:S(2)}, u32[]{:S(2)}) collective-permute-start(bf16[2,32,256]{2,1,0:T(8,128)(2,1)S(1)} %get-tuple-element.128), channel_id=1, source_target_pairs={{0,2},{1,3},{2,0},{3,1},{4,6},{5,7},{6,4},{7,5},{8,10},{9,11},{10,... | collective-permute-start | bytes 98312 | tf_op jit(solution)/shard_map/ppermute | solution.py:520
  45.1 3.9 %collective-permute-start.14 = (bf16[2,32,256]{2,1,0:T(8,128)(2,1)S(1)}, bf16[2,32,256]{2,1,0:T(8,128)(2,1)S(1)}, u32[]{:S(2)}, u32[]{:S(2)}) collective-permute-start(bf16[2,32,256]{2,1,0:T(8,128)(2,1)S(1)} %get-tuple-element.127), channel_id=1, source_target_pairs={{0,16},{1,17},{2,4},{3,5},{4,2},{5,3},{6,8},{7,9},{8,6},{9,7},{10,... | collective-permute-start | bytes 98312 | tf_op jit(solution)/shard_map/ppermute | solution.py:520
  49.2 1.2 %collective-permute-start.16 = (bf16[12,2,256]{2,1,0:T(2,128)(2,1)S(1)}, bf16[12,2,256]{2,1,0:T(2,128)(2,1)S(1)}, u32[]{:S(2)}, u32[]{:S(2)}) collective-permute-start(bf16[12,2,256]{2,1,0:T(2,128)(2,1)S(1)} %broadcast_select_fusion.4), channel_id=1, source_target_pairs={{0,1},{1,0},{2,3},{3,2},{4,5},{5,4},{6,7},{7,6},{8,9},{9,8},{10,11... | collective-permute-start | bytes 36872 | tf_op jit(solution)/shard_map/ppermute | solution.py:475

commit v7 on v6

--- a/solution.py
+++ b/solution.py
@@ -420,41 +420,86 @@
     )(bricks, cell_rows, features)
 
 
-def field_kernel(lines_ref, sides_ref, w1_ref, w2_ref, out_ref, field):
-    lines = BX + 4
+def convolve(field, w_ref, start, count):
+    lhs = jnp.concatenate(
+        [field[start + dy * LINE : start + dy * LINE + count] for dy in (-1, 0, 1)], axis=1
+    )
+    left, middle, right = weighted(lhs, w_ref)
+    return pltpu.roll(left, 1, 0) + middle + pltpu.roll(right, count - 1, 0)
+
+
+def weighted(lhs, w_ref):
+    return [
+        dot(lhs, jnp.concatenate([w_ref[dy, dx] for dy in range(3)], axis=0)) for dx in range(3)
+    ]
+
+
+def own_columns_kernel(lines_ref, w_ref, out_ref, field):
+    lines = lines_ref.shape[0]
+    for r in range(lines):
+        field[r * LINE : r * LINE + GAP] = jnp.zeros((GAP, field.shape[1]), BF16)
+        field[r * LINE + GAP : (r + 1) * LINE] = lines_ref[r]
+    field[lines * LINE :] = jnp.zeros((GAP, field.shape[1]), BF16)
+    out_ref[...] = convolve(field, w_ref, LINE, out_ref.shape[0])
+
+
+def own_columns(lines, conv_first):
+    count, _, channels = lines.shape
+    vmem = pl.BlockSpec(memory_space=pltpu.VMEM)
+    shown = (count - 2) * LINE + GAP
+    return pl.pallas_call(
+        own_columns_kernel,
+        in_specs=[vmem] * 2,
+        out_specs=vmem,
+        out_shape=jax.ShapeDtypeStruct((shown, channels), F32),
+        scratch_shapes=[pltpu.VMEM((count * LINE + GAP, channels), BF16)],
+        compiler_params=params(16 * 1024),
+        cost_estimate=pl.CostEstimate(
+            flops=18 * shown * channels * channels,
+            bytes_accessed=shown * channels * 8,
+            transcendentals=0,
+        ),
+        name="own_columns",
+    )(lines, conv_first)
+
+
+def field_kernel(first_ref, sides_ref, w1_ref, w2_ref, out_ref, first, field):
+    count, channels = first.shape
     wide, narrow = lax.axis_index("wide"), lax.axis_index("narrow")
     first_line, last_line = wide == 0, wide == lax.axis_size("wide") - 1
     first_column, last_column = narrow == 0, narrow == lax.axis_size("narrow") - 1
-    for r in range(lines):
-        field[r * LINE : r * LINE + GAP] = sides_ref[r]
-        field[r * LINE + GAP : (r + 1) * LINE] = lines_ref[r]
-    field[lines * LINE :] = sides_ref[lines]
-
-    def convolve(w_ref, start, count):
-        lhs = jnp.concatenate(
-            [field[start + dy * LINE : start + dy * LINE + count] for dy in (-1, 0, 1)], axis=1
+    gaps = sides_ref.shape[0] - 2
+    sides = sides_ref[...].reshape((gaps + 2) * GAP, channels)
+    lhs = jnp.concatenate([sides[dy * GAP : (dy + gaps) * GAP] for dy in range(3)], axis=1)
+    none = jnp.zeros((8, channels), F32)
+    left, middle, right = [
+        jnp.concatenate(
+            [part for g in range(gaps) for part in (none, given[g * GAP : (g + 1) * GAP], none)],
+            axis=0,
         )
-        left, middle, right = [
-            dot(lhs, jnp.concatenate([w_ref[dy, dx] for dy in range(3)], axis=0))
-            for dx in range(3)
-        ]
-        return pltpu.roll(left, 1, 0) + middle + pltpu.roll(right, count - 1, 0)
-
-    count = (BX + 2) * LINE + GAP
-    inner = jax.nn.gelu(convolve(w1_ref, LINE, count), approximate=True)
+        for given in weighted(lhs, w1_ref)
+    ]
+    span = GAP + 16
+    added = pltpu.roll(left, 1, 0) + middle + pltpu.roll(right, gaps * span - 1, 0)
+    first[...] = first_ref[...]
+    for g in range(gaps):
+        start, stop = max(g * LINE - 8, 0), min(g * LINE + GAP + 8, count)
+        at = g * span + 8 - g * LINE
+        first[start:stop] += added[start + at : stop + at]
+    inner = jax.nn.gelu(first[...], approximate=True)
     at = lax.broadcasted_iota(jnp.int32, (count, 1), 0)
     outside = first_line & (at <= LINE) | last_line & (at > (BX + 1) * LINE)
     for r in range(BX + 2):
         outside |= first_column & (at == r * LINE + GAP - 1)
         outside |= last_column & (at == (r + 1) * LINE)
-    field[LINE : LINE + count] = jnp.where(outside, 0.0, inner).astype(BF16)
-    flow = convolve(w2_ref, 2 * LINE, BX * LINE + GAP)
+    field[...] = jnp.where(outside, 0.0, inner).astype(BF16)
+    flow = convolve(field, w2_ref, LINE, BX * LINE + GAP)
     for r in range(BX):
         out_ref[r] = flow[r * LINE + GAP : (r + 1) * LINE]
 
 
-def field_flow(lines, left, right, conv_first, conv_second):
-    count, _, channels = lines.shape
+def field_flow(first, left, right, conv_first, conv_second):
+    count, channels = first.shape
     vmem = pl.BlockSpec(memory_space=pltpu.VMEM)
     sides = jnp.pad(right, ((1, 0), (0, GAP - 2), (0, 0))) + jnp.pad(
         left, ((0, 1), (GAP - 2, 0), (0, 0))
@@ -464,10 +509,10 @@
         in_specs=[vmem] * 4,
         out_specs=vmem,
         out_shape=jax.ShapeDtypeStruct((BX, BY, channels), F32),
-        scratch_shapes=[pltpu.VMEM((count * LINE + GAP, channels), BF16)],
+        scratch_shapes=[pltpu.VMEM((count, channels), F32), pltpu.VMEM((count, channels), BF16)],
         compiler_params=params(16 * 1024),
         name="field_flow",
-    )(lines, sides, conv_first, conv_second)
+    )(first, sides, conv_first, conv_second)
 
 
 def swap(array, axis, bit):
@@ -669,7 +714,7 @@
     above, below, middle = exchange_lines(outer, middle)
     lines = jnp.concatenate([above, outer[:2], middle, outer[2:], below], axis=0)
     left, right = side_columns(lines)
-    return field_flow(lines, left, right, conv_first, conv_second)
+    return field_flow(own_columns(lines, conv_first), left, right, conv_first, conv_second)
 
 
 def solution(mesh):

time: 53.5 us -> 53 us (level)
  waiting for transfers between devices: 17.9 us -> 17.2 us
    pallas_call x0 -> x1, Pallas kernels: none -> 0.76 us  [own_columns(): pl.pallas_call(own_columns_kernel, in_specs=[vmem] * 2, out_specs=vmem, o...]
    ppermute x9, waiting for transfers between devices: 13.9 us -> 13.2 us  [swap(): return lax.ppermute(array, axis, [(i, i ^ 1 << bit) for i in range(count)])]
  transfers between devices with their start and end apart: 17 -> 17, of which waited for: 12 -> 12; matrix products, arithmetic and copies ran while one was open for 0% -> 0% of each run, Pallas kernels for 16% -> 17%
where the time goes in v7:
time: 53 us; the launch traced here: 52.4 us
  Pallas kernels  18.1 us (34%)
  waiting for transfers between devices  17.2 us (32%)
  starting transfers between devices  16.5 us (31%)
    ppermute x9, waiting for transfers between devices, swap(): return lax.ppermute(array, axis, [(i, i ^ 1 << bit) for i in range(count)])  13.2 us
    ppermute x4, starting transfers between devices, swap_digit(): return lax.ppermute(array, axis, [(i, i ^ by << bit) for i in range(count)])  7.17 us
    ppermute x9, starting transfers between devices, swap(): return lax.ppermute(array, axis, [(i, i ^ 1 << bit) for i in range(count)])  6.24 us
    pallas_call x2, Pallas kernels, local_attention(): pl.pallas_call(functools.partial(local_kernel, first, count), in_specs=[v...  5.03 us
    pallas_call x1, Pallas kernels, key_value(): pl.pallas_call(functools.partial(key_value_kernel, spans), in_specs=[hbm,...  4.96 us
    ppermute x4, waiting for transfers between devices, swap_digit(): return lax.ppermute(array, axis, [(i, i ^ by << bit) for i in range(count)])  3.28 us
    ppermute x2, starting transfers between devices, exchange_lines(): got.append(lax.ppermute(out, ('group', 'wide', 'narrow'), pairs))  2.5 us
    pallas_call x1, Pallas kernels, field_flow(): pl.pallas_call(field_kernel, in_specs=[vmem] * 4, out_specs=vmem, out_sha...  1.94 us
  transfers between devices with their start and end apart: 17, of which 12 were waited for; matrix products, arithmetic and copies ran while one was open for 0% of the time, Pallas kernels for 17%

profile of v7, /device:TPU:0, one launch (start us, length us, event | category | flops | bytes accessed | tf_op | source)
XLA Modules:
  0.0 52.4 jit_solution(9956631344474547789)
XLA Ops:
  0.0 5.0 %key_value.1 = (bf16[1024,512]{1,0:T(8,128)(2,1)S(1)}, bf16[1024,512]{1,0:T(8,128)(2,1)S(1)}, bf16[1024,512]{1,0:T(8,128)(2,1)S(1)}, bf16[1024,512]{1,0:T(8,128)...) custom-call(bf16[2048,512]{1,0:T(8,128)(2,1)} %x_ref.1, ...), custom_call_target="tpu_custom_call" | custom-call | tf_op jit(solution)/shard_map/key_value/pallas_call | solution.py:113
  5.0 0.5 collective-permute-start
  5.5 0.8 %direct_features.1 = (f32[1024,256]{1,0:T(8,128)S(1)}, f32[1024,256]{1,0:T(8,128)S(1)}, bf16[512,256]{1,0:T(8,128)(2,1)S(1)}) custom-call(bf16[1024,512]{1,0:T(8,128)(2,1)S(1)} %get-tuple-element.69.refs_0_.x_ref, bf16[1024,512]{1,0:T(8,128)(2,1)S(1)} %get-tuple-element.70.refs_1_.x_ref, bf16[512,512]{1,0:T(8,128)(2,1)S(1)} %copy-done.2, ...), custom_call_target="tpu_custom_call" | custom-call | flops 671088640 | bytes 4194304 | tf_op jit(solution)/shard_map/direct_features/pallas_call | solution.py:181
  6.3 0.0 collective-permute-done.refs_1_.refs_2_
  6.4 2.9 %collective-permute-start.1 = (bf16[2,128,128]{2,1,0:T(8,128)(2,1)S(1)}, bf16[2,128,128]{2,1,0:T(8,128)(2,1)S(1)}, u32[]{:S(2)}, u32[]{:S(2)}) collective-permute-start(bf16[2,128,128]{2,1,0:T(8,128)(2,1)S(1)} %get-tuple-element.83), channel_id=1, source_target_pairs={{0,2},{2,0},{4,6},{6,4},{8,10},{10,8},{12,14},{14,12},{1,3},{3,1},... | collective-permute-start | bytes 196616 | tf_op jit(solution)/shard_map/ppermute | solution.py:525
  9.4 1.6 %collective-permute-start.2 = (bf16[2,128,128]{2,1,0:T(8,128)(2,1)S(1)}, bf16[2,128,128]{2,1,0:T(8,128)(2,1)S(1)}, u32[]{:S(2)}, u32[]{:S(2)}) collective-permute-start(bf16[2,128,128]{2,1,0:T(8,128)(2,1)S(1)} %get-tuple-element.83), channel_id=1, source_target_pairs={{0,4},{2,6},{4,0},{6,2},{8,12},{10,14},{12,8},{14,10},{1,5},{3,7},... | collective-permute-start | bytes 196616 | tf_op jit(solution)/shard_map/ppermute | solution.py:525
  10.9 0.0 collective-permute-start.3
  10.9 2.5 %local_attention.2 = (bf16[1024,512]{1,0:T(8,128)(2,1)S(1)}, f32[1024,512]{1,0:T(8,128)S(1)}) custom-call(bf16[1024,512]{1,0:T(8,128)(2,1)S(1)} %get-tuple-element.69.refs_0_.x_ref, bf16[512,512]{1,0:T(8,128)(2,1)S(1)} %get-tuple-element.66.wq_ref, bf16[1024,512]{1,0:T(8,128)(2,1)S(1)} %get-tuple-element.78.k_ref, ...), custom_call_target="tpu_custom_call" | custom-call | flops 1207959552 | bytes 6291456 | tf_op jit(solution)/shard_map/local_attention/pallas_call | solution.py:151
  13.5 0.0 collective-permute-done.1.refs_0_
  13.5 0.7 %collective-permute-done.2.refs_1_ = bf16[2,128,128]{2,1,0:T(8,128)(2,1)S(1)} collective-permute-done((bf16[2,128,128]{2,1,0:T(8,128)(2,1)S(1)}, bf16[2,128,128]{2,1,0:T(8,128)(2,1)S(1)}, u32[]{:S(2)}, u32[]{:S(2)}) %collective-permute-start.2) | collective-permute-done | bytes 65568 | tf_op jit(solution)/shard_map/ppermute | solution.py:525
  14.2 1.9 %collective-permute-done.3.refs_2_ = bf16[2,128,128]{2,1,0:T(8,128)(2,1)S(1)} collective-permute-done((bf16[2,128,128]{2,1,0:T(8,128)(2,1)S(1)}, bf16[2,128,128]{2,1,0:T(8,128)(2,1)S(1)}, u32[]{:S(2)}, u32[]{:S(2)}) %collective-permute-start.3) | collective-permute-done | bytes 65568 | tf_op jit(solution)/shard_map/ppermute | solution.py:525
  16.1 0.1 scan.1
  16.2 2.6 %collective-permute-start.4 = (bf16[2,128,128]{2,1,0:T(8,128)(2,1)S(1)}, bf16[2,128,128]{2,1,0:T(8,128)(2,1)S(1)}, u32[]{:S(2)}, u32[]{:S(2)}) collective-permute-start(bf16[2,128,128]{2,1,0:T(8,128)(2,1)S(1)} %get-tuple-element.95), channel_id=1, source_target_pairs={{0,8},{2,10},{4,12},{6,14},{8,0},{10,2},{12,4},{14,6},{1,9},{3,11}... | collective-permute-start | bytes 196616 | tf_op jit(solution)/shard_map/ppermute | solution.py:525
  18.8 2.5 %local_attention.3 = (bf16[1024,512]{1,0:T(8,128)(2,1)S(1)}, f32[1024,512]{1,0:T(8,128)S(1)}) custom-call(bf16[1024,512]{1,0:T(8,128)(2,1)S(1)} %get-tuple-element.70.refs_1_.x_ref, bf16[512,512]{1,0:T(8,128)(2,1)S(1)} %get-tuple-element.66.wq_ref, bf16[1024,512]{1,0:T(8,128)(2,1)S(1)} %get-tuple-element.91.k_ref, ...), custom_call_target="tpu_custom_call" | custom-call | flops 1207959552 | bytes 6291456 | tf_op jit(solution)/shard_map/local_attention/pallas_call | solution.py:151
  21.4 0.7 %collective-permute-done.4.refs_0_ = bf16[2,128,128]{2,1,0:T(8,128)(2,1)S(1)} collective-permute-done((bf16[2,128,128]{2,1,0:T(8,128)(2,1)S(1)}, bf16[2,128,128]{2,1,0:T(8,128)(2,1)S(1)}, u32[]{:S(2)}, u32[]{:S(2)}) %collective-permute-start.4) | collective-permute-done | bytes 65568 | tf_op jit(solution)/shard_map/ppermute | solution.py:525
  22.0 0.1 spread.1
  22.1 0.1 collective-permute-start.5
  22.2 0.0 copy-start.4
  22.2 0.0 copy-start.5
  22.2 1.1 %own_share.1 = (f32[1024,256]{1,0:T(8,128)S(1)}, f32[1024,256]{1,0:T(8,128)S(1)}) custom-call(bf16[2,128,128]{2,1,0:T(8,128)(2,1)S(1)} %get-tuple-element.101.state_ref, bf16[512,256]{1,0:T(8,128)(2,1)S(1)} %get-tuple-element.102.w_ref.refs_7_, bf16[1024,512]{1,0:T(8,128)(2,1)S(1)} %get-tuple-element.84.refs_0_, ...), custom_call_target="tpu_custom_call" | custom-call | flops 805306368 | bytes 4194304 | tf_op jit(solution)/shard_map/own_share/pallas_call | solution.py:287
  23.3 0.1 collective-permute-done.5.refs_6_
  23.4 1.9 %voxel_features.1 = (bf16[2048,256]{1,0:T(8,128)(2,1)S(1)}, bf16[2,128,256]{2,1,0:T(8,128)(2,1)S(1)}) custom-call(s32[16]{0:T(128)S(1)} %bitcast.7, bf16[1024,512]{1,0:T(8,128)(2,1)S(1)} %get-tuple-element.84.refs_0_, bf16[1024,512]{1,0:T(8,128)(2,1)S(1)} %get-tuple-element.96.refs_1_, f32[1024,512]{1,0:T(8,128)S(1)} %get-tuple-element.97.refs_2_, ...), custom_call_target="tpu_custom_call" | custom-call | tf_op jit(solution)/shard_map/voxel_features/pallas_call | solution.py:376
  25.4 0.7 %collective-permute-start.7 = (bf16[2,128,256]{2,1,0:T(8,128)(2,1)S(1)}, bf16[2,128,256]{2,1,0:T(8,128)(2,1)S(1)}, u32[]{:S(2)}, u32[]{:S(2)}) collective-permute-start(bf16[2,128,256]{2,1,0:T(8,128)(2,1)S(1)} %get-tuple-element.113), channel_id=1, source_target_pairs={{0,2},{2,0},{4,6},{6,4},{8,10},{10,8},{12,14},{14,12},{1,3},{3,1},... | collective-permute-start | bytes 393224 | tf_op jit(solution)/shard_map/ppermute | solution.py:520
  26.0 1.3 %pool.1 = (bf16[2,128,256]{2,1,0:T(8,128)(2,1)S(1)}, bf16[2,128,256]{2,1,0:T(8,128)(2,1)S(1)}, bf16[2,128,256]{2,1,0:T(8,128)(2,1)S(1)}, bf16[2,128,256]{2,1,0:T...) custom-call(s32[16]{0:T(128)S(1)} %bitcast.8, ...), custom_call_target="tpu_custom_call" | custom-call | flops 469762048 | bytes 1048576 | tf_op jit(solution)/shard_map/pool/pallas_call | solution.py:407
  27.3 0.0 copy-start
  27.4 0.5 %collective-permute-start.11 = (bf16[2,128,256]{2,1,0:T(8,128)(2,1)S(1)}, bf16[2,128,256]{2,1,0:T(8,128)(2,1)S(1)}, u32[]{:S(2)}, u32[]{:S(2)}) collective-permute-start(bf16[2,128,256]{2,1,0:T(8,128)(2,1)S(1)} %get-tuple-element.118), channel_id=1, source_target_pairs={{0,4},{2,6},{4,0},{6,2},{8,12},{10,14},{12,8},{14,10},{1,5},{3,7},... | collective-permute-start | bytes 393224 | tf_op jit(solution)/shard_map/ppermute | solution.py:520
  27.9 1.0 %collective-permute-start.6 = (bf16[2,128,256]{2,1,0:T(8,128)(2,1)S(1)}, bf16[2,128,256]{2,1,0:T(8,128)(2,1)S(1)}, u32[]{:S(2)}, u32[]{:S(2)}) collective-permute-start(bf16[2,128,256]{2,1,0:T(8,128)(2,1)S(1)} %get-tuple-element.110), channel_id=1, source_target_pairs={{0,2},{2,0},{4,6},{6,4},{8,10},{10,8},{12,14},{14,12},{1,3},{3,1},... | collective-permute-start | bytes 393224 | tf_op jit(solution)/shard_map/ppermute | solution.py:520
  28.9 2.8 %collective-permute-done.7 = bf16[2,128,256]{2,1,0:T(8,128)(2,1)S(1)} collective-permute-done((bf16[2,128,256]{2,1,0:T(8,128)(2,1)S(1)}, bf16[2,128,256]{2,1,0:T(8,128)(2,1)S(1)}, u32[]{:S(2)}, u32[]{:S(2)}) %collective-permute-start.7) | collective-permute-done | bytes 131104 | tf_op jit(solution)/shard_map/ppermute | solution.py:520
  31.8 0.1 collective-permute-start.8
  31.8 1.1 %collective-permute-done.11 = bf16[2,128,256]{2,1,0:T(8,128)(2,1)S(1)} collective-permute-done((bf16[2,128,256]{2,1,0:T(8,128)(2,1)S(1)}, bf16[2,128,256]{2,1,0:T(8,128)(2,1)S(1)}, u32[]{:S(2)}, u32[]{:S(2)}) %collective-permute-start.11) | collective-permute-done | bytes 131104 | tf_op jit(solution)/shard_map/ppermute | solution.py:520
  33.0 1.6 %collective-permute-start.12 = (bf16[2,128,256]{2,1,0:T(8,128)(2,1)S(1)}, bf16[2,128,256]{2,1,0:T(8,128)(2,1)S(1)}, u32[]{:S(2)}, u32[]{:S(2)}) collective-permute-start(bf16[2,128,256]{2,1,0:T(8,128)(2,1)S(1)} %add_convert_fusion.1), channel_id=1, source_target_pairs={{0,2},{2,0},{4,6},{6,4},{8,10},{10,8},{12,14},{14,12},{1,3},{3,1},... | collective-permute-start | bytes 393224 | tf_op jit(solution)/shard_map/ppermute | solution.py:520
  34.6 0.2 collective-permute-start.10
  34.8 2.7 %collective-permute-done.8 = bf16[2,128,256]{2,1,0:T(8,128)(2,1)S(1)} collective-permute-done((bf16[2,128,256]{2,1,0:T(8,128)(2,1)S(1)}, bf16[2,128,256]{2,1,0:T(8,128)(2,1)S(1)}, u32[]{:S(2)}, u32[]{:S(2)}) %collective-permute-start.8) | collective-permute-done | bytes 131104 | tf_op jit(solution)/shard_map/ppermute | solution.py:520
  37.5 0.1 add_convert_fusion.3
  37.6 1.2 %collective-permute-start.9 = (bf16[1,128,256]{2,1,0:T(8,128)(2,1)S(1)}, bf16[1,128,256]{2,1,0:T(8,128)(2,1)S(1)}, u32[]{:S(2)}, u32[]{:S(2)}) collective-permute-start(bf16[1,128,256]{2,1,0:T(8,128)(2,1)S(1)} %slice.45), channel_id=1, source_target_pairs={{0,8},{2,10},{4,12},{6,14},{8,0},{10,2},{12,4},{14,6},{1,9},{3,11}... | collective-permute-start | bytes 196616 | tf_op jit(solution)/shard_map/ppermute | solution.py:520
  38.8 1.5 %collective-permute-done.10 = bf16[2,128,256]{2,1,0:T(8,128)(2,1)S(1)} collective-permute-done((bf16[2,128,256]{2,1,0:T(8,128)(2,1)S(1)}, bf16[2,128,256]{2,1,0:T(8,128)(2,1)S(1)}, u32[]{:S(2)}, u32[]{:S(2)}) %collective-permute-start.10) | collective-permute-done | bytes 131104 | tf_op jit(solution)/shard_map/ppermute | solution.py:520
  40.3 0.1 add_convert_fusion
  40.4 2.7 %collective-permute-done.9 = bf16[1,128,256]{2,1,0:T(8,128)(2,1)S(1)} collective-permute-done((bf16[1,128,256]{2,1,0:T(8,128)(2,1)S(1)}, bf16[1,128,256]{2,1,0:T(8,128)(2,1)S(1)}, u32[]{:S(2)}, u32[]{:S(2)}) %collective-permute-start.9) | collective-permute-done | bytes 65568 | tf_op jit(solution)/shard_map/ppermute | solution.py:520
  43.1 0.9 %collective-permute-start.15 = (bf16[1,128,256]{2,1,0:T(8,128)(2,1)S(1)}, bf16[1,128,256]{2,1,0:T(8,128)(2,1)S(1)}, u32[]{:S(2)}, u32[]{:S(2)}) collective-permute-start(bf16[1,128,256]{2,1,0:T(8,128)(2,1)S(1)} %get-tuple-element.121), channel_id=1, source_target_pairs={{0,8},{2,10},{4,12},{6,14},{8,0},{10,2},{12,4},{14,6},{1,9},{3,11}... | collective-permute-start | bytes 196616 | tf_op jit(solution)/shard_map/ppermute | solution.py:520
  44.1 1.0 %collective-permute-start.13 = (bf16[2,32,256]{2,1,0:T(8,128)(2,1)S(1)}, bf16[2,32,256]{2,1,0:T(8,128)(2,1)S(1)}, u32[]{:S(2)}, u32[]{:S(2)}) collective-permute-start(bf16[2,32,256]{2,1,0:T(8,128)(2,1)S(1)} %get-tuple-element.128), channel_id=1, source_target_pairs={{0,2},{1,3},{2,0},{3,1},{4,6},{5,7},{6,4},{7,5},{8,10},{9,11},{10,... | collective-permute-start | bytes 98312 | tf_op jit(solution)/shard_map/ppermute | solution.py:565
  45.1 1.5 %collective-permute-start.14 = (bf16[2,32,256]{2,1,0:T(8,128)(2,1)S(1)}, bf16[2,32,256]{2,1,0:T(8,128)(2,1)S(1)}, u32[]{:S(2)}, u32[]{:S(2)}) collective-permute-start(bf16[2,32,256]{2,1,0:T(8,128)(2,1)S(1)} %get-tuple-element.127), channel_id=1, source_target_pairs={{0,16},{1,17},{2,4},{3,5},{4,2},{5,3},{6,8},{7,9},{8,6},{9,7},{10,... | collective-permute-start | bytes 98312 | tf_op jit(solution)/shard_map/ppermute | solution.py:565
  46.6 1.8 %collective-permute-done.15 = bf16[1,128,256]{2,1,0:T(8,128)(2,1)S(1)} collective-permute-done((bf16[1,128,256]{2,1,0:T(8,128)(2,1)S(1)}, bf16[1,128,256]{2,1,0:T(8,128)(2,1)S(1)}, u32[]{:S(2)}, u32[]{:S(2)}) %collective-permute-start.15) | collective-permute-done | bytes 65568 | tf_op jit(solution)/shard_map/ppermute | solution.py:520
  48.4 0.0 collective-permute-done.13
  48.4 0.6 %collective-permute-done.14 = bf16[2,32,256]{2,1,0:T(8,128)(2,1)S(1)} collective-permute-done((bf16[2,32,256]{2,1,0:T(8,128)(2,1)S(1)}, bf16[2,32,256]{2,1,0:T(8,128)(2,1)S(1)}, u32[]{:S(2)}, u32[]{:S(2)}) %collective-permute-start.14) | collective-permute-done | bytes 32800 | tf_op jit(solution)/shard_map/ppermute | solution.py:565
  49.1 0.1 collective-permute-start.16
  49.2 0.8 %own_columns.1.first_ref = f32[496,256]{1,0:T(8,128)S(1)} custom-call(bf16[12,32,256]{2,1,0:T(8,128)(2,1)S(1)} %select_dynamic-update-slice_fusion.lines_ref, bf16[3,3,256,256]{3,2,1,0:T(8,128)(2,1)S(1)} %copy-done), custom_call_target="tpu_custom_call" | custom-call | flops 585105408 | bytes 1015808 | tf_op jit(solution)/shard_map/own_columns/pallas_call | solution.py:450
  50.0 0.4 collective-permute-done.16
  50.4 1.9 %field_flow.1 = f32[8,32,256]{2,1,0:T(8,128)} custom-call(f32[496,256]{1,0:T(8,128)S(1)} %own_columns.1.first_ref, bf16[13,16,256]{2,1,0:T(8,128)(2,1)S(1)} %pad_add_fusion.sides_ref, bf16[3,3,256,256]{3,2,1,0:T(8,128)(2,1)S(1)} %copy-done, bf16[3,3,256,256]{3,2,1,0:T(8,128)(2,1)S(1)} %copy-done.1), custom_call_target="tpu_custom_call" | custom-call | tf_op jit(solution)/shard_map/field_flow/pallas_call | solution.py:507
  (29 shorter events, 0.3 us)
Async XLA Ops:
  0.0 5.5 %copy-start.2 = (bf16[512,512]{1,0:T(8,128)(2,1)S(1)}, bf16[512,512]{1,0:T(8,128)(2,1)}, u32[]{:S(2)}) copy-start(bf16[512,512]{1,0:T(8,128)(2,1)} %refs_2_.1) | copy-start | bytes 1572868
  0.0 5.5 %copy-start.3 = (bf16[512,256]{1,0:T(8,128)(2,1)S(1)}, bf16[512,256]{1,0:T(8,128)(2,1)}, u32[]{:S(2)}) copy-start(bf16[512,256]{1,0:T(8,128)(2,1)} %refs_3_.1) | copy-start | bytes 786436
  5.0 1.4 %collective-permute-start = (bf16[2,128,128]{2,1,0:T(8,128)(2,1)S(1)}, bf16[2,128,128]{2,1,0:T(8,128)(2,1)S(1)}, u32[]{:S(2)}, u32[]{:S(2)}) collective-permute-start(bf16[2,128,128]{2,1,0:T(8,128)(2,1)S(1)} %get-tuple-element.74), channel_id=1, source_target_pairs={{0,1},{1,0},{2,3},{3,2},{4,5},{5,4},{6,7},{7,6},{8,9},{9,8},{10,11... | collective-permute-start | bytes 196616 | tf_op jit(solution)/shard_map/ppermute | solution.py:537
  6.4 7.0 %collective-permute-start.1 = (bf16[2,128,128]{2,1,0:T(8,128)(2,1)S(1)}, bf16[2,128,128]{2,1,0:T(8,128)(2,1)S(1)}, u32[]{:S(2)}, u32[]{:S(2)}) collective-permute-start(bf16[2,128,128]{2,1,0:T(8,128)(2,1)S(1)} %get-tuple-element.83), channel_id=1, source_target_pairs={{0,2},{2,0},{4,6},{6,4},{8,10},{10,8},{12,14},{14,12},{1,3},{3,1},... | collective-permute-start | bytes 196616 | tf_op jit(solution)/shard_map/ppermute | solution.py:525
  9.4 4.8 %collective-permute-start.2 = (bf16[2,128,128]{2,1,0:T(8,128)(2,1)S(1)}, bf16[2,128,128]{2,1,0:T(8,128)(2,1)S(1)}, u32[]{:S(2)}, u32[]{:S(2)}) collective-permute-start(bf16[2,128,128]{2,1,0:T(8,128)(2,1)S(1)} %get-tuple-element.83), channel_id=1, source_target_pairs={{0,4},{2,6},{4,0},{6,2},{8,12},{10,14},{12,8},{14,10},{1,5},{3,7},... | collective-permute-start | bytes 196616 | tf_op jit(solution)/shard_map/ppermute | solution.py:525
  10.9 5.2 %collective-permute-start.3 = (bf16[2,128,128]{2,1,0:T(8,128)(2,1)S(1)}, bf16[2,128,128]{2,1,0:T(8,128)(2,1)S(1)}, u32[]{:S(2)}, u32[]{:S(2)}) collective-permute-start(bf16[2,128,128]{2,1,0:T(8,128)(2,1)S(1)} %get-tuple-element.83), channel_id=1, source_target_pairs={{0,6},{2,4},{4,2},{6,0},{8,14},{10,12},{12,10},{14,8},{1,7},{3,5},... | collective-permute-start | bytes 196616 | tf_op jit(solution)/shard_map/ppermute | solution.py:525
  16.2 5.8 %collective-permute-start.4 = (bf16[2,128,128]{2,1,0:T(8,128)(2,1)S(1)}, bf16[2,128,128]{2,1,0:T(8,128)(2,1)S(1)}, u32[]{:S(2)}, u32[]{:S(2)}) collective-permute-start(bf16[2,128,128]{2,1,0:T(8,128)(2,1)S(1)} %get-tuple-element.95), channel_id=1, source_target_pairs={{0,8},{2,10},{4,12},{6,14},{8,0},{10,2},{12,4},{14,6},{1,9},{3,11}... | collective-permute-start | bytes 196616 | tf_op jit(solution)/shard_map/ppermute | solution.py:525
  22.1 1.3 %collective-permute-start.5 = (bf16[2,128,128]{2,1,0:T(8,128)(2,1)S(1)}, bf16[2,128,128]{2,1,0:T(8,128)(2,1)S(1)}, u32[]{:S(2)}, u32[]{:S(2)}) collective-permute-start(bf16[2,128,128]{2,1,0:T(8,128)(2,1)S(1)} %get-tuple-element.107), channel_id=1, source_target_pairs={{0,1},{1,0},{2,3},{3,2},{4,5},{5,4},{6,7},{7,6},{8,9},{9,8},{10,11... | collective-permute-start | bytes 196616 | tf_op jit(solution)/shard_map/ppermute | solution.py:537
  22.2 1.2 %copy-start.4 = (s32[2048]{0:T(1024)S(1)}, s32[2048]{0:T(1024)}, u32[]{:S(2)}) copy-start(s32[2048]{0:T(1024)} %param.15) | copy-start | bytes 24580
  22.2 1.2 %copy-start.5 = (s32[16,1]{0,1:T(1,128)S(1)}, s32[16,1]{0,1:T(1,128)}, u32[]{:S(2)}) copy-start(s32[16,1]{0,1:T(1,128)} %param.14) | copy-start | bytes 196
  25.4 6.4 %collective-permute-start.7 = (bf16[2,128,256]{2,1,0:T(8,128)(2,1)S(1)}, bf16[2,128,256]{2,1,0:T(8,128)(2,1)S(1)}, u32[]{:S(2)}, u32[]{:S(2)}) collective-permute-start(bf16[2,128,256]{2,1,0:T(8,128)(2,1)S(1)} %get-tuple-element.113), channel_id=1, source_target_pairs={{0,2},{2,0},{4,6},{6,4},{8,10},{10,8},{12,14},{14,12},{1,3},{3,1},... | collective-permute-start | bytes 393224 | tf_op jit(solution)/shard_map/ppermute | solution.py:520
  27.3 21.9 %copy-start = (bf16[3,3,256,256]{3,2,1,0:T(8,128)(2,1)S(1)}, bf16[3,3,256,256]{3,2,1,0:T(8,128)(2,1)}, u32[]{:S(2)}) copy-start(bf16[3,3,256,256]{3,2,1,0:T(8,128)(2,1)} %w1_ref.1) | copy-start | bytes 3538948
  27.4 5.6 %collective-permute-start.11 = (bf16[2,128,256]{2,1,0:T(8,128)(2,1)S(1)}, bf16[2,128,256]{2,1,0:T(8,128)(2,1)S(1)}, u32[]{:S(2)}, u32[]{:S(2)}) collective-permute-start(bf16[2,128,256]{2,1,0:T(8,128)(2,1)S(1)} %get-tuple-element.118), channel_id=1, source_target_pairs={{0,4},{2,6},{4,0},{6,2},{8,12},{10,14},{12,8},{14,10},{1,5},{3,7},... | collective-permute-start | bytes 393224 | tf_op jit(solution)/shard_map/ppermute | solution.py:520
  27.9 6.9 %collective-permute-start.6 = (bf16[2,128,256]{2,1,0:T(8,128)(2,1)S(1)}, bf16[2,128,256]{2,1,0:T(8,128)(2,1)S(1)}, u32[]{:S(2)}, u32[]{:S(2)}) collective-permute-start(bf16[2,128,256]{2,1,0:T(8,128)(2,1)S(1)} %get-tuple-element.110), channel_id=1, source_target_pairs={{0,2},{2,0},{4,6},{6,4},{8,10},{10,8},{12,14},{14,12},{1,3},{3,1},... | collective-permute-start | bytes 393224 | tf_op jit(solution)/shard_map/ppermute | solution.py:520
  31.8 5.7 %collective-permute-start.8 = (bf16[2,128,256]{2,1,0:T(8,128)(2,1)S(1)}, bf16[2,128,256]{2,1,0:T(8,128)(2,1)S(1)}, u32[]{:S(2)}, u32[]{:S(2)}) collective-permute-start(bf16[2,128,256]{2,1,0:T(8,128)(2,1)S(1)} %add_convert_fusion.4), channel_id=1, source_target_pairs={{0,4},{2,6},{4,0},{6,2},{8,12},{10,14},{12,8},{14,10},{1,5},{3,7},... | collective-permute-start | bytes 393224 | tf_op jit(solution)/shard_map/ppermute | solution.py:520
  33.0 5.8 %collective-permute-start.12 = (bf16[2,128,256]{2,1,0:T(8,128)(2,1)S(1)}, bf16[2,128,256]{2,1,0:T(8,128)(2,1)S(1)}, u32[]{:S(2)}, u32[]{:S(2)}) collective-permute-start(bf16[2,128,256]{2,1,0:T(8,128)(2,1)S(1)} %add_convert_fusion.1), channel_id=1, source_target_pairs={{0,2},{2,0},{4,6},{6,4},{8,10},{10,8},{12,14},{14,12},{1,3},{3,1},... | collective-permute-start | bytes 393224 | tf_op jit(solution)/shard_map/ppermute | solution.py:520
  34.6 5.7 %collective-permute-start.10 = (bf16[2,128,256]{2,1,0:T(8,128)(2,1)S(1)}, bf16[2,128,256]{2,1,0:T(8,128)(2,1)S(1)}, u32[]{:S(2)}, u32[]{:S(2)}) collective-permute-start(bf16[2,128,256]{2,1,0:T(8,128)(2,1)S(1)} %get-tuple-element.116), channel_id=1, source_target_pairs={{0,4},{2,6},{4,0},{6,2},{8,12},{10,14},{12,8},{14,10},{1,5},{3,7},... | collective-permute-start | bytes 393224 | tf_op jit(solution)/shard_map/ppermute | solution.py:520
  37.6 5.5 %collective-permute-start.9 = (bf16[1,128,256]{2,1,0:T(8,128)(2,1)S(1)}, bf16[1,128,256]{2,1,0:T(8,128)(2,1)S(1)}, u32[]{:S(2)}, u32[]{:S(2)}) collective-permute-start(bf16[1,128,256]{2,1,0:T(8,128)(2,1)S(1)} %slice.45), channel_id=1, source_target_pairs={{0,8},{2,10},{4,12},{6,14},{8,0},{10,2},{12,4},{14,6},{1,9},{3,11}... | collective-permute-start | bytes 196616 | tf_op jit(solution)/shard_map/ppermute | solution.py:520
  40.3 10.1 %copy-start.1 = (bf16[3,3,256,256]{3,2,1,0:T(8,128)(2,1)S(1)}, bf16[3,3,256,256]{3,2,1,0:T(8,128)(2,1)}, u32[]{:S(2)}) copy-start(bf16[3,3,256,256]{3,2,1,0:T(8,128)(2,1)} %w2_ref.1) | copy-start | bytes 3538948
  43.1 5.3 %collective-permute-start.15 = (bf16[1,128,256]{2,1,0:T(8,128)(2,1)S(1)}, bf16[1,128,256]{2,1,0:T(8,128)(2,1)S(1)}, u32[]{:S(2)}, u32[]{:S(2)}) collective-permute-start(bf16[1,128,256]{2,1,0:T(8,128)(2,1)S(1)} %get-tuple-element.121), channel_id=1, source_target_pairs={{0,8},{2,10},{4,12},{6,14},{8,0},{10,2},{12,4},{14,6},{1,9},{3,11}... | collective-permute-start | bytes 196616 | tf_op jit(solution)/shard_map/ppermute | solution.py:520
  44.1 4.4 %collective-permute-start.13 = (bf16[2,32,256]{2,1,0:T(8,128)(2,1)S(1)}, bf16[2,32,256]{2,1,0:T(8,128)(2,1)S(1)}, u32[]{:S(2)}, u32[]{:S(2)}) collective-permute-start(bf16[2,32,256]{2,1,0:T(8,128)(2,1)S(1)} %get-tuple-element.128), channel_id=1, source_target_pairs={{0,2},{1,3},{2,0},{3,1},{4,6},{5,7},{6,4},{7,5},{8,10},{9,11},{10,... | collective-permute-start | bytes 98312 | tf_op jit(solution)/shard_map/ppermute | solution.py:565
  45.1 3.9 %collective-permute-start.14 = (bf16[2,32,256]{2,1,0:T(8,128)(2,1)S(1)}, bf16[2,32,256]{2,1,0:T(8,128)(2,1)S(1)}, u32[]{:S(2)}, u32[]{:S(2)}) collective-permute-start(bf16[2,32,256]{2,1,0:T(8,128)(2,1)S(1)} %get-tuple-element.127), channel_id=1, source_target_pairs={{0,16},{1,17},{2,4},{3,5},{4,2},{5,3},{6,8},{7,9},{8,6},{9,7},{10,... | collective-permute-start | bytes 98312 | tf_op jit(solution)/shard_map/ppermute | solution.py:565
  49.1 1.2 %collective-permute-start.16 = (bf16[12,2,256]{2,1,0:T(2,128)(2,1)S(1)}, bf16[12,2,256]{2,1,0:T(2,128)(2,1)S(1)}, u32[]{:S(2)}, u32[]{:S(2)}) collective-permute-start(bf16[12,2,256]{2,1,0:T(2,128)(2,1)S(1)} %broadcast_select_fusion.4), channel_id=1, source_target_pairs={{0,1},{1,0},{2,3},{3,2},{4,5},{5,4},{6,7},{7,6},{8,9},{9,8},{10,11... | collective-permute-start | bytes 36872 | tf_op jit(solution)/shard_map/ppermute | solution.py:520

commit v8 on v7

--- a/solution.py
+++ b/solution.py
@@ -33,7 +33,7 @@
     return lax.dot_general(a, b, (((1,), (1,)), ((), ())), preferred_element_type=F32)
 
 
-KEY_VALUE_KIB = 46592
+TOTALS_KIB = 50688
 
 
 def params(kib=24 * 1024):
@@ -44,126 +44,136 @@
     return slice(h * HEAD, (h + 1) * HEAD)
 
 
-def key_value_kernel(spans, x_ref, w_ref, *refs):
+def in_two(array):
+    high = array.astype(BF16)
+    return high, (array - high.astype(F32)).astype(BF16)
+
+
+def totals_kernel(spans, x_ref, w_ref, *refs):
     refs = list(refs)
     take = lambda n: [refs.pop(0) for _ in range(n)]
-    xs, ks, vs = take(len(spans)), take(len(spans)), take(len(spans))
-    wq, before_ref = take(2)
-    totals, (w, sems) = refs[:-2], refs[-2:]
+    xs, ws = take(len(spans)), take(3)
+    totals, sems = refs[:-1], refs[-1]
     inner = HEADS * HEAD
-
-    def columns(part, target):
-        return pltpu.make_async_copy(
-            w_ref.at[:, pl.ds(part * inner, inner)], target, sems.at[len(spans) + part]
-        )
-
     loads = [
         pltpu.make_async_copy(x_ref.at[pl.ds(first * BLK, count * BLK)], x, sems.at[n])
         for n, ((first, count), x) in enumerate(zip(spans, xs))
     ]
-    w_loads = [columns(0, wq), columns(1, w.at[0]), columns(2, w.at[1])]
-    w_loads[1].start()
-    loads[0].start()
-    w_loads[2].start()
-    for load in loads[1:]:
+    w_loads = [
+        pltpu.make_async_copy(
+            w_ref.at[:, pl.ds(part * inner, inner)], w, sems.at[len(spans) + part]
+        )
+        for part, w in enumerate(ws)
+    ]
+    for load in loads + w_loads[::-1]:
         load.start()
-    w_loads[0].start()
-    running = [jnp.zeros((HEAD, HEAD), F32) for _ in range(HEADS)]
-    for n, ((first, count), x, k_ref, v_ref) in enumerate(zip(spans, xs, ks, vs)):
-        if n == 0:
-            w_loads[1].wait()
-        loads[n].wait()
-        k = dot(x[...], w[0]).astype(BF16)
-        k_ref[...] = k
-        if n == 0:
-            w_loads[2].wait()
-        v = dot(x[...], w[1]).astype(BF16)
-        v_ref[...] = v
-        for b in range(count):
-            block = slice(b * BLK, (b + 1) * BLK)
-            for h in range(HEADS):
-                before_ref[first + b, h] = running[h].astype(BF16)
-            for pair in range(HEADS // 2):
-                cols = slice(pair * 2 * HEAD, (pair + 1) * 2 * HEAD)
-                outer = dot_t(k[block, cols], v[block, cols])
-                running[2 * pair] += outer[:HEAD, :HEAD]
-                running[2 * pair + 1] += outer[HEAD:, HEAD:]
-    share = HEADS // len(totals)
-    for h in range(HEADS):
+    gram = 0.0
+    for x, load in zip(xs, loads):
+        load.wait()
+        gram = gram + dot_t(x[...], x[...])
+    w_loads[2].wait()
+    weighed = sum(dot(part, ws[2][...]) for part in in_two(gram)).astype(BF16)
+    w_loads[1].wait()
+    cores, share = len(totals), HEADS // len(totals)
+    for n in range(cores):
+        cols = slice(n * share * HEAD, (n + 1) * share * HEAD)
+        outer = dot_t(ws[1][:, cols], weighed[:, cols])
         for k, total_ref in enumerate(totals):
 
-            @pl.when((lax.axis_index("narrow") + k) % len(totals) == h // share)
-            def _(total_ref=total_ref, h=h):
-                total_ref[h % share] = running[h].astype(BF16)
+            @pl.when((lax.axis_index("narrow") + k) % cores == n)
+            def _(total_ref=total_ref, outer=outer):
+                for j in range(share):
+                    total_ref[j] = outer[head_cols(j), head_cols(j)].astype(BF16)
 
     w_loads[0].wait()
 
 
-def key_value(spans, voxels, w_qkv, cores):
-    tokens, width = voxels.shape
+def device_totals(spans, voxels, w_qkv, cores):
+    width = voxels.shape[1]
     inner = HEADS * HEAD
     hbm = pl.BlockSpec(memory_space=pl.ANY)
     vmem = pl.BlockSpec(memory_space=pltpu.VMEM)
-    rows = [count * BLK for _, count in spans]
-    out_shape = [jax.ShapeDtypeStruct((n, cols), BF16) for cols in (width, inner, inner) for n in rows]
-    out_shape.append(jax.ShapeDtypeStruct((width, inner), BF16))
-    out_shape.append(jax.ShapeDtypeStruct((tokens // BLK, HEADS, HEAD, HEAD), BF16))
+    out_shape = [jax.ShapeDtypeStruct((count * BLK, width), BF16) for _, count in spans]
+    out_shape += [jax.ShapeDtypeStruct((width, inner), BF16)] * 3
     out_shape += [jax.ShapeDtypeStruct((HEADS // cores, HEAD, HEAD), BF16)] * cores
     outs = list(
         pl.pallas_call(
-            functools.partial(key_value_kernel, spans),
+            functools.partial(totals_kernel, spans),
             in_specs=[hbm, hbm],
             out_specs=[vmem] * len(out_shape),
             out_shape=out_shape,
-            scratch_shapes=[
-                pltpu.VMEM((2, width, inner), BF16),
-                pltpu.SemaphoreType.DMA((len(spans) + 3,)),
-            ],
-            compiler_params=params(KEY_VALUE_KIB),
-            name="key_value",
+            scratch_shapes=[pltpu.SemaphoreType.DMA((len(spans) + 3,))],
+            compiler_params=params(TOTALS_KIB),
+            name="device_totals",
         )(voxels, w_qkv)
     )
     n = len(spans)
-    return outs[:n], outs[n : 2 * n], outs[2 * n : 3 * n], outs[3 * n], outs[3 * n + 1], outs[3 * n + 2 :]
-
-
-def local_kernel(first, count, x_ref, wq_ref, k_ref, v_ref, before_ref, q_ref, part_ref):
+    return outs[:n], outs[n : n + 3], outs[n + 3 :]
+
+
+PAIR = 2 * HEAD
+
+
+def local_kernel(count, starts, ends, x_ref, wq_ref, wk_ref, wv_ref, *refs):
+    refs = list(refs)
+    before_ref = None if starts else refs.pop(0)
+    q_ref, part_ref = refs[:2]
+    k, v = refs[-2:]
     causal = lax.broadcasted_iota(jnp.int32, (BLK, BLK), 0) >= lax.broadcasted_iota(
         jnp.int32, (BLK, BLK), 1
     )
+    same_head = ones_blocks(PAIR) > 0
     q = dot(x_ref[...], wq_ref[...]).astype(BF16)
     q_ref[...] = q
-    for b in range(count):
-        rows = slice(b * BLK, (b + 1) * BLK)
-        for h in range(HEADS):
-            cols = head_cols(h)
-            scores = dot_nt(q[rows, cols], k_ref[rows, cols])
-            scores = jnp.where(causal, scores, 0.0).astype(BF16)
-            part_ref[rows, cols] = dot(scores, v_ref[rows, cols]) + dot(
-                q[rows, cols], before_ref[first + b, h]
-            )
-
-
-def local_attention(x, w_q, k, v, before, first, count):
+    k[...] = dot(x_ref[...], wk_ref[...]).astype(BF16)
+    v[...] = dot(x_ref[...], wv_ref[...]).astype(BF16)
+    for pair in range(HEADS // 2):
+        both = slice(pair * PAIR, (pair + 1) * PAIR)
+        state = None if starts else before_ref[pair]
+        for b in range(count):
+            rows = slice(b * BLK, (b + 1) * BLK)
+            if state is not None:
+                carried = dot(q[rows, both], jnp.where(same_head, state, 0.0).astype(BF16))
+            for h in range(2):
+                cols = head_cols(2 * pair + h)
+                scores = dot_nt(q[rows, cols], k[rows, cols])
+                scores = jnp.where(causal, scores, 0.0).astype(BF16)
+                attended = dot(scores, v[rows, cols])
+                if state is not None:
+                    attended += carried[:, head_cols(h)]
+                part_ref[rows, cols] = attended
+            if not (ends and b == count - 1):
+                outer = dot_t(k[rows, both], v[rows, both])
+                state = outer if state is None else state + outer
+        if not ends:
+            refs[2][pair] = state
+
+
+def local_attention(x, ws, before, ends):
     rows, width = x.shape
     inner = HEADS * HEAD
     vmem = pl.BlockSpec(memory_space=pltpu.VMEM)
+    inputs = [x, *ws] + ([] if before is None else [before])
+    out_shape = [
+        jax.ShapeDtypeStruct((rows, inner), BF16),
+        jax.ShapeDtypeStruct((rows, inner), F32),
+    ]
+    if not ends:
+        out_shape.append(jax.ShapeDtypeStruct((HEADS // 2, PAIR, PAIR), F32))
     return pl.pallas_call(
-        functools.partial(local_kernel, first, count),
-        in_specs=[vmem] * 5,
-        out_specs=[vmem] * 2,
-        out_shape=[
-            jax.ShapeDtypeStruct((rows, inner), BF16),
-            jax.ShapeDtypeStruct((rows, inner), F32),
-        ],
+        functools.partial(local_kernel, rows // BLK, before is None, ends),
+        in_specs=[vmem] * len(inputs),
+        out_specs=[vmem] * len(out_shape),
+        out_shape=out_shape,
+        scratch_shapes=[pltpu.VMEM((rows, inner), BF16)] * 2,
         compiler_params=params(),
         cost_estimate=pl.CostEstimate(
-            flops=2 * rows * inner * (width + 2 * BLK + HEAD),
+            flops=2 * rows * inner * (3 * width + 2 * BLK + 2 * HEAD),
             bytes_accessed=rows * inner * 12,
             transcendentals=0,
         ),
         name="local_attention",
-    )(x, w_q, k, v, before)
+    )(*inputs)
 
 
 def direct_kernel(*refs):
@@ -672,16 +682,20 @@
     blocks = tokens // BLK
     cuts = sorted({blocks * i // 2 for i in range(3)})
     spans = [(first, last - first) for first, last in zip(cuts, cuts[1:])]
-    xs, ks, vs, w_q, before, totals = key_value(spans, voxels, w_qkv, narrow_count)
+    xs, ws, totals = device_totals(spans, voxels, w_qkv, narrow_count)
 
     def direct(arrays):
         arrays, x = lax.optimization_barrier((arrays, xs[0]))
         return direct_features([x] + xs[1:], w_out, w_feature), arrays
 
+    after = [None]
+
     def work(n):
         def run(array):
-            array, k = lax.optimization_barrier((array, ks[n]))
-            return local_attention(xs[n], w_q, k, vs[n], before, *spans[n]), array
+            array, x = lax.optimization_barrier((array, xs[n]))
+            piece = local_attention(x, ws, after[-1], n == len(spans) - 1)
+            after.append(piece[-1])
+            return piece, array
 
         return run
 

time: 53 us -> 52.6 us (level)
  waiting for transfers between devices: 17.2 us -> 13.3 us
  Pallas kernels: 18.1 us -> 19.7 us
  starting transfers between devices: 16.5 us -> 18 us
    ppermute x4, waiting for transfers between devices: 3.28 us -> 1.46 us  [swap_digit(): return lax.ppermute(array, axis, [(i, i ^ by << bit) for i in range(count)])]
    pallas_call x3, Pallas kernels: 10 us -> 11.7 us  [the longest x2 7.39 us: local_attention(): pl.pallas_call(functools.partial(local_kernel, rows // BLK, before is Non...]
    ppermute x9, starting transfers between devices: 6.24 us -> 7.79 us  [swap(): return lax.ppermute(array, axis, [(i, i ^ 1 << bit) for i in range(count)])]
    ppermute x9, waiting for transfers between devices: 13.2 us -> 11.7 us  [swap(): return lax.ppermute(array, axis, [(i, i ^ 1 << bit) for i in range(count)])]
    ppermute x2, waiting for transfers between devices: 0.57 us -> 0.02 us  [exchange_lines(): got.append(lax.ppermute(out, ('group', 'wide', 'narrow'), pairs))]
  transfers between devices with their start and end apart: 17 -> 17, of which waited for: 12 -> 9; matrix products, arithmetic and copies ran while one was open for 0% -> 0% of each run, Pallas kernels for 17% -> 22%
where the time goes in v8:
time: 52.6 us; the launch traced here: 51.7 us
  Pallas kernels  19.7 us (37%)
  starting transfers between devices  18 us (34%)
  waiting for transfers between devices  13.3 us (25%)
    ppermute x9, waiting for transfers between devices, swap(): return lax.ppermute(array, axis, [(i, i ^ 1 << bit) for i in range(count)])  11.7 us
    ppermute x9, starting transfers between devices, swap(): return lax.ppermute(array, axis, [(i, i ^ 1 << bit) for i in range(count)])  7.79 us
    pallas_call x2, Pallas kernels, local_attention(): pl.pallas_call(functools.partial(local_kernel, rows // BLK, before is Non...  7.39 us
    ppermute x4, starting transfers between devices, swap_digit(): return lax.ppermute(array, axis, [(i, i ^ by << bit) for i in range(count)])  7.16 us
    pallas_call x1, Pallas kernels, device_totals(): pl.pallas_call(functools.partial(totals_kernel, spans), in_specs=[hbm, hb...  4.27 us
    ppermute x2, starting transfers between devices, exchange_lines(): got.append(lax.ppermute(out, ('group', 'wide', 'narrow'), pairs))  2.51 us
    pallas_call x1, Pallas kernels, field_flow(): pl.pallas_call(field_kernel, in_specs=[vmem] * 4, out_specs=vmem, out_sha...  1.94 us
    pallas_call x1, Pallas kernels, voxel_features(): pl.pallas_call(functools.partial(features_kernel, chosen, spans, cores),...  1.93 us
  transfers between devices with their start and end apart: 17, of which 9 were waited for; matrix products, arithmetic and copies ran while one was open for 0% of the time, Pallas kernels for 22%

profile of v8, /device:TPU:0, one launch (start us, length us, event | category | flops | bytes accessed | tf_op | source)
XLA Modules:
  0.0 51.7 jit_solution(15118096787381943396)
XLA Ops:
  0.0 4.3 %device_totals.1 = (bf16[1024,512]{1,0:T(8,128)(2,1)S(1)}, bf16[1024,512]{1,0:T(8,128)(2,1)S(1)}, bf16[512,512]{1,0:T(8,128)(2,1)S(1)}, bf16[512,512]{1,0:T(8,12...) custom-call(bf16[2048,512]{1,0:T(8,128)(2,1)} %x_ref.1, ...), custom_call_target="tpu_custom_call" | custom-call | tf_op jit(solution)/shard_map/device_totals/pallas_call | solution.py:100
  4.3 0.5 collective-permute-start
  4.8 0.8 %direct_features.1 = (f32[1024,256]{1,0:T(8,128)S(1)}, f32[1024,256]{1,0:T(8,128)S(1)}, bf16[512,256]{1,0:T(8,128)(2,1)S(1)}) custom-call(bf16[1024,512]{1,0:T(8,128)(2,1)S(1)} %get-tuple-element.74.refs_0_.x_ref, bf16[1024,512]{1,0:T(8,128)(2,1)S(1)} %get-tuple-element.88.refs_1_.x_ref, bf16[512,512]{1,0:T(8,128)(2,1)S(1)} %copy-done.2, ...), custom_call_target="tpu_custom_call" | custom-call | flops 671088640 | bytes 4194304 | tf_op jit(solution)/shard_map/direct_features/pallas_call | solution.py:191
  5.7 0.0 collective-permute-done.refs_1_.refs_2_
  5.7 2.9 %collective-permute-start.1 = (bf16[2,128,128]{2,1,0:T(8,128)(2,1)S(1)}, bf16[2,128,128]{2,1,0:T(8,128)(2,1)S(1)}, u32[]{:S(2)}, u32[]{:S(2)}) collective-permute-start(bf16[2,128,128]{2,1,0:T(8,128)(2,1)S(1)} %get-tuple-element.81), channel_id=1, source_target_pairs={{0,2},{2,0},{4,6},{6,4},{8,10},{10,8},{12,14},{14,12},{1,3},{3,1},... | collective-permute-start | bytes 196616 | tf_op jit(solution)/shard_map/ppermute | solution.py:535
  8.7 1.6 %collective-permute-start.2 = (bf16[2,128,128]{2,1,0:T(8,128)(2,1)S(1)}, bf16[2,128,128]{2,1,0:T(8,128)(2,1)S(1)}, u32[]{:S(2)}, u32[]{:S(2)}) collective-permute-start(bf16[2,128,128]{2,1,0:T(8,128)(2,1)S(1)} %get-tuple-element.81), channel_id=1, source_target_pairs={{0,4},{2,6},{4,0},{6,2},{8,12},{10,14},{12,8},{14,10},{1,5},{3,7},... | collective-permute-start | bytes 196616 | tf_op jit(solution)/shard_map/ppermute | solution.py:535
  10.2 0.0 collective-permute-start.3
  10.2 3.7 %local_attention.2 = (bf16[1024,512]{1,0:T(8,128)(2,1)S(1)}, f32[1024,512]{1,0:T(8,128)S(1)}, f32[2,256,256]{2,1,0:T(8,128)S(1)}) custom-call(bf16[1024,512]{1,0:T(8,128)(2,1)S(1)} %get-tuple-element.74.refs_0_.x_ref, bf16[512,512]{1,0:T(8,128)(2,1)S(1)} %get-tuple-element.75.wq_ref, bf16[512,512]{1,0:T(8,128)(2,1)S(1)} %get-tuple-element.76.wk_ref, ...), custom_call_target="tpu_custom_call" | custom-call | flops 2415919104 | bytes 6291456 | tf_op jit(solution)/shard_map/local_attention/pallas_call | solution.py:163
  13.9 0.0 collective-permute-done.1.refs_0_
  13.9 0.0 collective-permute-done.2.refs_1_
  13.9 1.5 %collective-permute-done.3.refs_2_ = bf16[2,128,128]{2,1,0:T(8,128)(2,1)S(1)} collective-permute-done((bf16[2,128,128]{2,1,0:T(8,128)(2,1)S(1)}, bf16[2,128,128]{2,1,0:T(8,128)(2,1)S(1)}, u32[]{:S(2)}, u32[]{:S(2)}) %collective-permute-start.3) | collective-permute-done | bytes 65568 | tf_op jit(solution)/shard_map/ppermute | solution.py:535
  15.4 0.1 scan.1
  15.5 2.7 %collective-permute-start.4 = (bf16[2,128,128]{2,1,0:T(8,128)(2,1)S(1)}, bf16[2,128,128]{2,1,0:T(8,128)(2,1)S(1)}, u32[]{:S(2)}, u32[]{:S(2)}) collective-permute-start(bf16[2,128,128]{2,1,0:T(8,128)(2,1)S(1)} %get-tuple-element.91), channel_id=1, source_target_pairs={{0,8},{2,10},{4,12},{6,14},{8,0},{10,2},{12,4},{14,6},{1,9},{3,11}... | collective-permute-start | bytes 196616 | tf_op jit(solution)/shard_map/ppermute | solution.py:535
  18.1 3.7 %local_attention.3 = (bf16[1024,512]{1,0:T(8,128)(2,1)S(1)}, f32[1024,512]{1,0:T(8,128)S(1)}) custom-call(bf16[1024,512]{1,0:T(8,128)(2,1)S(1)} %get-tuple-element.88.refs_1_.x_ref, bf16[512,512]{1,0:T(8,128)(2,1)S(1)} %get-tuple-element.75.wq_ref, bf16[512,512]{1,0:T(8,128)(2,1)S(1)} %get-tuple-element.76.wk_ref, ...), custom_call_target="tpu_custom_call" | custom-call | flops 2415919104 | bytes 6291456 | tf_op jit(solution)/shard_map/local_attention/pallas_call | solution.py:163
  21.9 0.0 collective-permute-done.4.refs_0_
  21.9 0.1 spread.1
  22.0 0.1 collective-permute-start.5
  22.0 0.0 copy-start.4
  22.1 0.0 copy-start.5
  22.1 1.1 %own_share.1 = (f32[1024,256]{1,0:T(8,128)S(1)}, f32[1024,256]{1,0:T(8,128)S(1)}) custom-call(bf16[2,128,128]{2,1,0:T(8,128)(2,1)S(1)} %get-tuple-element.97.state_ref, bf16[512,256]{1,0:T(8,128)(2,1)S(1)} %get-tuple-element.98.w_ref.refs_7_, bf16[1024,512]{1,0:T(8,128)(2,1)S(1)} %get-tuple-element.82.refs_0_, ...), custom_call_target="tpu_custom_call" | custom-call | flops 805306368 | bytes 4194304 | tf_op jit(solution)/shard_map/own_share/pallas_call | solution.py:297
  23.2 0.1 collective-permute-done.5.refs_6_
  23.3 1.9 %voxel_features.1 = (bf16[2048,256]{1,0:T(8,128)(2,1)S(1)}, bf16[2,128,256]{2,1,0:T(8,128)(2,1)S(1)}) custom-call(s32[16]{0:T(128)S(1)} %bitcast.7, bf16[1024,512]{1,0:T(8,128)(2,1)S(1)} %get-tuple-element.82.refs_0_, bf16[1024,512]{1,0:T(8,128)(2,1)S(1)} %get-tuple-element.92.refs_1_, f32[1024,512]{1,0:T(8,128)S(1)} %get-tuple-element.93.refs_2_, ...), custom_call_target="tpu_custom_call" | custom-call | tf_op jit(solution)/shard_map/voxel_features/pallas_call | solution.py:386
  25.2 0.6 %collective-permute-start.7 = (bf16[2,128,256]{2,1,0:T(8,128)(2,1)S(1)}, bf16[2,128,256]{2,1,0:T(8,128)(2,1)S(1)}, u32[]{:S(2)}, u32[]{:S(2)}) collective-permute-start(bf16[2,128,256]{2,1,0:T(8,128)(2,1)S(1)} %get-tuple-element.109), channel_id=1, source_target_pairs={{0,2},{2,0},{4,6},{6,4},{8,10},{10,8},{12,14},{14,12},{1,3},{3,1},... | collective-permute-start | bytes 393224 | tf_op jit(solution)/shard_map/ppermute | solution.py:530
  25.8 1.3 %pool.1 = (bf16[2,128,256]{2,1,0:T(8,128)(2,1)S(1)}, bf16[2,128,256]{2,1,0:T(8,128)(2,1)S(1)}, bf16[2,128,256]{2,1,0:T(8,128)(2,1)S(1)}, bf16[2,128,256]{2,1,0:T...) custom-call(s32[16]{0:T(128)S(1)} %bitcast.8, ...), custom_call_target="tpu_custom_call" | custom-call | flops 469762048 | bytes 1048576 | tf_op jit(solution)/shard_map/pool/pallas_call | solution.py:417
  27.1 0.0 copy-start
  27.1 1.6 %collective-permute-start.11 = (bf16[2,128,256]{2,1,0:T(8,128)(2,1)S(1)}, bf16[2,128,256]{2,1,0:T(8,128)(2,1)S(1)}, u32[]{:S(2)}, u32[]{:S(2)}) collective-permute-start(bf16[2,128,256]{2,1,0:T(8,128)(2,1)S(1)} %get-tuple-element.114), channel_id=1, source_target_pairs={{0,4},{2,6},{4,0},{6,2},{8,12},{10,14},{12,8},{14,10},{1,5},{3,7},... | collective-permute-start | bytes 393224 | tf_op jit(solution)/shard_map/ppermute | solution.py:530
  28.7 0.5 collective-permute-start.6
  29.2 1.9 %collective-permute-done.7 = bf16[2,128,256]{2,1,0:T(8,128)(2,1)S(1)} collective-permute-done((bf16[2,128,256]{2,1,0:T(8,128)(2,1)S(1)}, bf16[2,128,256]{2,1,0:T(8,128)(2,1)S(1)}, u32[]{:S(2)}, u32[]{:S(2)}) %collective-permute-start.7) | collective-permute-done | bytes 131104 | tf_op jit(solution)/shard_map/ppermute | solution.py:530
  31.2 0.6 %collective-permute-start.8 = (bf16[2,128,256]{2,1,0:T(8,128)(2,1)S(1)}, bf16[2,128,256]{2,1,0:T(8,128)(2,1)S(1)}, u32[]{:S(2)}, u32[]{:S(2)}) collective-permute-start(bf16[2,128,256]{2,1,0:T(8,128)(2,1)S(1)} %add_convert_fusion.4), channel_id=1, source_target_pairs={{0,4},{2,6},{4,0},{6,2},{8,12},{10,14},{12,8},{14,10},{1,5},{3,7},... | collective-permute-start | bytes 393224 | tf_op jit(solution)/shard_map/ppermute | solution.py:530
  31.8 1.0 %collective-permute-done.11 = bf16[2,128,256]{2,1,0:T(8,128)(2,1)S(1)} collective-permute-done((bf16[2,128,256]{2,1,0:T(8,128)(2,1)S(1)}, bf16[2,128,256]{2,1,0:T(8,128)(2,1)S(1)}, u32[]{:S(2)}, u32[]{:S(2)}) %collective-permute-start.11) | collective-permute-done | bytes 131104 | tf_op jit(solution)/shard_map/ppermute | solution.py:530
  32.8 1.8 %collective-permute-start.12 = (bf16[2,128,256]{2,1,0:T(8,128)(2,1)S(1)}, bf16[2,128,256]{2,1,0:T(8,128)(2,1)S(1)}, u32[]{:S(2)}, u32[]{:S(2)}) collective-permute-start(bf16[2,128,256]{2,1,0:T(8,128)(2,1)S(1)} %add_convert_fusion.1), channel_id=1, source_target_pairs={{0,2},{2,0},{4,6},{6,4},{8,10},{10,8},{12,14},{14,12},{1,3},{3,1},... | collective-permute-start | bytes 393224 | tf_op jit(solution)/shard_map/ppermute | solution.py:530
  34.5 0.3 collective-permute-start.10
  34.9 0.0 collective-permute-done.6
  34.9 1.7 %collective-permute-done.8 = bf16[2,128,256]{2,1,0:T(8,128)(2,1)S(1)} collective-permute-done((bf16[2,128,256]{2,1,0:T(8,128)(2,1)S(1)}, bf16[2,128,256]{2,1,0:T(8,128)(2,1)S(1)}, u32[]{:S(2)}, u32[]{:S(2)}) %collective-permute-start.8) | collective-permute-done | bytes 131104 | tf_op jit(solution)/shard_map/ppermute | solution.py:530
  36.5 0.1 add_convert_fusion.3
  36.6 1.5 %collective-permute-start.9 = (bf16[1,128,256]{2,1,0:T(8,128)(2,1)S(1)}, bf16[1,128,256]{2,1,0:T(8,128)(2,1)S(1)}, u32[]{:S(2)}, u32[]{:S(2)}) collective-permute-start(bf16[1,128,256]{2,1,0:T(8,128)(2,1)S(1)} %slice.45), channel_id=1, source_target_pairs={{0,8},{2,10},{4,12},{6,14},{8,0},{10,2},{12,4},{14,6},{1,9},{3,11}... | collective-permute-start | bytes 196616 | tf_op jit(solution)/shard_map/ppermute | solution.py:530
  38.1 2.1 %collective-permute-done.10 = bf16[2,128,256]{2,1,0:T(8,128)(2,1)S(1)} collective-permute-done((bf16[2,128,256]{2,1,0:T(8,128)(2,1)S(1)}, bf16[2,128,256]{2,1,0:T(8,128)(2,1)S(1)}, u32[]{:S(2)}, u32[]{:S(2)}) %collective-permute-start.10) | collective-permute-done | bytes 131104 | tf_op jit(solution)/shard_map/ppermute | solution.py:530
  40.2 0.1 add_convert_fusion
  40.3 2.3 %collective-permute-done.9 = bf16[1,128,256]{2,1,0:T(8,128)(2,1)S(1)} collective-permute-done((bf16[1,128,256]{2,1,0:T(8,128)(2,1)S(1)}, bf16[1,128,256]{2,1,0:T(8,128)(2,1)S(1)}, u32[]{:S(2)}, u32[]{:S(2)}) %collective-permute-start.9) | collective-permute-done | bytes 65568 | tf_op jit(solution)/shard_map/ppermute | solution.py:530
  42.6 0.8 %collective-permute-start.15 = (bf16[1,128,256]{2,1,0:T(8,128)(2,1)S(1)}, bf16[1,128,256]{2,1,0:T(8,128)(2,1)S(1)}, u32[]{:S(2)}, u32[]{:S(2)}) collective-permute-start(bf16[1,128,256]{2,1,0:T(8,128)(2,1)S(1)} %get-tuple-element.117), channel_id=1, source_target_pairs={{0,8},{2,10},{4,12},{6,14},{8,0},{10,2},{12,4},{14,6},{1,9},{3,11}... | collective-permute-start | bytes 196616 | tf_op jit(solution)/shard_map/ppermute | solution.py:530
  43.4 1.0 %collective-permute-start.13 = (bf16[2,32,256]{2,1,0:T(8,128)(2,1)S(1)}, bf16[2,32,256]{2,1,0:T(8,128)(2,1)S(1)}, u32[]{:S(2)}, u32[]{:S(2)}) collective-permute-start(bf16[2,32,256]{2,1,0:T(8,128)(2,1)S(1)} %get-tuple-element.124), channel_id=1, source_target_pairs={{0,2},{1,3},{2,0},{3,1},{4,6},{5,7},{6,4},{7,5},{8,10},{9,11},{10,... | collective-permute-start | bytes 98312 | tf_op jit(solution)/shard_map/ppermute | solution.py:575
  44.5 1.5 %collective-permute-start.14 = (bf16[2,32,256]{2,1,0:T(8,128)(2,1)S(1)}, bf16[2,32,256]{2,1,0:T(8,128)(2,1)S(1)}, u32[]{:S(2)}, u32[]{:S(2)}) collective-permute-start(bf16[2,32,256]{2,1,0:T(8,128)(2,1)S(1)} %get-tuple-element.123), channel_id=1, source_target_pairs={{0,16},{1,17},{2,4},{3,5},{4,2},{5,3},{6,8},{7,9},{8,6},{9,7},{10,... | collective-permute-start | bytes 98312 | tf_op jit(solution)/shard_map/ppermute | solution.py:575
  45.9 2.4 %collective-permute-done.15 = bf16[1,128,256]{2,1,0:T(8,128)(2,1)S(1)} collective-permute-done((bf16[1,128,256]{2,1,0:T(8,128)(2,1)S(1)}, bf16[1,128,256]{2,1,0:T(8,128)(2,1)S(1)}, u32[]{:S(2)}, u32[]{:S(2)}) %collective-permute-start.15) | collective-permute-done | bytes 65568 | tf_op jit(solution)/shard_map/ppermute | solution.py:530
  48.4 0.0 collective-permute-done.14
  48.5 0.1 collective-permute-start.16
  48.6 0.8 %own_columns.1.first_ref = f32[496,256]{1,0:T(8,128)S(1)} custom-call(bf16[12,32,256]{2,1,0:T(8,128)(2,1)S(1)} %select_dynamic-update-slice_fusion.lines_ref, bf16[3,3,256,256]{3,2,1,0:T(8,128)(2,1)S(1)} %copy-done), custom_call_target="tpu_custom_call" | custom-call | flops 585105408 | bytes 1015808 | tf_op jit(solution)/shard_map/own_columns/pallas_call | solution.py:460
  49.3 0.4 collective-permute-done.16
  49.8 1.9 %field_flow.1 = f32[8,32,256]{2,1,0:T(8,128)} custom-call(f32[496,256]{1,0:T(8,128)S(1)} %own_columns.1.first_ref, bf16[13,16,256]{2,1,0:T(8,128)(2,1)S(1)} %pad_add_fusion.sides_ref, bf16[3,3,256,256]{3,2,1,0:T(8,128)(2,1)S(1)} %copy-done, bf16[3,3,256,256]{3,2,1,0:T(8,128)(2,1)S(1)} %copy-done.1), custom_call_target="tpu_custom_call" | custom-call | tf_op jit(solution)/shard_map/field_flow/pallas_call | solution.py:517
  (29 shorter events, 0.3 us)
Async XLA Ops:
  0.0 4.8 %copy-start.2 = (bf16[512,512]{1,0:T(8,128)(2,1)S(1)}, bf16[512,512]{1,0:T(8,128)(2,1)}, u32[]{:S(2)}) copy-start(bf16[512,512]{1,0:T(8,128)(2,1)} %refs_2_.1) | copy-start | bytes 1572868
  0.0 4.8 %copy-start.3 = (bf16[512,256]{1,0:T(8,128)(2,1)S(1)}, bf16[512,256]{1,0:T(8,128)(2,1)}, u32[]{:S(2)}) copy-start(bf16[512,256]{1,0:T(8,128)(2,1)} %refs_3_.1) | copy-start | bytes 786436
  4.3 1.4 %collective-permute-start = (bf16[2,128,128]{2,1,0:T(8,128)(2,1)S(1)}, bf16[2,128,128]{2,1,0:T(8,128)(2,1)S(1)}, u32[]{:S(2)}, u32[]{:S(2)}) collective-permute-start(bf16[2,128,128]{2,1,0:T(8,128)(2,1)S(1)} %get-tuple-element.71), channel_id=1, source_target_pairs={{0,1},{1,0},{2,3},{3,2},{4,5},{5,4},{6,7},{7,6},{8,9},{9,8},{10,11... | collective-permute-start | bytes 196616 | tf_op jit(solution)/shard_map/ppermute | solution.py:547
  5.7 8.2 %collective-permute-start.1 = (bf16[2,128,128]{2,1,0:T(8,128)(2,1)S(1)}, bf16[2,128,128]{2,1,0:T(8,128)(2,1)S(1)}, u32[]{:S(2)}, u32[]{:S(2)}) collective-permute-start(bf16[2,128,128]{2,1,0:T(8,128)(2,1)S(1)} %get-tuple-element.81), channel_id=1, source_target_pairs={{0,2},{2,0},{4,6},{6,4},{8,10},{10,8},{12,14},{14,12},{1,3},{3,1},... | collective-permute-start | bytes 196616 | tf_op jit(solution)/shard_map/ppermute | solution.py:535
  8.7 5.3 %collective-permute-start.2 = (bf16[2,128,128]{2,1,0:T(8,128)(2,1)S(1)}, bf16[2,128,128]{2,1,0:T(8,128)(2,1)S(1)}, u32[]{:S(2)}, u32[]{:S(2)}) collective-permute-start(bf16[2,128,128]{2,1,0:T(8,128)(2,1)S(1)} %get-tuple-element.81), channel_id=1, source_target_pairs={{0,4},{2,6},{4,0},{6,2},{8,12},{10,14},{12,8},{14,10},{1,5},{3,7},... | collective-permute-start | bytes 196616 | tf_op jit(solution)/shard_map/ppermute | solution.py:535
  10.2 5.2 %collective-permute-start.3 = (bf16[2,128,128]{2,1,0:T(8,128)(2,1)S(1)}, bf16[2,128,128]{2,1,0:T(8,128)(2,1)S(1)}, u32[]{:S(2)}, u32[]{:S(2)}) collective-permute-start(bf16[2,128,128]{2,1,0:T(8,128)(2,1)S(1)} %get-tuple-element.81), channel_id=1, source_target_pairs={{0,6},{2,4},{4,2},{6,0},{8,14},{10,12},{12,10},{14,8},{1,7},{3,5},... | collective-permute-start | bytes 196616 | tf_op jit(solution)/shard_map/ppermute | solution.py:535
  15.5 6.4 %collective-permute-start.4 = (bf16[2,128,128]{2,1,0:T(8,128)(2,1)S(1)}, bf16[2,128,128]{2,1,0:T(8,128)(2,1)S(1)}, u32[]{:S(2)}, u32[]{:S(2)}) collective-permute-start(bf16[2,128,128]{2,1,0:T(8,128)(2,1)S(1)} %get-tuple-element.91), channel_id=1, source_target_pairs={{0,8},{2,10},{4,12},{6,14},{8,0},{10,2},{12,4},{14,6},{1,9},{3,11}... | collective-permute-start | bytes 196616 | tf_op jit(solution)/shard_map/ppermute | solution.py:535
  22.0 1.3 %collective-permute-start.5 = (bf16[2,128,128]{2,1,0:T(8,128)(2,1)S(1)}, bf16[2,128,128]{2,1,0:T(8,128)(2,1)S(1)}, u32[]{:S(2)}, u32[]{:S(2)}) collective-permute-start(bf16[2,128,128]{2,1,0:T(8,128)(2,1)S(1)} %get-tuple-element.103), channel_id=1, source_target_pairs={{0,1},{1,0},{2,3},{3,2},{4,5},{5,4},{6,7},{7,6},{8,9},{9,8},{10,11... | collective-permute-start | bytes 196616 | tf_op jit(solution)/shard_map/ppermute | solution.py:547
  22.0 1.2 %copy-start.4 = (s32[2048]{0:T(1024)S(1)}, s32[2048]{0:T(1024)}, u32[]{:S(2)}) copy-start(s32[2048]{0:T(1024)} %param.15) | copy-start | bytes 24580
  22.1 1.2 %copy-start.5 = (s32[16,1]{0,1:T(1,128)S(1)}, s32[16,1]{0,1:T(1,128)}, u32[]{:S(2)}) copy-start(s32[16,1]{0,1:T(1,128)} %param.14) | copy-start | bytes 196
  25.2 5.9 %collective-permute-start.7 = (bf16[2,128,256]{2,1,0:T(8,128)(2,1)S(1)}, bf16[2,128,256]{2,1,0:T(8,128)(2,1)S(1)}, u32[]{:S(2)}, u32[]{:S(2)}) collective-permute-start(bf16[2,128,256]{2,1,0:T(8,128)(2,1)S(1)} %get-tuple-element.109), channel_id=1, source_target_pairs={{0,2},{2,0},{4,6},{6,4},{8,10},{10,8},{12,14},{14,12},{1,3},{3,1},... | collective-permute-start | bytes 393224 | tf_op jit(solution)/shard_map/ppermute | solution.py:530
  27.1 21.5 %copy-start = (bf16[3,3,256,256]{3,2,1,0:T(8,128)(2,1)S(1)}, bf16[3,3,256,256]{3,2,1,0:T(8,128)(2,1)}, u32[]{:S(2)}) copy-start(bf16[3,3,256,256]{3,2,1,0:T(8,128)(2,1)} %w1_ref.1) | copy-start | bytes 3538948
  27.1 5.6 %collective-permute-start.11 = (bf16[2,128,256]{2,1,0:T(8,128)(2,1)S(1)}, bf16[2,128,256]{2,1,0:T(8,128)(2,1)S(1)}, u32[]{:S(2)}, u32[]{:S(2)}) collective-permute-start(bf16[2,128,256]{2,1,0:T(8,128)(2,1)S(1)} %get-tuple-element.114), channel_id=1, source_target_pairs={{0,4},{2,6},{4,0},{6,2},{8,12},{10,14},{12,8},{14,10},{1,5},{3,7},... | collective-permute-start | bytes 393224 | tf_op jit(solution)/shard_map/ppermute | solution.py:530
  28.7 6.2 %collective-permute-start.6 = (bf16[2,128,256]{2,1,0:T(8,128)(2,1)S(1)}, bf16[2,128,256]{2,1,0:T(8,128)(2,1)S(1)}, u32[]{:S(2)}, u32[]{:S(2)}) collective-permute-start(bf16[2,128,256]{2,1,0:T(8,128)(2,1)S(1)} %get-tuple-element.106), channel_id=1, source_target_pairs={{0,2},{2,0},{4,6},{6,4},{8,10},{10,8},{12,14},{14,12},{1,3},{3,1},... | collective-permute-start | bytes 393224 | tf_op jit(solution)/shard_map/ppermute | solution.py:530
  31.2 5.4 %collective-permute-start.8 = (bf16[2,128,256]{2,1,0:T(8,128)(2,1)S(1)}, bf16[2,128,256]{2,1,0:T(8,128)(2,1)S(1)}, u32[]{:S(2)}, u32[]{:S(2)}) collective-permute-start(bf16[2,128,256]{2,1,0:T(8,128)(2,1)S(1)} %add_convert_fusion.4), channel_id=1, source_target_pairs={{0,4},{2,6},{4,0},{6,2},{8,12},{10,14},{12,8},{14,10},{1,5},{3,7},... | collective-permute-start | bytes 393224 | tf_op jit(solution)/shard_map/ppermute | solution.py:530
  32.8 5.3 %collective-permute-start.12 = (bf16[2,128,256]{2,1,0:T(8,128)(2,1)S(1)}, bf16[2,128,256]{2,1,0:T(8,128)(2,1)S(1)}, u32[]{:S(2)}, u32[]{:S(2)}) collective-permute-start(bf16[2,128,256]{2,1,0:T(8,128)(2,1)S(1)} %add_convert_fusion.1), channel_id=1, source_target_pairs={{0,2},{2,0},{4,6},{6,4},{8,10},{10,8},{12,14},{14,12},{1,3},{3,1},... | collective-permute-start | bytes 393224 | tf_op jit(solution)/shard_map/ppermute | solution.py:530
  34.5 5.7 %collective-permute-start.10 = (bf16[2,128,256]{2,1,0:T(8,128)(2,1)S(1)}, bf16[2,128,256]{2,1,0:T(8,128)(2,1)S(1)}, u32[]{:S(2)}, u32[]{:S(2)}) collective-permute-start(bf16[2,128,256]{2,1,0:T(8,128)(2,1)S(1)} %get-tuple-element.112), channel_id=1, source_target_pairs={{0,4},{2,6},{4,0},{6,2},{8,12},{10,14},{12,8},{14,10},{1,5},{3,7},... | collective-permute-start | bytes 393224 | tf_op jit(solution)/shard_map/ppermute | solution.py:530
  36.6 5.9 %collective-permute-start.9 = (bf16[1,128,256]{2,1,0:T(8,128)(2,1)S(1)}, bf16[1,128,256]{2,1,0:T(8,128)(2,1)S(1)}, u32[]{:S(2)}, u32[]{:S(2)}) collective-permute-start(bf16[1,128,256]{2,1,0:T(8,128)(2,1)S(1)} %slice.45), channel_id=1, source_target_pairs={{0,8},{2,10},{4,12},{6,14},{8,0},{10,2},{12,4},{14,6},{1,9},{3,11}... | collective-permute-start | bytes 196616 | tf_op jit(solution)/shard_map/ppermute | solution.py:530
  40.2 9.6 %copy-start.1 = (bf16[3,3,256,256]{3,2,1,0:T(8,128)(2,1)S(1)}, bf16[3,3,256,256]{3,2,1,0:T(8,128)(2,1)}, u32[]{:S(2)}) copy-start(bf16[3,3,256,256]{3,2,1,0:T(8,128)(2,1)} %w2_ref.1) | copy-start | bytes 3538948
  42.6 5.8 %collective-permute-start.15 = (bf16[1,128,256]{2,1,0:T(8,128)(2,1)S(1)}, bf16[1,128,256]{2,1,0:T(8,128)(2,1)S(1)}, u32[]{:S(2)}, u32[]{:S(2)}) collective-permute-start(bf16[1,128,256]{2,1,0:T(8,128)(2,1)S(1)} %get-tuple-element.117), channel_id=1, source_target_pairs={{0,8},{2,10},{4,12},{6,14},{8,0},{10,2},{12,4},{14,6},{1,9},{3,11}... | collective-permute-start | bytes 196616 | tf_op jit(solution)/shard_map/ppermute | solution.py:530
  43.4 4.9 %collective-permute-start.13 = (bf16[2,32,256]{2,1,0:T(8,128)(2,1)S(1)}, bf16[2,32,256]{2,1,0:T(8,128)(2,1)S(1)}, u32[]{:S(2)}, u32[]{:S(2)}) collective-permute-start(bf16[2,32,256]{2,1,0:T(8,128)(2,1)S(1)} %get-tuple-element.124), channel_id=1, source_target_pairs={{0,2},{1,3},{2,0},{3,1},{4,6},{5,7},{6,4},{7,5},{8,10},{9,11},{10,... | collective-permute-start | bytes 98312 | tf_op jit(solution)/shard_map/ppermute | solution.py:575
  44.5 3.9 %collective-permute-start.14 = (bf16[2,32,256]{2,1,0:T(8,128)(2,1)S(1)}, bf16[2,32,256]{2,1,0:T(8,128)(2,1)S(1)}, u32[]{:S(2)}, u32[]{:S(2)}) collective-permute-start(bf16[2,32,256]{2,1,0:T(8,128)(2,1)S(1)} %get-tuple-element.123), channel_id=1, source_target_pairs={{0,16},{1,17},{2,4},{3,5},{4,2},{5,3},{6,8},{7,9},{8,6},{9,7},{10,... | collective-permute-start | bytes 98312 | tf_op jit(solution)/shard_map/ppermute | solution.py:575
  48.5 1.2 %collective-permute-start.16 = (bf16[12,2,256]{2,1,0:T(2,128)(2,1)S(1)}, bf16[12,2,256]{2,1,0:T(2,128)(2,1)S(1)}, u32[]{:S(2)}, u32[]{:S(2)}) collective-permute-start(bf16[12,2,256]{2,1,0:T(2,128)(2,1)S(1)} %broadcast_select_fusion.4), channel_id=1, source_target_pairs={{0,1},{1,0},{2,3},{3,2},{4,5},{5,4},{6,7},{7,6},{8,9},{9,8},{10,11... | collective-permute-start | bytes 36872 | tf_op jit(solution)/shard_map/ppermute | solution.py:530

commit v9 on v8

--- a/solution.py
+++ b/solution.py
@@ -127,25 +127,27 @@
     q_ref[...] = q
     k[...] = dot(x_ref[...], wk_ref[...]).astype(BF16)
     v[...] = dot(x_ref[...], wv_ref[...]).astype(BF16)
-    for pair in range(HEADS // 2):
-        both = slice(pair * PAIR, (pair + 1) * PAIR)
-        state = None if starts else before_ref[pair]
-        for b in range(count):
-            rows = slice(b * BLK, (b + 1) * BLK)
-            if state is not None:
-                carried = dot(q[rows, both], jnp.where(same_head, state, 0.0).astype(BF16))
-            for h in range(2):
-                cols = head_cols(2 * pair + h)
-                scores = dot_nt(q[rows, cols], k[rows, cols])
-                scores = jnp.where(causal, scores, 0.0).astype(BF16)
-                attended = dot(scores, v[rows, cols])
-                if state is not None:
-                    attended += carried[:, head_cols(h)]
-                part_ref[rows, cols] = attended
-            if not (ends and b == count - 1):
-                outer = dot_t(k[rows, both], v[rows, both])
-                state = outer if state is None else state + outer
-        if not ends:
+    pairs = [slice(pair * PAIR, (pair + 1) * PAIR) for pair in range(HEADS // 2)]
+    states = None if starts else [before_ref[pair] for pair in range(HEADS // 2)]
+    for b in range(count):
+        rows = slice(b * BLK, (b + 1) * BLK)
+        scores = [dot_nt(q[rows, head_cols(h)], k[rows, head_cols(h)]) for h in range(HEADS)]
+        if states is not None:
+            carried = [
+                dot(q[rows, both], jnp.where(same_head, state, 0.0).astype(BF16))
+                for both, state in zip(pairs, states)
+            ]
+        scores = [jnp.where(causal, score, 0.0).astype(BF16) for score in scores]
+        attended = [dot(score, v[rows, head_cols(h)]) for h, score in enumerate(scores)]
+        for h in range(HEADS):
+            if states is not None:
+                attended[h] += carried[h // 2][:, head_cols(h % 2)]
+            part_ref[rows, head_cols(h)] = attended[h]
+        if not (ends and b == count - 1):
+            outer = [dot_t(k[rows, both], v[rows, both]) for both in pairs]
+            states = outer if states is None else [x + y for x, y in zip(states, outer)]
+    if not ends:
+        for pair, state in enumerate(states):
             refs[2][pair] = state
 
 

time: 52.6 us -> 52 us (0.989)
  waiting for transfers between devices: 13.3 us -> 14 us
  Pallas kernels: 19.7 us -> 19.1 us
    pallas_call x2, Pallas kernels: 7.39 us -> 6.77 us  [local_attention(): pl.pallas_call(functools.partial(local_kernel, rows // BLK, before is Non...]
  transfers between devices with their start and end apart: 17 -> 17, of which waited for: 9 -> 10; matrix products, arithmetic and copies ran while one was open for 0% -> 0% of each run, Pallas kernels for 22% -> 21%
where the time goes in v9:
time: 52 us; the launch traced here: 51.5 us
  Pallas kernels  19.1 us (37%)
  starting transfers between devices  17.7 us (34%)
  waiting for transfers between devices  14 us (27%)
    ppermute x9, waiting for transfers between devices, swap(): return lax.ppermute(array, axis, [(i, i ^ 1 << bit) for i in range(count)])  11.7 us
    ppermute x9, starting transfers between devices, swap(): return lax.ppermute(array, axis, [(i, i ^ 1 << bit) for i in range(count)])  7.74 us
    ppermute x4, starting transfers between devices, swap_digit(): return lax.ppermute(array, axis, [(i, i ^ by << bit) for i in range(count)])  7.16 us
    pallas_call x2, Pallas kernels, local_attention(): pl.pallas_call(functools.partial(local_kernel, rows // BLK, before is Non...  6.77 us
    pallas_call x1, Pallas kernels, device_totals(): pl.pallas_call(functools.partial(totals_kernel, spans), in_specs=[hbm, hb...  4.27 us
    ppermute x2, starting transfers between devices, exchange_lines(): got.append(lax.ppermute(out, ('group', 'wide', 'narrow'), pairs))  2.2 us
    pallas_call x1, Pallas kernels, field_flow(): pl.pallas_call(field_kernel, in_specs=[vmem] * 4, out_specs=vmem, out_sha...  1.94 us
    pallas_call x1, Pallas kernels, voxel_features(): pl.pallas_call(functools.partial(features_kernel, chosen, spans, cores),...  1.93 us
  transfers between devices with their start and end apart: 17, of which 10 were waited for; matrix products, arithmetic and copies ran while one was open for 0% of the time, Pallas kernels for 21%

profile of v9, /device:TPU:0, one launch (start us, length us, event | category | flops | bytes accessed | tf_op | source)
XLA Modules:
  0.0 51.5 jit_solution(8170108041986765164)
XLA Ops:
  0.0 4.3 %device_totals.1 = (bf16[1024,512]{1,0:T(8,128)(2,1)S(1)}, bf16[1024,512]{1,0:T(8,128)(2,1)S(1)}, bf16[512,512]{1,0:T(8,128)(2,1)S(1)}, bf16[512,512]{1,0:T(8,12...) custom-call(bf16[2048,512]{1,0:T(8,128)(2,1)} %x_ref.1, ...), custom_call_target="tpu_custom_call" | custom-call | tf_op jit(solution)/shard_map/device_totals/pallas_call | solution.py:100
  4.3 0.5 %collective-permute-start = (bf16[2,128,128]{2,1,0:T(8,128)(2,1)S(1)}, bf16[2,128,128]{2,1,0:T(8,128)(2,1)S(1)}, u32[]{:S(2)}, u32[]{:S(2)}) collective-permute-start(bf16[2,128,128]{2,1,0:T(8,128)(2,1)S(1)} %get-tuple-element.71), channel_id=1, source_target_pairs={{0,1},{1,0},{2,3},{3,2},{4,5},{5,4},{6,7},{7,6},{8,9},{9,8},{10,11... | collective-permute-start | bytes 196616 | tf_op jit(solution)/shard_map/ppermute | solution.py:549
  4.8 0.8 %direct_features.1 = (f32[1024,256]{1,0:T(8,128)S(1)}, f32[1024,256]{1,0:T(8,128)S(1)}, bf16[512,256]{1,0:T(8,128)(2,1)S(1)}) custom-call(bf16[1024,512]{1,0:T(8,128)(2,1)S(1)} %get-tuple-element.74.refs_0_.x_ref, bf16[1024,512]{1,0:T(8,128)(2,1)S(1)} %get-tuple-element.88.refs_1_.x_ref, bf16[512,512]{1,0:T(8,128)(2,1)S(1)} %copy-done.2, ...), custom_call_target="tpu_custom_call" | custom-call | flops 671088640 | bytes 4194304 | tf_op jit(solution)/shard_map/direct_features/pallas_call | solution.py:193
  5.7 0.0 collective-permute-done.refs_1_.refs_2_
  5.7 2.9 %collective-permute-start.1 = (bf16[2,128,128]{2,1,0:T(8,128)(2,1)S(1)}, bf16[2,128,128]{2,1,0:T(8,128)(2,1)S(1)}, u32[]{:S(2)}, u32[]{:S(2)}) collective-permute-start(bf16[2,128,128]{2,1,0:T(8,128)(2,1)S(1)} %get-tuple-element.81), channel_id=1, source_target_pairs={{0,2},{2,0},{4,6},{6,4},{8,10},{10,8},{12,14},{14,12},{1,3},{3,1},... | collective-permute-start | bytes 196616 | tf_op jit(solution)/shard_map/ppermute | solution.py:537
  8.7 1.6 %collective-permute-start.2 = (bf16[2,128,128]{2,1,0:T(8,128)(2,1)S(1)}, bf16[2,128,128]{2,1,0:T(8,128)(2,1)S(1)}, u32[]{:S(2)}, u32[]{:S(2)}) collective-permute-start(bf16[2,128,128]{2,1,0:T(8,128)(2,1)S(1)} %get-tuple-element.81), channel_id=1, source_target_pairs={{0,4},{2,6},{4,0},{6,2},{8,12},{10,14},{12,8},{14,10},{1,5},{3,7},... | collective-permute-start | bytes 196616 | tf_op jit(solution)/shard_map/ppermute | solution.py:537
  10.2 0.0 collective-permute-start.3
  10.2 3.4 %local_attention.2 = (bf16[1024,512]{1,0:T(8,128)(2,1)S(1)}, f32[1024,512]{1,0:T(8,128)S(1)}, f32[2,256,256]{2,1,0:T(8,128)S(1)}) custom-call(bf16[1024,512]{1,0:T(8,128)(2,1)S(1)} %get-tuple-element.74.refs_0_.x_ref, bf16[512,512]{1,0:T(8,128)(2,1)S(1)} %get-tuple-element.75.wq_ref, bf16[512,512]{1,0:T(8,128)(2,1)S(1)} %get-tuple-element.76.wk_ref, ...), custom_call_target="tpu_custom_call" | custom-call | flops 2415919104 | bytes 6291456 | tf_op jit(solution)/shard_map/local_attention/pallas_call | solution.py:165
  13.6 0.0 collective-permute-done.1.refs_0_
  13.6 1.8 %collective-permute-done.3.refs_2_ = bf16[2,128,128]{2,1,0:T(8,128)(2,1)S(1)} collective-permute-done((bf16[2,128,128]{2,1,0:T(8,128)(2,1)S(1)}, bf16[2,128,128]{2,1,0:T(8,128)(2,1)S(1)}, u32[]{:S(2)}, u32[]{:S(2)}) %collective-permute-start.3) | collective-permute-done | bytes 65568 | tf_op jit(solution)/shard_map/ppermute | solution.py:537
  15.4 0.1 scan.1
  15.5 2.7 %collective-permute-start.4 = (bf16[2,128,128]{2,1,0:T(8,128)(2,1)S(1)}, bf16[2,128,128]{2,1,0:T(8,128)(2,1)S(1)}, u32[]{:S(2)}, u32[]{:S(2)}) collective-permute-start(bf16[2,128,128]{2,1,0:T(8,128)(2,1)S(1)} %get-tuple-element.91), channel_id=1, source_target_pairs={{0,8},{2,10},{4,12},{6,14},{8,0},{10,2},{12,4},{14,6},{1,9},{3,11}... | collective-permute-start | bytes 196616 | tf_op jit(solution)/shard_map/ppermute | solution.py:537
  18.1 3.4 %local_attention.3 = (bf16[1024,512]{1,0:T(8,128)(2,1)S(1)}, f32[1024,512]{1,0:T(8,128)S(1)}) custom-call(bf16[1024,512]{1,0:T(8,128)(2,1)S(1)} %get-tuple-element.88.refs_1_.x_ref, bf16[512,512]{1,0:T(8,128)(2,1)S(1)} %get-tuple-element.75.wq_ref, bf16[512,512]{1,0:T(8,128)(2,1)S(1)} %get-tuple-element.76.wk_ref, ...), custom_call_target="tpu_custom_call" | custom-call | flops 2415919104 | bytes 6291456 | tf_op jit(solution)/shard_map/local_attention/pallas_call | solution.py:165
  21.5 0.0 collective-permute-done.4.refs_0_
  21.6 0.1 spread.1
  21.7 0.1 collective-permute-start.5
  21.7 0.0 copy-start.4
  21.7 0.0 copy-start.5
  21.8 1.1 %own_share.1 = (f32[1024,256]{1,0:T(8,128)S(1)}, f32[1024,256]{1,0:T(8,128)S(1)}) custom-call(bf16[2,128,128]{2,1,0:T(8,128)(2,1)S(1)} %get-tuple-element.97.state_ref, bf16[512,256]{1,0:T(8,128)(2,1)S(1)} %get-tuple-element.98.w_ref.refs_7_, bf16[1024,512]{1,0:T(8,128)(2,1)S(1)} %get-tuple-element.82.refs_0_, ...), custom_call_target="tpu_custom_call" | custom-call | flops 805306368 | bytes 4194304 | tf_op jit(solution)/shard_map/own_share/pallas_call | solution.py:299
  22.9 0.1 collective-permute-done.5.refs_6_
  23.0 1.9 %voxel_features.1 = (bf16[2048,256]{1,0:T(8,128)(2,1)S(1)}, bf16[2,128,256]{2,1,0:T(8,128)(2,1)S(1)}) custom-call(s32[16]{0:T(128)S(1)} %bitcast.7, bf16[1024,512]{1,0:T(8,128)(2,1)S(1)} %get-tuple-element.82.refs_0_, bf16[1024,512]{1,0:T(8,128)(2,1)S(1)} %get-tuple-element.92.refs_1_, f32[1024,512]{1,0:T(8,128)S(1)} %get-tuple-element.93.refs_2_, ...), custom_call_target="tpu_custom_call" | custom-call | tf_op jit(solution)/shard_map/voxel_features/pallas_call | solution.py:388
  24.9 0.6 %collective-permute-start.7 = (bf16[2,128,256]{2,1,0:T(8,128)(2,1)S(1)}, bf16[2,128,256]{2,1,0:T(8,128)(2,1)S(1)}, u32[]{:S(2)}, u32[]{:S(2)}) collective-permute-start(bf16[2,128,256]{2,1,0:T(8,128)(2,1)S(1)} %get-tuple-element.109), channel_id=1, source_target_pairs={{0,2},{2,0},{4,6},{6,4},{8,10},{10,8},{12,14},{14,12},{1,3},{3,1},... | collective-permute-start | bytes 393224 | tf_op jit(solution)/shard_map/ppermute | solution.py:532
  25.5 1.3 %pool.1 = (bf16[2,128,256]{2,1,0:T(8,128)(2,1)S(1)}, bf16[2,128,256]{2,1,0:T(8,128)(2,1)S(1)}, bf16[2,128,256]{2,1,0:T(8,128)(2,1)S(1)}, bf16[2,128,256]{2,1,0:T...) custom-call(s32[16]{0:T(128)S(1)} %bitcast.8, ...), custom_call_target="tpu_custom_call" | custom-call | flops 469762048 | bytes 1048576 | tf_op jit(solution)/shard_map/pool/pallas_call | solution.py:419
  26.8 0.0 copy-start
  26.8 1.3 %collective-permute-start.11 = (bf16[2,128,256]{2,1,0:T(8,128)(2,1)S(1)}, bf16[2,128,256]{2,1,0:T(8,128)(2,1)S(1)}, u32[]{:S(2)}, u32[]{:S(2)}) collective-permute-start(bf16[2,128,256]{2,1,0:T(8,128)(2,1)S(1)} %get-tuple-element.114), channel_id=1, source_target_pairs={{0,4},{2,6},{4,0},{6,2},{8,12},{10,14},{12,8},{14,10},{1,5},{3,7},... | collective-permute-start | bytes 393224 | tf_op jit(solution)/shard_map/ppermute | solution.py:532
  28.1 0.7 %collective-permute-start.6 = (bf16[2,128,256]{2,1,0:T(8,128)(2,1)S(1)}, bf16[2,128,256]{2,1,0:T(8,128)(2,1)S(1)}, u32[]{:S(2)}, u32[]{:S(2)}) collective-permute-start(bf16[2,128,256]{2,1,0:T(8,128)(2,1)S(1)} %get-tuple-element.106), channel_id=1, source_target_pairs={{0,2},{2,0},{4,6},{6,4},{8,10},{10,8},{12,14},{14,12},{1,3},{3,1},... | collective-permute-start | bytes 393224 | tf_op jit(solution)/shard_map/ppermute | solution.py:532
  28.8 2.2 %collective-permute-done.7 = bf16[2,128,256]{2,1,0:T(8,128)(2,1)S(1)} collective-permute-done((bf16[2,128,256]{2,1,0:T(8,128)(2,1)S(1)}, bf16[2,128,256]{2,1,0:T(8,128)(2,1)S(1)}, u32[]{:S(2)}, u32[]{:S(2)}) %collective-permute-start.7) | collective-permute-done | bytes 131104 | tf_op jit(solution)/shard_map/ppermute | solution.py:532
  31.0 0.3 collective-permute-start.8
  31.4 1.1 %collective-permute-done.11 = bf16[2,128,256]{2,1,0:T(8,128)(2,1)S(1)} collective-permute-done((bf16[2,128,256]{2,1,0:T(8,128)(2,1)S(1)}, bf16[2,128,256]{2,1,0:T(8,128)(2,1)S(1)}, u32[]{:S(2)}, u32[]{:S(2)}) %collective-permute-start.11) | collective-permute-done | bytes 131104 | tf_op jit(solution)/shard_map/ppermute | solution.py:532
  32.5 1.8 %collective-permute-start.12 = (bf16[2,128,256]{2,1,0:T(8,128)(2,1)S(1)}, bf16[2,128,256]{2,1,0:T(8,128)(2,1)S(1)}, u32[]{:S(2)}, u32[]{:S(2)}) collective-permute-start(bf16[2,128,256]{2,1,0:T(8,128)(2,1)S(1)} %add_convert_fusion.1), channel_id=1, source_target_pairs={{0,2},{2,0},{4,6},{6,4},{8,10},{10,8},{12,14},{14,12},{1,3},{3,1},... | collective-permute-start | bytes 393224 | tf_op jit(solution)/shard_map/ppermute | solution.py:532
  34.2 0.2 collective-permute-start.10
  34.5 0.0 collective-permute-done.6
  34.5 2.0 %collective-permute-done.8 = bf16[2,128,256]{2,1,0:T(8,128)(2,1)S(1)} collective-permute-done((bf16[2,128,256]{2,1,0:T(8,128)(2,1)S(1)}, bf16[2,128,256]{2,1,0:T(8,128)(2,1)S(1)}, u32[]{:S(2)}, u32[]{:S(2)}) %collective-permute-start.8) | collective-permute-done | bytes 131104 | tf_op jit(solution)/shard_map/ppermute | solution.py:532
  36.5 0.1 add_convert_fusion.3
  36.6 1.5 %collective-permute-start.9 = (bf16[1,128,256]{2,1,0:T(8,128)(2,1)S(1)}, bf16[1,128,256]{2,1,0:T(8,128)(2,1)S(1)}, u32[]{:S(2)}, u32[]{:S(2)}) collective-permute-start(bf16[1,128,256]{2,1,0:T(8,128)(2,1)S(1)} %slice.45), channel_id=1, source_target_pairs={{0,8},{2,10},{4,12},{6,14},{8,0},{10,2},{12,4},{14,6},{1,9},{3,11}... | collective-permute-start | bytes 196616 | tf_op jit(solution)/shard_map/ppermute | solution.py:532
  38.1 0.0 collective-permute-done.12
  38.1 1.8 %collective-permute-done.10 = bf16[2,128,256]{2,1,0:T(8,128)(2,1)S(1)} collective-permute-done((bf16[2,128,256]{2,1,0:T(8,128)(2,1)S(1)}, bf16[2,128,256]{2,1,0:T(8,128)(2,1)S(1)}, u32[]{:S(2)}, u32[]{:S(2)}) %collective-permute-start.10) | collective-permute-done | bytes 131104 | tf_op jit(solution)/shard_map/ppermute | solution.py:532
  39.9 0.1 add_convert_fusion
  40.0 2.2 %collective-permute-done.9 = bf16[1,128,256]{2,1,0:T(8,128)(2,1)S(1)} collective-permute-done((bf16[1,128,256]{2,1,0:T(8,128)(2,1)S(1)}, bf16[1,128,256]{2,1,0:T(8,128)(2,1)S(1)}, u32[]{:S(2)}, u32[]{:S(2)}) %collective-permute-start.9) | collective-permute-done | bytes 65568 | tf_op jit(solution)/shard_map/ppermute | solution.py:532
  42.2 1.2 %collective-permute-start.15 = (bf16[1,128,256]{2,1,0:T(8,128)(2,1)S(1)}, bf16[1,128,256]{2,1,0:T(8,128)(2,1)S(1)}, u32[]{:S(2)}, u32[]{:S(2)}) collective-permute-start(bf16[1,128,256]{2,1,0:T(8,128)(2,1)S(1)} %get-tuple-element.117), channel_id=1, source_target_pairs={{0,8},{2,10},{4,12},{6,14},{8,0},{10,2},{12,4},{14,6},{1,9},{3,11}... | collective-permute-start | bytes 196616 | tf_op jit(solution)/shard_map/ppermute | solution.py:532
  43.4 0.7 %collective-permute-start.13 = (bf16[2,32,256]{2,1,0:T(8,128)(2,1)S(1)}, bf16[2,32,256]{2,1,0:T(8,128)(2,1)S(1)}, u32[]{:S(2)}, u32[]{:S(2)}) collective-permute-start(bf16[2,32,256]{2,1,0:T(8,128)(2,1)S(1)} %get-tuple-element.124), channel_id=1, source_target_pairs={{0,2},{1,3},{2,0},{3,1},{4,6},{5,7},{6,4},{7,5},{8,10},{9,11},{10,... | collective-permute-start | bytes 98312 | tf_op jit(solution)/shard_map/ppermute | solution.py:577
  44.2 1.5 %collective-permute-start.14 = (bf16[2,32,256]{2,1,0:T(8,128)(2,1)S(1)}, bf16[2,32,256]{2,1,0:T(8,128)(2,1)S(1)}, u32[]{:S(2)}, u32[]{:S(2)}) collective-permute-start(bf16[2,32,256]{2,1,0:T(8,128)(2,1)S(1)} %get-tuple-element.123), channel_id=1, source_target_pairs={{0,16},{1,17},{2,4},{3,5},{4,2},{5,3},{6,8},{7,9},{8,6},{9,7},{10,... | collective-permute-start | bytes 98312 | tf_op jit(solution)/shard_map/ppermute | solution.py:577
  45.6 2.1 %collective-permute-done.15 = bf16[1,128,256]{2,1,0:T(8,128)(2,1)S(1)} collective-permute-done((bf16[1,128,256]{2,1,0:T(8,128)(2,1)S(1)}, bf16[1,128,256]{2,1,0:T(8,128)(2,1)S(1)}, u32[]{:S(2)}, u32[]{:S(2)}) %collective-permute-start.15) | collective-permute-done | bytes 65568 | tf_op jit(solution)/shard_map/ppermute | solution.py:532
  47.8 0.3 collective-permute-done.14
  48.2 0.1 collective-permute-start.16
  48.3 0.8 %own_columns.1.first_ref = f32[496,256]{1,0:T(8,128)S(1)} custom-call(bf16[12,32,256]{2,1,0:T(8,128)(2,1)S(1)} %select_dynamic-update-slice_fusion.lines_ref, bf16[3,3,256,256]{3,2,1,0:T(8,128)(2,1)S(1)} %copy-done), custom_call_target="tpu_custom_call" | custom-call | flops 585105408 | bytes 1015808 | tf_op jit(solution)/shard_map/own_columns/pallas_call | solution.py:462
  49.1 0.4 collective-permute-done.16
  49.5 1.9 %field_flow.1 = f32[8,32,256]{2,1,0:T(8,128)} custom-call(f32[496,256]{1,0:T(8,128)S(1)} %own_columns.1.first_ref, bf16[13,16,256]{2,1,0:T(8,128)(2,1)S(1)} %pad_add_fusion.sides_ref, bf16[3,3,256,256]{3,2,1,0:T(8,128)(2,1)S(1)} %copy-done, bf16[3,3,256,256]{3,2,1,0:T(8,128)(2,1)S(1)} %copy-done.1), custom_call_target="tpu_custom_call" | custom-call | tf_op jit(solution)/shard_map/field_flow/pallas_call | solution.py:519
  (29 shorter events, 0.3 us)
Async XLA Ops:
  0.0 4.8 %copy-start.2 = (bf16[512,512]{1,0:T(8,128)(2,1)S(1)}, bf16[512,512]{1,0:T(8,128)(2,1)}, u32[]{:S(2)}) copy-start(bf16[512,512]{1,0:T(8,128)(2,1)} %refs_2_.1) | copy-start | bytes 1572868
  0.0 4.8 %copy-start.3 = (bf16[512,256]{1,0:T(8,128)(2,1)S(1)}, bf16[512,256]{1,0:T(8,128)(2,1)}, u32[]{:S(2)}) copy-start(bf16[512,256]{1,0:T(8,128)(2,1)} %refs_3_.1) | copy-start | bytes 786436
  4.3 1.4 %collective-permute-start = (bf16[2,128,128]{2,1,0:T(8,128)(2,1)S(1)}, bf16[2,128,128]{2,1,0:T(8,128)(2,1)S(1)}, u32[]{:S(2)}, u32[]{:S(2)}) collective-permute-start(bf16[2,128,128]{2,1,0:T(8,128)(2,1)S(1)} %get-tuple-element.71), channel_id=1, source_target_pairs={{0,1},{1,0},{2,3},{3,2},{4,5},{5,4},{6,7},{7,6},{8,9},{9,8},{10,11... | collective-permute-start | bytes 196616 | tf_op jit(solution)/shard_map/ppermute | solution.py:549
  5.7 7.9 %collective-permute-start.1 = (bf16[2,128,128]{2,1,0:T(8,128)(2,1)S(1)}, bf16[2,128,128]{2,1,0:T(8,128)(2,1)S(1)}, u32[]{:S(2)}, u32[]{:S(2)}) collective-permute-start(bf16[2,128,128]{2,1,0:T(8,128)(2,1)S(1)} %get-tuple-element.81), channel_id=1, source_target_pairs={{0,2},{2,0},{4,6},{6,4},{8,10},{10,8},{12,14},{14,12},{1,3},{3,1},... | collective-permute-start | bytes 196616 | tf_op jit(solution)/shard_map/ppermute | solution.py:537
  8.7 5.0 %collective-permute-start.2 = (bf16[2,128,128]{2,1,0:T(8,128)(2,1)S(1)}, bf16[2,128,128]{2,1,0:T(8,128)(2,1)S(1)}, u32[]{:S(2)}, u32[]{:S(2)}) collective-permute-start(bf16[2,128,128]{2,1,0:T(8,128)(2,1)S(1)} %get-tuple-element.81), channel_id=1, source_target_pairs={{0,4},{2,6},{4,0},{6,2},{8,12},{10,14},{12,8},{14,10},{1,5},{3,7},... | collective-permute-start | bytes 196616 | tf_op jit(solution)/shard_map/ppermute | solution.py:537
  10.2 5.2 %collective-permute-start.3 = (bf16[2,128,128]{2,1,0:T(8,128)(2,1)S(1)}, bf16[2,128,128]{2,1,0:T(8,128)(2,1)S(1)}, u32[]{:S(2)}, u32[]{:S(2)}) collective-permute-start(bf16[2,128,128]{2,1,0:T(8,128)(2,1)S(1)} %get-tuple-element.81), channel_id=1, source_target_pairs={{0,6},{2,4},{4,2},{6,0},{8,14},{10,12},{12,10},{14,8},{1,7},{3,5},... | collective-permute-start | bytes 196616 | tf_op jit(solution)/shard_map/ppermute | solution.py:537
  15.5 6.1 %collective-permute-start.4 = (bf16[2,128,128]{2,1,0:T(8,128)(2,1)S(1)}, bf16[2,128,128]{2,1,0:T(8,128)(2,1)S(1)}, u32[]{:S(2)}, u32[]{:S(2)}) collective-permute-start(bf16[2,128,128]{2,1,0:T(8,128)(2,1)S(1)} %get-tuple-element.91), channel_id=1, source_target_pairs={{0,8},{2,10},{4,12},{6,14},{8,0},{10,2},{12,4},{14,6},{1,9},{3,11}... | collective-permute-start | bytes 196616 | tf_op jit(solution)/shard_map/ppermute | solution.py:537
  21.7 1.3 %collective-permute-start.5 = (bf16[2,128,128]{2,1,0:T(8,128)(2,1)S(1)}, bf16[2,128,128]{2,1,0:T(8,128)(2,1)S(1)}, u32[]{:S(2)}, u32[]{:S(2)}) collective-permute-start(bf16[2,128,128]{2,1,0:T(8,128)(2,1)S(1)} %get-tuple-element.103), channel_id=1, source_target_pairs={{0,1},{1,0},{2,3},{3,2},{4,5},{5,4},{6,7},{7,6},{8,9},{9,8},{10,11... | collective-permute-start | bytes 196616 | tf_op jit(solution)/shard_map/ppermute | solution.py:549
  21.7 1.2 %copy-start.4 = (s32[2048]{0:T(1024)S(1)}, s32[2048]{0:T(1024)}, u32[]{:S(2)}) copy-start(s32[2048]{0:T(1024)} %param.15) | copy-start | bytes 24580
  21.7 1.2 %copy-start.5 = (s32[16,1]{0,1:T(1,128)S(1)}, s32[16,1]{0,1:T(1,128)}, u32[]{:S(2)}) copy-start(s32[16,1]{0,1:T(1,128)} %param.14) | copy-start | bytes 196
  24.9 6.1 %collective-permute-start.7 = (bf16[2,128,256]{2,1,0:T(8,128)(2,1)S(1)}, bf16[2,128,256]{2,1,0:T(8,128)(2,1)S(1)}, u32[]{:S(2)}, u32[]{:S(2)}) collective-permute-start(bf16[2,128,256]{2,1,0:T(8,128)(2,1)S(1)} %get-tuple-element.109), channel_id=1, source_target_pairs={{0,2},{2,0},{4,6},{6,4},{8,10},{10,8},{12,14},{14,12},{1,3},{3,1},... | collective-permute-start | bytes 393224 | tf_op jit(solution)/shard_map/ppermute | solution.py:532
  26.8 21.5 %copy-start = (bf16[3,3,256,256]{3,2,1,0:T(8,128)(2,1)S(1)}, bf16[3,3,256,256]{3,2,1,0:T(8,128)(2,1)}, u32[]{:S(2)}) copy-start(bf16[3,3,256,256]{3,2,1,0:T(8,128)(2,1)} %w1_ref.1) | copy-start | bytes 3538948
  26.8 5.6 %collective-permute-start.11 = (bf16[2,128,256]{2,1,0:T(8,128)(2,1)S(1)}, bf16[2,128,256]{2,1,0:T(8,128)(2,1)S(1)}, u32[]{:S(2)}, u32[]{:S(2)}) collective-permute-start(bf16[2,128,256]{2,1,0:T(8,128)(2,1)S(1)} %get-tuple-element.114), channel_id=1, source_target_pairs={{0,4},{2,6},{4,0},{6,2},{8,12},{10,14},{12,8},{14,10},{1,5},{3,7},... | collective-permute-start | bytes 393224 | tf_op jit(solution)/shard_map/ppermute | solution.py:532
  28.1 6.4 %collective-permute-start.6 = (bf16[2,128,256]{2,1,0:T(8,128)(2,1)S(1)}, bf16[2,128,256]{2,1,0:T(8,128)(2,1)S(1)}, u32[]{:S(2)}, u32[]{:S(2)}) collective-permute-start(bf16[2,128,256]{2,1,0:T(8,128)(2,1)S(1)} %get-tuple-element.106), channel_id=1, source_target_pairs={{0,2},{2,0},{4,6},{6,4},{8,10},{10,8},{12,14},{14,12},{1,3},{3,1},... | collective-permute-start | bytes 393224 | tf_op jit(solution)/shard_map/ppermute | solution.py:532
  31.0 5.4 %collective-permute-start.8 = (bf16[2,128,256]{2,1,0:T(8,128)(2,1)S(1)}, bf16[2,128,256]{2,1,0:T(8,128)(2,1)S(1)}, u32[]{:S(2)}, u32[]{:S(2)}) collective-permute-start(bf16[2,128,256]{2,1,0:T(8,128)(2,1)S(1)} %add_convert_fusion.4), channel_id=1, source_target_pairs={{0,4},{2,6},{4,0},{6,2},{8,12},{10,14},{12,8},{14,10},{1,5},{3,7},... | collective-permute-start | bytes 393224 | tf_op jit(solution)/shard_map/ppermute | solution.py:532
  32.5 5.6 %collective-permute-start.12 = (bf16[2,128,256]{2,1,0:T(8,128)(2,1)S(1)}, bf16[2,128,256]{2,1,0:T(8,128)(2,1)S(1)}, u32[]{:S(2)}, u32[]{:S(2)}) collective-permute-start(bf16[2,128,256]{2,1,0:T(8,128)(2,1)S(1)} %add_convert_fusion.1), channel_id=1, source_target_pairs={{0,2},{2,0},{4,6},{6,4},{8,10},{10,8},{12,14},{14,12},{1,3},{3,1},... | collective-permute-start | bytes 393224 | tf_op jit(solution)/shard_map/ppermute | solution.py:532
  34.2 5.7 %collective-permute-start.10 = (bf16[2,128,256]{2,1,0:T(8,128)(2,1)S(1)}, bf16[2,128,256]{2,1,0:T(8,128)(2,1)S(1)}, u32[]{:S(2)}, u32[]{:S(2)}) collective-permute-start(bf16[2,128,256]{2,1,0:T(8,128)(2,1)S(1)} %get-tuple-element.112), channel_id=1, source_target_pairs={{0,4},{2,6},{4,0},{6,2},{8,12},{10,14},{12,8},{14,10},{1,5},{3,7},... | collective-permute-start | bytes 393224 | tf_op jit(solution)/shard_map/ppermute | solution.py:532
  36.6 5.6 %collective-permute-start.9 = (bf16[1,128,256]{2,1,0:T(8,128)(2,1)S(1)}, bf16[1,128,256]{2,1,0:T(8,128)(2,1)S(1)}, u32[]{:S(2)}, u32[]{:S(2)}) collective-permute-start(bf16[1,128,256]{2,1,0:T(8,128)(2,1)S(1)} %slice.45), channel_id=1, source_target_pairs={{0,8},{2,10},{4,12},{6,14},{8,0},{10,2},{12,4},{14,6},{1,9},{3,11}... | collective-permute-start | bytes 196616 | tf_op jit(solution)/shard_map/ppermute | solution.py:532
  39.9 9.6 %copy-start.1 = (bf16[3,3,256,256]{3,2,1,0:T(8,128)(2,1)S(1)}, bf16[3,3,256,256]{3,2,1,0:T(8,128)(2,1)}, u32[]{:S(2)}) copy-start(bf16[3,3,256,256]{3,2,1,0:T(8,128)(2,1)} %w2_ref.1) | copy-start | bytes 3538948
  42.2 5.5 %collective-permute-start.15 = (bf16[1,128,256]{2,1,0:T(8,128)(2,1)S(1)}, bf16[1,128,256]{2,1,0:T(8,128)(2,1)S(1)}, u32[]{:S(2)}, u32[]{:S(2)}) collective-permute-start(bf16[1,128,256]{2,1,0:T(8,128)(2,1)S(1)} %get-tuple-element.117), channel_id=1, source_target_pairs={{0,8},{2,10},{4,12},{6,14},{8,0},{10,2},{12,4},{14,6},{1,9},{3,11}... | collective-permute-start | bytes 196616 | tf_op jit(solution)/shard_map/ppermute | solution.py:532
  43.4 4.3 %collective-permute-start.13 = (bf16[2,32,256]{2,1,0:T(8,128)(2,1)S(1)}, bf16[2,32,256]{2,1,0:T(8,128)(2,1)S(1)}, u32[]{:S(2)}, u32[]{:S(2)}) collective-permute-start(bf16[2,32,256]{2,1,0:T(8,128)(2,1)S(1)} %get-tuple-element.124), channel_id=1, source_target_pairs={{0,2},{1,3},{2,0},{3,1},{4,6},{5,7},{6,4},{7,5},{8,10},{9,11},{10,... | collective-permute-start | bytes 98312 | tf_op jit(solution)/shard_map/ppermute | solution.py:577
  44.2 3.9 %collective-permute-start.14 = (bf16[2,32,256]{2,1,0:T(8,128)(2,1)S(1)}, bf16[2,32,256]{2,1,0:T(8,128)(2,1)S(1)}, u32[]{:S(2)}, u32[]{:S(2)}) collective-permute-start(bf16[2,32,256]{2,1,0:T(8,128)(2,1)S(1)} %get-tuple-element.123), channel_id=1, source_target_pairs={{0,16},{1,17},{2,4},{3,5},{4,2},{5,3},{6,8},{7,9},{8,6},{9,7},{10,... | collective-permute-start | bytes 98312 | tf_op jit(solution)/shard_map/ppermute | solution.py:577
  48.2 1.2 %collective-permute-start.16 = (bf16[12,2,256]{2,1,0:T(2,128)(2,1)S(1)}, bf16[12,2,256]{2,1,0:T(2,128)(2,1)S(1)}, u32[]{:S(2)}, u32[]{:S(2)}) collective-permute-start(bf16[12,2,256]{2,1,0:T(2,128)(2,1)S(1)} %broadcast_select_fusion.4), channel_id=1, source_target_pairs={{0,1},{1,0},{2,3},{3,2},{4,5},{5,4},{6,7},{7,6},{8,9},{9,8},{10,11... | collective-permute-start | bytes 36872 | tf_op jit(solution)/shard_map/ppermute | solution.py:532

commit v10 on v9

--- a/solution.py
+++ b/solution.py
@@ -142,7 +142,7 @@
         for h in range(HEADS):
             if states is not None:
                 attended[h] += carried[h // 2][:, head_cols(h % 2)]
-            part_ref[rows, head_cols(h)] = attended[h]
+            part_ref[rows, head_cols(h)] = attended[h].astype(BF16)
         if not (ends and b == count - 1):
             outer = [dot_t(k[rows, both], v[rows, both]) for both in pairs]
             states = outer if states is None else [x + y for x, y in zip(states, outer)]
@@ -156,10 +156,7 @@
     inner = HEADS * HEAD
     vmem = pl.BlockSpec(memory_space=pltpu.VMEM)
     inputs = [x, *ws] + ([] if before is None else [before])
-    out_shape = [
-        jax.ShapeDtypeStruct((rows, inner), BF16),
-        jax.ShapeDtypeStruct((rows, inner), F32),
-    ]
+    out_shape = [jax.ShapeDtypeStruct((rows, inner), BF16)] * 2
     if not ends:
         out_shape.append(jax.ShapeDtypeStruct((HEADS // 2, PAIR, PAIR), F32))
     return pl.pallas_call(
@@ -171,7 +168,7 @@
         compiler_params=params(),
         cost_estimate=pl.CostEstimate(
             flops=2 * rows * inner * (3 * width + 2 * BLK + 2 * HEAD),
-            bytes_accessed=rows * inner * 12,
+            bytes_accessed=rows * inner * 10,
             transcendentals=0,
         ),
         name="local_attention",
@@ -270,7 +267,7 @@
 
 
 def norm_share(q, part, state, ones):
-    attended = part + dot(q, state)
+    attended = part.astype(F32) + dot(q, state)
     squares = dot((attended * attended).astype(BF16), ones)
     return (attended * lax.rsqrt(squares * (1 / HEAD) + EPS)).astype(BF16)
 

time: 52 us -> 52.1 us (level)
  no operation moved by 1% of the time
where the time goes in v10:
time: 52.1 us; the launch traced here: 51.4 us
  Pallas kernels  19.1 us (37%)
  starting transfers between devices  17.7 us (34%)
  waiting for transfers between devices  13.9 us (27%)
    ppermute x9, waiting for transfers between devices, swap(): return lax.ppermute(array, axis, [(i, i ^ 1 << bit) for i in range(count)])  11.7 us
    ppermute x9, starting transfers between devices, swap(): return lax.ppermute(array, axis, [(i, i ^ 1 << bit) for i in range(count)])  7.79 us
    ppermute x4, starting transfers between devices, swap_digit(): return lax.ppermute(array, axis, [(i, i ^ by << bit) for i in range(count)])  7.16 us
    pallas_call x2, Pallas kernels, local_attention(): pl.pallas_call(functools.partial(local_kernel, rows // BLK, before is Non...  6.77 us
    pallas_call x1, Pallas kernels, device_totals(): pl.pallas_call(functools.partial(totals_kernel, spans), in_specs=[hbm, hb...  4.27 us
    ppermute x2, starting transfers between devices, exchange_lines(): got.append(lax.ppermute(out, ('group', 'wide', 'narrow'), pairs))  2.14 us
    pallas_call x1, Pallas kernels, field_flow(): pl.pallas_call(field_kernel, in_specs=[vmem] * 4, out_specs=vmem, out_sha...  1.94 us
    pallas_call x1, Pallas kernels, voxel_features(): pl.pallas_call(functools.partial(features_kernel, chosen, spans, cores),...  1.92 us
  transfers between devices with their start and end apart: 17, of which 10 were waited for; matrix products, arithmetic and copies ran while one was open for 0% of the time, Pallas kernels for 21%

profile of v10, /device:TPU:0, one launch (start us, length us, event | category | flops | bytes accessed | tf_op | source)
XLA Modules:
  0.0 51.4 jit_solution(16753364269204617214)
XLA Ops:
  0.0 4.3 %device_totals.1 = (bf16[1024,512]{1,0:T(8,128)(2,1)S(1)}, bf16[1024,512]{1,0:T(8,128)(2,1)S(1)}, bf16[512,512]{1,0:T(8,128)(2,1)S(1)}, bf16[512,512]{1,0:T(8,12...) custom-call(bf16[2048,512]{1,0:T(8,128)(2,1)} %x_ref.1, ...), custom_call_target="tpu_custom_call" | custom-call | tf_op jit(solution)/shard_map/device_totals/pallas_call | solution.py:100
  4.3 0.5 %collective-permute-start = (bf16[2,128,128]{2,1,0:T(8,128)(2,1)S(1)}, bf16[2,128,128]{2,1,0:T(8,128)(2,1)S(1)}, u32[]{:S(2)}, u32[]{:S(2)}) collective-permute-start(bf16[2,128,128]{2,1,0:T(8,128)(2,1)S(1)} %get-tuple-element.71), channel_id=1, source_target_pairs={{0,1},{1,0},{2,3},{3,2},{4,5},{5,4},{6,7},{7,6},{8,9},{9,8},{10,11... | collective-permute-start | bytes 196616 | tf_op jit(solution)/shard_map/ppermute | solution.py:546
  4.8 0.8 %direct_features.1 = (f32[1024,256]{1,0:T(8,128)S(1)}, f32[1024,256]{1,0:T(8,128)S(1)}, bf16[512,256]{1,0:T(8,128)(2,1)S(1)}) custom-call(bf16[1024,512]{1,0:T(8,128)(2,1)S(1)} %get-tuple-element.74.refs_0_.x_ref, bf16[1024,512]{1,0:T(8,128)(2,1)S(1)} %get-tuple-element.88.refs_1_.x_ref, bf16[512,512]{1,0:T(8,128)(2,1)S(1)} %copy-done.2, ...), custom_call_target="tpu_custom_call" | custom-call | flops 671088640 | bytes 4194304 | tf_op jit(solution)/shard_map/direct_features/pallas_call | solution.py:190
  5.7 0.0 collective-permute-done.refs_1_.refs_2_
  5.7 2.9 %collective-permute-start.1 = (bf16[2,128,128]{2,1,0:T(8,128)(2,1)S(1)}, bf16[2,128,128]{2,1,0:T(8,128)(2,1)S(1)}, u32[]{:S(2)}, u32[]{:S(2)}) collective-permute-start(bf16[2,128,128]{2,1,0:T(8,128)(2,1)S(1)} %get-tuple-element.81), channel_id=1, source_target_pairs={{0,2},{2,0},{4,6},{6,4},{8,10},{10,8},{12,14},{14,12},{1,3},{3,1},... | collective-permute-start | bytes 196616 | tf_op jit(solution)/shard_map/ppermute | solution.py:534
  8.7 1.6 %collective-permute-start.2 = (bf16[2,128,128]{2,1,0:T(8,128)(2,1)S(1)}, bf16[2,128,128]{2,1,0:T(8,128)(2,1)S(1)}, u32[]{:S(2)}, u32[]{:S(2)}) collective-permute-start(bf16[2,128,128]{2,1,0:T(8,128)(2,1)S(1)} %get-tuple-element.81), channel_id=1, source_target_pairs={{0,4},{2,6},{4,0},{6,2},{8,12},{10,14},{12,8},{14,10},{1,5},{3,7},... | collective-permute-start | bytes 196616 | tf_op jit(solution)/shard_map/ppermute | solution.py:534
  10.2 0.0 collective-permute-start.3
  10.2 3.4 %local_attention.2 = (bf16[1024,512]{1,0:T(8,128)(2,1)S(1)}, bf16[1024,512]{1,0:T(8,128)(2,1)S(1)}, f32[2,256,256]{2,1,0:T(8,128)S(1)}) custom-call(bf16[1024,512]{1,0:T(8,128)(2,1)S(1)} %get-tuple-element.74.refs_0_.x_ref, bf16[512,512]{1,0:T(8,128)(2,1)S(1)} %get-tuple-element.75.wq_ref, bf16[512,512]{1,0:T(8,128)(2,1)S(1)} %get-tuple-element.76.wk_ref, ...), custom_call_target="tpu_custom_call" | custom-call | flops 2415919104 | bytes 5242880 | tf_op jit(solution)/shard_map/local_attention/pallas_call | solution.py:162
  13.6 0.0 collective-permute-done.1.refs_0_
  13.6 0.0 collective-permute-done.2.refs_1_
  13.6 1.8 %collective-permute-done.3.refs_2_ = bf16[2,128,128]{2,1,0:T(8,128)(2,1)S(1)} collective-permute-done((bf16[2,128,128]{2,1,0:T(8,128)(2,1)S(1)}, bf16[2,128,128]{2,1,0:T(8,128)(2,1)S(1)}, u32[]{:S(2)}, u32[]{:S(2)}) %collective-permute-start.3) | collective-permute-done | bytes 65568 | tf_op jit(solution)/shard_map/ppermute | solution.py:534
  15.4 0.1 scan.1
  15.5 2.7 %collective-permute-start.4 = (bf16[2,128,128]{2,1,0:T(8,128)(2,1)S(1)}, bf16[2,128,128]{2,1,0:T(8,128)(2,1)S(1)}, u32[]{:S(2)}, u32[]{:S(2)}) collective-permute-start(bf16[2,128,128]{2,1,0:T(8,128)(2,1)S(1)} %get-tuple-element.91), channel_id=1, source_target_pairs={{0,8},{2,10},{4,12},{6,14},{8,0},{10,2},{12,4},{14,6},{1,9},{3,11}... | collective-permute-start | bytes 196616 | tf_op jit(solution)/shard_map/ppermute | solution.py:534
  18.1 3.4 %local_attention.3 = (bf16[1024,512]{1,0:T(8,128)(2,1)S(1)}, bf16[1024,512]{1,0:T(8,128)(2,1)S(1)}) custom-call(bf16[1024,512]{1,0:T(8,128)(2,1)S(1)} %get-tuple-element.88.refs_1_.x_ref, bf16[512,512]{1,0:T(8,128)(2,1)S(1)} %get-tuple-element.75.wq_ref, bf16[512,512]{1,0:T(8,128)(2,1)S(1)} %get-tuple-element.76.wk_ref, ...), custom_call_target="tpu_custom_call" | custom-call | flops 2415919104 | bytes 5242880 | tf_op jit(solution)/shard_map/local_attention/pallas_call | solution.py:162
  21.5 0.0 collective-permute-done.4.refs_0_
  21.6 0.1 spread.1
  21.6 0.1 collective-permute-start.5
  21.7 0.0 copy-start.4
  21.7 0.0 copy-start.5
  21.8 1.1 %own_share.1 = (f32[1024,256]{1,0:T(8,128)S(1)}, f32[1024,256]{1,0:T(8,128)S(1)}) custom-call(bf16[2,128,128]{2,1,0:T(8,128)(2,1)S(1)} %get-tuple-element.97.state_ref, bf16[512,256]{1,0:T(8,128)(2,1)S(1)} %get-tuple-element.98.w_ref.refs_7_, bf16[1024,512]{1,0:T(8,128)(2,1)S(1)} %get-tuple-element.82.refs_0_, ...), custom_call_target="tpu_custom_call" | custom-call | flops 805306368 | bytes 4194304 | tf_op jit(solution)/shard_map/own_share/pallas_call | solution.py:296
  22.9 0.1 collective-permute-done.5.refs_6_
  23.0 1.9 %voxel_features.1 = (bf16[2048,256]{1,0:T(8,128)(2,1)S(1)}, bf16[2,128,256]{2,1,0:T(8,128)(2,1)S(1)}) custom-call(s32[16]{0:T(128)S(1)} %bitcast.7, bf16[1024,512]{1,0:T(8,128)(2,1)S(1)} %get-tuple-element.82.refs_0_, bf16[1024,512]{1,0:T(8,128)(2,1)S(1)} %get-tuple-element.92.refs_1_, bf16[1024,512]{1,0:T(8,128)(2,1)S(1)} %get-tuple-element.93.refs_2_, ...), custom_call_target="tpu_custom_call" | custom-call | tf_op jit(solution)/shard_map/voxel_features/pallas_call | solution.py:385
  24.9 0.6 %collective-permute-start.7 = (bf16[2,128,256]{2,1,0:T(8,128)(2,1)S(1)}, bf16[2,128,256]{2,1,0:T(8,128)(2,1)S(1)}, u32[]{:S(2)}, u32[]{:S(2)}) collective-permute-start(bf16[2,128,256]{2,1,0:T(8,128)(2,1)S(1)} %get-tuple-element.109), channel_id=1, source_target_pairs={{0,2},{2,0},{4,6},{6,4},{8,10},{10,8},{12,14},{14,12},{1,3},{3,1},... | collective-permute-start | bytes 393224 | tf_op jit(solution)/shard_map/ppermute | solution.py:529
  25.5 1.3 %pool.1 = (bf16[2,128,256]{2,1,0:T(8,128)(2,1)S(1)}, bf16[2,128,256]{2,1,0:T(8,128)(2,1)S(1)}, bf16[2,128,256]{2,1,0:T(8,128)(2,1)S(1)}, bf16[2,128,256]{2,1,0:T...) custom-call(s32[16]{0:T(128)S(1)} %bitcast.8, ...), custom_call_target="tpu_custom_call" | custom-call | flops 469762048 | bytes 1048576 | tf_op jit(solution)/shard_map/pool/pallas_call | solution.py:416
  26.8 1.3 %collective-permute-start.11 = (bf16[2,128,256]{2,1,0:T(8,128)(2,1)S(1)}, bf16[2,128,256]{2,1,0:T(8,128)(2,1)S(1)}, u32[]{:S(2)}, u32[]{:S(2)}) collective-permute-start(bf16[2,128,256]{2,1,0:T(8,128)(2,1)S(1)} %get-tuple-element.114), channel_id=1, source_target_pairs={{0,4},{2,6},{4,0},{6,2},{8,12},{10,14},{12,8},{14,10},{1,5},{3,7},... | collective-permute-start | bytes 393224 | tf_op jit(solution)/shard_map/ppermute | solution.py:529
  28.1 0.7 %collective-permute-start.6 = (bf16[2,128,256]{2,1,0:T(8,128)(2,1)S(1)}, bf16[2,128,256]{2,1,0:T(8,128)(2,1)S(1)}, u32[]{:S(2)}, u32[]{:S(2)}) collective-permute-start(bf16[2,128,256]{2,1,0:T(8,128)(2,1)S(1)} %get-tuple-element.106), channel_id=1, source_target_pairs={{0,2},{2,0},{4,6},{6,4},{8,10},{10,8},{12,14},{14,12},{1,3},{3,1},... | collective-permute-start | bytes 393224 | tf_op jit(solution)/shard_map/ppermute | solution.py:529
  28.8 2.2 %collective-permute-done.7 = bf16[2,128,256]{2,1,0:T(8,128)(2,1)S(1)} collective-permute-done((bf16[2,128,256]{2,1,0:T(8,128)(2,1)S(1)}, bf16[2,128,256]{2,1,0:T(8,128)(2,1)S(1)}, u32[]{:S(2)}, u32[]{:S(2)}) %collective-permute-start.7) | collective-permute-done | bytes 131104 | tf_op jit(solution)/shard_map/ppermute | solution.py:529
  31.0 0.0 copy-start
  31.0 0.3 collective-permute-start.8
  31.4 1.0 %collective-permute-done.11 = bf16[2,128,256]{2,1,0:T(8,128)(2,1)S(1)} collective-permute-done((bf16[2,128,256]{2,1,0:T(8,128)(2,1)S(1)}, bf16[2,128,256]{2,1,0:T(8,128)(2,1)S(1)}, u32[]{:S(2)}, u32[]{:S(2)}) %collective-permute-start.11) | collective-permute-done | bytes 131104 | tf_op jit(solution)/shard_map/ppermute | solution.py:529
  32.4 1.8 %collective-permute-start.12 = (bf16[2,128,256]{2,1,0:T(8,128)(2,1)S(1)}, bf16[2,128,256]{2,1,0:T(8,128)(2,1)S(1)}, u32[]{:S(2)}, u32[]{:S(2)}) collective-permute-start(bf16[2,128,256]{2,1,0:T(8,128)(2,1)S(1)} %add_convert_fusion.1), channel_id=1, source_target_pairs={{0,2},{2,0},{4,6},{6,4},{8,10},{10,8},{12,14},{14,12},{1,3},{3,1},... | collective-permute-start | bytes 393224 | tf_op jit(solution)/shard_map/ppermute | solution.py:529
  34.2 0.3 collective-permute-start.10
  34.5 2.1 %collective-permute-done.8 = bf16[2,128,256]{2,1,0:T(8,128)(2,1)S(1)} collective-permute-done((bf16[2,128,256]{2,1,0:T(8,128)(2,1)S(1)}, bf16[2,128,256]{2,1,0:T(8,128)(2,1)S(1)}, u32[]{:S(2)}, u32[]{:S(2)}) %collective-permute-start.8) | collective-permute-done | bytes 131104 | tf_op jit(solution)/shard_map/ppermute | solution.py:529
  36.5 0.1 add_convert_fusion.3
  36.6 1.6 %collective-permute-start.9 = (bf16[1,128,256]{2,1,0:T(8,128)(2,1)S(1)}, bf16[1,128,256]{2,1,0:T(8,128)(2,1)S(1)}, u32[]{:S(2)}, u32[]{:S(2)}) collective-permute-start(bf16[1,128,256]{2,1,0:T(8,128)(2,1)S(1)} %slice.45), channel_id=1, source_target_pairs={{0,8},{2,10},{4,12},{6,14},{8,0},{10,2},{12,4},{14,6},{1,9},{3,11}... | collective-permute-start | bytes 196616 | tf_op jit(solution)/shard_map/ppermute | solution.py:529
  38.1 1.7 %collective-permute-done.10 = bf16[2,128,256]{2,1,0:T(8,128)(2,1)S(1)} collective-permute-done((bf16[2,128,256]{2,1,0:T(8,128)(2,1)S(1)}, bf16[2,128,256]{2,1,0:T(8,128)(2,1)S(1)}, u32[]{:S(2)}, u32[]{:S(2)}) %collective-permute-start.10) | collective-permute-done | bytes 131104 | tf_op jit(solution)/shard_map/ppermute | solution.py:529
  39.9 0.1 add_convert_fusion
  39.9 2.2 %collective-permute-done.9 = bf16[1,128,256]{2,1,0:T(8,128)(2,1)S(1)} collective-permute-done((bf16[1,128,256]{2,1,0:T(8,128)(2,1)S(1)}, bf16[1,128,256]{2,1,0:T(8,128)(2,1)S(1)}, u32[]{:S(2)}, u32[]{:S(2)}) %collective-permute-start.9) | collective-permute-done | bytes 65568 | tf_op jit(solution)/shard_map/ppermute | solution.py:529
  42.2 1.2 %collective-permute-start.15 = (bf16[1,128,256]{2,1,0:T(8,128)(2,1)S(1)}, bf16[1,128,256]{2,1,0:T(8,128)(2,1)S(1)}, u32[]{:S(2)}, u32[]{:S(2)}) collective-permute-start(bf16[1,128,256]{2,1,0:T(8,128)(2,1)S(1)} %get-tuple-element.117), channel_id=1, source_target_pairs={{0,8},{2,10},{4,12},{6,14},{8,0},{10,2},{12,4},{14,6},{1,9},{3,11}... | collective-permute-start | bytes 196616 | tf_op jit(solution)/shard_map/ppermute | solution.py:529
  43.4 0.0 copy-start.1
  43.5 0.7 %collective-permute-start.13 = (bf16[2,32,256]{2,1,0:T(8,128)(2,1)S(1)}, bf16[2,32,256]{2,1,0:T(8,128)(2,1)S(1)}, u32[]{:S(2)}, u32[]{:S(2)}) collective-permute-start(bf16[2,32,256]{2,1,0:T(8,128)(2,1)S(1)} %get-tuple-element.124), channel_id=1, source_target_pairs={{0,2},{1,3},{2,0},{3,1},{4,6},{5,7},{6,4},{7,5},{8,10},{9,11},{10,... | collective-permute-start | bytes 98312 | tf_op jit(solution)/shard_map/ppermute | solution.py:574
  44.1 1.5 %collective-permute-start.14 = (bf16[2,32,256]{2,1,0:T(8,128)(2,1)S(1)}, bf16[2,32,256]{2,1,0:T(8,128)(2,1)S(1)}, u32[]{:S(2)}, u32[]{:S(2)}) collective-permute-start(bf16[2,32,256]{2,1,0:T(8,128)(2,1)S(1)} %get-tuple-element.123), channel_id=1, source_target_pairs={{0,16},{1,17},{2,4},{3,5},{4,2},{5,3},{6,8},{7,9},{8,6},{9,7},{10,... | collective-permute-start | bytes 98312 | tf_op jit(solution)/shard_map/ppermute | solution.py:574
  45.6 2.1 %collective-permute-done.15 = bf16[1,128,256]{2,1,0:T(8,128)(2,1)S(1)} collective-permute-done((bf16[1,128,256]{2,1,0:T(8,128)(2,1)S(1)}, bf16[1,128,256]{2,1,0:T(8,128)(2,1)S(1)}, u32[]{:S(2)}, u32[]{:S(2)}) %collective-permute-start.15) | collective-permute-done | bytes 65568 | tf_op jit(solution)/shard_map/ppermute | solution.py:529
  47.7 0.3 collective-permute-done.14
  48.2 0.1 collective-permute-start.16
  48.3 0.8 %own_columns.1.first_ref = f32[496,256]{1,0:T(8,128)S(1)} custom-call(bf16[12,32,256]{2,1,0:T(8,128)(2,1)S(1)} %select_dynamic-update-slice_fusion.lines_ref, bf16[3,3,256,256]{3,2,1,0:T(8,128)(2,1)S(1)} %copy-done), custom_call_target="tpu_custom_call" | custom-call | flops 585105408 | bytes 1015808 | tf_op jit(solution)/shard_map/own_columns/pallas_call | solution.py:459
  49.0 0.4 collective-permute-done.16
  49.5 1.9 %field_flow.1 = f32[8,32,256]{2,1,0:T(8,128)} custom-call(f32[496,256]{1,0:T(8,128)S(1)} %own_columns.1.first_ref, bf16[13,16,256]{2,1,0:T(8,128)(2,1)S(1)} %pad_add_fusion.sides_ref, bf16[3,3,256,256]{3,2,1,0:T(8,128)(2,1)S(1)} %copy-done, bf16[3,3,256,256]{3,2,1,0:T(8,128)(2,1)S(1)} %copy-done.1), custom_call_target="tpu_custom_call" | custom-call | tf_op jit(solution)/shard_map/field_flow/pallas_call | solution.py:516
  (29 shorter events, 0.3 us)
Async XLA Ops:
  0.0 4.8 %copy-start.2 = (bf16[512,512]{1,0:T(8,128)(2,1)S(1)}, bf16[512,512]{1,0:T(8,128)(2,1)}, u32[]{:S(2)}) copy-start(bf16[512,512]{1,0:T(8,128)(2,1)} %refs_2_.1) | copy-start | bytes 1572868
  0.0 4.8 %copy-start.3 = (bf16[512,256]{1,0:T(8,128)(2,1)S(1)}, bf16[512,256]{1,0:T(8,128)(2,1)}, u32[]{:S(2)}) copy-start(bf16[512,256]{1,0:T(8,128)(2,1)} %refs_3_.1) | copy-start | bytes 786436
  4.3 1.4 %collective-permute-start = (bf16[2,128,128]{2,1,0:T(8,128)(2,1)S(1)}, bf16[2,128,128]{2,1,0:T(8,128)(2,1)S(1)}, u32[]{:S(2)}, u32[]{:S(2)}) collective-permute-start(bf16[2,128,128]{2,1,0:T(8,128)(2,1)S(1)} %get-tuple-element.71), channel_id=1, source_target_pairs={{0,1},{1,0},{2,3},{3,2},{4,5},{5,4},{6,7},{7,6},{8,9},{9,8},{10,11... | collective-permute-start | bytes 196616 | tf_op jit(solution)/shard_map/ppermute | solution.py:546
  5.7 7.9 %collective-permute-start.1 = (bf16[2,128,128]{2,1,0:T(8,128)(2,1)S(1)}, bf16[2,128,128]{2,1,0:T(8,128)(2,1)S(1)}, u32[]{:S(2)}, u32[]{:S(2)}) collective-permute-start(bf16[2,128,128]{2,1,0:T(8,128)(2,1)S(1)} %get-tuple-element.81), channel_id=1, source_target_pairs={{0,2},{2,0},{4,6},{6,4},{8,10},{10,8},{12,14},{14,12},{1,3},{3,1},... | collective-permute-start | bytes 196616 | tf_op jit(solution)/shard_map/ppermute | solution.py:534
  8.7 5.0 %collective-permute-start.2 = (bf16[2,128,128]{2,1,0:T(8,128)(2,1)S(1)}, bf16[2,128,128]{2,1,0:T(8,128)(2,1)S(1)}, u32[]{:S(2)}, u32[]{:S(2)}) collective-permute-start(bf16[2,128,128]{2,1,0:T(8,128)(2,1)S(1)} %get-tuple-element.81), channel_id=1, source_target_pairs={{0,4},{2,6},{4,0},{6,2},{8,12},{10,14},{12,8},{14,10},{1,5},{3,7},... | collective-permute-start | bytes 196616 | tf_op jit(solution)/shard_map/ppermute | solution.py:534
  10.2 5.2 %collective-permute-start.3 = (bf16[2,128,128]{2,1,0:T(8,128)(2,1)S(1)}, bf16[2,128,128]{2,1,0:T(8,128)(2,1)S(1)}, u32[]{:S(2)}, u32[]{:S(2)}) collective-permute-start(bf16[2,128,128]{2,1,0:T(8,128)(2,1)S(1)} %get-tuple-element.81), channel_id=1, source_target_pairs={{0,6},{2,4},{4,2},{6,0},{8,14},{10,12},{12,10},{14,8},{1,7},{3,5},... | collective-permute-start | bytes 196616 | tf_op jit(solution)/shard_map/ppermute | solution.py:534
  15.5 6.1 %collective-permute-start.4 = (bf16[2,128,128]{2,1,0:T(8,128)(2,1)S(1)}, bf16[2,128,128]{2,1,0:T(8,128)(2,1)S(1)}, u32[]{:S(2)}, u32[]{:S(2)}) collective-permute-start(bf16[2,128,128]{2,1,0:T(8,128)(2,1)S(1)} %get-tuple-element.91), channel_id=1, source_target_pairs={{0,8},{2,10},{4,12},{6,14},{8,0},{10,2},{12,4},{14,6},{1,9},{3,11}... | collective-permute-start | bytes 196616 | tf_op jit(solution)/shard_map/ppermute | solution.py:534
  21.6 1.3 %collective-permute-start.5 = (bf16[2,128,128]{2,1,0:T(8,128)(2,1)S(1)}, bf16[2,128,128]{2,1,0:T(8,128)(2,1)S(1)}, u32[]{:S(2)}, u32[]{:S(2)}) collective-permute-start(bf16[2,128,128]{2,1,0:T(8,128)(2,1)S(1)} %get-tuple-element.103), channel_id=1, source_target_pairs={{0,1},{1,0},{2,3},{3,2},{4,5},{5,4},{6,7},{7,6},{8,9},{9,8},{10,11... | collective-permute-start | bytes 196616 | tf_op jit(solution)/shard_map/ppermute | solution.py:546
  21.7 1.2 %copy-start.4 = (s32[2048]{0:T(1024)S(1)}, s32[2048]{0:T(1024)}, u32[]{:S(2)}) copy-start(s32[2048]{0:T(1024)} %param.15) | copy-start | bytes 24580
  21.7 1.2 %copy-start.5 = (s32[16,1]{0,1:T(1,128)S(1)}, s32[16,1]{0,1:T(1,128)}, u32[]{:S(2)}) copy-start(s32[16,1]{0,1:T(1,128)} %param.14) | copy-start | bytes 196
  24.9 6.1 %collective-permute-start.7 = (bf16[2,128,256]{2,1,0:T(8,128)(2,1)S(1)}, bf16[2,128,256]{2,1,0:T(8,128)(2,1)S(1)}, u32[]{:S(2)}, u32[]{:S(2)}) collective-permute-start(bf16[2,128,256]{2,1,0:T(8,128)(2,1)S(1)} %get-tuple-element.109), channel_id=1, source_target_pairs={{0,2},{2,0},{4,6},{6,4},{8,10},{10,8},{12,14},{14,12},{1,3},{3,1},... | collective-permute-start | bytes 393224 | tf_op jit(solution)/shard_map/ppermute | solution.py:529
  26.8 5.6 %collective-permute-start.11 = (bf16[2,128,256]{2,1,0:T(8,128)(2,1)S(1)}, bf16[2,128,256]{2,1,0:T(8,128)(2,1)S(1)}, u32[]{:S(2)}, u32[]{:S(2)}) collective-permute-start(bf16[2,128,256]{2,1,0:T(8,128)(2,1)S(1)} %get-tuple-element.114), channel_id=1, source_target_pairs={{0,4},{2,6},{4,0},{6,2},{8,12},{10,14},{12,8},{14,10},{1,5},{3,7},... | collective-permute-start | bytes 393224 | tf_op jit(solution)/shard_map/ppermute | solution.py:529
  28.1 6.4 %collective-permute-start.6 = (bf16[2,128,256]{2,1,0:T(8,128)(2,1)S(1)}, bf16[2,128,256]{2,1,0:T(8,128)(2,1)S(1)}, u32[]{:S(2)}, u32[]{:S(2)}) collective-permute-start(bf16[2,128,256]{2,1,0:T(8,128)(2,1)S(1)} %get-tuple-element.106), channel_id=1, source_target_pairs={{0,2},{2,0},{4,6},{6,4},{8,10},{10,8},{12,14},{14,12},{1,3},{3,1},... | collective-permute-start | bytes 393224 | tf_op jit(solution)/shard_map/ppermute | solution.py:529
  31.0 17.2 %copy-start = (bf16[3,3,256,256]{3,2,1,0:T(8,128)(2,1)S(1)}, bf16[3,3,256,256]{3,2,1,0:T(8,128)(2,1)}, u32[]{:S(2)}) copy-start(bf16[3,3,256,256]{3,2,1,0:T(8,128)(2,1)} %w1_ref.1) | copy-start | bytes 3538948
  31.0 5.5 %collective-permute-start.8 = (bf16[2,128,256]{2,1,0:T(8,128)(2,1)S(1)}, bf16[2,128,256]{2,1,0:T(8,128)(2,1)S(1)}, u32[]{:S(2)}, u32[]{:S(2)}) collective-permute-start(bf16[2,128,256]{2,1,0:T(8,128)(2,1)S(1)} %add_convert_fusion.4), channel_id=1, source_target_pairs={{0,4},{2,6},{4,0},{6,2},{8,12},{10,14},{12,8},{14,10},{1,5},{3,7},... | collective-permute-start | bytes 393224 | tf_op jit(solution)/shard_map/ppermute | solution.py:529
  32.4 5.7 %collective-permute-start.12 = (bf16[2,128,256]{2,1,0:T(8,128)(2,1)S(1)}, bf16[2,128,256]{2,1,0:T(8,128)(2,1)S(1)}, u32[]{:S(2)}, u32[]{:S(2)}) collective-permute-start(bf16[2,128,256]{2,1,0:T(8,128)(2,1)S(1)} %add_convert_fusion.1), channel_id=1, source_target_pairs={{0,2},{2,0},{4,6},{6,4},{8,10},{10,8},{12,14},{14,12},{1,3},{3,1},... | collective-permute-start | bytes 393224 | tf_op jit(solution)/shard_map/ppermute | solution.py:529
  34.2 5.7 %collective-permute-start.10 = (bf16[2,128,256]{2,1,0:T(8,128)(2,1)S(1)}, bf16[2,128,256]{2,1,0:T(8,128)(2,1)S(1)}, u32[]{:S(2)}, u32[]{:S(2)}) collective-permute-start(bf16[2,128,256]{2,1,0:T(8,128)(2,1)S(1)} %get-tuple-element.112), channel_id=1, source_target_pairs={{0,4},{2,6},{4,0},{6,2},{8,12},{10,14},{12,8},{14,10},{1,5},{3,7},... | collective-permute-start | bytes 393224 | tf_op jit(solution)/shard_map/ppermute | solution.py:529
  36.6 5.6 %collective-permute-start.9 = (bf16[1,128,256]{2,1,0:T(8,128)(2,1)S(1)}, bf16[1,128,256]{2,1,0:T(8,128)(2,1)S(1)}, u32[]{:S(2)}, u32[]{:S(2)}) collective-permute-start(bf16[1,128,256]{2,1,0:T(8,128)(2,1)S(1)} %slice.45), channel_id=1, source_target_pairs={{0,8},{2,10},{4,12},{6,14},{8,0},{10,2},{12,4},{14,6},{1,9},{3,11}... | collective-permute-start | bytes 196616 | tf_op jit(solution)/shard_map/ppermute | solution.py:529
  42.2 5.5 %collective-permute-start.15 = (bf16[1,128,256]{2,1,0:T(8,128)(2,1)S(1)}, bf16[1,128,256]{2,1,0:T(8,128)(2,1)S(1)}, u32[]{:S(2)}, u32[]{:S(2)}) collective-permute-start(bf16[1,128,256]{2,1,0:T(8,128)(2,1)S(1)} %get-tuple-element.117), channel_id=1, source_target_pairs={{0,8},{2,10},{4,12},{6,14},{8,0},{10,2},{12,4},{14,6},{1,9},{3,11}... | collective-permute-start | bytes 196616 | tf_op jit(solution)/shard_map/ppermute | solution.py:529
  43.4 6.0 %copy-start.1 = (bf16[3,3,256,256]{3,2,1,0:T(8,128)(2,1)S(1)}, bf16[3,3,256,256]{3,2,1,0:T(8,128)(2,1)}, u32[]{:S(2)}) copy-start(bf16[3,3,256,256]{3,2,1,0:T(8,128)(2,1)} %w2_ref.1) | copy-start | bytes 3538948
  43.5 4.3 %collective-permute-start.13 = (bf16[2,32,256]{2,1,0:T(8,128)(2,1)S(1)}, bf16[2,32,256]{2,1,0:T(8,128)(2,1)S(1)}, u32[]{:S(2)}, u32[]{:S(2)}) collective-permute-start(bf16[2,32,256]{2,1,0:T(8,128)(2,1)S(1)} %get-tuple-element.124), channel_id=1, source_target_pairs={{0,2},{1,3},{2,0},{3,1},{4,6},{5,7},{6,4},{7,5},{8,10},{9,11},{10,... | collective-permute-start | bytes 98312 | tf_op jit(solution)/shard_map/ppermute | solution.py:574
  44.1 3.9 %collective-permute-start.14 = (bf16[2,32,256]{2,1,0:T(8,128)(2,1)S(1)}, bf16[2,32,256]{2,1,0:T(8,128)(2,1)S(1)}, u32[]{:S(2)}, u32[]{:S(2)}) collective-permute-start(bf16[2,32,256]{2,1,0:T(8,128)(2,1)S(1)} %get-tuple-element.123), channel_id=1, source_target_pairs={{0,16},{1,17},{2,4},{3,5},{4,2},{5,3},{6,8},{7,9},{8,6},{9,7},{10,... | collective-permute-start | bytes 98312 | tf_op jit(solution)/shard_map/ppermute | solution.py:574
  48.2 1.2 %collective-permute-start.16 = (bf16[12,2,256]{2,1,0:T(2,128)(2,1)S(1)}, bf16[12,2,256]{2,1,0:T(2,128)(2,1)S(1)}, u32[]{:S(2)}, u32[]{:S(2)}) collective-permute-start(bf16[12,2,256]{2,1,0:T(2,128)(2,1)S(1)} %broadcast_select_fusion.4), channel_id=1, source_target_pairs={{0,1},{1,0},{2,3},{3,2},{4,5},{5,4},{6,7},{7,6},{8,9},{9,8},{10,11... | collective-permute-start | bytes 36872 | tf_op jit(solution)/shard_map/ppermute | solution.py:529

commit v11 on v9

--- a/solution.py
+++ b/solution.py
@@ -475,7 +475,7 @@
     )(lines, conv_first)
 
 
-def field_kernel(first_ref, sides_ref, w1_ref, w2_ref, out_ref, first, field):
+def field_kernel(first_ref, sides_ref, w1_ref, w2_ref, out_ref, first, field, flow, sems):
     count, channels = first.shape
     wide, narrow = lax.axis_index("wide"), lax.axis_index("narrow")
     first_line, last_line = wide == 0, wide == lax.axis_size("wide") - 1
@@ -505,9 +505,17 @@
         outside |= first_column & (at == r * LINE + GAP - 1)
         outside |= last_column & (at == (r + 1) * LINE)
     field[...] = jnp.where(outside, 0.0, inner).astype(BF16)
-    flow = convolve(field, w2_ref, LINE, BX * LINE + GAP)
-    for r in range(BX):
-        out_ref[r] = flow[r * LINE + GAP : (r + 1) * LINE]
+    half = BX // 2
+    copies = []
+    for n in range(2):
+        given = convolve(field, w2_ref, (1 + n * half) * LINE, half * LINE + GAP)
+        for r in range(half):
+            flow[n * half + r] = given[r * LINE + GAP : (r + 1) * LINE]
+        lines = pl.ds(n * half, half)
+        copies.append(pltpu.make_async_copy(flow.at[lines], out_ref.at[lines], sems.at[n]))
+        copies[-1].start()
+    for copy in copies:
+        copy.wait()
 
 
 def field_flow(first, left, right, conv_first, conv_second):
@@ -519,9 +527,14 @@
     return pl.pallas_call(
         field_kernel,
         in_specs=[vmem] * 4,
-        out_specs=vmem,
+        out_specs=pl.BlockSpec(memory_space=pl.ANY),
         out_shape=jax.ShapeDtypeStruct((BX, BY, channels), F32),
-        scratch_shapes=[pltpu.VMEM((count, channels), F32), pltpu.VMEM((count, channels), BF16)],
+        scratch_shapes=[
+            pltpu.VMEM((count, channels), F32),
+            pltpu.VMEM((count, channels), BF16),
+            pltpu.VMEM((BX, BY, channels), F32),
+            pltpu.SemaphoreType.DMA((2,)),
+        ],
         compiler_params=params(16 * 1024),
         name="field_flow",
     )(first, sides, conv_first, conv_second)

time: 52 us -> 52 us (level)
  no operation moved by 1% of the time
where the time goes in v11:
time: 52 us; the launch traced here: 51.4 us
  Pallas kernels  19.1 us (37%)
  starting transfers between devices  17.7 us (34%)
  waiting for transfers between devices  13.9 us (27%)
    ppermute x9, waiting for transfers between devices, swap(): return lax.ppermute(array, axis, [(i, i ^ 1 << bit) for i in range(count)])  11.7 us
    ppermute x9, starting transfers between devices, swap(): return lax.ppermute(array, axis, [(i, i ^ 1 << bit) for i in range(count)])  7.8 us
    ppermute x4, starting transfers between devices, swap_digit(): return lax.ppermute(array, axis, [(i, i ^ by << bit) for i in range(count)])  7.16 us
    pallas_call x2, Pallas kernels, local_attention(): pl.pallas_call(functools.partial(local_kernel, rows // BLK, before is Non...  6.77 us
    pallas_call x1, Pallas kernels, device_totals(): pl.pallas_call(functools.partial(totals_kernel, spans), in_specs=[hbm, hb...  4.27 us
    ppermute x2, starting transfers between devices, exchange_lines(): got.append(lax.ppermute(out, ('group', 'wide', 'narrow'), pairs))  2.19 us
    pallas_call x1, Pallas kernels, voxel_features(): pl.pallas_call(functools.partial(features_kernel, chosen, spans, cores),...  1.93 us
    pallas_call x1, Pallas kernels, field_flow(): pl.pallas_call(field_kernel, in_specs=[vmem] * 4, out_specs=pl.BlockSpec(...  1.9 us
  transfers between devices with their start and end apart: 17, of which 10 were waited for; matrix products, arithmetic and copies ran while one was open for 0% of the time, Pallas kernels for 21%

profile of v11, /device:TPU:0, one launch (start us, length us, event | category | flops | bytes accessed | tf_op | source)
XLA Modules:
  0.0 51.4 jit_solution(57374611508454206)
XLA Ops:
  0.0 4.3 %device_totals.1 = (bf16[1024,512]{1,0:T(8,128)(2,1)S(1)}, bf16[1024,512]{1,0:T(8,128)(2,1)S(1)}, bf16[512,512]{1,0:T(8,128)(2,1)S(1)}, bf16[512,512]{1,0:T(8,12...) custom-call(bf16[2048,512]{1,0:T(8,128)(2,1)} %x_ref.1, ...), custom_call_target="tpu_custom_call" | custom-call | tf_op jit(solution)/shard_map/device_totals/pallas_call | solution.py:100
  4.3 0.5 %collective-permute-start = (bf16[2,128,128]{2,1,0:T(8,128)(2,1)S(1)}, bf16[2,128,128]{2,1,0:T(8,128)(2,1)S(1)}, u32[]{:S(2)}, u32[]{:S(2)}) collective-permute-start(bf16[2,128,128]{2,1,0:T(8,128)(2,1)S(1)} %get-tuple-element.71), channel_id=1, source_target_pairs={{0,1},{1,0},{2,3},{3,2},{4,5},{5,4},{6,7},{7,6},{8,9},{9,8},{10,11... | collective-permute-start | bytes 196616 | tf_op jit(solution)/shard_map/ppermute | solution.py:562
  4.8 0.8 %direct_features.1 = (f32[1024,256]{1,0:T(8,128)S(1)}, f32[1024,256]{1,0:T(8,128)S(1)}, bf16[512,256]{1,0:T(8,128)(2,1)S(1)}) custom-call(bf16[1024,512]{1,0:T(8,128)(2,1)S(1)} %get-tuple-element.74.refs_0_.x_ref, bf16[1024,512]{1,0:T(8,128)(2,1)S(1)} %get-tuple-element.88.refs_1_.x_ref, bf16[512,512]{1,0:T(8,128)(2,1)S(1)} %copy-done.2, ...), custom_call_target="tpu_custom_call" | custom-call | flops 671088640 | bytes 4194304 | tf_op jit(solution)/shard_map/direct_features/pallas_call | solution.py:193
  5.7 0.0 collective-permute-done.refs_1_.refs_2_
  5.7 2.9 %collective-permute-start.1 = (bf16[2,128,128]{2,1,0:T(8,128)(2,1)S(1)}, bf16[2,128,128]{2,1,0:T(8,128)(2,1)S(1)}, u32[]{:S(2)}, u32[]{:S(2)}) collective-permute-start(bf16[2,128,128]{2,1,0:T(8,128)(2,1)S(1)} %get-tuple-element.81), channel_id=1, source_target_pairs={{0,2},{2,0},{4,6},{6,4},{8,10},{10,8},{12,14},{14,12},{1,3},{3,1},... | collective-permute-start | bytes 196616 | tf_op jit(solution)/shard_map/ppermute | solution.py:550
  8.7 1.6 %collective-permute-start.2 = (bf16[2,128,128]{2,1,0:T(8,128)(2,1)S(1)}, bf16[2,128,128]{2,1,0:T(8,128)(2,1)S(1)}, u32[]{:S(2)}, u32[]{:S(2)}) collective-permute-start(bf16[2,128,128]{2,1,0:T(8,128)(2,1)S(1)} %get-tuple-element.81), channel_id=1, source_target_pairs={{0,4},{2,6},{4,0},{6,2},{8,12},{10,14},{12,8},{14,10},{1,5},{3,7},... | collective-permute-start | bytes 196616 | tf_op jit(solution)/shard_map/ppermute | solution.py:550
  10.2 0.0 collective-permute-start.3
  10.2 3.4 %local_attention.2 = (bf16[1024,512]{1,0:T(8,128)(2,1)S(1)}, f32[1024,512]{1,0:T(8,128)S(1)}, f32[2,256,256]{2,1,0:T(8,128)S(1)}) custom-call(bf16[1024,512]{1,0:T(8,128)(2,1)S(1)} %get-tuple-element.74.refs_0_.x_ref, bf16[512,512]{1,0:T(8,128)(2,1)S(1)} %get-tuple-element.75.wq_ref, bf16[512,512]{1,0:T(8,128)(2,1)S(1)} %get-tuple-element.76.wk_ref, ...), custom_call_target="tpu_custom_call" | custom-call | flops 2415919104 | bytes 6291456 | tf_op jit(solution)/shard_map/local_attention/pallas_call | solution.py:165
  13.6 0.0 collective-permute-done.1.refs_0_
  13.6 0.0 collective-permute-done.2.refs_1_
  13.6 1.8 %collective-permute-done.3.refs_2_ = bf16[2,128,128]{2,1,0:T(8,128)(2,1)S(1)} collective-permute-done((bf16[2,128,128]{2,1,0:T(8,128)(2,1)S(1)}, bf16[2,128,128]{2,1,0:T(8,128)(2,1)S(1)}, u32[]{:S(2)}, u32[]{:S(2)}) %collective-permute-start.3) | collective-permute-done | bytes 65568 | tf_op jit(solution)/shard_map/ppermute | solution.py:550
  15.4 0.1 scan.1
  15.5 2.7 %collective-permute-start.4 = (bf16[2,128,128]{2,1,0:T(8,128)(2,1)S(1)}, bf16[2,128,128]{2,1,0:T(8,128)(2,1)S(1)}, u32[]{:S(2)}, u32[]{:S(2)}) collective-permute-start(bf16[2,128,128]{2,1,0:T(8,128)(2,1)S(1)} %get-tuple-element.91), channel_id=1, source_target_pairs={{0,8},{2,10},{4,12},{6,14},{8,0},{10,2},{12,4},{14,6},{1,9},{3,11}... | collective-permute-start | bytes 196616 | tf_op jit(solution)/shard_map/ppermute | solution.py:550
  18.1 3.4 %local_attention.3 = (bf16[1024,512]{1,0:T(8,128)(2,1)S(1)}, f32[1024,512]{1,0:T(8,128)S(1)}) custom-call(bf16[1024,512]{1,0:T(8,128)(2,1)S(1)} %get-tuple-element.88.refs_1_.x_ref, bf16[512,512]{1,0:T(8,128)(2,1)S(1)} %get-tuple-element.75.wq_ref, bf16[512,512]{1,0:T(8,128)(2,1)S(1)} %get-tuple-element.76.wk_ref, ...), custom_call_target="tpu_custom_call" | custom-call | flops 2415919104 | bytes 6291456 | tf_op jit(solution)/shard_map/local_attention/pallas_call | solution.py:165
  21.6 0.1 spread.1
  21.7 0.1 collective-permute-start.5
  21.7 0.0 copy-start.4
  21.7 0.0 copy-start.5
  21.8 1.1 %own_share.1 = (f32[1024,256]{1,0:T(8,128)S(1)}, f32[1024,256]{1,0:T(8,128)S(1)}) custom-call(bf16[2,128,128]{2,1,0:T(8,128)(2,1)S(1)} %get-tuple-element.97.state_ref, bf16[512,256]{1,0:T(8,128)(2,1)S(1)} %get-tuple-element.98.w_ref.refs_7_, bf16[1024,512]{1,0:T(8,128)(2,1)S(1)} %get-tuple-element.82.refs_0_, ...), custom_call_target="tpu_custom_call" | custom-call | flops 805306368 | bytes 4194304 | tf_op jit(solution)/shard_map/own_share/pallas_call | solution.py:299
  22.9 0.1 collective-permute-done.5.refs_6_
  23.0 1.9 %voxel_features.1 = (bf16[2048,256]{1,0:T(8,128)(2,1)S(1)}, bf16[2,128,256]{2,1,0:T(8,128)(2,1)S(1)}) custom-call(s32[16]{0:T(128)S(1)} %bitcast.7, bf16[1024,512]{1,0:T(8,128)(2,1)S(1)} %get-tuple-element.82.refs_0_, bf16[1024,512]{1,0:T(8,128)(2,1)S(1)} %get-tuple-element.92.refs_1_, f32[1024,512]{1,0:T(8,128)S(1)} %get-tuple-element.93.refs_2_, ...), custom_call_target="tpu_custom_call" | custom-call | tf_op jit(solution)/shard_map/voxel_features/pallas_call | solution.py:388
  24.9 0.6 %collective-permute-start.7 = (bf16[2,128,256]{2,1,0:T(8,128)(2,1)S(1)}, bf16[2,128,256]{2,1,0:T(8,128)(2,1)S(1)}, u32[]{:S(2)}, u32[]{:S(2)}) collective-permute-start(bf16[2,128,256]{2,1,0:T(8,128)(2,1)S(1)} %get-tuple-element.109), channel_id=1, source_target_pairs={{0,2},{2,0},{4,6},{6,4},{8,10},{10,8},{12,14},{14,12},{1,3},{3,1},... | collective-permute-start | bytes 393224 | tf_op jit(solution)/shard_map/ppermute | solution.py:545
  25.5 1.3 %pool.1 = (bf16[2,128,256]{2,1,0:T(8,128)(2,1)S(1)}, bf16[2,128,256]{2,1,0:T(8,128)(2,1)S(1)}, bf16[2,128,256]{2,1,0:T(8,128)(2,1)S(1)}, bf16[2,128,256]{2,1,0:T...) custom-call(s32[16]{0:T(128)S(1)} %bitcast.8, ...), custom_call_target="tpu_custom_call" | custom-call | flops 469762048 | bytes 1048576 | tf_op jit(solution)/shard_map/pool/pallas_call | solution.py:419
  26.8 0.0 copy-start
  26.8 1.3 %collective-permute-start.11 = (bf16[2,128,256]{2,1,0:T(8,128)(2,1)S(1)}, bf16[2,128,256]{2,1,0:T(8,128)(2,1)S(1)}, u32[]{:S(2)}, u32[]{:S(2)}) collective-permute-start(bf16[2,128,256]{2,1,0:T(8,128)(2,1)S(1)} %get-tuple-element.114), channel_id=1, source_target_pairs={{0,4},{2,6},{4,0},{6,2},{8,12},{10,14},{12,8},{14,10},{1,5},{3,7},... | collective-permute-start | bytes 393224 | tf_op jit(solution)/shard_map/ppermute | solution.py:545
  28.1 0.7 %collective-permute-start.6 = (bf16[2,128,256]{2,1,0:T(8,128)(2,1)S(1)}, bf16[2,128,256]{2,1,0:T(8,128)(2,1)S(1)}, u32[]{:S(2)}, u32[]{:S(2)}) collective-permute-start(bf16[2,128,256]{2,1,0:T(8,128)(2,1)S(1)} %get-tuple-element.106), channel_id=1, source_target_pairs={{0,2},{2,0},{4,6},{6,4},{8,10},{10,8},{12,14},{14,12},{1,3},{3,1},... | collective-permute-start | bytes 393224 | tf_op jit(solution)/shard_map/ppermute | solution.py:545
  28.8 2.2 %collective-permute-done.7 = bf16[2,128,256]{2,1,0:T(8,128)(2,1)S(1)} collective-permute-done((bf16[2,128,256]{2,1,0:T(8,128)(2,1)S(1)}, bf16[2,128,256]{2,1,0:T(8,128)(2,1)S(1)}, u32[]{:S(2)}, u32[]{:S(2)}) %collective-permute-start.7) | collective-permute-done | bytes 131104 | tf_op jit(solution)/shard_map/ppermute | solution.py:545
  31.0 0.3 collective-permute-start.8
  31.4 1.1 %collective-permute-done.11 = bf16[2,128,256]{2,1,0:T(8,128)(2,1)S(1)} collective-permute-done((bf16[2,128,256]{2,1,0:T(8,128)(2,1)S(1)}, bf16[2,128,256]{2,1,0:T(8,128)(2,1)S(1)}, u32[]{:S(2)}, u32[]{:S(2)}) %collective-permute-start.11) | collective-permute-done | bytes 131104 | tf_op jit(solution)/shard_map/ppermute | solution.py:545
  32.5 1.8 %collective-permute-start.12 = (bf16[2,128,256]{2,1,0:T(8,128)(2,1)S(1)}, bf16[2,128,256]{2,1,0:T(8,128)(2,1)S(1)}, u32[]{:S(2)}, u32[]{:S(2)}) collective-permute-start(bf16[2,128,256]{2,1,0:T(8,128)(2,1)S(1)} %add_convert_fusion.1), channel_id=1, source_target_pairs={{0,2},{2,0},{4,6},{6,4},{8,10},{10,8},{12,14},{14,12},{1,3},{3,1},... | collective-permute-start | bytes 393224 | tf_op jit(solution)/shard_map/ppermute | solution.py:545
  34.2 0.3 collective-permute-start.10
  34.5 2.0 %collective-permute-done.8 = bf16[2,128,256]{2,1,0:T(8,128)(2,1)S(1)} collective-permute-done((bf16[2,128,256]{2,1,0:T(8,128)(2,1)S(1)}, bf16[2,128,256]{2,1,0:T(8,128)(2,1)S(1)}, u32[]{:S(2)}, u32[]{:S(2)}) %collective-permute-start.8) | collective-permute-done | bytes 131104 | tf_op jit(solution)/shard_map/ppermute | solution.py:545
  36.5 0.1 add_convert_fusion.3
  36.5 1.6 %collective-permute-start.9 = (bf16[1,128,256]{2,1,0:T(8,128)(2,1)S(1)}, bf16[1,128,256]{2,1,0:T(8,128)(2,1)S(1)}, u32[]{:S(2)}, u32[]{:S(2)}) collective-permute-start(bf16[1,128,256]{2,1,0:T(8,128)(2,1)S(1)} %slice.45), channel_id=1, source_target_pairs={{0,8},{2,10},{4,12},{6,14},{8,0},{10,2},{12,4},{14,6},{1,9},{3,11}... | collective-permute-start | bytes 196616 | tf_op jit(solution)/shard_map/ppermute | solution.py:545
  38.1 0.0 collective-permute-done.12
  38.1 1.8 %collective-permute-done.10 = bf16[2,128,256]{2,1,0:T(8,128)(2,1)S(1)} collective-permute-done((bf16[2,128,256]{2,1,0:T(8,128)(2,1)S(1)}, bf16[2,128,256]{2,1,0:T(8,128)(2,1)S(1)}, u32[]{:S(2)}, u32[]{:S(2)}) %collective-permute-start.10) | collective-permute-done | bytes 131104 | tf_op jit(solution)/shard_map/ppermute | solution.py:545
  39.9 0.1 add_convert_fusion
  40.0 2.2 %collective-permute-done.9 = bf16[1,128,256]{2,1,0:T(8,128)(2,1)S(1)} collective-permute-done((bf16[1,128,256]{2,1,0:T(8,128)(2,1)S(1)}, bf16[1,128,256]{2,1,0:T(8,128)(2,1)S(1)}, u32[]{:S(2)}, u32[]{:S(2)}) %collective-permute-start.9) | collective-permute-done | bytes 65568 | tf_op jit(solution)/shard_map/ppermute | solution.py:545
  42.2 1.2 %collective-permute-start.15 = (bf16[1,128,256]{2,1,0:T(8,128)(2,1)S(1)}, bf16[1,128,256]{2,1,0:T(8,128)(2,1)S(1)}, u32[]{:S(2)}, u32[]{:S(2)}) collective-permute-start(bf16[1,128,256]{2,1,0:T(8,128)(2,1)S(1)} %get-tuple-element.117), channel_id=1, source_target_pairs={{0,8},{2,10},{4,12},{6,14},{8,0},{10,2},{12,4},{14,6},{1,9},{3,11}... | collective-permute-start | bytes 196616 | tf_op jit(solution)/shard_map/ppermute | solution.py:545
  43.4 0.7 %collective-permute-start.13 = (bf16[2,32,256]{2,1,0:T(8,128)(2,1)S(1)}, bf16[2,32,256]{2,1,0:T(8,128)(2,1)S(1)}, u32[]{:S(2)}, u32[]{:S(2)}) collective-permute-start(bf16[2,32,256]{2,1,0:T(8,128)(2,1)S(1)} %get-tuple-element.124), channel_id=1, source_target_pairs={{0,2},{1,3},{2,0},{3,1},{4,6},{5,7},{6,4},{7,5},{8,10},{9,11},{10,... | collective-permute-start | bytes 98312 | tf_op jit(solution)/shard_map/ppermute | solution.py:590
  44.2 1.5 %collective-permute-start.14 = (bf16[2,32,256]{2,1,0:T(8,128)(2,1)S(1)}, bf16[2,32,256]{2,1,0:T(8,128)(2,1)S(1)}, u32[]{:S(2)}, u32[]{:S(2)}) collective-permute-start(bf16[2,32,256]{2,1,0:T(8,128)(2,1)S(1)} %get-tuple-element.123), channel_id=1, source_target_pairs={{0,16},{1,17},{2,4},{3,5},{4,2},{5,3},{6,8},{7,9},{8,6},{9,7},{10,... | collective-permute-start | bytes 98312 | tf_op jit(solution)/shard_map/ppermute | solution.py:590
  45.6 2.1 %collective-permute-done.15 = bf16[1,128,256]{2,1,0:T(8,128)(2,1)S(1)} collective-permute-done((bf16[1,128,256]{2,1,0:T(8,128)(2,1)S(1)}, bf16[1,128,256]{2,1,0:T(8,128)(2,1)S(1)}, u32[]{:S(2)}, u32[]{:S(2)}) %collective-permute-start.15) | collective-permute-done | bytes 65568 | tf_op jit(solution)/shard_map/ppermute | solution.py:545
  47.7 0.0 collective-permute-done.13
  47.8 0.3 collective-permute-done.14
  48.2 0.1 collective-permute-start.16
  48.3 0.8 %own_columns.1.first_ref = f32[496,256]{1,0:T(8,128)S(1)} custom-call(bf16[12,32,256]{2,1,0:T(8,128)(2,1)S(1)} %select_dynamic-update-slice_fusion.lines_ref, bf16[3,3,256,256]{3,2,1,0:T(8,128)(2,1)S(1)} %copy-done), custom_call_target="tpu_custom_call" | custom-call | flops 585105408 | bytes 1015808 | tf_op jit(solution)/shard_map/own_columns/pallas_call | solution.py:462
  49.0 0.4 collective-permute-done.16
  49.5 1.9 %field_flow.1 = f32[8,32,256]{2,1,0:T(8,128)} custom-call(f32[496,256]{1,0:T(8,128)S(1)} %own_columns.1.first_ref, bf16[13,16,256]{2,1,0:T(8,128)(2,1)S(1)} %pad_add_fusion.sides_ref, bf16[3,3,256,256]{3,2,1,0:T(8,128)(2,1)S(1)} %copy-done, bf16[3,3,256,256]{3,2,1,0:T(8,128)(2,1)S(1)} %copy-done.1), custom_call_target="tpu_custom_call" | custom-call | tf_op jit(solution)/shard_map/field_flow/pallas_call | solution.py:527
  (29 shorter events, 0.3 us)
Async XLA Ops:
  0.0 4.8 %copy-start.2 = (bf16[512,512]{1,0:T(8,128)(2,1)S(1)}, bf16[512,512]{1,0:T(8,128)(2,1)}, u32[]{:S(2)}) copy-start(bf16[512,512]{1,0:T(8,128)(2,1)} %refs_2_.1) | copy-start | bytes 1572868
  0.0 4.8 %copy-start.3 = (bf16[512,256]{1,0:T(8,128)(2,1)S(1)}, bf16[512,256]{1,0:T(8,128)(2,1)}, u32[]{:S(2)}) copy-start(bf16[512,256]{1,0:T(8,128)(2,1)} %refs_3_.1) | copy-start | bytes 786436
  4.3 1.4 %collective-permute-start = (bf16[2,128,128]{2,1,0:T(8,128)(2,1)S(1)}, bf16[2,128,128]{2,1,0:T(8,128)(2,1)S(1)}, u32[]{:S(2)}, u32[]{:S(2)}) collective-permute-start(bf16[2,128,128]{2,1,0:T(8,128)(2,1)S(1)} %get-tuple-element.71), channel_id=1, source_target_pairs={{0,1},{1,0},{2,3},{3,2},{4,5},{5,4},{6,7},{7,6},{8,9},{9,8},{10,11... | collective-permute-start | bytes 196616 | tf_op jit(solution)/shard_map/ppermute | solution.py:562
  5.7 7.9 %collective-permute-start.1 = (bf16[2,128,128]{2,1,0:T(8,128)(2,1)S(1)}, bf16[2,128,128]{2,1,0:T(8,128)(2,1)S(1)}, u32[]{:S(2)}, u32[]{:S(2)}) collective-permute-start(bf16[2,128,128]{2,1,0:T(8,128)(2,1)S(1)} %get-tuple-element.81), channel_id=1, source_target_pairs={{0,2},{2,0},{4,6},{6,4},{8,10},{10,8},{12,14},{14,12},{1,3},{3,1},... | collective-permute-start | bytes 196616 | tf_op jit(solution)/shard_map/ppermute | solution.py:550
  8.7 5.0 %collective-permute-start.2 = (bf16[2,128,128]{2,1,0:T(8,128)(2,1)S(1)}, bf16[2,128,128]{2,1,0:T(8,128)(2,1)S(1)}, u32[]{:S(2)}, u32[]{:S(2)}) collective-permute-start(bf16[2,128,128]{2,1,0:T(8,128)(2,1)S(1)} %get-tuple-element.81), channel_id=1, source_target_pairs={{0,4},{2,6},{4,0},{6,2},{8,12},{10,14},{12,8},{14,10},{1,5},{3,7},... | collective-permute-start | bytes 196616 | tf_op jit(solution)/shard_map/ppermute | solution.py:550
  10.2 5.2 %collective-permute-start.3 = (bf16[2,128,128]{2,1,0:T(8,128)(2,1)S(1)}, bf16[2,128,128]{2,1,0:T(8,128)(2,1)S(1)}, u32[]{:S(2)}, u32[]{:S(2)}) collective-permute-start(bf16[2,128,128]{2,1,0:T(8,128)(2,1)S(1)} %get-tuple-element.81), channel_id=1, source_target_pairs={{0,6},{2,4},{4,2},{6,0},{8,14},{10,12},{12,10},{14,8},{1,7},{3,5},... | collective-permute-start | bytes 196616 | tf_op jit(solution)/shard_map/ppermute | solution.py:550
  15.5 6.1 %collective-permute-start.4 = (bf16[2,128,128]{2,1,0:T(8,128)(2,1)S(1)}, bf16[2,128,128]{2,1,0:T(8,128)(2,1)S(1)}, u32[]{:S(2)}, u32[]{:S(2)}) collective-permute-start(bf16[2,128,128]{2,1,0:T(8,128)(2,1)S(1)} %get-tuple-element.91), channel_id=1, source_target_pairs={{0,8},{2,10},{4,12},{6,14},{8,0},{10,2},{12,4},{14,6},{1,9},{3,11}... | collective-permute-start | bytes 196616 | tf_op jit(solution)/shard_map/ppermute | solution.py:550
  21.7 1.3 %collective-permute-start.5 = (bf16[2,128,128]{2,1,0:T(8,128)(2,1)S(1)}, bf16[2,128,128]{2,1,0:T(8,128)(2,1)S(1)}, u32[]{:S(2)}, u32[]{:S(2)}) collective-permute-start(bf16[2,128,128]{2,1,0:T(8,128)(2,1)S(1)} %get-tuple-element.103), channel_id=1, source_target_pairs={{0,1},{1,0},{2,3},{3,2},{4,5},{5,4},{6,7},{7,6},{8,9},{9,8},{10,11... | collective-permute-start | bytes 196616 | tf_op jit(solution)/shard_map/ppermute | solution.py:562
  21.7 1.2 %copy-start.4 = (s32[2048]{0:T(1024)S(1)}, s32[2048]{0:T(1024)}, u32[]{:S(2)}) copy-start(s32[2048]{0:T(1024)} %param.15) | copy-start | bytes 24580
  21.7 1.2 %copy-start.5 = (s32[16,1]{0,1:T(1,128)S(1)}, s32[16,1]{0,1:T(1,128)}, u32[]{:S(2)}) copy-start(s32[16,1]{0,1:T(1,128)} %param.14) | copy-start | bytes 196
  24.9 6.1 %collective-permute-start.7 = (bf16[2,128,256]{2,1,0:T(8,128)(2,1)S(1)}, bf16[2,128,256]{2,1,0:T(8,128)(2,1)S(1)}, u32[]{:S(2)}, u32[]{:S(2)}) collective-permute-start(bf16[2,128,256]{2,1,0:T(8,128)(2,1)S(1)} %get-tuple-element.109), channel_id=1, source_target_pairs={{0,2},{2,0},{4,6},{6,4},{8,10},{10,8},{12,14},{14,12},{1,3},{3,1},... | collective-permute-start | bytes 393224 | tf_op jit(solution)/shard_map/ppermute | solution.py:545
  26.8 21.5 %copy-start = (bf16[3,3,256,256]{3,2,1,0:T(8,128)(2,1)S(1)}, bf16[3,3,256,256]{3,2,1,0:T(8,128)(2,1)}, u32[]{:S(2)}) copy-start(bf16[3,3,256,256]{3,2,1,0:T(8,128)(2,1)} %w1_ref.1) | copy-start | bytes 3538948
  26.8 5.6 %collective-permute-start.11 = (bf16[2,128,256]{2,1,0:T(8,128)(2,1)S(1)}, bf16[2,128,256]{2,1,0:T(8,128)(2,1)S(1)}, u32[]{:S(2)}, u32[]{:S(2)}) collective-permute-start(bf16[2,128,256]{2,1,0:T(8,128)(2,1)S(1)} %get-tuple-element.114), channel_id=1, source_target_pairs={{0,4},{2,6},{4,0},{6,2},{8,12},{10,14},{12,8},{14,10},{1,5},{3,7},... | collective-permute-start | bytes 393224 | tf_op jit(solution)/shard_map/ppermute | solution.py:545
  28.1 6.4 %collective-permute-start.6 = (bf16[2,128,256]{2,1,0:T(8,128)(2,1)S(1)}, bf16[2,128,256]{2,1,0:T(8,128)(2,1)S(1)}, u32[]{:S(2)}, u32[]{:S(2)}) collective-permute-start(bf16[2,128,256]{2,1,0:T(8,128)(2,1)S(1)} %get-tuple-element.106), channel_id=1, source_target_pairs={{0,2},{2,0},{4,6},{6,4},{8,10},{10,8},{12,14},{14,12},{1,3},{3,1},... | collective-permute-start | bytes 393224 | tf_op jit(solution)/shard_map/ppermute | solution.py:545
  31.0 5.4 %collective-permute-start.8 = (bf16[2,128,256]{2,1,0:T(8,128)(2,1)S(1)}, bf16[2,128,256]{2,1,0:T(8,128)(2,1)S(1)}, u32[]{:S(2)}, u32[]{:S(2)}) collective-permute-start(bf16[2,128,256]{2,1,0:T(8,128)(2,1)S(1)} %add_convert_fusion.4), channel_id=1, source_target_pairs={{0,4},{2,6},{4,0},{6,2},{8,12},{10,14},{12,8},{14,10},{1,5},{3,7},... | collective-permute-start | bytes 393224 | tf_op jit(solution)/shard_map/ppermute | solution.py:545
  32.5 5.7 %collective-permute-start.12 = (bf16[2,128,256]{2,1,0:T(8,128)(2,1)S(1)}, bf16[2,128,256]{2,1,0:T(8,128)(2,1)S(1)}, u32[]{:S(2)}, u32[]{:S(2)}) collective-permute-start(bf16[2,128,256]{2,1,0:T(8,128)(2,1)S(1)} %add_convert_fusion.1), channel_id=1, source_target_pairs={{0,2},{2,0},{4,6},{6,4},{8,10},{10,8},{12,14},{14,12},{1,3},{3,1},... | collective-permute-start | bytes 393224 | tf_op jit(solution)/shard_map/ppermute | solution.py:545
  34.2 5.7 %collective-permute-start.10 = (bf16[2,128,256]{2,1,0:T(8,128)(2,1)S(1)}, bf16[2,128,256]{2,1,0:T(8,128)(2,1)S(1)}, u32[]{:S(2)}, u32[]{:S(2)}) collective-permute-start(bf16[2,128,256]{2,1,0:T(8,128)(2,1)S(1)} %get-tuple-element.112), channel_id=1, source_target_pairs={{0,4},{2,6},{4,0},{6,2},{8,12},{10,14},{12,8},{14,10},{1,5},{3,7},... | collective-permute-start | bytes 393224 | tf_op jit(solution)/shard_map/ppermute | solution.py:545
  36.5 5.7 %collective-permute-start.9 = (bf16[1,128,256]{2,1,0:T(8,128)(2,1)S(1)}, bf16[1,128,256]{2,1,0:T(8,128)(2,1)S(1)}, u32[]{:S(2)}, u32[]{:S(2)}) collective-permute-start(bf16[1,128,256]{2,1,0:T(8,128)(2,1)S(1)} %slice.45), channel_id=1, source_target_pairs={{0,8},{2,10},{4,12},{6,14},{8,0},{10,2},{12,4},{14,6},{1,9},{3,11}... | collective-permute-start | bytes 196616 | tf_op jit(solution)/shard_map/ppermute | solution.py:545
  39.9 9.6 %copy-start.1 = (bf16[3,3,256,256]{3,2,1,0:T(8,128)(2,1)S(1)}, bf16[3,3,256,256]{3,2,1,0:T(8,128)(2,1)}, u32[]{:S(2)}) copy-start(bf16[3,3,256,256]{3,2,1,0:T(8,128)(2,1)} %w2_ref.1) | copy-start | bytes 3538948
  42.2 5.5 %collective-permute-start.15 = (bf16[1,128,256]{2,1,0:T(8,128)(2,1)S(1)}, bf16[1,128,256]{2,1,0:T(8,128)(2,1)S(1)}, u32[]{:S(2)}, u32[]{:S(2)}) collective-permute-start(bf16[1,128,256]{2,1,0:T(8,128)(2,1)S(1)} %get-tuple-element.117), channel_id=1, source_target_pairs={{0,8},{2,10},{4,12},{6,14},{8,0},{10,2},{12,4},{14,6},{1,9},{3,11}... | collective-permute-start | bytes 196616 | tf_op jit(solution)/shard_map/ppermute | solution.py:545
  43.4 4.3 %collective-permute-start.13 = (bf16[2,32,256]{2,1,0:T(8,128)(2,1)S(1)}, bf16[2,32,256]{2,1,0:T(8,128)(2,1)S(1)}, u32[]{:S(2)}, u32[]{:S(2)}) collective-permute-start(bf16[2,32,256]{2,1,0:T(8,128)(2,1)S(1)} %get-tuple-element.124), channel_id=1, source_target_pairs={{0,2},{1,3},{2,0},{3,1},{4,6},{5,7},{6,4},{7,5},{8,10},{9,11},{10,... | collective-permute-start | bytes 98312 | tf_op jit(solution)/shard_map/ppermute | solution.py:590
  44.2 3.9 %collective-permute-start.14 = (bf16[2,32,256]{2,1,0:T(8,128)(2,1)S(1)}, bf16[2,32,256]{2,1,0:T(8,128)(2,1)S(1)}, u32[]{:S(2)}, u32[]{:S(2)}) collective-permute-start(bf16[2,32,256]{2,1,0:T(8,128)(2,1)S(1)} %get-tuple-element.123), channel_id=1, source_target_pairs={{0,16},{1,17},{2,4},{3,5},{4,2},{5,3},{6,8},{7,9},{8,6},{9,7},{10,... | collective-permute-start | bytes 98312 | tf_op jit(solution)/shard_map/ppermute | solution.py:590
  48.2 1.2 %collective-permute-start.16 = (bf16[12,2,256]{2,1,0:T(2,128)(2,1)S(1)}, bf16[12,2,256]{2,1,0:T(2,128)(2,1)S(1)}, u32[]{:S(2)}, u32[]{:S(2)}) collective-permute-start(bf16[12,2,256]{2,1,0:T(2,128)(2,1)S(1)} %broadcast_select_fusion.4), channel_id=1, source_target_pairs={{0,1},{1,0},{2,3},{3,2},{4,5},{5,4},{6,7},{7,6},{8,9},{9,8},{10,11... | collective-permute-start | bytes 36872 | tf_op jit(solution)/shard_map/ppermute | solution.py:545
